TPU v7x, 32 devices: a whole 2x2x4 slice. The times are simulated.
32 devices in a mesh: rows: 4 (over y, x), blk: 4 (over z), rep: 2 (over core).
Axes of the slice: x: 2, y: 2, z: 4, core: 2. Of those that a mesh axis runs over, the one named last changes fastest.
Arguments:
- pair_left: bfloat16 [512, 64, 128], P(('rep', 'rows'), 'blk'), parts along dimension 0, may hold values from -6 to 6
- pair_right: bfloat16 [256, 64, 128], P(('rep', 'blk'), 'rows'), parts along dimension 0, may hold values from -6 to 6
- pair_middle: bfloat16 [512, 128, 128], P(('rep', 'rows'), 'blk'), parts along dimension 0, may hold values from -6 to 6
- cotangent: bfloat16 [512, 128, 128], P(('rep', 'rows'), 'blk'), parts along dimension 0, may hold values from -6 to 6
- left_weight: bfloat16 [128, 256], replicated, may hold values from -0.5 to 0.5
- right_weight: bfloat16 [128, 256], replicated, may hold values from -0.5 to 0.5
- gate_weight: bfloat16 [128, 128], replicated, may hold values from -0.5 to 0.5
- output_weight: bfloat16 [128, 128], replicated, may hold values from -0.5 to 0.5
Outputs:
- update: bfloat16 [512, 128, 128], P(('rep', 'rows'), 'blk'), parts along dimension 0
- grad_left: bfloat16 [512, 64, 128], P(('rep', 'rows'), 'blk'), parts along dimension 0
- grad_right: bfloat16 [256, 64, 128], P(('rep', 'blk'), 'rows'), parts along dimension 0
- grad_middle: bfloat16 [512, 128, 128], P(('rep', 'rows'), 'blk'), parts along dimension 0
- left_delta: float32 [256, 256], P('rep'), parts along dimension 0
- right_delta: float32 [256, 256], P('rep'), parts along dimension 0
- gate_delta: float32 [256, 128], P('rep'), parts along dimension 0
- output_delta: float32 [256, 128], P('rep'), parts along dimension 0
There are 2 independent parts, one for each index of `rep`. A program takes and returns all parts, laid end to end along the dimension named above; an argument that names none is the same for every part. Nothing has to cross between parts.
All inputs are finite; a program needn't handle non-finite values.
Results may differ from a plain program's by a relative error of at most 0.025.
Values may be sent and summed in bfloat16 or wider, within the bound.
No kernel may reach another device: no remote copies, remote signals or barrier semaphores. Data moves between devices by JAX's collectives and lax.ppermute only.
A program may use at most 64 MiB of HBM per device.

v0:
```python
import jax
import jax.numpy as jnp
from jax import lax
from jax.sharding import PartitionSpec as P

epsilon = 1e-05


def normalize(field):
    values = field.astype(jnp.float32)
    centred = values - jnp.mean(values, axis=-1, keepdims=True)
    inverse = lax.rsqrt(jnp.mean(centred * centred, axis=-1, keepdims=True) + epsilon)
    return (centred * inverse, inverse)


def normalize_back(normed, inverse, upstream):
    first = jnp.mean(upstream, axis=-1, keepdims=True)
    second = jnp.mean(upstream * normed, axis=-1, keepdims=True)
    return inverse * (upstream - first - normed * second)


def flat_dot(inputs, weight):
    flat = inputs.reshape(-1, inputs.shape[-1])
    result = jnp.dot(flat, weight, preferred_element_type=jnp.float32)
    return result.reshape(inputs.shape[:-1] + (weight.shape[1],))


def outer_sum(inputs, grads):
    flat_in = inputs.reshape(-1, inputs.shape[-1])
    flat_back = grads.reshape(-1, grads.shape[-1])
    return jnp.einsum("rc,rd->cd", flat_in, flat_back, preferred_element_type=jnp.float32)


def gated_project(inputs, weight):
    width = weight.shape[1] // 2
    mixed_cols = flat_dot(inputs, weight)
    linear = mixed_cols[..., :width]
    switch = jax.nn.sigmoid(mixed_cols[..., width:])
    return (switch * linear, switch, linear)


def gated_back(inputs, switch, linear, upstream, weight):
    back_linear = upstream * switch
    back_gate = upstream * linear * switch * (1.0 - switch)
    joined = jnp.concatenate([back_linear, back_gate], axis=-1).astype(jnp.bfloat16)
    input_term = jnp.einsum("...d,cd->...c", joined, weight, preferred_element_type=jnp.float32)
    return (outer_sum(inputs, joined), input_term)


def per_device(
    pair_left,
    pair_right,
    pair_middle,
    cotangent,
    left_weight,
    right_weight,
    gate_weight,
    output_weight,
):
    left_norm, left_inverse = normalize(pair_left)
    left_input = left_norm.astype(jnp.bfloat16)
    left_act, left_switch, left_linear = gated_project(left_input, left_weight)
    left_slab = left_act.astype(jnp.bfloat16)
    right_norm, right_inverse = normalize(pair_right)
    right_input = right_norm.astype(jnp.bfloat16)
    right_act, right_switch, right_linear = gated_project(right_input, right_weight)
    right_slab = right_act.astype(jnp.bfloat16)
    right_whole = lax.all_gather(right_slab, "rows", axis=1, tiled=True)
    left_whole = lax.all_gather(left_slab, "blk", axis=1, tiled=True)
    triangle = jnp.einsum(
        "ikc,jkc->ijc", left_whole, right_whole, preferred_element_type=jnp.float32
    )
    tri_norm, tri_inverse = normalize(triangle)
    tri_input = tri_norm.astype(jnp.bfloat16)
    middle_norm, middle_inverse = normalize(pair_middle)
    middle_input = middle_norm.astype(jnp.bfloat16)
    gate = jax.nn.sigmoid(flat_dot(middle_input, gate_weight))
    head = flat_dot(tri_input, output_weight)
    update = (gate * head).astype(jnp.bfloat16)
    upstream = cotangent.astype(jnp.float32)
    head_back = (upstream * gate).astype(jnp.bfloat16)
    pre_back = (upstream * head * gate * (1.0 - gate)).astype(jnp.bfloat16)
    output_part = outer_sum(tri_input, head_back)
    gate_part = outer_sum(middle_input, pre_back)
    middle_up = jnp.einsum("ijd,cd->ijc", pre_back, gate_weight, preferred_element_type=jnp.float32)
    grad_middle = normalize_back(middle_norm, middle_inverse, middle_up).astype(jnp.bfloat16)
    tri_up = jnp.einsum("ijd,cd->ijc", head_back, output_weight, preferred_element_type=jnp.float32)
    tri_back = normalize_back(tri_norm, tri_inverse, tri_up).astype(jnp.bfloat16)
    partner = right_whole
    left_sums = lax.psum_scatter(
        jnp.einsum("ijc,jkc->kic", tri_back, partner, preferred_element_type=jnp.float32).astype(
            jnp.bfloat16
        ),
        "blk",
        scatter_dimension=0,
        tiled=True,
    ).astype(jnp.float32)
    left_back = jnp.transpose(left_sums, (1, 0, 2))
    partner = left_whole
    right_sums = lax.psum_scatter(
        jnp.einsum("ijc,ikc->kjc", tri_back, partner, preferred_element_type=jnp.float32).astype(
            jnp.bfloat16
        ),
        "rows",
        scatter_dimension=0,
        tiled=True,
    ).astype(jnp.float32)
    right_back = jnp.transpose(right_sums, (1, 0, 2))
    left_part, left_up = gated_back(left_input, left_switch, left_linear, left_back, left_weight)
    right_part, right_up = gated_back(
        right_input, right_switch, right_linear, right_back, right_weight
    )
    grad_left = normalize_back(left_norm, left_inverse, left_up).astype(jnp.bfloat16)
    grad_right = normalize_back(right_norm, right_inverse, right_up).astype(jnp.bfloat16)
    left_delta, right_delta, gate_delta, output_delta = lax.psum(
        (left_part, right_part, gate_part, output_part), ("rows", "blk")
    )
    return (
        update,
        grad_left,
        grad_right,
        grad_middle,
        left_delta,
        right_delta,
        gate_delta,
        output_delta,
    )


def solution(mesh):
    placed = (
        P(("rep", "rows"), "blk", None),
        P(("rep", "blk"), "rows", None),
        P(("rep", "rows"), "blk", None),
        P(("rep", "rows"), "blk", None),
        P(),
        P(),
        P(),
        P(),
    )
    return jax.shard_map(
        per_device,
        mesh=mesh,
        in_specs=placed,
        out_specs=(
            P(("rep", "rows"), "blk", None),
            P(("rep", "rows"), "blk", None),
            P(("rep", "blk"), "rows", None),
            P(("rep", "rows"), "blk", None),
            P("rep", None),
            P("rep", None),
            P("rep", None),
            P("rep", None),
        ),
        check_vma=False,
    )
```

profile of v0, /device:TPU:0, one launch (start us, length us, event | category | flops | bytes accessed | tf_op | source)
XLA Modules:
  0.0 245.5 jit_solution(5224931673824884464)
XLA Ops:
  7.2 1.2 convert_reduce_fusion.1
  8.5 1.3 fusion.28
  9.8 1.4 fusion.58
  11.2 0.8 multiply_convert_fusion.2
  12.2 0.3 convert_reduce_fusion
  12.7 0.6 fusion.14
  13.5 1.4 fusion.4
  15.0 1.0 copy-done.4
  15.9 1.4 fusion.83
  18.2 0.7 copy-done.8
  18.9 16.4 %all_gather.6 = bf16[32,64,128]{2,1,0:T(8,128)(2,1)} all-gather(bf16[32,16,128]{2,1,0:T(8,128)(2,1)S(1)} %multiply_convert_fusion.3), channel_id=1, replica_groups=mesh['rows'=4,'blk'=4,'rep'=2] {'rows'}, dimensions={1}, use_global_device_ids=true | all-gather | bytes 655360 | tf_op jit(solution)/shard_map/all_gather | solution.py:68
  35.4 4.5 %copy.79 = bf16[32,64,128]{0,1,2:T(8,128)(2,1)S(1)} copy(bf16[32,64,128]{2,1,0:T(8,128)(2,1)} %all_gather.6) | data formatting | bytes 1048576 | tf_op jit(solution)/shard_map/all_gather | solution.py:68
  39.9 4.0 %copy.83 = f32[64,32,128]{0,1,2:T(8,128)} copy(f32[64,32,128]{2,1,0:T(8,128)} %get-tuple-element.29) | data formatting | bytes 2097152 | tf_op jit(solution)/shard_map/ijd,cd->ijc/dot_general | solution.py:87
  43.9 1.2 all-gather.2.cloned.1.call-done
  45.2 5.5 %copy.80 = bf16[64,64,128]{0,1,2:T(8,128)(2,1)} copy(bf16[64,64,128]{2,1,0:T(8,128)(2,1)} %all-gather.2.cloned.1.call-done) | data formatting | bytes 2097152 | tf_op jit(solution)/shard_map/all_gather | solution.py:69
  50.7 2.3 bitcast_reduce_fusion
  53.0 0.3 multiply_reduce_fusion.1
  53.4 1.2 copy-done.2
  54.6 0.6 multiply_reduce_fusion
  55.2 1.6 multiply_convert_fusion
  56.8 1.0 copy-done.3
  57.7 2.2 fusion.85
  59.9 3.0 %copy.88 = bf16[128,64,32]{0,1,2:T(8,128)(2,1)} copy(bf16[128,64,32]{1,2,0:T(8,128)(2,1)} %fusion.85) | data formatting | bytes 1048576 | tf_op jit(solution)/shard_map/ijc,ikc->kjc/dot_general | solution.py:101
  63.0 3.6 %copy.81 = bf16[64,32,128]{2,1,0:T(8,128)(2,1)} copy(bf16[64,32,128]{0,1,2:T(8,128)(2,1)} %get-tuple-element.19) | data formatting | bytes 1048576 | tf_op jit(solution)/shard_map/convert_element_type | solution.py:74
  66.8 3.3 %fusion.84 = bf16[128,64,64]{2,1,0:T(8,128)(2,1)} fusion(bf16[32,64,128]{0,1,2:T(8,128)(2,1)S(1)} %copy.79, bf16[64,32,128]{0,1,2:T(8,128)(2,1)} %copy-done.3), kind=kOutput, calls=%fused_computation.123 | convolution fusion | flops 33554432 | bytes 2097152 | tf_op jit(solution)/shard_map/ijc,jkc->kic/dot_general | solution.py:91
  70.1 5.4 %copy.86 = bf16[128,64,64]{0,1,2:T(8,128)(2,1)} copy(bf16[128,64,64]{2,1,0:T(8,128)(2,1)} %fusion.84) | data formatting | bytes 2097152 | tf_op jit(solution)/shard_map/ijc,jkc->kic/dot_general | solution.py:91
  75.5 2.3 fusion.18
  77.8 0.8 copy-done.14
  78.6 2.1 fusion.80
  81.0 0.7 copy.92
  81.7 2.7 %convolution_bitcast_fusion.3 = f32[128,128]{1,0:T(8,128)} fusion(bf16[64,32,128]{2,1,0:T(8,128)(2,1)} %copy-done.14, bf16[64,32,128]{2,1,0:T(8,128)(2,1)S(1)} %copy-done.7, f32[64,32]{1,0:T(8,128)S(1)} %copy.78, f32[64,32]{1,0:T(8,128)S(1)} %copy.76), kind=kOutput, calls=%fused_computation.23 | convolution fusion | flops 68157440 | bytes 1130496 | tf_op jit(solution)/shard_map/rc,rd->cd/dot_general | solution.py:31
  84.4 2.3 convolution_bitcast_fusion.2
  86.7 1.9 fusion.13
  88.7 1.2 reduce-scatter.5.cloned.1.call-done
  89.9 1.0 fusion.52
  90.9 1.0 convolution_bitcast_fusion
  92.0 0.4 fusion.82
  92.4 1.0 fusion.47
  93.4 26.1 %reduce-scatter.3.cloned.1.call-done = bf16[16,64,128]{2,0,1:T(8,128)(2,1)} async-done(((bf16[64,64,128]{2,0,1:T(8,128)(2,1)}), bf16[16,64,128]{2,0,1:T(8,128)(2,1)}) %reduce-scatter.3.cloned.1.call-update) | async-done | bytes 262160 | tf_op jit(solution)/shard_map/reduce_scatter | solution.py:90
  119.5 1.2 fusion.32
  120.6 1.2 convolution_bitcast_fusion.1
  121.9 0.8 fusion.81
  122.8 1.3 fusion.27
  124.1 108.8 %all-reduce.3.cloned.1.call-done = (f32[128,256]{1,0:T(8,128)}, f32[128,256]{1,0:T(8,128)}, f32[128,128]{1,0:T(8,128)}, f32[128,128]{1,0:T(8,128)}) async-done(((f32[128,256]{1,0:T(8,128)}, f32[128,256]{1,0:T(8,128)}, f32[128,128]{1,0:T(8,128)}, f32[128,128]{1,0:T(8,128)}), (f32[128,256]{1,0:T(8,128)}, f32[128,256]{1,0:T(8,128)}, f32[128,128]{1,0:T(8,128)}, ...) | async-done | bytes 393232 | tf_op jit(solution)/shard_map/psum | solution.py:115
  232.8 1.6 copy.98
  234.4 1.6 copy.99
  236.0 1.5 copy.100
  237.5 1.5 copy.101
  (74 shorter events, 2.0 us)
Async XLA Ops:
  7.2 2.6 %copy-start = (bf16[128,256]{1,0:T(8,128)(2,1)S(1)}, bf16[128,256]{1,0:T(8,128)(2,1)}, u32[]{:S(2)}) copy-start(bf16[128,256]{1,0:T(8,128)(2,1)} %param.12) | copy-start | bytes 196612
  7.2 5.0 %copy-start.6 = (bf16[64,32,128]{2,1,0:T(8,128)(2,1)S(1)}, bf16[64,32,128]{2,1,0:T(8,128)(2,1)}, u32[]{:S(2)}) copy-start(bf16[64,32,128]{2,1,0:T(8,128)(2,1)} %param.10) | copy-start | bytes 1572868
  7.2 38.0 %all-gather.2.cloned.1.call-start = ((), (), s32[]{:S(2)}) async-start(), calls=%async_computation.2 | async-start | bytes 1310720 | tf_op jit(solution)/shard_map/all_gather | solution.py:69
  9.8 3.7 %copy-start.20 = (bf16[128,128]{1,0:T(8,128)(2,1)S(1)}, bf16[128,128]{1,0:T(8,128)(2,1)}, u32[]{:S(2)}) copy-start(bf16[128,128]{1,0:T(8,128)(2,1)} %param.14) | copy-start | bytes 98308
  12.1 77.8 %reduce-scatter.5.cloned.1.call-start = ((), (), s32[]{:S(2)}) async-start(), calls=%async_computation.4 | async-start | bytes 655360 | tf_op jit(solution)/shard_map/reduce_scatter | solution.py:100
  13.5 2.4 copy-start.11
  13.5 2.4 copy-start.16
  15.0 1.0 copy-start.4
  15.9 1.4 copy-start.15
  15.9 1.9 copy-start.18
  18.1 0.8 copy-start.8
  53.0 1.6 copy-start.2
  55.2 2.6 %copy-start.1 = (bf16[64,64,128]{0,1,2:T(8,128)(2,1)S(1)}, bf16[64,64,128]{0,1,2:T(8,128)(2,1)}, u32[]{:S(2)}) copy-start(bf16[64,64,128]{0,1,2:T(8,128)(2,1)} %copy.80) | copy-start | bytes 3145732
  56.8 1.0 copy-start.3
  66.6 52.9 %reduce-scatter.3.cloned.1.call-start = ((), (), s32[]{:S(2)}) async-start(), calls=%async_computation.3 | async-start | bytes 1310720 | tf_op jit(solution)/shard_map/reduce_scatter | solution.py:90
  70.1 5.4 %copy-start.5 = (f32[64,32,128]{2,1,0:T(8,128)S(1)}, f32[64,32,128]{2,1,0:T(8,128)}, u32[]{:S(2)}) copy-start(f32[64,32,128]{2,1,0:T(8,128)} %copy-done.4) | copy-start | bytes 3145732
  70.1 5.4 %copy-start.10 = (bf16[64,32,128]{2,1,0:T(8,128)(2,1)S(1)}, bf16[64,32,128]{2,1,0:T(8,128)(2,1)}, u32[]{:S(2)}) copy-start(bf16[64,32,128]{2,1,0:T(8,128)(2,1)} %copy.81) | copy-start | bytes 1572868
  75.5 3.2 %copy-start.7 = (bf16[64,32,128]{2,1,0:T(8,128)(2,1)S(1)}, bf16[64,32,128]{2,1,0:T(8,128)(2,1)}, u32[]{:S(2)}) copy-start(bf16[64,32,128]{2,1,0:T(8,128)(2,1)} %param.10) | copy-start | bytes 1572868
  75.5 3.2 %copy-start.21 = (bf16[128,128]{1,0:T(8,128)(2,1)S(1)}, bf16[128,128]{1,0:T(8,128)(2,1)}, u32[]{:S(2)}) copy-start(bf16[128,128]{1,0:T(8,128)(2,1)} %param.14) | copy-start | bytes 98308
  77.8 0.8 copy-start.14
  80.9 152.0 %all-reduce.3.cloned.1.call-start = ((), (), s32[]{:S(2)}) async-start(), calls=%async_computation.5 | async-start | bytes 786432 | tf_op jit(solution)/shard_map/psum | solution.py:115
  81.7 5.0 %copy-start.12 = (f32[64,32,128]{2,1,0:T(8,128)S(1)}, f32[64,32,128]{2,1,0:T(8,128)}, u32[]{:S(2)}) copy-start(f32[64,32,128]{2,1,0:T(8,128)} %get-tuple-element.32) | copy-start | bytes 3145732
  81.7 5.0 %copy-start.17 = (f32[64,32]{1,0:T(8,128)S(1)}, f32[64,32]{1,0:T(8,128)}, u32[]{:S(2)}) copy-start(f32[64,32]{1,0:T(8,128)} %copy.92) | copy-start | bytes 24580
  84.4 5.5 %copy-start.9 = (f32[32,16,256]{2,1,0:T(8,128)S(1)}, f32[32,16,256]{2,1,0:T(8,128)}, u32[]{:S(2)}) copy-start(f32[32,16,256]{2,1,0:T(8,128)} %copy-done.8) | copy-start | bytes 1572868
  86.7 5.3 %copy-start.19 = (bf16[128,256]{1,0:T(8,128)(2,1)S(1)}, bf16[128,256]{1,0:T(8,128)(2,1)}, u32[]{:S(2)}) copy-start(bf16[128,256]{1,0:T(8,128)(2,1)} %param.13) | copy-start | bytes 196612
  90.9 29.7 %copy-start.13 = (bf16[64,16,128]{2,1,0:T(8,128)(2,1)S(1)}, bf16[64,16,128]{2,1,0:T(8,128)(2,1)}, u32[]{:S(2)}) copy-start(bf16[64,16,128]{2,1,0:T(8,128)(2,1)} %param.8) | copy-start | bytes 786436
Sparse Core Ops, SparseCore 0:
  12.2 32.8 all-gather.1
  66.7 23.1 reduce-scatter.4
  92.3 27.1 reduce-scatter.2
  125.4 107.3 all-reduce.2
where the time goes:
time: 246 us; the launch traced here: 245 us
  waiting for transfers between devices  137 us (56%)
  local copies, waits for them, and re-layouts  38.1 us (15%)
  matrix products  25.1 us (10%)
  blocking collectives  16.4 us (7%)
  between operations  14.1 us (6%)
  other arithmetic  13.9 us (6%)
    psum x1, waiting for transfers between devices, per_device(): lax.psum((left_part, right_part, gate_part, output_part), ('rows', 'blk'))  109 us
    reduce_scatter x1, waiting for transfers between devices, per_device(): lax.psum_scatter(jnp.einsum('ijc,jkc->kic', tri_back, partner, preferred_...  26.1 us
    all_gather x1, blocking collectives, per_device(): right_whole = lax.all_gather(right_slab, 'rows', axis=1, tiled=True)  16.4 us
    unnamed x48, local copies, waits for them, and re-layouts  10.9 us
    dot_general x4, matrix products, outer_sum(): jnp.einsum('rc,rd->cd', flat_in, flat_back, preferred_element_type=jnp.fl...  7.26 us
    all_gather x1, local copies, waits for them, and re-layouts, per_device(): left_whole = lax.all_gather(left_slab, 'blk', axis=1, tiled=True)  5.48 us
    dot_general x4, matrix products, flat_dot(): result = jnp.dot(flat, weight, preferred_element_type=jnp.float32)  5.47 us
    dot_general x1, local copies, waits for them, and re-layouts, per_device(): jnp.einsum('ijc,jkc->kic', tri_back, partner, preferred_element_type=jnp....  5.37 us
  transfers between devices with their start and end apart: 4, of which 4 were waited for; matrix products, arithmetic and copies ran while one was open for 16% of the time, Pallas kernels for 0%

commit v1 on v0

v1 whole, which is shorter than its diff:
```python
import functools
import math

import jax
import jax.numpy as jnp
from jax import lax
from jax.experimental import pallas as pl
from jax.experimental.pallas import tpu as pltpu
from jax.sharding import PartitionSpec as P

epsilon = 1e-05
f32 = jnp.float32
bf16 = jnp.bfloat16
SCOPED = 6 * 1024 * 1024


def normalize(values):
    centred = values - jnp.mean(values, axis=-1, keepdims=True)
    inverse = lax.rsqrt(jnp.mean(centred * centred, axis=-1, keepdims=True) + epsilon)
    return (centred * inverse, inverse)


def normalize_back(normed, inverse, upstream):
    first = jnp.mean(upstream, axis=-1, keepdims=True)
    second = jnp.mean(upstream * normed, axis=-1, keepdims=True)
    return inverse * (upstream - first - normed * second)


def sigmoid(x):
    return 0.5 * jnp.tanh(0.5 * x) + 0.5


def dot(a, b):
    return lax.dot_general(a, b, (((1,), (0,)), ((), ())), preferred_element_type=f32)


def dot_nt(a, b):
    return lax.dot_general(a, b, (((1,), (1,)), ((), ())), preferred_element_type=f32)


def dot_tn(a, b):
    return lax.dot_general(a, b, (((0,), (0,)), ((), ())), preferred_element_type=f32)


def gated(inputs, weight):
    pre = dot(inputs, weight)
    width = weight.shape[1] // 2
    return pre[:, :width], sigmoid(pre[:, width:])


def joined_grad(back, lin, sw):
    return jnp.concatenate([back * sw, back * lin * sw * (1.0 - sw)], axis=-1).astype(bf16)


def middle_kernel(middle, cotangent, gate_weight, output_weight, gate, middle_in, head_back, tri_up):
    n_i, n_j, width = middle.shape
    step = 8

    def body(at, _):
        rows = pl.ds(at * step, step)
        normed, _ = normalize(middle[rows].astype(f32).reshape(step * n_j, width))
        inputs = normed.astype(bf16)
        opened = sigmoid(dot(inputs, gate_weight[...]))
        back = (cotangent[rows].astype(f32).reshape(step * n_j, width) * opened).astype(bf16)
        gate[rows] = opened.reshape(step, n_j, width)
        middle_in[rows] = inputs.reshape(step, n_j, width)
        head_back[rows] = back.reshape(step, n_j, width)
        tri_up[rows] = dot_nt(back, output_weight[...]).reshape(step, n_j, width)
        return 0

    lax.fori_loop(0, n_i // step, body, 0, unroll=2)


def right_kernel(n_rows, n_blk, k_left, ids, *refs):
    raw, (weight, act_out, in_out, *flip_out) = refs[:n_rows], refs[n_rows:]
    n_j, k_right, width = raw[0].shape
    n_k = k_left * n_blk
    unit = math.gcd(k_left, k_right)
    step = 16
    for s in range(n_rows):

        def body(at, _, s=s):
            rows = pl.ds(at * step, step)
            normed, _ = normalize(raw[s][rows].astype(f32).reshape(step * k_right, width))
            inputs = normed.astype(bf16)
            in_out[s, rows] = inputs.reshape(step, k_right, width)
            lin, sw = gated(inputs, weight[...])
            act = (sw * lin).astype(bf16).astype(f32).reshape(step, k_right, width)
            for part in range(k_right // unit):
                at_k = place(ids, n_rows, n_blk, k_left, k_right, s, part)
                for j in range(step):
                    start = pl.multiple_of((at * step + j) * n_k + at_k, unit)
                    act_out[pl.ds(start, unit), :] = act[j, part * unit : (part + 1) * unit]
            return 0

        lax.fori_loop(0, n_j // step, body, 0)

    for s in range(n_blk):

        def flip(k, _, s=s):
            flip_out[s][k] = act_out[pl.ds(s * k_left + k, n_j, stride=n_k), :]
            return 0

        lax.fori_loop(0, k_left, flip, 0, unroll=True)


def place(ids, n_rows, n_blk, k_left, k_right, piece, part):
    unit = math.gcd(k_left, k_right)
    vertex = lax.rem(ids[0] - piece + n_rows, n_rows) * k_right + part * unit
    block = vertex // k_left
    at = lax.rem(ids[1] - block + n_blk, n_blk) * k_left + vertex - block * k_left
    return pl.multiple_of(at, unit)


def project_left(raw, weight, act_out, in_out):
    n_i, k_left, width = raw.shape
    step = 8

    def body(at, _):
        rows = pl.ds(at * step, step)
        normed, _ = normalize(raw[rows].astype(f32).reshape(step * k_left, width))
        inputs = normed.astype(bf16)
        in_out[rows] = inputs.reshape(step, k_left, width)
        lin, sw = gated(inputs, weight[...])
        act_out[rows] = (sw * lin).astype(bf16).astype(f32).reshape(step, k_left, width)
        return 0

    lax.fori_loop(0, n_i // step, body, 0, unroll=2)


def add_vertices(total, rows, act, flip):
    for k in range(act.shape[1]):
        total = total + act[rows, k : k + 1, :] * flip[k][None]
    return total


def left_kernel(first, raw, weight, flip, *refs):
    total_in, (act_out, in_out, total_out) = refs[: 0 if first else 1], refs[0 if first else 1 :]
    n_i, n_j, width = total_out.shape
    step = 8
    project_left(raw, weight, act_out, in_out)

    def body(at, _):
        rows = pl.ds(at * step, step)
        total = jnp.zeros((step, n_j, width), f32) if first else total_in[0][rows]
        total_out[rows] = add_vertices(total, rows, act_out, flip)
        return 0

    lax.fori_loop(0, n_i // step, body, 0)


def triangle_kernel(
    has_total, raw, left_w, flip, out_w, gate, middle_in, head_back, tri_up, cotangent, *refs
):
    total_in, refs = refs[: 1 if has_total else 0], refs[1 if has_total else 0 :]
    act_out, in_out, update, pre_back, tri_back, gate_part, output_part = refs
    n_i, n_j, width = update.shape
    step = 8
    project_left(raw, left_w, act_out, in_out)
    gate_part[...] = jnp.zeros_like(gate_part)
    output_part[...] = jnp.zeros_like(output_part)

    def triangle_rows(at, _):
        rows = pl.ds(at * step, step)
        total = total_in[0][rows] if has_total else jnp.zeros((step, n_j, width), f32)
        total = add_vertices(total, rows, act_out, flip)
        flat = step * n_j
        normed, inverse = normalize(total.reshape(flat, width))
        tri_in = normed.astype(bf16)
        head = dot(tri_in, out_w[...])
        opened = gate[rows].reshape(flat, width)
        update[rows] = (opened * head).astype(bf16).reshape(step, n_j, width)
        upstream = cotangent[rows].astype(f32).reshape(flat, width)
        pre = (upstream * head * opened * (1.0 - opened)).astype(bf16)
        pre_back[rows] = pre.reshape(step, n_j, width)
        gate_part[...] += dot_tn(middle_in[rows].reshape(flat, width), pre)
        output_part[...] += dot_tn(tri_in, head_back[rows].reshape(flat, width))
        back = normalize_back(normed, inverse, tri_up[rows].reshape(flat, width))
        tri_back[rows] = back.astype(bf16).astype(f32).reshape(step, n_j, width)
        return 0

    lax.fori_loop(0, n_i // step, triangle_rows, 0, unroll=2)


def vertex_step(n_k, unit):
    size = unit
    while size * 2 <= 64 and n_k % (size * 2) == 0:
        size *= 2
    return size


def left_back_kernel(tri_back, right_act, *left_out):
    n_i, n_j, width = tri_back.shape
    k_left = left_out[0].shape[1]
    n_k = k_left * len(left_out)
    few = 4
    k_step = vertex_step(n_k, k_left)
    for k0 in range(0, n_k, k_step):

        def rows_sum(at, _, k0=k0):
            rows = pl.ds(at * few, few)
            total = jnp.zeros((few, k_step, width), f32)
            for j in range(n_j):
                start = j * n_k + k0
                total = total + tri_back[rows, j : j + 1, :] * right_act[start : start + k_step, :][None]
            total = total.astype(bf16)
            for s in range(k0 // k_left, (k0 + k_step) // k_left):
                left_out[s][rows] = total[:, s * k_left - k0 : (s + 1) * k_left - k0]
            return 0

        lax.fori_loop(0, n_i // few, rows_sum, 0)


def right_back_kernel(n_rows, n_blk, ids, tri_back, *refs):
    left_act, refs = refs[:n_blk], refs[n_blk + 1 :]
    right_out, (right_sum,) = refs[:n_rows], refs[n_rows:]
    n_i, n_j, width = tri_back.shape
    k_left = left_act[0].shape[1]
    n_k = k_left * n_blk
    k_right = right_out[0].shape[1]
    unit = math.gcd(k_left, k_right)
    few = 4
    k_step = vertex_step(n_k, k_left)
    for k0 in range(0, n_k, k_step):
        blocks = range(k0 // k_left, (k0 + k_step) // k_left)

        def rows_sum(at, _, k0=k0, blocks=blocks):
            eight = pl.ds(pl.multiple_of(at * 8, 8), 8)
            for half in range(0, 8, few):

                def add(i, totals):
                    some = tri_back[i, eight, :][half : half + few][:, None]
                    return tuple(
                        total + some * left_act[s][i][None] for s, total in zip(blocks, totals)
                    )

                zeros = tuple(jnp.zeros((few, k_left, width), f32) for _ in blocks)
                totals = lax.fori_loop(0, n_i, add, zeros, unroll=16)
                for s, total in zip(blocks, totals):
                    right_sum[pl.ds(at * 8 + half, few), s * k_left : (s + 1) * k_left, :] = total.astype(bf16)
            return 0

        lax.fori_loop(0, n_j // 8, rows_sum, 0)
    for s in range(n_rows):
        for part in range(k_right // unit):
            right_out[s][:, part * unit : (part + 1) * unit, :] = right_sum[
                :, pl.ds(place(ids, n_rows, n_blk, k_left, k_right, s, part), unit), :
            ]


def weights_kernel(n_rows, n_blk, right_in, left_w, right_w, *refs):
    left_in, refs = refs[:n_blk], refs[n_blk:]
    left_out, refs = refs[:n_blk], refs[n_blk:]
    right_out, (left_part, right_part) = refs[:n_rows], refs[n_rows:]
    for inputs_ref, weight, backs, part in (
        (left_in, left_w, left_out, left_part),
        (right_in, right_w, right_out, right_part),
    ):
        part[...] = jnp.zeros_like(part)
        n, k, width = backs[0].shape
        step = 16
        flat = step * k
        for s, back_ref in enumerate(backs):

            def body(at, _, s=s, back_ref=back_ref, inputs_ref=inputs_ref, weight=weight, part=part, flat=flat, width=width):
                rows = pl.ds(at * step, step)
                inputs = (inputs_ref[s] if isinstance(inputs_ref, tuple) else inputs_ref.at[s])[rows].reshape(flat, width)
                lin, sw = gated(inputs, weight[...])
                back = back_ref[rows].reshape(flat, width).astype(f32)
                part[...] += dot_tn(inputs, joined_grad(back, lin, sw))
                return 0

            lax.fori_loop(0, n // step, body, 0, unroll=2)


def grad_middle_kernel(middle, pre_back, gate_weight, grad_middle):
    n_i, n_j, width = middle.shape
    step = 8

    def body(at, _):
        rows = pl.ds(at * step, step)
        flat = step * n_j
        normed, inverse = normalize(middle[rows].astype(f32).reshape(flat, width))
        up = dot_nt(pre_back[rows].reshape(flat, width), gate_weight[...])
        grad_middle[rows] = normalize_back(normed, inverse, up).astype(bf16).reshape(step, n_j, width)
        return 0

    lax.fori_loop(0, n_i // step, body, 0, unroll=2)


def side_kernel(n_left, n_right, *refs):
    left, right, left_w, right_w = refs[:4]
    left_back, refs = refs[4 : 4 + n_left], refs[4 + n_left :]
    right_back, refs = refs[:n_right], refs[n_right:]
    for raw, weight, backs, grad in (
        (left, left_w, left_back, refs[0]),
        (right, right_w, right_back, refs[1]),
    ):
        n, k, width = raw.shape
        step = 16
        flat = step * k

        def body(at, _, raw=raw, weight=weight, backs=backs, grad=grad, step=step, flat=flat, k=k, width=width):
            rows = pl.ds(at * step, step)
            normed, inverse = normalize(raw[rows].astype(f32).reshape(flat, width))
            lin, sw = gated(normed.astype(bf16), weight[...])
            back = backs[0][rows].astype(f32)
            for other in backs[1:]:
                back = back + other[rows].astype(f32)
            up = dot_nt(joined_grad(back.reshape(flat, width), lin, sw), weight[...])
            grad[rows] = normalize_back(normed, inverse, up).astype(bf16).reshape(step, k, width)
            return 0

        lax.fori_loop(0, n // step, body, 0, unroll=2)


def shift(x, axis, n, step):
    return lax.ppermute(x, axis, [(a, (a + step) % n) for a in range(n)])


def combine_kernel(blocks, *refs):
    refs[-1][...] = jnp.sum(blocks[...].astype(f32), axis=0).astype(bf16)


def sum_all(x, n, after):
    axes = ("rows", "blk")
    blocks = lax.all_to_all(x.reshape(n, -1, 128), axes, 0, 0)
    (total,) = call(combine_kernel, "combine", [shape(blocks.shape[1:], bf16)], after=len(after))(
        blocks, *after
    )
    whole = lax.all_to_all(jnp.broadcast_to(total[None], blocks.shape), axes, 0, 0)
    return whole.reshape(x.shape).astype(f32)


def shape(dims, kind):
    return jax.ShapeDtypeStruct(tuple(dims), kind)


def call(kernel, name, outs, scalars=0, scratch=(), after=0):
    def run(*operands):
        spaces = [pltpu.SMEM] * scalars + [pltpu.VMEM] * (len(operands) - scalars - after) + [pl.ANY] * after
        held = sum(math.prod(x.shape) * x.dtype.itemsize for x in scratch)
        return pl.pallas_call(
            kernel,
            in_specs=[pl.BlockSpec(memory_space=space) for space in spaces],
            out_specs=[pl.BlockSpec(memory_space=pltpu.VMEM)] * len(outs),
            out_shape=outs,
            scratch_shapes=list(scratch),
            compiler_params=pltpu.CompilerParams(vmem_limit_bytes=held + SCOPED),
            cost_estimate=pl.CostEstimate(flops=1000, bytes_accessed=1000, transcendentals=0),
            name=name,
        )(*operands)

    return run


def per_device(
    n_rows,
    n_blk,
    pair_left,
    pair_right,
    pair_middle,
    cotangent,
    left_weight,
    right_weight,
    gate_weight,
    output_weight,
):
    n_i, k_left, width = pair_left.shape
    n_j, k_right, _ = pair_right.shape
    n_k = k_left * n_blk
    left_raw = [pair_left] + [shift(pair_left, "blk", n_blk, s) for s in range(1, n_blk)]
    right_raw = [pair_right] + [shift(pair_right, "rows", n_rows, s) for s in range(1, n_rows)]
    middle_shape = (n_i, n_j, width)
    gate, middle_in, head_back, tri_up = call(
        middle_kernel,
        "middle",
        [shape(middle_shape, f32), shape(middle_shape, bf16), shape(middle_shape, bf16), shape(middle_shape, f32)],
    )(pair_middle, cotangent, gate_weight, output_weight)
    ids = jnp.stack([lax.axis_index("rows"), lax.axis_index("blk")]).astype(jnp.int32)
    right_act, right_in, *right_flip = call(
        functools.partial(right_kernel, n_rows, n_blk, k_left),
        "right",
        [shape((n_j * n_k, width), f32), shape((n_rows, n_j, k_right, width), bf16)]
        + [shape((k_left, n_j, width), f32)] * n_blk,
        scalars=1,
    )(ids, *right_raw, right_weight)
    left_act, left_in, total = [], [], []
    act_shape = shape(pair_left.shape, f32)
    in_shape = shape(pair_left.shape, bf16)
    for s in range(n_blk - 1):
        act, inputs, total = call(
            functools.partial(left_kernel, s == 0),
            "left",
            [act_shape, in_shape, shape(middle_shape, f32)],
        )(left_raw[s], left_weight, right_flip[s], *total)
        left_act.append(act)
        left_in.append(inputs)
        total = [total]
    act, inputs, update, pre_back, tri_back, gate_part, output_part = call(
        functools.partial(triangle_kernel, n_blk > 1),
        "triangle",
        [
            act_shape,
            in_shape,
            shape(middle_shape, bf16),
            shape(middle_shape, bf16),
            shape(middle_shape, f32),
            shape(gate_weight.shape, f32),
            shape(output_weight.shape, f32),
        ],
    )(
        left_raw[-1],
        left_weight,
        right_flip[-1],
        output_weight,
        gate,
        middle_in,
        head_back,
        tri_up,
        cotangent,
        *total,
    )
    left_act.append(act)
    left_in.append(inputs)
    left_out = call(left_back_kernel, "left_back", [shape(pair_left.shape, bf16)] * n_blk)(
        tri_back, right_act
    )
    left_back = [left_out[0]] + [shift(left_out[s], "blk", n_blk, n_blk - s) for s in range(1, n_blk)]
    right_out = call(
        functools.partial(right_back_kernel, n_rows, n_blk),
        "right_back",
        [shape(pair_right.shape, bf16)] * n_rows,
        scalars=1,
        scratch=[pltpu.VMEM((n_j, n_k, width), bf16)],
        after=1,
    )(ids, tri_back, *left_act, left_out[0])
    right_back = [right_out[0]] + [
        shift(right_out[s], "rows", n_rows, n_rows - s) for s in range(1, n_rows)
    ]
    left_part, right_part = call(
        functools.partial(weights_kernel, n_rows, n_blk),
        "weights",
        [shape(left_weight.shape, f32), shape(right_weight.shape, f32)],
    )(right_in, left_weight, right_weight, *left_in, *left_out, *right_out)
    parts = jnp.concatenate([left_part, right_part, gate_part, output_part], axis=1).astype(bf16)
    summed = sum_all(parts, n_rows * n_blk, (*left_back[1:], *right_back[1:]))
    (grad_middle,) = call(grad_middle_kernel, "grad_middle", [shape(middle_shape, bf16)])(
        pair_middle, pre_back, gate_weight
    )
    grad_left, grad_right = call(
        functools.partial(side_kernel, n_blk, n_rows),
        "sides",
        [shape(pair_left.shape, bf16), shape(pair_right.shape, bf16)],
    )(pair_left, pair_right, left_weight, right_weight, *left_back, *right_back)
    cuts = (2 * width, 4 * width, 5 * width)
    left_delta, right_delta, gate_delta, output_delta = jnp.split(summed, cuts, axis=1)
    return (
        update,
        grad_left,
        grad_right,
        grad_middle,
        left_delta,
        right_delta,
        gate_delta,
        output_delta,
    )


def solution(mesh):
    sides = P(("rep", "rows"), "blk", None)
    right = P(("rep", "blk"), "rows", None)
    return jax.shard_map(
        functools.partial(per_device, mesh.shape["rows"], mesh.shape["blk"]),
        mesh=mesh,
        in_specs=(sides, right, sides, sides, P(), P(), P(), P()),
        out_specs=(sides, sides, right, sides) + (P("rep", None),) * 4,
        check_vma=False,
    )
```

time: 246 us -> 106 us (0.43)
  waiting for transfers between devices: 137 us -> 23.6 us
  Pallas kernels: 0 us -> 44.4 us
  local copies, waits for them, and re-layouts: 38.1 us -> 7.55 us
  starting transfers between devices: 0.38 us -> 28.6 us
  matrix products: 25.1 us -> 0 us
  blocking collectives: 16.4 us -> 0 us
  other arithmetic: 13.9 us -> 0.13 us
  between operations: 14.1 us -> 0.91 us
    psum x1 -> x0, waiting for transfers between devices: 109 us -> none  [per_device(): lax.psum((left_part, right_part, gate_part, output_part), ('rows', 'blk'))]
    pallas_call x0 -> x12, Pallas kernels: none -> 44.4 us  [run(): pl.pallas_call(kernel, in_specs=[pl.BlockSpec(memory_space=space) for spa...]
    reduce_scatter x2 -> x0, waiting for transfers between devices: 27.3 us -> none  [the longest x1 26.1 us: per_device(): lax.psum_scatter(jnp.einsum('ijc,jkc->kic', tri_back, partner, preferred_...]
    dot_general x15 -> x0, matrix products: 25.1 us -> none  [the longest x4 7.26 us: outer_sum(): jnp.einsum('rc,rd->cd', flat_in, flat_back, preferred_element_type=jnp.fl...]
    ppermute x0 -> x12, waiting for transfers between devices: none -> 20.7 us  [shift(): return lax.ppermute(x, axis, [(a, (a + step) % n) for a in range(n)])]
    ppermute x0 -> x12, starting transfers between devices: none -> 18.9 us  [shift(): return lax.ppermute(x, axis, [(a, (a + step) % n) for a in range(n)])]
    all_gather x1 -> x0, blocking collectives: 16.4 us -> none  [per_device(): right_whole = lax.all_gather(right_slab, 'rows', axis=1, tiled=True)]
    dot_general x3 -> x0, local copies, waits for them, and re-layouts: 12.4 us -> none  [the longest x1 5.37 us: per_device(): jnp.einsum('ijc,jkc->kic', tri_back, partner, preferred_element_type=jnp....]
  transfers between devices with their start and end apart: 4 -> 14, of which waited for: 4 -> 3; matrix products, arithmetic and copies ran while one was open for 16% -> 0% of each run, Pallas kernels for 0% -> 20%
where the time goes in v1:
time: 106 us; the launch traced here: 105 us
  Pallas kernels  44.4 us (42%)
  starting transfers between devices  28.6 us (27%)
  waiting for transfers between devices  23.6 us (22%)
  local copies, waits for them, and re-layouts  7.55 us (7%)
    pallas_call x12, Pallas kernels, run(): pl.pallas_call(kernel, in_specs=[pl.BlockSpec(memory_space=space) for spa...  44.4 us
    ppermute x12, waiting for transfers between devices, shift(): return lax.ppermute(x, axis, [(a, (a + step) % n) for a in range(n)])  20.7 us
    ppermute x12, starting transfers between devices, shift(): return lax.ppermute(x, axis, [(a, (a + step) % n) for a in range(n)])  18.9 us
    all_to_all x1, starting transfers between devices, sum_all(): blocks = lax.all_to_all(x.reshape(n, -1, 128), axes, 0, 0)  5.79 us
    unnamed x32, local copies, waits for them, and re-layouts  4.45 us
    all_to_all x1, starting transfers between devices, sum_all(): lax.all_to_all(jnp.broadcast_to(total[None], blocks.shape), axes, 0, 0)  3.84 us
    all_to_all x1, waiting for transfers between devices, sum_all(): lax.all_to_all(jnp.broadcast_to(total[None], blocks.shape), axes, 0, 0)  2.98 us
  transfers between devices with their start and end apart: 14, of which 3 were waited for; matrix products, arithmetic and copies ran while one was open for 0% of the time, Pallas kernels for 20%

profile of v1, /device:TPU:0, one launch (start us, length us, event | category | flops | bytes accessed | tf_op | source)
XLA Modules:
  0.0 105.1 jit_solution(10201397468253984641)
XLA Ops:
  0.6 3.9 %collective-permute-start.3 = (bf16[32,16,128]{2,1,0:T(8,128)(2,1)}, bf16[32,16,128]{2,1,0:T(8,128)(2,1)S(1)}, u32[]{:S(2)}, u32[]{:S(2)}) collective-permute-start(bf16[32,16,128]{2,1,0:T(8,128)(2,1)} %refs_1_.1), channel_id=1, source_target_pairs={{0,24},{8,0},{16,8},{24,16},{1,25},{9,1},{17,9},{25,17},{2,26},{10... | collective-permute-start | bytes 393224 | tf_op jit(solution)/shard_map/ppermute | solution.py:318
  4.6 1.6 %collective-permute-start.5 = (bf16[64,16,128]{2,1,0:T(8,128)(2,1)}, bf16[64,16,128]{2,1,0:T(8,128)(2,1)}, u32[]{:S(2)}, u32[]{:S(2)}) collective-permute-start(bf16[64,16,128]{2,1,0:T(8,128)(2,1)} %refs_0_.3), channel_id=1, source_target_pairs={{0,2},{2,4},{4,6},{6,0},{1,3},{3,5},{5,7},{7,1},{8,10},{10,12},{12... | collective-permute-start | bytes 786440 | tf_op jit(solution)/shard_map/ppermute | solution.py:318
  6.2 2.6 %collective-permute-start.4 = (bf16[64,16,128]{2,1,0:T(8,128)(2,1)}, bf16[64,16,128]{2,1,0:T(8,128)(2,1)S(1)}, u32[]{:S(2)}, u32[]{:S(2)}) collective-permute-start(bf16[64,16,128]{2,1,0:T(8,128)(2,1)} %refs_0_.3), channel_id=1, source_target_pairs={{0,4},{2,6},{4,0},{6,2},{1,5},{3,7},{5,1},{7,3},{8,12},{10,14},{12... | collective-permute-start | bytes 786440 | tf_op jit(solution)/shard_map/ppermute | solution.py:318
  8.7 1.3 %collective-permute-start = (bf16[64,16,128]{2,1,0:T(8,128)(2,1)}, bf16[64,16,128]{2,1,0:T(8,128)(2,1)}, u32[]{:S(2)}, u32[]{:S(2)}) collective-permute-start(bf16[64,16,128]{2,1,0:T(8,128)(2,1)} %refs_0_.3), channel_id=1, source_target_pairs={{0,6},{2,0},{4,2},{6,4},{1,7},{3,1},{5,3},{7,5},{8,14},{10,8},{12,... | collective-permute-start | bytes 786440 | tf_op jit(solution)/shard_map/ppermute | solution.py:318
  10.1 0.5 collective-permute-start.2
  10.6 0.0 collective-permute-done.3.refs_3_
  10.6 0.6 collective-permute-start.1
  11.2 1.0 copy-done.1
  12.2 1.0 copy-done.3
  13.3 0.8 copy-done.12
  14.0 0.8 copy-done.14
  14.8 2.1 %middle.3 = (f32[64,32,128]{2,1,0:T(8,128)S(1)}, bf16[64,32,128]{2,1,0:T(8,128)(2,1)S(1)}, bf16[64,32,128]{2,1,0:T(8,128)(2,1)S(1)}, f32[64,32,128]{2,1,0:T(8,128)S(1)}) custom-call(bf16[64,32,128]{2,1,0:T(8,128)(2,1)S(1)} %copy-done.1, bf16[64,32,128]{2,1,0:T(8,128)(2,1)S(1)} %copy-done.3, bf16[128,128]{1,0:T(8,128)(2,1)S(1)} %copy-done.14, ...), custom_call_target="tpu_custom_call" | custom-call | flops 1000 | bytes 1000 | tf_op jit(solution)/shard_map/middle/pallas_call | solution.py:343
  16.9 0.8 copy-done.10
  17.7 0.1 pad_add_fusion.ids
  17.8 0.0 collective-permute-done.1.refs_1_
  17.8 4.4 %right.1 = (f32[2048,128]{1,0:T(8,128)S(1)}, bf16[4,32,16,128]{3,2,1,0:T(8,128)(2,1)S(1)}, f32[16,32,128]{2,1,0:T(8,128)S(1)}, f32[16,32,128]{2,1,0:T(8,128)S(1)...) custom-call(s32[2]{0:T(128)S(1)} %pad_add_fusion.ids, bf16[32,16,128]{2,1,0:T(8,128)(2,1)S(1)} %copy-done.7, ...), custom_call_target="tpu_custom_call" | custom-call | flops 1000 | bytes 1000 | tf_op jit(solution)/shard_map/right/pallas_call | solution.py:343
  22.3 2.5 %left.3 = (f32[64,16,128]{2,1,0:T(8,128)S(1)}, bf16[64,16,128]{2,1,0:T(8,128)(2,1)S(1)}, f32[64,32,128]{2,1,0:T(8,128)S(1)}) custom-call(bf16[64,16,128]{2,1,0:T(8,128)(2,1)S(1)} %copy-done.5, bf16[128,256]{1,0:T(8,128)(2,1)S(1)} %copy-done, f32[16,32,128]{2,1,0:T(8,128)S(1)} %get-tuple-element.53.flip), custom_call_target="tpu_custom_call" | custom-call | flops 1000 | bytes 1000 | tf_op jit(solution)/shard_map/left/pallas_call | solution.py:343
  24.8 0.0 collective-permute-done.5.raw
  24.8 3.6 %left.4 = (f32[64,16,128]{2,1,0:T(8,128)S(1)}, bf16[64,16,128]{2,1,0:T(8,128)(2,1)S(1)}, f32[64,32,128]{2,1,0:T(8,128)S(1)}) custom-call(bf16[64,16,128]{2,1,0:T(8,128)(2,1)} %collective-permute-done.5.raw, bf16[128,256]{1,0:T(8,128)(2,1)S(1)} %copy-done, f32[16,32,128]{2,1,0:T(8,128)S(1)} %get-tuple-element.52.flip, ...), custom_call_target="tpu_custom_call" | custom-call | flops 1000 | bytes 1000 | tf_op jit(solution)/shard_map/left/pallas_call | solution.py:343
  28.4 0.0 collective-permute-done.4.raw
  28.5 0.0 copy-start.4
  28.5 0.0 copy-start.9
  28.5 0.0 copy-start.11
  28.5 0.0 copy-start.13
  28.5 2.6 %left.5 = (f32[64,16,128]{2,1,0:T(8,128)S(1)}, bf16[64,16,128]{2,1,0:T(8,128)(2,1)S(1)}, f32[64,32,128]{2,1,0:T(8,128)S(1)}) custom-call(bf16[64,16,128]{2,1,0:T(8,128)(2,1)S(1)} %collective-permute-done.4.raw, bf16[128,256]{1,0:T(8,128)(2,1)S(1)} %copy-done, f32[16,32,128]{2,1,0:T(8,128)S(1)} %get-tuple-element.51.flip, ...), custom_call_target="tpu_custom_call" | custom-call | flops 1000 | bytes 1000 | tf_op jit(solution)/shard_map/left/pallas_call | solution.py:343
  31.1 0.0 collective-permute-done.raw
  31.2 6.4 %triangle.1 = (f32[64,16,128]{2,1,0:T(8,128)S(1)}, bf16[64,16,128]{2,1,0:T(8,128)(2,1)S(1)}, bf16[64,32,128]{2,1,0:T(8,128)(2,1)}, bf16[64,32,128]{2,1,0:T(8,128...) custom-call(bf16[64,16,128]{2,1,0:T(8,128)(2,1)} %collective-permute-done.raw, ...), custom_call_target="tpu_custom_call" | custom-call | flops 1000 | bytes 1000 | tf_op jit(solution)/shard_map/triangle/pallas_call | solution.py:343
  37.6 5.4 %left_back.1 = (bf16[64,16,128]{2,1,0:T(8,128)(2,1)S(1)}, bf16[64,16,128]{2,1,0:T(8,128)(2,1)}, bf16[64,16,128]{2,1,0:T(8,128)(2,1)S(1)}, bf16[64,16,128]{2,1,0:T(8,128)(2,1)S(1)}) custom-call(f32[64,32,128]{2,1,0:T(8,128)S(1)} %get-tuple-element.58.tri_back, f32[2048,128]{1,0:T(8,128)S(1)} %get-tuple-element.59.right_act), custom_call_target="tpu_custom_call" | custom-call | flops 1000 | bytes 1000 | tf_op jit(solution)/shard_map/left_back/pallas_call | solution.py:343
  42.9 6.7 %right_back.1 = (bf16[32,16,128]{2,1,0:T(8,128)(2,1)S(1)}, bf16[32,16,128]{2,1,0:T(8,128)(2,1)S(1)}, bf16[32,16,128]{2,1,0:T(8,128)(2,1)}, bf16[32,16,128]{2,1,0:T(8,128)(2,1)S(1)}) custom-call(s32[2]{0:T(128)S(1)} %pad_add_fusion.ids, f32[64,32,128]{2,1,0:T(8,128)S(1)} %get-tuple-element.58.tri_back, f32[64,16,128]{2,1,0:T(8,128)S(1)} %get-tuple-element.64.refs_0_, ...), custom_call_target="tpu_custom_call" | custom-call | flops 1000 | bytes 1000 | tf_op jit(solution)/shard_map/right_back/pallas_call | solution.py:343
  49.6 5.2 %weights.1 = (f32[128,256]{1,0:T(8,128)S(1)}, f32[128,256]{1,0:T(8,128)S(1)}) custom-call(bf16[4,32,16,128]{3,2,1,0:T(8,128)(2,1)S(1)} %get-tuple-element.75.right_in, bf16[128,256]{1,0:T(8,128)(2,1)S(1)} %copy-done, bf16[128,256]{1,0:T(8,128)(2,1)S(1)} %copy-done.6, bf16[64,16,128]{2,1,0:T(8,128)(2,1)S(1)} %get-tuple-element.76.refs_0_, ...), custom_call_target="tpu_custom_call" | custom-call | flops 1000 | bytes 1000 | tf_op jit(solution)/shard_map/weights/pallas_call | solution.py:343
  55.0 0.9 convert_element_type.11
  55.8 5.8 %all-to-all-start = ((bf16[16,48,128]{2,1,0:T(8,128)(2,1)}), bf16[16,48,128]{2,1,0:T(8,128)(2,1)S(1)}, u32[]{:S(2)}, u32[]{:S(2)}) async-start(bf16[16,48,128]{2,1,0:T(8,128)(2,1)} %convert_element_type.11), calls=%async_computation | async-start | bytes 393216 | tf_op jit(solution)/shard_map/all_to_all | solution.py:327
  61.6 2.8 %collective-permute-start.9 = (bf16[32,16,128]{2,1,0:T(8,128)(2,1)S(1)}, bf16[32,16,128]{2,1,0:T(8,128)(2,1)S(1)}, u32[]{:S(2)}, u32[]{:S(2)}) collective-permute-start(bf16[32,16,128]{2,1,0:T(8,128)(2,1)S(1)} %get-tuple-element.69.refs_9_), channel_id=1, source_target_pairs={{0,24},{8,0},{16,8},{24,16},{1,25},{9,1},{17,9},{25,17},{2,26},{10... | collective-permute-start | bytes 393224 | tf_op jit(solution)/shard_map/ppermute | solution.py:318
  64.5 3.3 %collective-permute-start.6 = (bf16[64,16,128]{2,1,0:T(8,128)(2,1)}, bf16[64,16,128]{2,1,0:T(8,128)(2,1)S(1)}, u32[]{:S(2)}, u32[]{:S(2)}) collective-permute-start(bf16[64,16,128]{2,1,0:T(8,128)(2,1)} %get-tuple-element.61.refs_5_), channel_id=1, source_target_pairs={{0,6},{2,0},{4,2},{6,4},{1,7},{3,1},{5,3},{7,5},{8,14},{10,8},{12,... | collective-permute-start | bytes 786440 | tf_op jit(solution)/shard_map/ppermute | solution.py:318
  67.7 1.1 %collective-permute-start.8 = (bf16[64,16,128]{2,1,0:T(8,128)(2,1)S(1)}, bf16[64,16,128]{2,1,0:T(8,128)(2,1)S(1)}, u32[]{:S(2)}, u32[]{:S(2)}) collective-permute-start(bf16[64,16,128]{2,1,0:T(8,128)(2,1)S(1)} %get-tuple-element.63.refs_7_), channel_id=1, source_target_pairs={{0,2},{2,4},{4,6},{6,0},{1,3},{3,5},{5,7},{7,1},{8,10},{10,12},{12... | collective-permute-start | bytes 786440 | tf_op jit(solution)/shard_map/ppermute | solution.py:318
  68.8 0.6 collective-permute-start.10
  69.4 0.6 collective-permute-start.11
  70.0 5.4 %collective-permute-done.10.refs_10_.refs_4_ = bf16[32,16,128]{2,1,0:T(8,128)(2,1)S(1)} collective-permute-done((bf16[32,16,128]{2,1,0:T(8,128)(2,1)}, bf16[32,16,128]{2,1,0:T(8,128)(2,1)S(1)}, u32[]{:S(2)}, u32[]{:S(2)}) %collective-permute-start.10) | collective-permute-done | bytes 131104 | tf_op jit(solution)/shard_map/ppermute | solution.py:318
  75.4 15.2 %collective-permute-done.7.refs_6_.refs_1_ = bf16[64,16,128]{2,1,0:T(8,128)(2,1)S(1)} collective-permute-done((bf16[64,16,128]{2,1,0:T(8,128)(2,1)S(1)}, bf16[64,16,128]{2,1,0:T(8,128)(2,1)S(1)}, u32[]{:S(2)}, u32[]{:S(2)}) %collective-permute-start.7) | collective-permute-done | bytes 262176 | tf_op jit(solution)/shard_map/ppermute | solution.py:318
  90.7 0.0 copy-start.2
  90.7 0.7 broadcast_in_dim.2
  91.4 3.8 %all-to-all-start.1 = ((bf16[16,48,128]{2,1,0:T(8,128)(2,1)}), bf16[16,48,128]{2,1,0:T(8,128)(2,1)S(1)}, u32[]{:S(2)}, u32[]{:S(2)}) async-start(bf16[16,48,128]{2,1,0:T(8,128)(2,1)} %broadcast_in_dim.2), calls=%async_computation.1 | async-start | bytes 393216 | tf_op jit(solution)/shard_map/all_to_all | solution.py:331
  95.3 2.4 %grad_middle.1 = bf16[64,32,128]{2,1,0:T(8,128)(2,1)} custom-call(bf16[64,32,128]{2,1,0:T(8,128)(2,1)S(1)} %copy-done.2, bf16[64,32,128]{2,1,0:T(8,128)(2,1)S(1)} %get-tuple-element.74.pre_back, bf16[128,128]{1,0:T(8,128)(2,1)S(1)} %copy-done.15), custom_call_target="tpu_custom_call" | custom-call | flops 1000 | bytes 1000 | tf_op jit(solution)/shard_map/grad_middle/pallas_call | solution.py:343
  97.7 2.9 %sides.1 = (bf16[64,16,128]{2,1,0:T(8,128)(2,1)}, bf16[32,16,128]{2,1,0:T(8,128)(2,1)}) custom-call(bf16[64,16,128]{2,1,0:T(8,128)(2,1)S(1)} %copy-done.5, bf16[32,16,128]{2,1,0:T(8,128)(2,1)S(1)} %copy-done.7, bf16[128,256]{1,0:T(8,128)(2,1)S(1)} %copy-done, bf16[128,256]{1,0:T(8,128)(2,1)S(1)} %copy-done.6, ...), custom_call_target="tpu_custom_call" | custom-call | flops 1000 | bytes 1000 | tf_op jit(solution)/shard_map/sides/pallas_call | solution.py:343
  100.6 3.0 %all-to-all-done.1 = bf16[16,48,128]{2,1,0:T(8,128)(2,1)S(1)} async-done(((bf16[16,48,128]{2,1,0:T(8,128)(2,1)}), bf16[16,48,128]{2,1,0:T(8,128)(2,1)S(1)}, u32[]{:S(2)}, u32[]{:S(2)}) %all-to-all-start.1) | async-done | bytes 196640 | tf_op jit(solution)/shard_map/all_to_all | solution.py:331
  103.6 0.2 reshape.23
  103.8 0.7 fusion
  104.4 0.7 fusion.1
  (35 shorter events, 0.1 us)
Async XLA Ops:
  0.6 10.0 %collective-permute-start.3 = (bf16[32,16,128]{2,1,0:T(8,128)(2,1)}, bf16[32,16,128]{2,1,0:T(8,128)(2,1)S(1)}, u32[]{:S(2)}, u32[]{:S(2)}) collective-permute-start(bf16[32,16,128]{2,1,0:T(8,128)(2,1)} %refs_1_.1), channel_id=1, source_target_pairs={{0,24},{8,0},{16,8},{24,16},{1,25},{9,1},{17,9},{25,17},{2,26},{10... | collective-permute-start | bytes 393224 | tf_op jit(solution)/shard_map/ppermute | solution.py:318
  4.6 20.3 %collective-permute-start.5 = (bf16[64,16,128]{2,1,0:T(8,128)(2,1)}, bf16[64,16,128]{2,1,0:T(8,128)(2,1)}, u32[]{:S(2)}, u32[]{:S(2)}) collective-permute-start(bf16[64,16,128]{2,1,0:T(8,128)(2,1)} %refs_0_.3), channel_id=1, source_target_pairs={{0,2},{2,4},{4,6},{6,0},{1,3},{3,5},{5,7},{7,1},{8,10},{10,12},{12... | collective-permute-start | bytes 786440 | tf_op jit(solution)/shard_map/ppermute | solution.py:318
  6.2 22.3 %collective-permute-start.4 = (bf16[64,16,128]{2,1,0:T(8,128)(2,1)}, bf16[64,16,128]{2,1,0:T(8,128)(2,1)S(1)}, u32[]{:S(2)}, u32[]{:S(2)}) collective-permute-start(bf16[64,16,128]{2,1,0:T(8,128)(2,1)} %refs_0_.3), channel_id=1, source_target_pairs={{0,4},{2,6},{4,0},{6,2},{1,5},{3,7},{5,1},{7,3},{8,12},{10,14},{12... | collective-permute-start | bytes 786440 | tf_op jit(solution)/shard_map/ppermute | solution.py:318
  8.7 22.4 %collective-permute-start = (bf16[64,16,128]{2,1,0:T(8,128)(2,1)}, bf16[64,16,128]{2,1,0:T(8,128)(2,1)}, u32[]{:S(2)}, u32[]{:S(2)}) collective-permute-start(bf16[64,16,128]{2,1,0:T(8,128)(2,1)} %refs_0_.3), channel_id=1, source_target_pairs={{0,6},{2,0},{4,2},{6,4},{1,7},{3,1},{5,3},{7,5},{8,14},{10,8},{12,... | collective-permute-start | bytes 786440 | tf_op jit(solution)/shard_map/ppermute | solution.py:318
  10.1 7.7 %collective-permute-start.2 = (bf16[32,16,128]{2,1,0:T(8,128)(2,1)}, bf16[32,16,128]{2,1,0:T(8,128)(2,1)}, u32[]{:S(2)}, u32[]{:S(2)}) collective-permute-start(bf16[32,16,128]{2,1,0:T(8,128)(2,1)} %refs_1_.1), channel_id=1, source_target_pairs={{0,16},{8,24},{16,0},{24,8},{1,17},{9,25},{17,1},{25,9},{2,18},{10... | collective-permute-start | bytes 393224 | tf_op jit(solution)/shard_map/ppermute | solution.py:318
  10.6 7.2 %collective-permute-start.1 = (bf16[32,16,128]{2,1,0:T(8,128)(2,1)}, bf16[32,16,128]{2,1,0:T(8,128)(2,1)}, u32[]{:S(2)}, u32[]{:S(2)}) collective-permute-start(bf16[32,16,128]{2,1,0:T(8,128)(2,1)} %refs_1_.1), channel_id=1, source_target_pairs={{0,8},{8,16},{16,24},{24,0},{1,9},{9,17},{17,25},{25,1},{2,10},{10... | collective-permute-start | bytes 393224 | tf_op jit(solution)/shard_map/ppermute | solution.py:318
  11.2 1.0 copy-start.1
  12.2 1.0 copy-start.3
  13.3 0.8 copy-start.12
  14.0 0.8 copy-start.14
  14.8 3.0 %copy-start.6 = (bf16[128,256]{1,0:T(8,128)(2,1)S(1)}, bf16[128,256]{1,0:T(8,128)(2,1)}, u32[]{:S(2)}) copy-start(bf16[128,256]{1,0:T(8,128)(2,1)} %right_w.1) | copy-start | bytes 196612
  14.8 3.0 %copy-start.7 = (bf16[32,16,128]{2,1,0:T(8,128)(2,1)S(1)}, bf16[32,16,128]{2,1,0:T(8,128)(2,1)}, u32[]{:S(2)}) copy-start(bf16[32,16,128]{2,1,0:T(8,128)(2,1)} %refs_1_.1) | copy-start | bytes 393220
  16.9 0.8 copy-start.10
  17.7 7.1 %copy-start.8 = (bf16[64,32,128]{2,1,0:T(8,128)(2,1)}, bf16[64,32,128]{2,1,0:T(8,128)(2,1)S(1)}, u32[]{:S(2)}) copy-start(bf16[64,32,128]{2,1,0:T(8,128)(2,1)S(1)} %get-tuple-element.48.middle_in) | copy-start | bytes 1572868
  17.8 4.5 %copy-start = (bf16[128,256]{1,0:T(8,128)(2,1)S(1)}, bf16[128,256]{1,0:T(8,128)(2,1)}, u32[]{:S(2)}) copy-start(bf16[128,256]{1,0:T(8,128)(2,1)} %left_w.3) | copy-start | bytes 196612
  17.8 4.5 %copy-start.5 = (bf16[64,16,128]{2,1,0:T(8,128)(2,1)S(1)}, bf16[64,16,128]{2,1,0:T(8,128)(2,1)}, u32[]{:S(2)}) copy-start(bf16[64,16,128]{2,1,0:T(8,128)(2,1)} %refs_0_.3) | copy-start | bytes 786436
  28.5 2.7 %copy-start.4 = (bf16[64,32,128]{2,1,0:T(8,128)(2,1)S(1)}, bf16[64,32,128]{2,1,0:T(8,128)(2,1)}, u32[]{:S(2)}) copy-start(bf16[64,32,128]{2,1,0:T(8,128)(2,1)} %cotangent.3) | copy-start | bytes 1572868
  28.5 2.7 %copy-start.9 = (bf16[64,32,128]{2,1,0:T(8,128)(2,1)S(1)}, bf16[64,32,128]{2,1,0:T(8,128)(2,1)}, u32[]{:S(2)}) copy-start(bf16[64,32,128]{2,1,0:T(8,128)(2,1)} %copy-done.8) | copy-start | bytes 1572868
  28.5 2.7 %copy-start.11 = (bf16[64,32,128]{2,1,0:T(8,128)(2,1)S(1)}, bf16[64,32,128]{2,1,0:T(8,128)(2,1)}, u32[]{:S(2)}) copy-start(bf16[64,32,128]{2,1,0:T(8,128)(2,1)} %copy-done.10) | copy-start | bytes 1572868
  28.5 2.7 %copy-start.13 = (bf16[128,128]{1,0:T(8,128)(2,1)S(1)}, bf16[128,128]{1,0:T(8,128)(2,1)}, u32[]{:S(2)}) copy-start(bf16[128,128]{1,0:T(8,128)(2,1)} %out_w.1) | copy-start | bytes 98308
  55.8 34.8 %all-to-all-start = ((bf16[16,48,128]{2,1,0:T(8,128)(2,1)}), bf16[16,48,128]{2,1,0:T(8,128)(2,1)S(1)}, u32[]{:S(2)}, u32[]{:S(2)}) async-start(bf16[16,48,128]{2,1,0:T(8,128)(2,1)} %convert_element_type.11), calls=%async_computation | async-start | bytes 393216 | tf_op jit(solution)/shard_map/all_to_all | solution.py:327
  61.6 7.8 %collective-permute-start.9 = (bf16[32,16,128]{2,1,0:T(8,128)(2,1)S(1)}, bf16[32,16,128]{2,1,0:T(8,128)(2,1)S(1)}, u32[]{:S(2)}, u32[]{:S(2)}) collective-permute-start(bf16[32,16,128]{2,1,0:T(8,128)(2,1)S(1)} %get-tuple-element.69.refs_9_), channel_id=1, source_target_pairs={{0,24},{8,0},{16,8},{24,16},{1,25},{9,1},{17,9},{25,17},{2,26},{10... | collective-permute-start | bytes 393224 | tf_op jit(solution)/shard_map/ppermute | solution.py:318
  64.5 11.0 %collective-permute-start.6 = (bf16[64,16,128]{2,1,0:T(8,128)(2,1)}, bf16[64,16,128]{2,1,0:T(8,128)(2,1)S(1)}, u32[]{:S(2)}, u32[]{:S(2)}) collective-permute-start(bf16[64,16,128]{2,1,0:T(8,128)(2,1)} %get-tuple-element.61.refs_5_), channel_id=1, source_target_pairs={{0,6},{2,0},{4,2},{6,4},{1,7},{3,1},{5,3},{7,5},{8,14},{10,8},{12,... | collective-permute-start | bytes 786440 | tf_op jit(solution)/shard_map/ppermute | solution.py:318
  67.7 22.9 %collective-permute-start.7 = (bf16[64,16,128]{2,1,0:T(8,128)(2,1)S(1)}, bf16[64,16,128]{2,1,0:T(8,128)(2,1)S(1)}, u32[]{:S(2)}, u32[]{:S(2)}) collective-permute-start(bf16[64,16,128]{2,1,0:T(8,128)(2,1)S(1)} %get-tuple-element.62.refs_6_), channel_id=1, source_target_pairs={{0,4},{2,6},{4,0},{6,2},{1,5},{3,7},{5,1},{7,3},{8,12},{10,14},{12... | collective-permute-start | bytes 786440 | tf_op jit(solution)/shard_map/ppermute | solution.py:318
  67.7 22.9 %collective-permute-start.8 = (bf16[64,16,128]{2,1,0:T(8,128)(2,1)S(1)}, bf16[64,16,128]{2,1,0:T(8,128)(2,1)S(1)}, u32[]{:S(2)}, u32[]{:S(2)}) collective-permute-start(bf16[64,16,128]{2,1,0:T(8,128)(2,1)S(1)} %get-tuple-element.63.refs_7_), channel_id=1, source_target_pairs={{0,2},{2,4},{4,6},{6,0},{1,3},{3,5},{5,7},{7,1},{8,10},{10,12},{12... | collective-permute-start | bytes 786440 | tf_op jit(solution)/shard_map/ppermute | solution.py:318
  68.8 6.6 %collective-permute-start.10 = (bf16[32,16,128]{2,1,0:T(8,128)(2,1)}, bf16[32,16,128]{2,1,0:T(8,128)(2,1)S(1)}, u32[]{:S(2)}, u32[]{:S(2)}) collective-permute-start(bf16[32,16,128]{2,1,0:T(8,128)(2,1)} %get-tuple-element.70.refs_10_), channel_id=1, source_target_pairs={{0,16},{8,24},{16,0},{24,8},{1,17},{9,25},{17,1},{25,9},{2,18},{10... | collective-permute-start | bytes 393224 | tf_op jit(solution)/shard_map/ppermute | solution.py:318
  69.4 6.0 %collective-permute-start.11 = (bf16[32,16,128]{2,1,0:T(8,128)(2,1)S(1)}, bf16[32,16,128]{2,1,0:T(8,128)(2,1)S(1)}, u32[]{:S(2)}, u32[]{:S(2)}) collective-permute-start(bf16[32,16,128]{2,1,0:T(8,128)(2,1)S(1)} %get-tuple-element.71.refs_11_), channel_id=1, source_target_pairs={{0,8},{8,16},{16,24},{24,0},{1,9},{9,17},{17,25},{25,1},{2,10},{10... | collective-permute-start | bytes 393224 | tf_op jit(solution)/shard_map/ppermute | solution.py:318
  90.7 4.6 %copy-start.2 = (bf16[64,32,128]{2,1,0:T(8,128)(2,1)S(1)}, bf16[64,32,128]{2,1,0:T(8,128)(2,1)}, u32[]{:S(2)}) copy-start(bf16[64,32,128]{2,1,0:T(8,128)(2,1)} %middle.5) | copy-start | bytes 1572868
  91.4 3.9 %copy-start.15 = (bf16[128,128]{1,0:T(8,128)(2,1)S(1)}, bf16[128,128]{1,0:T(8,128)(2,1)}, u32[]{:S(2)}) copy-start(bf16[128,128]{1,0:T(8,128)(2,1)} %gate_weight.3) | copy-start | bytes 98308
  91.4 12.2 %all-to-all-start.1 = ((bf16[16,48,128]{2,1,0:T(8,128)(2,1)}), bf16[16,48,128]{2,1,0:T(8,128)(2,1)S(1)}, u32[]{:S(2)}, u32[]{:S(2)}) async-start(bf16[16,48,128]{2,1,0:T(8,128)(2,1)} %broadcast_in_dim.2), calls=%async_computation.1 | async-start | bytes 393216 | tf_op jit(solution)/shard_map/all_to_all | solution.py:331

commit v2 on v1

--- a/solution.py
+++ b/solution.py
@@ -189,10 +189,10 @@
     return size
 
 
-def left_back_kernel(tri_back, right_act, *left_out):
+def left_back_kernel(ids, tri_back, right_act, left_out):
     n_i, n_j, width = tri_back.shape
-    k_left = left_out[0].shape[1]
-    n_k = k_left * len(left_out)
+    n_blk, _, k_left, _ = left_out.shape
+    n_k = k_left * n_blk
     few = 4
     k_step = vertex_step(n_k, k_left)
     for k0 in range(0, n_k, k_step):
@@ -205,10 +205,14 @@
                 total = total + tri_back[rows, j : j + 1, :] * right_act[start : start + k_step, :][None]
             total = total.astype(bf16)
             for s in range(k0 // k_left, (k0 + k_step) // k_left):
-                left_out[s][rows] = total[:, s * k_left - k0 : (s + 1) * k_left - k0]
+                left_out[owner(ids, n_blk, s), rows] = total[:, s * k_left - k0 : (s + 1) * k_left - k0]
             return 0
 
         lax.fori_loop(0, n_i // few, rows_sum, 0)
+
+
+def owner(ids, n_blk, piece):
+    return lax.rem(ids[1] - piece + n_blk, n_blk)
 
 
 def right_back_kernel(n_rows, n_blk, ids, tri_back, *refs):
@@ -248,23 +252,24 @@
             ]
 
 
-def weights_kernel(n_rows, n_blk, right_in, left_w, right_w, *refs):
+def weights_kernel(n_rows, n_blk, ids, right_in, left_w, right_w, *refs):
     left_in, refs = refs[:n_blk], refs[n_blk:]
-    left_out, refs = refs[:n_blk], refs[n_blk:]
-    right_out, (left_part, right_part) = refs[:n_rows], refs[n_rows:]
-    for inputs_ref, weight, backs, part in (
-        (left_in, left_w, left_out, left_part),
-        (right_in, right_w, right_out, right_part),
+    left_out, right_out, (left_part, right_part) = refs[0], refs[1 : 1 + n_rows], refs[1 + n_rows :]
+    left_backs = [left_out.at[owner(ids, n_blk, s)] for s in range(n_blk)]
+    right_ins = [right_in.at[s] for s in range(n_rows)]
+    for inputs_refs, weight, backs, part in (
+        (left_in, left_w, left_backs, left_part),
+        (right_ins, right_w, right_out, right_part),
     ):
         part[...] = jnp.zeros_like(part)
-        n, k, width = backs[0].shape
+        n, k, width = inputs_refs[0].shape
         step = 16
         flat = step * k
-        for s, back_ref in enumerate(backs):
-
-            def body(at, _, s=s, back_ref=back_ref, inputs_ref=inputs_ref, weight=weight, part=part, flat=flat, width=width):
+        for inputs_ref, back_ref in zip(inputs_refs, backs):
+
+            def body(at, _, inputs_ref=inputs_ref, back_ref=back_ref, weight=weight, part=part, flat=flat, width=width):
                 rows = pl.ds(at * step, step)
-                inputs = (inputs_ref[s] if isinstance(inputs_ref, tuple) else inputs_ref.at[s])[rows].reshape(flat, width)
+                inputs = inputs_ref[rows].reshape(flat, width)
                 lin, sw = gated(inputs, weight[...])
                 back = back_ref[rows].reshape(flat, width).astype(f32)
                 part[...] += dot_tn(inputs, joined_grad(back, lin, sw))
@@ -288,9 +293,10 @@
     lax.fori_loop(0, n_i // step, body, 0, unroll=2)
 
 
-def side_kernel(n_left, n_right, *refs):
-    left, right, left_w, right_w = refs[:4]
-    left_back, refs = refs[4 : 4 + n_left], refs[4 + n_left :]
+def side_kernel(n_right, *refs):
+    left, right, left_w, right_w, left_backs = refs[:5]
+    refs = refs[5:]
+    left_back = [left_backs.at[s] for s in range(left_backs.shape[0])]
     right_back, refs = refs[:n_right], refs[n_right:]
     for raw, weight, backs, grad in (
         (left, left_w, left_back, refs[0]),
@@ -423,10 +429,10 @@
     )
     left_act.append(act)
     left_in.append(inputs)
-    left_out = call(left_back_kernel, "left_back", [shape(pair_left.shape, bf16)] * n_blk)(
-        tri_back, right_act
-    )
-    left_back = [left_out[0]] + [shift(left_out[s], "blk", n_blk, n_blk - s) for s in range(1, n_blk)]
+    (left_out,) = call(
+        left_back_kernel, "left_back", [shape((n_blk,) + pair_left.shape, bf16)], scalars=1
+    )(ids, tri_back, right_act)
+    left_back = lax.all_to_all(left_out, "blk", 0, 0)
     right_out = call(
         functools.partial(right_back_kernel, n_rows, n_blk),
         "right_back",
@@ -434,7 +440,7 @@
         scalars=1,
         scratch=[pltpu.VMEM((n_j, n_k, width), bf16)],
         after=1,
-    )(ids, tri_back, *left_act, left_out[0])
+    )(ids, tri_back, *left_act, left_out)
     right_back = [right_out[0]] + [
         shift(right_out[s], "rows", n_rows, n_rows - s) for s in range(1, n_rows)
     ]
@@ -442,17 +448,18 @@
         functools.partial(weights_kernel, n_rows, n_blk),
         "weights",
         [shape(left_weight.shape, f32), shape(right_weight.shape, f32)],
-    )(right_in, left_weight, right_weight, *left_in, *left_out, *right_out)
+        scalars=1,
+    )(ids, right_in, left_weight, right_weight, *left_in, left_out, *right_out)
     parts = jnp.concatenate([left_part, right_part, gate_part, output_part], axis=1).astype(bf16)
-    summed = sum_all(parts, n_rows * n_blk, (*left_back[1:], *right_back[1:]))
+    summed = sum_all(parts, n_rows * n_blk, tuple(right_back[1:]))
     (grad_middle,) = call(grad_middle_kernel, "grad_middle", [shape(middle_shape, bf16)])(
         pair_middle, pre_back, gate_weight
     )
     grad_left, grad_right = call(
-        functools.partial(side_kernel, n_blk, n_rows),
+        functools.partial(side_kernel, n_rows),
         "sides",
         [shape(pair_left.shape, bf16), shape(pair_right.shape, bf16)],
-    )(pair_left, pair_right, left_weight, right_weight, *left_back, *right_back)
+    )(pair_left, pair_right, left_weight, right_weight, left_back, *right_back)
     cuts = (2 * width, 4 * width, 5 * width)
     left_delta, right_delta, gate_delta, output_delta = jnp.split(summed, cuts, axis=1)
     return (

time: 106 us -> 116 us (1.094)
  blocking collectives: 0 us -> 13 us
  starting transfers between devices: 28.6 us -> 23.9 us
  waiting for transfers between devices: 23.6 us -> 25.9 us
    all_to_all x1, waiting for transfers between devices: 2.98 us -> 19.5 us  [per_device(): left_back = lax.all_to_all(left_out, 'blk', 0, 0)]
    ppermute x12 -> x9, waiting for transfers between devices: 20.7 us -> 6.36 us  [shift(): return lax.ppermute(x, axis, [(a, (a + step) % n) for a in range(n)])]
    all_to_all x0 -> x1, blocking collectives: none -> 13 us  [sum_all(): lax.all_to_all(jnp.broadcast_to(total[None], blocks.shape), axes, 0, 0)]
    ppermute x12 -> x9, starting transfers between devices: 18.9 us -> 14.5 us  [shift(): return lax.ppermute(x, axis, [(a, (a + step) % n) for a in range(n)])]
  transfers between devices with their start and end apart: 14 -> 11, of which waited for: 3 -> 3; matrix products, arithmetic and copies ran while one was open for 0% -> 1% of each run, Pallas kernels for 20% -> 15%
where the time goes in v2:
time: 116 us
  Pallas kernels  44.8 us (39%)
  waiting for transfers between devices  25.9 us (22%)
  starting transfers between devices  23.9 us (21%)
  blocking collectives  13 us (11%)
  local copies, waits for them, and re-layouts  6.88 us (6%)
    pallas_call x12, Pallas kernels, run(): pl.pallas_call(kernel, in_specs=[pl.BlockSpec(memory_space=space) for spa...  44.8 us
    all_to_all x1, waiting for transfers between devices, per_device(): left_back = lax.all_to_all(left_out, 'blk', 0, 0)  19.5 us
    ppermute x9, starting transfers between devices, shift(): return lax.ppermute(x, axis, [(a, (a + step) % n) for a in range(n)])  14.5 us
    all_to_all x1, blocking collectives, sum_all(): lax.all_to_all(jnp.broadcast_to(total[None], blocks.shape), axes, 0, 0)  13 us
    ppermute x9, waiting for transfers between devices, shift(): return lax.ppermute(x, axis, [(a, (a + step) % n) for a in range(n)])  6.36 us
    all_to_all x1, starting transfers between devices, sum_all(): blocks = lax.all_to_all(x.reshape(n, -1, 128), axes, 0, 0)  5.72 us
    unnamed x32, local copies, waits for them, and re-layouts  4.45 us
    all_to_all x1, starting transfers between devices, per_device(): left_back = lax.all_to_all(left_out, 'blk', 0, 0)  3.65 us
  transfers between devices with their start and end apart: 11, of which 3 were waited for; matrix products, arithmetic and copies ran while one was open for 1% of the time, Pallas kernels for 15%

profile of v2, /device:TPU:0, one launch (start us, length us, event | category | flops | bytes accessed | tf_op | source)
XLA Modules:
  0.0 115.5 jit_solution(17005269348169022005)
XLA Ops:
  0.6 3.9 %collective-permute-start.3 = (bf16[32,16,128]{2,1,0:T(8,128)(2,1)}, bf16[32,16,128]{2,1,0:T(8,128)(2,1)S(1)}, u32[]{:S(2)}, u32[]{:S(2)}) collective-permute-start(bf16[32,16,128]{2,1,0:T(8,128)(2,1)} %refs_1_.1), channel_id=1, source_target_pairs={{0,24},{8,0},{16,8},{24,16},{1,25},{9,1},{17,9},{25,17},{2,26},{10... | collective-permute-start | bytes 393224 | tf_op jit(solution)/shard_map/ppermute | solution.py:324
  4.6 1.6 %collective-permute-start.5 = (bf16[64,16,128]{2,1,0:T(8,128)(2,1)}, bf16[64,16,128]{2,1,0:T(8,128)(2,1)}, u32[]{:S(2)}, u32[]{:S(2)}) collective-permute-start(bf16[64,16,128]{2,1,0:T(8,128)(2,1)} %refs_0_.3), channel_id=1, source_target_pairs={{0,2},{2,4},{4,6},{6,0},{1,3},{3,5},{5,7},{7,1},{8,10},{10,12},{12... | collective-permute-start | bytes 786440 | tf_op jit(solution)/shard_map/ppermute | solution.py:324
  6.2 2.6 %collective-permute-start.4 = (bf16[64,16,128]{2,1,0:T(8,128)(2,1)}, bf16[64,16,128]{2,1,0:T(8,128)(2,1)S(1)}, u32[]{:S(2)}, u32[]{:S(2)}) collective-permute-start(bf16[64,16,128]{2,1,0:T(8,128)(2,1)} %refs_0_.3), channel_id=1, source_target_pairs={{0,4},{2,6},{4,0},{6,2},{1,5},{3,7},{5,1},{7,3},{8,12},{10,14},{12... | collective-permute-start | bytes 786440 | tf_op jit(solution)/shard_map/ppermute | solution.py:324
  8.7 1.3 %collective-permute-start = (bf16[64,16,128]{2,1,0:T(8,128)(2,1)}, bf16[64,16,128]{2,1,0:T(8,128)(2,1)}, u32[]{:S(2)}, u32[]{:S(2)}) collective-permute-start(bf16[64,16,128]{2,1,0:T(8,128)(2,1)} %refs_0_.3), channel_id=1, source_target_pairs={{0,6},{2,0},{4,2},{6,4},{1,7},{3,1},{5,3},{7,5},{8,14},{10,8},{12,... | collective-permute-start | bytes 786440 | tf_op jit(solution)/shard_map/ppermute | solution.py:324
  10.1 0.5 collective-permute-start.2
  10.6 0.0 collective-permute-done.3.refs_3_
  10.6 0.6 collective-permute-start.1
  11.2 1.0 copy-done.1
  12.2 1.0 copy-done.3
  13.3 0.8 copy-done.12
  14.0 0.8 copy-done.14
  14.8 2.1 %middle.3 = (f32[64,32,128]{2,1,0:T(8,128)S(1)}, bf16[64,32,128]{2,1,0:T(8,128)(2,1)S(1)}, bf16[64,32,128]{2,1,0:T(8,128)(2,1)S(1)}, f32[64,32,128]{2,1,0:T(8,128)S(1)}) custom-call(bf16[64,32,128]{2,1,0:T(8,128)(2,1)S(1)} %copy-done.1, bf16[64,32,128]{2,1,0:T(8,128)(2,1)S(1)} %copy-done.3, bf16[128,128]{1,0:T(8,128)(2,1)S(1)} %copy-done.14, ...), custom_call_target="tpu_custom_call" | custom-call | flops 1000 | bytes 1000 | tf_op jit(solution)/shard_map/middle/pallas_call | solution.py:349
  16.9 0.8 copy-done.10
  17.7 0.1 pad_add_fusion.ids
  17.8 0.0 collective-permute-done.2.refs_2_
  17.8 0.0 collective-permute-done.1.refs_1_
  17.8 4.4 %right.1 = (f32[2048,128]{1,0:T(8,128)S(1)}, bf16[4,32,16,128]{3,2,1,0:T(8,128)(2,1)S(1)}, f32[16,32,128]{2,1,0:T(8,128)S(1)}, f32[16,32,128]{2,1,0:T(8,128)S(1)...) custom-call(s32[2]{0:T(128)S(1)} %pad_add_fusion.ids, bf16[32,16,128]{2,1,0:T(8,128)(2,1)S(1)} %copy-done.7, ...), custom_call_target="tpu_custom_call" | custom-call | flops 1000 | bytes 1000 | tf_op jit(solution)/shard_map/right/pallas_call | solution.py:349
  22.3 2.6 %left.3 = (f32[64,16,128]{2,1,0:T(8,128)S(1)}, bf16[64,16,128]{2,1,0:T(8,128)(2,1)S(1)}, f32[64,32,128]{2,1,0:T(8,128)S(1)}) custom-call(bf16[64,16,128]{2,1,0:T(8,128)(2,1)S(1)} %copy-done.5, bf16[128,256]{1,0:T(8,128)(2,1)S(1)} %copy-done, f32[16,32,128]{2,1,0:T(8,128)S(1)} %get-tuple-element.49.flip), custom_call_target="tpu_custom_call" | custom-call | flops 1000 | bytes 1000 | tf_op jit(solution)/shard_map/left/pallas_call | solution.py:349
  24.9 0.0 collective-permute-done.5.raw
  24.9 3.6 %left.4 = (f32[64,16,128]{2,1,0:T(8,128)S(1)}, bf16[64,16,128]{2,1,0:T(8,128)(2,1)S(1)}, f32[64,32,128]{2,1,0:T(8,128)S(1)}) custom-call(bf16[64,16,128]{2,1,0:T(8,128)(2,1)} %collective-permute-done.5.raw, bf16[128,256]{1,0:T(8,128)(2,1)S(1)} %copy-done, f32[16,32,128]{2,1,0:T(8,128)S(1)} %get-tuple-element.48.flip, ...), custom_call_target="tpu_custom_call" | custom-call | flops 1000 | bytes 1000 | tf_op jit(solution)/shard_map/left/pallas_call | solution.py:349
  28.5 0.0 collective-permute-done.4.raw
  28.5 0.0 copy-start.4
  28.5 0.0 copy-start.9
  28.5 0.0 copy-start.11
  28.6 0.0 copy-start.13
  28.6 2.6 %left.5 = (f32[64,16,128]{2,1,0:T(8,128)S(1)}, bf16[64,16,128]{2,1,0:T(8,128)(2,1)S(1)}, f32[64,32,128]{2,1,0:T(8,128)S(1)}) custom-call(bf16[64,16,128]{2,1,0:T(8,128)(2,1)S(1)} %collective-permute-done.4.raw, bf16[128,256]{1,0:T(8,128)(2,1)S(1)} %copy-done, f32[16,32,128]{2,1,0:T(8,128)S(1)} %get-tuple-element.47.flip, ...), custom_call_target="tpu_custom_call" | custom-call | flops 1000 | bytes 1000 | tf_op jit(solution)/shard_map/left/pallas_call | solution.py:349
  31.2 0.0 collective-permute-done.raw
  31.2 6.4 %triangle.1 = (f32[64,16,128]{2,1,0:T(8,128)S(1)}, bf16[64,16,128]{2,1,0:T(8,128)(2,1)S(1)}, bf16[64,32,128]{2,1,0:T(8,128)(2,1)}, bf16[64,32,128]{2,1,0:T(8,128...) custom-call(bf16[64,16,128]{2,1,0:T(8,128)(2,1)} %collective-permute-done.raw, ...), custom_call_target="tpu_custom_call" | custom-call | flops 1000 | bytes 1000 | tf_op jit(solution)/shard_map/triangle/pallas_call | solution.py:349
  37.6 6.2 %left_back.1.refs_4_ = bf16[4,64,16,128]{3,2,1,0:T(8,128)(2,1)} custom-call(s32[2]{0:T(128)S(1)} %pad_add_fusion.ids, f32[64,32,128]{2,1,0:T(8,128)S(1)} %get-tuple-element.54.tri_back, f32[2048,128]{1,0:T(8,128)S(1)} %get-tuple-element.55.right_act), custom_call_target="tpu_custom_call" | custom-call | flops 1000 | bytes 1000 | tf_op jit(solution)/shard_map/left_back/pallas_call | solution.py:349
  43.8 6.1 %right_back.1 = (bf16[32,16,128]{2,1,0:T(8,128)(2,1)S(1)}, bf16[32,16,128]{2,1,0:T(8,128)(2,1)S(1)}, bf16[32,16,128]{2,1,0:T(8,128)(2,1)S(1)}, bf16[32,16,128]{2,1,0:T(8,128)(2,1)S(1)}) custom-call(s32[2]{0:T(128)S(1)} %pad_add_fusion.ids, f32[64,32,128]{2,1,0:T(8,128)S(1)} %get-tuple-element.54.tri_back, f32[64,16,128]{2,1,0:T(8,128)S(1)} %get-tuple-element.56.refs_0_, ...), custom_call_target="tpu_custom_call" | custom-call | flops 1000 | bytes 1000 | tf_op jit(solution)/shard_map/right_back/pallas_call | solution.py:349
  49.9 5.5 %weights.1 = (f32[128,256]{1,0:T(8,128)S(1)}, f32[128,256]{1,0:T(8,128)S(1)}) custom-call(s32[2]{0:T(128)S(1)} %pad_add_fusion.ids, bf16[4,32,16,128]{3,2,1,0:T(8,128)(2,1)S(1)} %get-tuple-element.67.right_in, bf16[128,256]{1,0:T(8,128)(2,1)S(1)} %copy-done, bf16[128,256]{1,0:T(8,128)(2,1)S(1)} %copy-done.6, ...), custom_call_target="tpu_custom_call" | custom-call | flops 1000 | bytes 1000 | tf_op jit(solution)/shard_map/weights/pallas_call | solution.py:349
  55.5 0.9 convert_element_type.11
  56.3 5.7 %all-to-all-start.1 = ((bf16[16,48,128]{2,1,0:T(8,128)(2,1)}), bf16[16,48,128]{2,1,0:T(8,128)(2,1)S(1)}, u32[]{:S(2)}, u32[]{:S(2)}) async-start(bf16[16,48,128]{2,1,0:T(8,128)(2,1)} %convert_element_type.11), calls=%async_computation.1 | async-start | bytes 393216 | tf_op jit(solution)/shard_map/all_to_all | solution.py:333
  62.1 2.8 %collective-permute-start.6 = (bf16[32,16,128]{2,1,0:T(8,128)(2,1)S(1)}, bf16[32,16,128]{2,1,0:T(8,128)(2,1)S(1)}, u32[]{:S(2)}, u32[]{:S(2)}) collective-permute-start(bf16[32,16,128]{2,1,0:T(8,128)(2,1)S(1)} %get-tuple-element.61.refs_6_), channel_id=1, source_target_pairs={{0,24},{8,0},{16,8},{24,16},{1,25},{9,1},{17,9},{25,17},{2,26},{10... | collective-permute-start | bytes 393224 | tf_op jit(solution)/shard_map/ppermute | solution.py:324
  64.9 0.6 collective-permute-start.7
  65.4 0.6 collective-permute-start.8
  66.0 3.7 %collective-permute-done.6.refs_6_.refs_0_ = bf16[32,16,128]{2,1,0:T(8,128)(2,1)S(1)} collective-permute-done((bf16[32,16,128]{2,1,0:T(8,128)(2,1)S(1)}, bf16[32,16,128]{2,1,0:T(8,128)(2,1)S(1)}, u32[]{:S(2)}, u32[]{:S(2)}) %collective-permute-start.6) | collective-permute-done | bytes 131104 | tf_op jit(solution)/shard_map/ppermute | solution.py:324
  69.8 2.6 %collective-permute-done.7.refs_7_.refs_1_ = bf16[32,16,128]{2,1,0:T(8,128)(2,1)S(1)} collective-permute-done((bf16[32,16,128]{2,1,0:T(8,128)(2,1)S(1)}, bf16[32,16,128]{2,1,0:T(8,128)(2,1)S(1)}, u32[]{:S(2)}, u32[]{:S(2)}) %collective-permute-start.7) | collective-permute-done | bytes 131104 | tf_op jit(solution)/shard_map/ppermute | solution.py:324
  72.4 0.0 collective-permute-done.8.refs_8_.refs_2_
  72.4 0.0 all-to-all-done.1.blocks
  72.4 13.0 %all_to_all.15 = bf16[16,48,128]{2,1,0:T(8,128)(2,1)S(1)} all-to-all(bf16[16,48,128]{2,1,0:T(8,128)(2,1)S(1)} %broadcast_in_dim.2), channel_id=1, replica_groups=mesh['rows'=4,'blk'=4,'rep'=2] {'rows','blk'}, dimensions={0} | all-to-all | bytes 393216 | tf_op jit(solution)/shard_map/all_to_all | solution.py:337
  85.4 3.6 %all-to-all-start = ((bf16[4,64,16,128]{3,2,1,0:T(8,128)(2,1)}), bf16[4,64,16,128]{3,2,1,0:T(8,128)(2,1)S(1)}, u32[]{:S(2)}, u32[]{:S(2)}) async-start(bf16[4,64,16,128]{3,2,1,0:T(8,128)(2,1)} %left_back.1.refs_4_), calls=%async_computation | async-start | bytes 2097152 | tf_op jit(solution)/shard_map/all_to_all | solution.py:435
  89.1 2.4 %grad_middle.1 = bf16[64,32,128]{2,1,0:T(8,128)(2,1)} custom-call(bf16[64,32,128]{2,1,0:T(8,128)(2,1)S(1)} %copy-done.2, bf16[64,32,128]{2,1,0:T(8,128)(2,1)S(1)} %get-tuple-element.66.pre_back, bf16[128,128]{1,0:T(8,128)(2,1)S(1)} %copy-done.15), custom_call_target="tpu_custom_call" | custom-call | flops 1000 | bytes 1000 | tf_op jit(solution)/shard_map/grad_middle/pallas_call | solution.py:349
  91.6 0.2 reshape.23
  91.7 0.7 fusion
  92.4 0.7 fusion.1
  93.1 19.5 %all-to-all-done.refs_4_ = bf16[4,64,16,128]{3,2,1,0:T(8,128)(2,1)S(1)} async-done(((bf16[4,64,16,128]{3,2,1,0:T(8,128)(2,1)}), bf16[4,64,16,128]{3,2,1,0:T(8,128)(2,1)S(1)}, u32[]{:S(2)}, u32[]{:S(2)}) %all-to-all-start) | async-done | bytes 1048608 | tf_op jit(solution)/shard_map/all_to_all | solution.py:435
  112.6 2.9 %sides.1 = (bf16[64,16,128]{2,1,0:T(8,128)(2,1)}, bf16[32,16,128]{2,1,0:T(8,128)(2,1)}) custom-call(bf16[64,16,128]{2,1,0:T(8,128)(2,1)S(1)} %copy-done.5, bf16[32,16,128]{2,1,0:T(8,128)(2,1)S(1)} %copy-done.7, bf16[128,256]{1,0:T(8,128)(2,1)S(1)} %copy-done, bf16[128,256]{1,0:T(8,128)(2,1)S(1)} %copy-done.6, ...), custom_call_target="tpu_custom_call" | custom-call | flops 1000 | bytes 1000 | tf_op jit(solution)/shard_map/sides/pallas_call | solution.py:349
  (30 shorter events, 0.2 us)
Async XLA Ops:
  0.6 10.0 %collective-permute-start.3 = (bf16[32,16,128]{2,1,0:T(8,128)(2,1)}, bf16[32,16,128]{2,1,0:T(8,128)(2,1)S(1)}, u32[]{:S(2)}, u32[]{:S(2)}) collective-permute-start(bf16[32,16,128]{2,1,0:T(8,128)(2,1)} %refs_1_.1), channel_id=1, source_target_pairs={{0,24},{8,0},{16,8},{24,16},{1,25},{9,1},{17,9},{25,17},{2,26},{10... | collective-permute-start | bytes 393224 | tf_op jit(solution)/shard_map/ppermute | solution.py:324
  4.6 20.3 %collective-permute-start.5 = (bf16[64,16,128]{2,1,0:T(8,128)(2,1)}, bf16[64,16,128]{2,1,0:T(8,128)(2,1)}, u32[]{:S(2)}, u32[]{:S(2)}) collective-permute-start(bf16[64,16,128]{2,1,0:T(8,128)(2,1)} %refs_0_.3), channel_id=1, source_target_pairs={{0,2},{2,4},{4,6},{6,0},{1,3},{3,5},{5,7},{7,1},{8,10},{10,12},{12... | collective-permute-start | bytes 786440 | tf_op jit(solution)/shard_map/ppermute | solution.py:324
  6.2 22.4 %collective-permute-start.4 = (bf16[64,16,128]{2,1,0:T(8,128)(2,1)}, bf16[64,16,128]{2,1,0:T(8,128)(2,1)S(1)}, u32[]{:S(2)}, u32[]{:S(2)}) collective-permute-start(bf16[64,16,128]{2,1,0:T(8,128)(2,1)} %refs_0_.3), channel_id=1, source_target_pairs={{0,4},{2,6},{4,0},{6,2},{1,5},{3,7},{5,1},{7,3},{8,12},{10,14},{12... | collective-permute-start | bytes 786440 | tf_op jit(solution)/shard_map/ppermute | solution.py:324
  8.7 22.4 %collective-permute-start = (bf16[64,16,128]{2,1,0:T(8,128)(2,1)}, bf16[64,16,128]{2,1,0:T(8,128)(2,1)}, u32[]{:S(2)}, u32[]{:S(2)}) collective-permute-start(bf16[64,16,128]{2,1,0:T(8,128)(2,1)} %refs_0_.3), channel_id=1, source_target_pairs={{0,6},{2,0},{4,2},{6,4},{1,7},{3,1},{5,3},{7,5},{8,14},{10,8},{12,... | collective-permute-start | bytes 786440 | tf_op jit(solution)/shard_map/ppermute | solution.py:324
  10.1 7.7 %collective-permute-start.2 = (bf16[32,16,128]{2,1,0:T(8,128)(2,1)}, bf16[32,16,128]{2,1,0:T(8,128)(2,1)}, u32[]{:S(2)}, u32[]{:S(2)}) collective-permute-start(bf16[32,16,128]{2,1,0:T(8,128)(2,1)} %refs_1_.1), channel_id=1, source_target_pairs={{0,16},{8,24},{16,0},{24,8},{1,17},{9,25},{17,1},{25,9},{2,18},{10... | collective-permute-start | bytes 393224 | tf_op jit(solution)/shard_map/ppermute | solution.py:324
  10.6 7.2 %collective-permute-start.1 = (bf16[32,16,128]{2,1,0:T(8,128)(2,1)}, bf16[32,16,128]{2,1,0:T(8,128)(2,1)}, u32[]{:S(2)}, u32[]{:S(2)}) collective-permute-start(bf16[32,16,128]{2,1,0:T(8,128)(2,1)} %refs_1_.1), channel_id=1, source_target_pairs={{0,8},{8,16},{16,24},{24,0},{1,9},{9,17},{17,25},{25,1},{2,10},{10... | collective-permute-start | bytes 393224 | tf_op jit(solution)/shard_map/ppermute | solution.py:324
  11.2 1.0 copy-start.1
  12.2 1.0 copy-start.3
  13.3 0.8 copy-start.12
  14.0 0.8 copy-start.14
  14.8 3.0 %copy-start.6 = (bf16[128,256]{1,0:T(8,128)(2,1)S(1)}, bf16[128,256]{1,0:T(8,128)(2,1)}, u32[]{:S(2)}) copy-start(bf16[128,256]{1,0:T(8,128)(2,1)} %right_w.1) | copy-start | bytes 196612
  14.8 3.0 %copy-start.7 = (bf16[32,16,128]{2,1,0:T(8,128)(2,1)S(1)}, bf16[32,16,128]{2,1,0:T(8,128)(2,1)}, u32[]{:S(2)}) copy-start(bf16[32,16,128]{2,1,0:T(8,128)(2,1)} %refs_1_.1) | copy-start | bytes 393220
  16.9 0.8 copy-start.10
  17.7 7.2 %copy-start.8 = (bf16[64,32,128]{2,1,0:T(8,128)(2,1)}, bf16[64,32,128]{2,1,0:T(8,128)(2,1)S(1)}, u32[]{:S(2)}) copy-start(bf16[64,32,128]{2,1,0:T(8,128)(2,1)S(1)} %get-tuple-element.44.middle_in) | copy-start | bytes 1572868
  17.8 4.5 %copy-start = (bf16[128,256]{1,0:T(8,128)(2,1)S(1)}, bf16[128,256]{1,0:T(8,128)(2,1)}, u32[]{:S(2)}) copy-start(bf16[128,256]{1,0:T(8,128)(2,1)} %left_w.3) | copy-start | bytes 196612
  17.8 4.5 %copy-start.5 = (bf16[64,16,128]{2,1,0:T(8,128)(2,1)S(1)}, bf16[64,16,128]{2,1,0:T(8,128)(2,1)}, u32[]{:S(2)}) copy-start(bf16[64,16,128]{2,1,0:T(8,128)(2,1)} %refs_0_.3) | copy-start | bytes 786436
  28.5 2.7 %copy-start.4 = (bf16[64,32,128]{2,1,0:T(8,128)(2,1)S(1)}, bf16[64,32,128]{2,1,0:T(8,128)(2,1)}, u32[]{:S(2)}) copy-start(bf16[64,32,128]{2,1,0:T(8,128)(2,1)} %cotangent.3) | copy-start | bytes 1572868
  28.5 2.7 %copy-start.9 = (bf16[64,32,128]{2,1,0:T(8,128)(2,1)S(1)}, bf16[64,32,128]{2,1,0:T(8,128)(2,1)}, u32[]{:S(2)}) copy-start(bf16[64,32,128]{2,1,0:T(8,128)(2,1)} %copy-done.8) | copy-start | bytes 1572868
  28.5 2.7 %copy-start.11 = (bf16[64,32,128]{2,1,0:T(8,128)(2,1)S(1)}, bf16[64,32,128]{2,1,0:T(8,128)(2,1)}, u32[]{:S(2)}) copy-start(bf16[64,32,128]{2,1,0:T(8,128)(2,1)} %copy-done.10) | copy-start | bytes 1572868
  28.6 2.7 %copy-start.13 = (bf16[128,128]{1,0:T(8,128)(2,1)S(1)}, bf16[128,128]{1,0:T(8,128)(2,1)}, u32[]{:S(2)}) copy-start(bf16[128,128]{1,0:T(8,128)(2,1)} %out_w.1) | copy-start | bytes 98308
  56.3 16.0 %all-to-all-start.1 = ((bf16[16,48,128]{2,1,0:T(8,128)(2,1)}), bf16[16,48,128]{2,1,0:T(8,128)(2,1)S(1)}, u32[]{:S(2)}, u32[]{:S(2)}) async-start(bf16[16,48,128]{2,1,0:T(8,128)(2,1)} %convert_element_type.11), calls=%async_computation.1 | async-start | bytes 393216 | tf_op jit(solution)/shard_map/all_to_all | solution.py:333
  62.1 7.7 %collective-permute-start.6 = (bf16[32,16,128]{2,1,0:T(8,128)(2,1)S(1)}, bf16[32,16,128]{2,1,0:T(8,128)(2,1)S(1)}, u32[]{:S(2)}, u32[]{:S(2)}) collective-permute-start(bf16[32,16,128]{2,1,0:T(8,128)(2,1)S(1)} %get-tuple-element.61.refs_6_), channel_id=1, source_target_pairs={{0,24},{8,0},{16,8},{24,16},{1,25},{9,1},{17,9},{25,17},{2,26},{10... | collective-permute-start | bytes 393224 | tf_op jit(solution)/shard_map/ppermute | solution.py:324
  64.9 7.5 %collective-permute-start.7 = (bf16[32,16,128]{2,1,0:T(8,128)(2,1)S(1)}, bf16[32,16,128]{2,1,0:T(8,128)(2,1)S(1)}, u32[]{:S(2)}, u32[]{:S(2)}) collective-permute-start(bf16[32,16,128]{2,1,0:T(8,128)(2,1)S(1)} %get-tuple-element.62.refs_7_), channel_id=1, source_target_pairs={{0,16},{8,24},{16,0},{24,8},{1,17},{9,25},{17,1},{25,9},{2,18},{10... | collective-permute-start | bytes 393224 | tf_op jit(solution)/shard_map/ppermute | solution.py:324
  65.4 6.9 %collective-permute-start.8 = (bf16[32,16,128]{2,1,0:T(8,128)(2,1)S(1)}, bf16[32,16,128]{2,1,0:T(8,128)(2,1)S(1)}, u32[]{:S(2)}, u32[]{:S(2)}) collective-permute-start(bf16[32,16,128]{2,1,0:T(8,128)(2,1)S(1)} %get-tuple-element.63.refs_8_), channel_id=1, source_target_pairs={{0,8},{8,16},{16,24},{24,0},{1,9},{9,17},{17,25},{25,1},{2,10},{10... | collective-permute-start | bytes 393224 | tf_op jit(solution)/shard_map/ppermute | solution.py:324
  85.4 3.7 %copy-start.2 = (bf16[64,32,128]{2,1,0:T(8,128)(2,1)S(1)}, bf16[64,32,128]{2,1,0:T(8,128)(2,1)}, u32[]{:S(2)}) copy-start(bf16[64,32,128]{2,1,0:T(8,128)(2,1)} %middle.5) | copy-start | bytes 1572868
  85.4 3.7 %copy-start.15 = (bf16[128,128]{1,0:T(8,128)(2,1)S(1)}, bf16[128,128]{1,0:T(8,128)(2,1)}, u32[]{:S(2)}) copy-start(bf16[128,128]{1,0:T(8,128)(2,1)} %gate_weight.3) | copy-start | bytes 98308
  85.4 27.2 %all-to-all-start = ((bf16[4,64,16,128]{3,2,1,0:T(8,128)(2,1)}), bf16[4,64,16,128]{3,2,1,0:T(8,128)(2,1)S(1)}, u32[]{:S(2)}, u32[]{:S(2)}) async-start(bf16[4,64,16,128]{3,2,1,0:T(8,128)(2,1)} %left_back.1.refs_4_), calls=%async_computation | async-start | bytes 2097152 | tf_op jit(solution)/shard_map/all_to_all | solution.py:435

commit v3 on v2

--- a/solution.py
+++ b/solution.py
@@ -252,30 +252,39 @@
             ]
 
 
-def weights_kernel(n_rows, n_blk, ids, right_in, left_w, right_w, *refs):
+def weights_kernel(n_rows, n_blk, ids, right_in, left_w, right_w, gate_part, output_part, *refs):
     left_in, refs = refs[:n_blk], refs[n_blk:]
-    left_out, right_out, (left_part, right_part) = refs[0], refs[1 : 1 + n_rows], refs[1 + n_rows :]
+    left_out, right_out, refs = refs[0], refs[1 : 1 + n_rows], refs[1 + n_rows :]
+    pieces, (total,) = refs[:n_rows], refs[n_rows:]
     left_backs = [left_out.at[owner(ids, n_blk, s)] for s in range(n_blk)]
     right_ins = [right_in.at[s] for s in range(n_rows)]
-    for inputs_refs, weight, backs, part in (
-        (left_in, left_w, left_backs, left_part),
-        (right_ins, right_w, right_out, right_part),
+    width = gate_part.shape[0]
+    total[:, 4 * width : 5 * width] = gate_part[...]
+    total[:, 5 * width :] = output_part[...]
+    for inputs_refs, weight, backs, first in (
+        (left_in, left_w, left_backs, 0),
+        (right_ins, right_w, right_out, 2 * width),
     ):
-        part[...] = jnp.zeros_like(part)
-        n, k, width = inputs_refs[0].shape
+        columns = slice(first, first + 2 * width)
+        total[:, columns] = jnp.zeros((width, 2 * width), f32)
+        n, k, _ = inputs_refs[0].shape
         step = 16
         flat = step * k
         for inputs_ref, back_ref in zip(inputs_refs, backs):
 
-            def body(at, _, inputs_ref=inputs_ref, back_ref=back_ref, weight=weight, part=part, flat=flat, width=width):
+            def body(at, _, inputs_ref=inputs_ref, back_ref=back_ref, weight=weight, columns=columns, flat=flat):
                 rows = pl.ds(at * step, step)
                 inputs = inputs_ref[rows].reshape(flat, width)
                 lin, sw = gated(inputs, weight[...])
                 back = back_ref[rows].reshape(flat, width).astype(f32)
-                part[...] += dot_tn(inputs, joined_grad(back, lin, sw))
+                total[:, columns] += dot_tn(inputs, joined_grad(back, lin, sw))
                 return 0
 
             lax.fori_loop(0, n // step, body, 0, unroll=2)
+    size = width // n_rows
+    for s, piece in enumerate(pieces):
+        start = pl.multiple_of(lax.rem(ids[0] + s, n_rows) * size, size)
+        piece[...] = total[pl.ds(start, size), :].astype(bf16)
 
 
 def grad_middle_kernel(middle, pre_back, gate_weight, grad_middle):
@@ -324,18 +333,33 @@
     return lax.ppermute(x, axis, [(a, (a + step) % n) for a in range(n)])
 
 
-def combine_kernel(blocks, *refs):
-    refs[-1][...] = jnp.sum(blocks[...].astype(f32), axis=0).astype(bf16)
-
-
-def sum_all(x, n, after):
-    axes = ("rows", "blk")
-    blocks = lax.all_to_all(x.reshape(n, -1, 128), axes, 0, 0)
-    (total,) = call(combine_kernel, "combine", [shape(blocks.shape[1:], bf16)], after=len(after))(
-        blocks, *after
-    )
-    whole = lax.all_to_all(jnp.broadcast_to(total[None], blocks.shape), axes, 0, 0)
-    return whole.reshape(x.shape).astype(f32)
+def combine_kernel(n, *refs):
+    total = refs[0][...].astype(f32)
+    for other in refs[1:n]:
+        total = total + other[...].astype(f32)
+    refs[-1][...] = total.astype(bf16)
+
+
+def combine(pieces, after=()):
+    (total,) = call(
+        functools.partial(combine_kernel, len(pieces)),
+        "combine",
+        [shape(pieces[0].shape, bf16)],
+        after=len(after),
+    )(*pieces, *after)
+    return total
+
+
+def deltas_kernel(n_rows, ids, *refs):
+    pieces, outs = refs[:n_rows], refs[n_rows:]
+    size = pieces[0].shape[0]
+    for s, piece in enumerate(pieces):
+        start = pl.multiple_of(lax.rem(ids[0] - s + n_rows, n_rows) * size, size)
+        first = 0
+        for out in outs:
+            last = first + out.shape[1]
+            out[pl.ds(start, size), :] = piece[:, first:last].astype(f32)
+            first = last
 
 
 def shape(dims, kind):
@@ -444,14 +468,23 @@
     right_back = [right_out[0]] + [
         shift(right_out[s], "rows", n_rows, n_rows - s) for s in range(1, n_rows)
     ]
-    left_part, right_part = call(
+    pieces = call(
         functools.partial(weights_kernel, n_rows, n_blk),
         "weights",
-        [shape(left_weight.shape, f32), shape(right_weight.shape, f32)],
+        [shape((width // n_rows, 6 * width), bf16)] * n_rows,
         scalars=1,
-    )(ids, right_in, left_weight, right_weight, *left_in, left_out, *right_out)
-    parts = jnp.concatenate([left_part, right_part, gate_part, output_part], axis=1).astype(bf16)
-    summed = sum_all(parts, n_rows * n_blk, tuple(right_back[1:]))
+        scratch=[pltpu.VMEM((width, 6 * width), f32)],
+    )(ids, right_in, left_weight, right_weight, gate_part, output_part, *left_in, left_out, *right_out)
+    pieces = [pieces[0]] + [shift(pieces[s], "rows", n_rows, s) for s in range(1, n_rows)]
+    part = combine(pieces, (left_back, *right_back[1:]))
+    part = combine([part] + [shift(part, "blk", n_blk, s) for s in range(1, n_blk)])
+    pieces = [part] + [shift(part, "rows", n_rows, s) for s in range(1, n_rows)]
+    deltas = call(
+        functools.partial(deltas_kernel, n_rows),
+        "deltas",
+        [shape(x.shape, f32) for x in (left_weight, right_weight, gate_weight, output_weight)],
+        scalars=1,
+    )(ids, *pieces)
     (grad_middle,) = call(grad_middle_kernel, "grad_middle", [shape(middle_shape, bf16)])(
         pair_middle, pre_back, gate_weight
     )
@@ -460,17 +493,12 @@
         "sides",
         [shape(pair_left.shape, bf16), shape(pair_right.shape, bf16)],
     )(pair_left, pair_right, left_weight, right_weight, left_back, *right_back)
-    cuts = (2 * width, 4 * width, 5 * width)
-    left_delta, right_delta, gate_delta, output_delta = jnp.split(summed, cuts, axis=1)
     return (
         update,
         grad_left,
         grad_right,
         grad_middle,
-        left_delta,
-        right_delta,
-        gate_delta,
-        output_delta,
+        *deltas,
     )
 
 

time: 116 us -> 104 us (0.90)
  waiting for transfers between devices: 25.9 us -> 8.61 us
  blocking collectives: 13 us -> 0 us
  starting transfers between devices: 23.9 us -> 32.4 us
  local copies, waits for them, and re-layouts: 6.88 us -> 14 us
  Pallas kernels: 44.8 us -> 46.9 us
    all_to_all x1, waiting for transfers between devices: 19.5 us -> 0.01 us  [per_device(): left_back = lax.all_to_all(left_out, 'blk', 0, 0)]
    ppermute x9 -> x18, starting transfers between devices: 14.5 us -> 28.3 us  [shift(): return lax.ppermute(x, axis, [(a, (a + step) % n) for a in range(n)])]
    all_to_all x1 -> x0, blocking collectives: 13 us -> none  [sum_all(): lax.all_to_all(jnp.broadcast_to(total[None], blocks.shape), axes, 0, 0)]
    unnamed x32 -> x86, local copies, waits for them, and re-layouts: 4.45 us -> 14 us
    all_to_all x1 -> x0, starting transfers between devices: 5.72 us -> none  [sum_all(): blocks = lax.all_to_all(x.reshape(n, -1, 128), axes, 0, 0)]
    ppermute x9 -> x18, waiting for transfers between devices: 6.36 us -> 8.6 us  [shift(): return lax.ppermute(x, axis, [(a, (a + step) % n) for a in range(n)])]
    pallas_call x12 -> x14, Pallas kernels: 44.8 us -> 46.9 us  [run(): pl.pallas_call(kernel, in_specs=[pl.BlockSpec(memory_space=space) for spa...]
    split x2 -> x0, local copies, waits for them, and re-layouts: 1.37 us -> none  [per_device(): jnp.split(summed, cuts, axis=1)]
  transfers between devices with their start and end apart: 11 -> 19, of which waited for: 3 -> 5; matrix products, arithmetic and copies ran while one was open for 1% -> 0% of each run, Pallas kernels for 15% -> 32%
where the time goes in v3:
time: 104 us; the launch traced here: 103 us
  Pallas kernels  46.9 us (45%)
  starting transfers between devices  32.4 us (31%)
  local copies, waits for them, and re-layouts  14 us (13%)
  waiting for transfers between devices  8.61 us (8%)
    pallas_call x14, Pallas kernels, run(): pl.pallas_call(kernel, in_specs=[pl.BlockSpec(memory_space=space) for spa...  46.9 us
    ppermute x18, starting transfers between devices, shift(): return lax.ppermute(x, axis, [(a, (a + step) % n) for a in range(n)])  28.3 us
    unnamed x86, local copies, waits for them, and re-layouts  14 us
    ppermute x18, waiting for transfers between devices, shift(): return lax.ppermute(x, axis, [(a, (a + step) % n) for a in range(n)])  8.6 us
    all_to_all x1, starting transfers between devices, per_device(): left_back = lax.all_to_all(left_out, 'blk', 0, 0)  4.09 us
  transfers between devices with their start and end apart: 19, of which 5 were waited for; matrix products, arithmetic and copies ran while one was open for 0% of the time, Pallas kernels for 32%

profile of v3, /device:TPU:0, one launch (start us, length us, event | category | flops | bytes accessed | tf_op | source)
XLA Modules:
  0.0 102.9 jit_solution(17030009202252178508)
XLA Ops:
  0.6 3.9 %collective-permute-start.3 = (bf16[32,16,128]{2,1,0:T(8,128)(2,1)}, bf16[32,16,128]{2,1,0:T(8,128)(2,1)S(1)}, u32[]{:S(2)}, u32[]{:S(2)}) collective-permute-start(bf16[32,16,128]{2,1,0:T(8,128)(2,1)} %refs_1_.1), channel_id=1, source_target_pairs={{0,24},{8,0},{16,8},{24,16},{1,25},{9,1},{17,9},{25,17},{2,26},{10... | collective-permute-start | bytes 393224 | tf_op jit(solution)/shard_map/ppermute | solution.py:333
  4.6 1.6 %collective-permute-start.5 = (bf16[64,16,128]{2,1,0:T(8,128)(2,1)}, bf16[64,16,128]{2,1,0:T(8,128)(2,1)}, u32[]{:S(2)}, u32[]{:S(2)}) collective-permute-start(bf16[64,16,128]{2,1,0:T(8,128)(2,1)} %refs_0_.3), channel_id=1, source_target_pairs={{0,2},{2,4},{4,6},{6,0},{1,3},{3,5},{5,7},{7,1},{8,10},{10,12},{12... | collective-permute-start | bytes 786440 | tf_op jit(solution)/shard_map/ppermute | solution.py:333
  6.2 2.6 %collective-permute-start.4 = (bf16[64,16,128]{2,1,0:T(8,128)(2,1)}, bf16[64,16,128]{2,1,0:T(8,128)(2,1)}, u32[]{:S(2)}, u32[]{:S(2)}) collective-permute-start(bf16[64,16,128]{2,1,0:T(8,128)(2,1)} %refs_0_.3), channel_id=1, source_target_pairs={{0,4},{2,6},{4,0},{6,2},{1,5},{3,7},{5,1},{7,3},{8,12},{10,14},{12... | collective-permute-start | bytes 786440 | tf_op jit(solution)/shard_map/ppermute | solution.py:333
  8.7 1.3 %collective-permute-start = (bf16[64,16,128]{2,1,0:T(8,128)(2,1)}, bf16[64,16,128]{2,1,0:T(8,128)(2,1)}, u32[]{:S(2)}, u32[]{:S(2)}) collective-permute-start(bf16[64,16,128]{2,1,0:T(8,128)(2,1)} %refs_0_.3), channel_id=1, source_target_pairs={{0,6},{2,0},{4,2},{6,4},{1,7},{3,1},{5,3},{7,5},{8,14},{10,8},{12,... | collective-permute-start | bytes 786440 | tf_op jit(solution)/shard_map/ppermute | solution.py:333
  10.6 0.6 collective-permute-start.1
  11.2 1.0 %copy-done.1 = bf16[64,32,128]{2,1,0:T(8,128)(2,1)S(1)} copy-done((bf16[64,32,128]{2,1,0:T(8,128)(2,1)S(1)}, bf16[64,32,128]{2,1,0:T(8,128)(2,1)}, u32[]{:S(2)}) %copy-start.1) | copy-done | bytes 524312
  12.2 1.0 %copy-done.3 = bf16[64,32,128]{2,1,0:T(8,128)(2,1)S(1)} copy-done((bf16[64,32,128]{2,1,0:T(8,128)(2,1)S(1)}, bf16[64,32,128]{2,1,0:T(8,128)(2,1)}, u32[]{:S(2)}) %copy-start.3) | copy-done | bytes 524312
  13.3 0.8 copy-done.35
  14.0 0.8 copy-done.37
  14.8 2.1 %middle.3 = (f32[64,32,128]{2,1,0:T(8,128)S(1)}, bf16[64,32,128]{2,1,0:T(8,128)(2,1)S(1)}, bf16[64,32,128]{2,1,0:T(8,128)(2,1)S(1)}, f32[64,32,128]{2,1,0:T(8,128)S(1)}) custom-call(bf16[64,32,128]{2,1,0:T(8,128)(2,1)S(1)} %copy-done.1, bf16[64,32,128]{2,1,0:T(8,128)(2,1)S(1)} %copy-done.3, bf16[128,128]{1,0:T(8,128)(2,1)S(1)} %copy-done.37, ...), custom_call_target="tpu_custom_call" | custom-call | flops 1000 | bytes 1000 | tf_op jit(solution)/shard_map/middle/pallas_call | solution.py:373
  16.9 0.8 copy-done.23
  17.7 0.8 copy-done.25
  18.6 3.9 %right.1 = (f32[2048,128]{1,0:T(8,128)S(1)}, bf16[4,32,16,128]{3,2,1,0:T(8,128)(2,1)S(1)}, f32[16,32,128]{2,1,0:T(8,128)S(1)}, f32[16,32,128]{2,1,0:T(8,128)S(1)...) custom-call(s32[2]{0:T(128)S(1)} %pad_add_fusion.ids, bf16[32,16,128]{2,1,0:T(8,128)(2,1)S(1)} %copy-done.19, ...), custom_call_target="tpu_custom_call" | custom-call | flops 1000 | bytes 1000 | tf_op jit(solution)/shard_map/right/pallas_call | solution.py:373
  22.5 2.5 %left.3 = (f32[64,16,128]{2,1,0:T(8,128)S(1)}, bf16[64,16,128]{2,1,0:T(8,128)(2,1)S(1)}, f32[64,32,128]{2,1,0:T(8,128)S(1)}) custom-call(bf16[64,16,128]{2,1,0:T(8,128)(2,1)S(1)} %copy-done.5, bf16[128,256]{1,0:T(8,128)(2,1)S(1)} %copy-done, f32[16,32,128]{2,1,0:T(8,128)S(1)} %get-tuple-element.55.flip), custom_call_target="tpu_custom_call" | custom-call | flops 1000 | bytes 1000 | tf_op jit(solution)/shard_map/left/pallas_call | solution.py:373
  25.1 3.7 %left.4 = (f32[64,16,128]{2,1,0:T(8,128)S(1)}, bf16[64,16,128]{2,1,0:T(8,128)(2,1)S(1)}, f32[64,32,128]{2,1,0:T(8,128)S(1)}) custom-call(bf16[64,16,128]{2,1,0:T(8,128)(2,1)} %collective-permute-done.5.raw, bf16[128,256]{1,0:T(8,128)(2,1)S(1)} %copy-done, f32[16,32,128]{2,1,0:T(8,128)S(1)} %get-tuple-element.54.flip, ...), custom_call_target="tpu_custom_call" | custom-call | flops 1000 | bytes 1000 | tf_op jit(solution)/shard_map/left/pallas_call | solution.py:373
  28.8 0.8 copy-done.11
  29.6 0.7 copy-done.29
  30.4 3.7 %left.5 = (f32[64,16,128]{2,1,0:T(8,128)S(1)}, bf16[64,16,128]{2,1,0:T(8,128)(2,1)S(1)}, f32[64,32,128]{2,1,0:T(8,128)S(1)}) custom-call(bf16[64,16,128]{2,1,0:T(8,128)(2,1)} %collective-permute-done.4.raw, bf16[128,256]{1,0:T(8,128)(2,1)S(1)} %copy-done, f32[16,32,128]{2,1,0:T(8,128)S(1)} %get-tuple-element.53.flip, ...), custom_call_target="tpu_custom_call" | custom-call | flops 1000 | bytes 1000 | tf_op jit(solution)/shard_map/left/pallas_call | solution.py:373
  34.0 0.8 copy-done.13
  34.8 0.7 copy-done.31
  35.6 6.4 %triangle.1 = (f32[64,16,128]{2,1,0:T(8,128)S(1)}, bf16[64,16,128]{2,1,0:T(8,128)(2,1)S(1)}, bf16[64,32,128]{2,1,0:T(8,128)(2,1)}, bf16[64,32,128]{2,1,0:T(8,128...) custom-call(bf16[64,16,128]{2,1,0:T(8,128)(2,1)} %collective-permute-done.raw, ...), custom_call_target="tpu_custom_call" | custom-call | flops 1000 | bytes 1000 | tf_op jit(solution)/shard_map/triangle/pallas_call | solution.py:373
  42.0 0.8 copy-done.7
  42.8 0.8 copy-done.15
  43.6 0.7 copy-done.33
  44.3 0.6 copy-done.39
  44.9 0.6 copy-done.41
  45.5 6.2 %left_back.1.refs_4_ = bf16[4,64,16,128]{3,2,1,0:T(8,128)(2,1)} custom-call(s32[2]{0:T(128)S(1)} %pad_add_fusion.ids, f32[64,32,128]{2,1,0:T(8,128)S(1)} %get-tuple-element.60.tri_back, f32[2048,128]{1,0:T(8,128)S(1)} %get-tuple-element.61.right_act), custom_call_target="tpu_custom_call" | custom-call | flops 1000 | bytes 1000 | tf_op jit(solution)/shard_map/left_back/pallas_call | solution.py:373
  51.8 4.1 %all-to-all-start = ((bf16[4,64,16,128]{3,2,1,0:T(8,128)(2,1)}), bf16[4,64,16,128]{3,2,1,0:T(8,128)(2,1)S(1)}, u32[]{:S(2)}, u32[]{:S(2)}) async-start(bf16[4,64,16,128]{3,2,1,0:T(8,128)(2,1)} %left_back.1.refs_4_), calls=%async_computation | async-start | bytes 2097152 | tf_op jit(solution)/shard_map/all_to_all | solution.py:459
  55.9 1.0 %copy-done.14 = f32[64,16,128]{2,1,0:T(8,128)S(1)} copy-done((f32[64,16,128]{2,1,0:T(8,128)S(1)}, f32[64,16,128]{2,1,0:T(8,128)}, u32[]{:S(2)}) %copy-start.14) | copy-done | bytes 524312
  56.9 1.0 %copy-done.16 = f32[64,16,128]{2,1,0:T(8,128)S(1)} copy-done((f32[64,16,128]{2,1,0:T(8,128)S(1)}, f32[64,16,128]{2,1,0:T(8,128)}, u32[]{:S(2)}) %copy-start.16) | copy-done | bytes 524312
  58.0 6.1 %right_back.1 = (bf16[32,16,128]{2,1,0:T(8,128)(2,1)S(1)}, bf16[32,16,128]{2,1,0:T(8,128)(2,1)S(1)}, bf16[32,16,128]{2,1,0:T(8,128)(2,1)S(1)}, bf16[32,16,128]{2,1,0:T(8,128)(2,1)S(1)}) custom-call(s32[2]{0:T(128)S(1)} %pad_add_fusion.ids, f32[64,32,128]{2,1,0:T(8,128)S(1)} %get-tuple-element.60.tri_back, f32[64,16,128]{2,1,0:T(8,128)S(1)} %copy-done.10, ...), custom_call_target="tpu_custom_call" | custom-call | flops 1000 | bytes 1000 | tf_op jit(solution)/shard_map/right_back/pallas_call | solution.py:373
  64.1 2.0 %collective-permute-start.6 = (bf16[32,16,128]{2,1,0:T(8,128)(2,1)S(1)}, bf16[32,16,128]{2,1,0:T(8,128)(2,1)S(1)}, u32[]{:S(2)}, u32[]{:S(2)}) collective-permute-start(bf16[32,16,128]{2,1,0:T(8,128)(2,1)S(1)} %get-tuple-element.67.refs_6_), channel_id=1, source_target_pairs={{0,24},{8,0},{16,8},{24,16},{1,25},{9,1},{17,9},{25,17},{2,26},{10... | collective-permute-start | bytes 393224 | tf_op jit(solution)/shard_map/ppermute | solution.py:333
  66.1 1.5 %collective-permute-start.7 = (bf16[32,16,128]{2,1,0:T(8,128)(2,1)S(1)}, bf16[32,16,128]{2,1,0:T(8,128)(2,1)S(1)}, u32[]{:S(2)}, u32[]{:S(2)}) collective-permute-start(bf16[32,16,128]{2,1,0:T(8,128)(2,1)S(1)} %get-tuple-element.68.refs_7_), channel_id=1, source_target_pairs={{0,16},{8,24},{16,0},{24,8},{1,17},{9,25},{17,1},{25,9},{2,18},{10... | collective-permute-start | bytes 393224 | tf_op jit(solution)/shard_map/ppermute | solution.py:333
  67.7 5.6 %weights.1 = (bf16[32,768]{1,0:T(8,128)(2,1)S(1)}, bf16[32,768]{1,0:T(8,128)(2,1)S(1)}, bf16[32,768]{1,0:T(8,128)(2,1)S(1)}, bf16[32,768]{1,0:T(8,128)(2,1)S(1)}) custom-call(s32[2]{0:T(128)S(1)} %pad_add_fusion.ids, bf16[4,32,16,128]{3,2,1,0:T(8,128)(2,1)S(1)} %copy-done.22, bf16[128,256]{1,0:T(8,128)(2,1)S(1)} %copy-done, bf16[128,256]{1,0:T(8,128)(2,1)S(1)} %copy-done.6, ...), custom_call_target="tpu_custom_call" | custom-call | flops 1000 | bytes 1000 | tf_op jit(solution)/shard_map/weights/pallas_call | solution.py:373
  73.2 2.0 %collective-permute-start.9 = (bf16[32,768]{1,0:T(8,128)(2,1)S(1)}, bf16[32,768]{1,0:T(8,128)(2,1)S(1)}, u32[]{:S(2)}, u32[]{:S(2)}) collective-permute-start(bf16[32,768]{1,0:T(8,128)(2,1)S(1)} %get-tuple-element.81), channel_id=1, source_target_pairs={{0,8},{8,16},{16,24},{24,0},{1,9},{9,17},{17,25},{25,1},{2,10},{10... | collective-permute-start | bytes 147464 | tf_op jit(solution)/shard_map/ppermute | solution.py:333
  75.3 1.5 %collective-permute-start.10 = (bf16[32,768]{1,0:T(8,128)(2,1)S(1)}, bf16[32,768]{1,0:T(8,128)(2,1)S(1)}, u32[]{:S(2)}, u32[]{:S(2)}) collective-permute-start(bf16[32,768]{1,0:T(8,128)(2,1)S(1)} %get-tuple-element.82), channel_id=1, source_target_pairs={{0,16},{8,24},{16,0},{24,8},{1,17},{9,25},{17,1},{25,9},{2,18},{10... | collective-permute-start | bytes 147464 | tf_op jit(solution)/shard_map/ppermute | solution.py:333
  76.8 1.7 %collective-permute-done.9.refs_1_ = bf16[32,768]{1,0:T(8,128)(2,1)S(1)} collective-permute-done((bf16[32,768]{1,0:T(8,128)(2,1)S(1)}, bf16[32,768]{1,0:T(8,128)(2,1)S(1)}, u32[]{:S(2)}, u32[]{:S(2)}) %collective-permute-start.9) | collective-permute-done | bytes 49184 | tf_op jit(solution)/shard_map/ppermute | solution.py:333
  78.4 1.9 %collective-permute-start.11 = (bf16[32,768]{1,0:T(8,128)(2,1)S(1)}, bf16[32,768]{1,0:T(8,128)(2,1)S(1)}, u32[]{:S(2)}, u32[]{:S(2)}) collective-permute-start(bf16[32,768]{1,0:T(8,128)(2,1)S(1)} %get-tuple-element.83), channel_id=1, source_target_pairs={{0,24},{8,0},{16,8},{24,16},{1,25},{9,1},{17,9},{25,17},{2,26},{10... | collective-permute-start | bytes 147464 | tf_op jit(solution)/shard_map/ppermute | solution.py:333
  80.3 2.2 %collective-permute-done.11.refs_3_ = bf16[32,768]{1,0:T(8,128)(2,1)S(1)} collective-permute-done((bf16[32,768]{1,0:T(8,128)(2,1)S(1)}, bf16[32,768]{1,0:T(8,128)(2,1)S(1)}, u32[]{:S(2)}, u32[]{:S(2)}) %collective-permute-start.11) | collective-permute-done | bytes 49184 | tf_op jit(solution)/shard_map/ppermute | solution.py:333
  82.6 3.7 %collective-permute-start.14 = (bf16[32,768]{1,0:T(8,128)(2,1)S(1)}, bf16[32,768]{1,0:T(8,128)(2,1)S(1)}, u32[]{:S(2)}, u32[]{:S(2)}) collective-permute-start(bf16[32,768]{1,0:T(8,128)(2,1)S(1)} %combine.2.refs_0_), channel_id=1, source_target_pairs={{0,6},{2,0},{4,2},{6,4},{1,7},{3,1},{5,3},{7,5},{8,14},{10,8},{12,... | collective-permute-start | bytes 147464 | tf_op jit(solution)/shard_map/ppermute | solution.py:333
  86.3 1.2 %collective-permute-start.12 = (bf16[32,768]{1,0:T(8,128)(2,1)S(1)}, bf16[32,768]{1,0:T(8,128)(2,1)S(1)}, u32[]{:S(2)}, u32[]{:S(2)}) collective-permute-start(bf16[32,768]{1,0:T(8,128)(2,1)S(1)} %combine.2.refs_0_), channel_id=1, source_target_pairs={{0,2},{2,4},{4,6},{6,0},{1,3},{3,5},{5,7},{7,1},{8,10},{10,12},{12... | collective-permute-start | bytes 147464 | tf_op jit(solution)/shard_map/ppermute | solution.py:333
  88.1 3.2 %collective-permute-done.13.refs_2_ = bf16[32,768]{1,0:T(8,128)(2,1)S(1)} collective-permute-done((bf16[32,768]{1,0:T(8,128)(2,1)S(1)}, bf16[32,768]{1,0:T(8,128)(2,1)S(1)}, u32[]{:S(2)}, u32[]{:S(2)}) %collective-permute-start.13) | collective-permute-done | bytes 49184 | tf_op jit(solution)/shard_map/ppermute | solution.py:333
  91.3 0.9 collective-permute-done.12.refs_1_
  92.2 3.0 %collective-permute-start.17 = (bf16[32,768]{1,0:T(8,128)(2,1)S(1)}, bf16[32,768]{1,0:T(8,128)(2,1)S(1)}, u32[]{:S(2)}, u32[]{:S(2)}) collective-permute-start(bf16[32,768]{1,0:T(8,128)(2,1)S(1)} %combine.3.refs_0_), channel_id=1, source_target_pairs={{0,24},{8,0},{16,8},{24,16},{1,25},{9,1},{17,9},{25,17},{2,26},{10... | collective-permute-start | bytes 147464 | tf_op jit(solution)/shard_map/ppermute | solution.py:333
  95.2 1.0 collective-permute-start.16
  96.2 2.4 %grad_middle.1 = bf16[64,32,128]{2,1,0:T(8,128)(2,1)} custom-call(bf16[64,32,128]{2,1,0:T(8,128)(2,1)S(1)} %copy-done.2, bf16[64,32,128]{2,1,0:T(8,128)(2,1)S(1)} %copy-done.8, bf16[128,128]{1,0:T(8,128)(2,1)S(1)} %copy-done.38), custom_call_target="tpu_custom_call" | custom-call | flops 1000 | bytes 1000 | tf_op jit(solution)/shard_map/grad_middle/pallas_call | solution.py:373
  98.7 2.9 %sides.1 = (bf16[64,16,128]{2,1,0:T(8,128)(2,1)}, bf16[32,16,128]{2,1,0:T(8,128)(2,1)}) custom-call(bf16[64,16,128]{2,1,0:T(8,128)(2,1)S(1)} %copy-done.5, bf16[32,16,128]{2,1,0:T(8,128)(2,1)S(1)} %copy-done.20, bf16[128,256]{1,0:T(8,128)(2,1)S(1)} %copy-done, bf16[128,256]{1,0:T(8,128)(2,1)S(1)} %copy-done.6, ...), custom_call_target="tpu_custom_call" | custom-call | flops 1000 | bytes 1000 | tf_op jit(solution)/shard_map/sides/pallas_call | solution.py:373
  101.6 1.3 %deltas.1 = (f32[128,256]{1,0:T(8,128)}, f32[128,256]{1,0:T(8,128)}, f32[128,128]{1,0:T(8,128)}, f32[128,128]{1,0:T(8,128)}) custom-call(s32[2]{0:T(128)S(1)} %pad_add_fusion.ids, bf16[32,768]{1,0:T(8,128)(2,1)S(1)} %combine.3.refs_0_, bf16[32,768]{1,0:T(8,128)(2,1)S(1)} %collective-permute-done.15.refs_1_, ...), custom_call_target="tpu_custom_call" | custom-call | flops 1000 | bytes 1000 | tf_op jit(solution)/shard_map/deltas/pallas_call | solution.py:373
  (91 shorter events, 1.4 us)
Async XLA Ops:
  0.6 10.0 %collective-permute-start.3 = (bf16[32,16,128]{2,1,0:T(8,128)(2,1)}, bf16[32,16,128]{2,1,0:T(8,128)(2,1)S(1)}, u32[]{:S(2)}, u32[]{:S(2)}) collective-permute-start(bf16[32,16,128]{2,1,0:T(8,128)(2,1)} %refs_1_.1), channel_id=1, source_target_pairs={{0,24},{8,0},{16,8},{24,16},{1,25},{9,1},{17,9},{25,17},{2,26},{10... | collective-permute-start | bytes 393224 | tf_op jit(solution)/shard_map/ppermute | solution.py:333
  4.6 20.5 %collective-permute-start.5 = (bf16[64,16,128]{2,1,0:T(8,128)(2,1)}, bf16[64,16,128]{2,1,0:T(8,128)(2,1)}, u32[]{:S(2)}, u32[]{:S(2)}) collective-permute-start(bf16[64,16,128]{2,1,0:T(8,128)(2,1)} %refs_0_.3), channel_id=1, source_target_pairs={{0,2},{2,4},{4,6},{6,0},{1,3},{3,5},{5,7},{7,1},{8,10},{10,12},{12... | collective-permute-start | bytes 786440 | tf_op jit(solution)/shard_map/ppermute | solution.py:333
  6.2 24.2 %collective-permute-start.4 = (bf16[64,16,128]{2,1,0:T(8,128)(2,1)}, bf16[64,16,128]{2,1,0:T(8,128)(2,1)}, u32[]{:S(2)}, u32[]{:S(2)}) collective-permute-start(bf16[64,16,128]{2,1,0:T(8,128)(2,1)} %refs_0_.3), channel_id=1, source_target_pairs={{0,4},{2,6},{4,0},{6,2},{1,5},{3,7},{5,1},{7,3},{8,12},{10,14},{12... | collective-permute-start | bytes 786440 | tf_op jit(solution)/shard_map/ppermute | solution.py:333
  8.7 26.8 %collective-permute-start = (bf16[64,16,128]{2,1,0:T(8,128)(2,1)}, bf16[64,16,128]{2,1,0:T(8,128)(2,1)}, u32[]{:S(2)}, u32[]{:S(2)}) collective-permute-start(bf16[64,16,128]{2,1,0:T(8,128)(2,1)} %refs_0_.3), channel_id=1, source_target_pairs={{0,6},{2,0},{4,2},{6,4},{1,7},{3,1},{5,3},{7,5},{8,14},{10,8},{12,... | collective-permute-start | bytes 786440 | tf_op jit(solution)/shard_map/ppermute | solution.py:333
  10.1 8.5 %collective-permute-start.2 = (bf16[32,16,128]{2,1,0:T(8,128)(2,1)}, bf16[32,16,128]{2,1,0:T(8,128)(2,1)S(1)}, u32[]{:S(2)}, u32[]{:S(2)}) collective-permute-start(bf16[32,16,128]{2,1,0:T(8,128)(2,1)} %refs_1_.1), channel_id=1, source_target_pairs={{0,16},{8,24},{16,0},{24,8},{1,17},{9,25},{17,1},{25,9},{2,18},{10... | collective-permute-start | bytes 393224 | tf_op jit(solution)/shard_map/ppermute | solution.py:333
  10.6 7.9 %collective-permute-start.1 = (bf16[32,16,128]{2,1,0:T(8,128)(2,1)}, bf16[32,16,128]{2,1,0:T(8,128)(2,1)S(1)}, u32[]{:S(2)}, u32[]{:S(2)}) collective-permute-start(bf16[32,16,128]{2,1,0:T(8,128)(2,1)} %refs_1_.1), channel_id=1, source_target_pairs={{0,8},{8,16},{16,24},{24,0},{1,9},{9,17},{17,25},{25,1},{2,10},{10... | collective-permute-start | bytes 393224 | tf_op jit(solution)/shard_map/ppermute | solution.py:333
  11.2 1.0 %copy-start.1 = (bf16[64,32,128]{2,1,0:T(8,128)(2,1)S(1)}, bf16[64,32,128]{2,1,0:T(8,128)(2,1)}, u32[]{:S(2)}) copy-start(bf16[64,32,128]{2,1,0:T(8,128)(2,1)} %middle.5) | copy-start | bytes 1572868
  12.2 1.0 %copy-start.3 = (bf16[64,32,128]{2,1,0:T(8,128)(2,1)S(1)}, bf16[64,32,128]{2,1,0:T(8,128)(2,1)}, u32[]{:S(2)}) copy-start(bf16[64,32,128]{2,1,0:T(8,128)(2,1)} %cotangent.3) | copy-start | bytes 1572868
  14.8 3.8 %copy-start.6 = (bf16[128,256]{1,0:T(8,128)(2,1)S(1)}, bf16[128,256]{1,0:T(8,128)(2,1)}, u32[]{:S(2)}) copy-start(bf16[128,256]{1,0:T(8,128)(2,1)} %right_w.1) | copy-start | bytes 196612
  14.8 3.8 %copy-start.19 = (bf16[32,16,128]{2,1,0:T(8,128)(2,1)S(1)}, bf16[32,16,128]{2,1,0:T(8,128)(2,1)}, u32[]{:S(2)}) copy-start(bf16[32,16,128]{2,1,0:T(8,128)(2,1)} %refs_1_.1) | copy-start | bytes 393220
  18.5 3.9 %copy-start = (bf16[128,256]{1,0:T(8,128)(2,1)S(1)}, bf16[128,256]{1,0:T(8,128)(2,1)}, u32[]{:S(2)}) copy-start(bf16[128,256]{1,0:T(8,128)(2,1)} %left_w.3) | copy-start | bytes 196612
  18.5 3.9 %copy-start.5 = (bf16[64,16,128]{2,1,0:T(8,128)(2,1)S(1)}, bf16[64,16,128]{2,1,0:T(8,128)(2,1)}, u32[]{:S(2)}) copy-start(bf16[64,16,128]{2,1,0:T(8,128)(2,1)} %refs_0_.3) | copy-start | bytes 786436
  22.4 6.4 %copy-start.21 = (bf16[4,32,16,128]{3,2,1,0:T(8,128)(2,1)}, bf16[4,32,16,128]{3,2,1,0:T(8,128)(2,1)S(1)}, u32[]{:S(2)}) copy-start(bf16[4,32,16,128]{3,2,1,0:T(8,128)(2,1)S(1)} %get-tuple-element.73.right_in) | copy-start | bytes 1572868
  25.0 3.8 %copy-start.9 = (f32[64,16,128]{2,1,0:T(8,128)}, f32[64,16,128]{2,1,0:T(8,128)S(1)}, u32[]{:S(2)}) copy-start(f32[64,16,128]{2,1,0:T(8,128)S(1)} %get-tuple-element.62.refs_0_) | copy-start | bytes 1572868
  25.0 3.8 %copy-start.27 = (bf16[64,16,128]{2,1,0:T(8,128)(2,1)}, bf16[64,16,128]{2,1,0:T(8,128)(2,1)S(1)}, u32[]{:S(2)}) copy-start(bf16[64,16,128]{2,1,0:T(8,128)(2,1)S(1)} %get-tuple-element.76.refs_0_) | copy-start | bytes 786436
  30.3 5.2 %copy-start.4 = (bf16[64,32,128]{2,1,0:T(8,128)(2,1)S(1)}, bf16[64,32,128]{2,1,0:T(8,128)(2,1)}, u32[]{:S(2)}) copy-start(bf16[64,32,128]{2,1,0:T(8,128)(2,1)} %cotangent.3) | copy-start | bytes 1572868
  30.3 5.2 %copy-start.24 = (bf16[64,32,128]{2,1,0:T(8,128)(2,1)S(1)}, bf16[64,32,128]{2,1,0:T(8,128)(2,1)}, u32[]{:S(2)}) copy-start(bf16[64,32,128]{2,1,0:T(8,128)(2,1)} %copy-done.23) | copy-start | bytes 1572868
  30.3 5.2 %copy-start.26 = (bf16[64,32,128]{2,1,0:T(8,128)(2,1)S(1)}, bf16[64,32,128]{2,1,0:T(8,128)(2,1)}, u32[]{:S(2)}) copy-start(bf16[64,32,128]{2,1,0:T(8,128)(2,1)} %copy-done.25) | copy-start | bytes 1572868
  30.4 5.2 %copy-start.36 = (bf16[128,128]{1,0:T(8,128)(2,1)S(1)}, bf16[128,128]{1,0:T(8,128)(2,1)}, u32[]{:S(2)}) copy-start(bf16[128,128]{1,0:T(8,128)(2,1)} %out_w.1) | copy-start | bytes 98308
  51.8 4.1 %copy-start.10 = (f32[64,16,128]{2,1,0:T(8,128)S(1)}, f32[64,16,128]{2,1,0:T(8,128)}, u32[]{:S(2)}) copy-start(f32[64,16,128]{2,1,0:T(8,128)} %copy-done.9) | copy-start | bytes 1572868
  51.8 4.1 %copy-start.12 = (f32[64,16,128]{2,1,0:T(8,128)S(1)}, f32[64,16,128]{2,1,0:T(8,128)}, u32[]{:S(2)}) copy-start(f32[64,16,128]{2,1,0:T(8,128)} %copy-done.11) | copy-start | bytes 1572868
  51.8 30.8 %all-to-all-start = ((bf16[4,64,16,128]{3,2,1,0:T(8,128)(2,1)}), bf16[4,64,16,128]{3,2,1,0:T(8,128)(2,1)S(1)}, u32[]{:S(2)}, u32[]{:S(2)}) async-start(bf16[4,64,16,128]{3,2,1,0:T(8,128)(2,1)} %left_back.1.refs_4_), calls=%async_computation | async-start | bytes 2097152 | tf_op jit(solution)/shard_map/all_to_all | solution.py:459
  55.9 1.0 %copy-start.14 = (f32[64,16,128]{2,1,0:T(8,128)S(1)}, f32[64,16,128]{2,1,0:T(8,128)}, u32[]{:S(2)}) copy-start(f32[64,16,128]{2,1,0:T(8,128)} %copy-done.13) | copy-start | bytes 1572868
  58.0 9.6 %copy-start.22 = (bf16[4,32,16,128]{3,2,1,0:T(8,128)(2,1)S(1)}, bf16[4,32,16,128]{3,2,1,0:T(8,128)(2,1)}, u32[]{:S(2)}) copy-start(bf16[4,32,16,128]{3,2,1,0:T(8,128)(2,1)} %copy-done.21) | copy-start | bytes 1572868
  58.0 9.6 %copy-start.28 = (bf16[64,16,128]{2,1,0:T(8,128)(2,1)S(1)}, bf16[64,16,128]{2,1,0:T(8,128)(2,1)}, u32[]{:S(2)}) copy-start(bf16[64,16,128]{2,1,0:T(8,128)(2,1)} %copy-done.27) | copy-start | bytes 786436
  58.0 9.7 %copy-start.30 = (bf16[64,16,128]{2,1,0:T(8,128)(2,1)S(1)}, bf16[64,16,128]{2,1,0:T(8,128)(2,1)}, u32[]{:S(2)}) copy-start(bf16[64,16,128]{2,1,0:T(8,128)(2,1)} %copy-done.29) | copy-start | bytes 786436
  58.0 9.7 %copy-start.32 = (bf16[64,16,128]{2,1,0:T(8,128)(2,1)S(1)}, bf16[64,16,128]{2,1,0:T(8,128)(2,1)}, u32[]{:S(2)}) copy-start(bf16[64,16,128]{2,1,0:T(8,128)(2,1)} %copy-done.31) | copy-start | bytes 786436
  58.0 9.7 %copy-start.34 = (bf16[64,16,128]{2,1,0:T(8,128)(2,1)S(1)}, bf16[64,16,128]{2,1,0:T(8,128)(2,1)}, u32[]{:S(2)}) copy-start(bf16[64,16,128]{2,1,0:T(8,128)(2,1)} %copy-done.33) | copy-start | bytes 786436
  58.0 9.7 %copy-start.40 = (f32[128,128]{1,0:T(8,128)S(1)}, f32[128,128]{1,0:T(8,128)}, u32[]{:S(2)}) copy-start(f32[128,128]{1,0:T(8,128)} %copy-done.39) | copy-start | bytes 196612
  58.0 9.7 %copy-start.42 = (f32[128,128]{1,0:T(8,128)S(1)}, f32[128,128]{1,0:T(8,128)}, u32[]{:S(2)}) copy-start(f32[128,128]{1,0:T(8,128)} %copy-done.41) | copy-start | bytes 196612
  64.1 9.1 %copy-start.17 = (bf16[32,16,128]{2,1,0:T(8,128)(2,1)}, bf16[32,16,128]{2,1,0:T(8,128)(2,1)S(1)}, u32[]{:S(2)}) copy-start(bf16[32,16,128]{2,1,0:T(8,128)(2,1)S(1)} %get-tuple-element.66.refs_5_) | copy-start | bytes 393220
  64.1 18.4 %collective-permute-start.6 = (bf16[32,16,128]{2,1,0:T(8,128)(2,1)S(1)}, bf16[32,16,128]{2,1,0:T(8,128)(2,1)S(1)}, u32[]{:S(2)}, u32[]{:S(2)}) collective-permute-start(bf16[32,16,128]{2,1,0:T(8,128)(2,1)S(1)} %get-tuple-element.67.refs_6_), channel_id=1, source_target_pairs={{0,24},{8,0},{16,8},{24,16},{1,25},{9,1},{17,9},{25,17},{2,26},{10... | collective-permute-start | bytes 393224 | tf_op jit(solution)/shard_map/ppermute | solution.py:333
  66.1 16.5 %collective-permute-start.7 = (bf16[32,16,128]{2,1,0:T(8,128)(2,1)S(1)}, bf16[32,16,128]{2,1,0:T(8,128)(2,1)S(1)}, u32[]{:S(2)}, u32[]{:S(2)}) collective-permute-start(bf16[32,16,128]{2,1,0:T(8,128)(2,1)S(1)} %get-tuple-element.68.refs_7_), channel_id=1, source_target_pairs={{0,16},{8,24},{16,0},{24,8},{1,17},{9,25},{17,1},{25,9},{2,18},{10... | collective-permute-start | bytes 393224 | tf_op jit(solution)/shard_map/ppermute | solution.py:333
  67.6 14.9 %collective-permute-start.8 = (bf16[32,16,128]{2,1,0:T(8,128)(2,1)S(1)}, bf16[32,16,128]{2,1,0:T(8,128)(2,1)S(1)}, u32[]{:S(2)}, u32[]{:S(2)}) collective-permute-start(bf16[32,16,128]{2,1,0:T(8,128)(2,1)S(1)} %get-tuple-element.69.refs_8_), channel_id=1, source_target_pairs={{0,8},{8,16},{16,24},{24,0},{1,9},{9,17},{17,25},{25,1},{2,10},{10... | collective-permute-start | bytes 393224 | tf_op jit(solution)/shard_map/ppermute | solution.py:333
  73.2 5.2 %collective-permute-start.9 = (bf16[32,768]{1,0:T(8,128)(2,1)S(1)}, bf16[32,768]{1,0:T(8,128)(2,1)S(1)}, u32[]{:S(2)}, u32[]{:S(2)}) collective-permute-start(bf16[32,768]{1,0:T(8,128)(2,1)S(1)} %get-tuple-element.81), channel_id=1, source_target_pairs={{0,8},{8,16},{16,24},{24,0},{1,9},{9,17},{17,25},{25,1},{2,10},{10... | collective-permute-start | bytes 147464 | tf_op jit(solution)/shard_map/ppermute | solution.py:333
  75.3 5.0 %collective-permute-start.10 = (bf16[32,768]{1,0:T(8,128)(2,1)S(1)}, bf16[32,768]{1,0:T(8,128)(2,1)S(1)}, u32[]{:S(2)}, u32[]{:S(2)}) collective-permute-start(bf16[32,768]{1,0:T(8,128)(2,1)S(1)} %get-tuple-element.82), channel_id=1, source_target_pairs={{0,16},{8,24},{16,0},{24,8},{1,17},{9,25},{17,1},{25,9},{2,18},{10... | collective-permute-start | bytes 147464 | tf_op jit(solution)/shard_map/ppermute | solution.py:333
  78.4 4.1 %collective-permute-start.11 = (bf16[32,768]{1,0:T(8,128)(2,1)S(1)}, bf16[32,768]{1,0:T(8,128)(2,1)S(1)}, u32[]{:S(2)}, u32[]{:S(2)}) collective-permute-start(bf16[32,768]{1,0:T(8,128)(2,1)S(1)} %get-tuple-element.83), channel_id=1, source_target_pairs={{0,24},{8,0},{16,8},{24,16},{1,25},{9,1},{17,9},{25,17},{2,26},{10... | collective-permute-start | bytes 147464 | tf_op jit(solution)/shard_map/ppermute | solution.py:333
  82.5 13.6 %copy-start.2 = (bf16[64,32,128]{2,1,0:T(8,128)(2,1)S(1)}, bf16[64,32,128]{2,1,0:T(8,128)(2,1)}, u32[]{:S(2)}) copy-start(bf16[64,32,128]{2,1,0:T(8,128)(2,1)} %middle.5) | copy-start | bytes 1572868
  82.6 13.6 %copy-start.8 = (bf16[64,32,128]{2,1,0:T(8,128)(2,1)S(1)}, bf16[64,32,128]{2,1,0:T(8,128)(2,1)}, u32[]{:S(2)}) copy-start(bf16[64,32,128]{2,1,0:T(8,128)(2,1)} %copy-done.7) | copy-start | bytes 1572868
  82.6 13.6 %copy-start.38 = (bf16[128,128]{1,0:T(8,128)(2,1)S(1)}, bf16[128,128]{1,0:T(8,128)(2,1)}, u32[]{:S(2)}) copy-start(bf16[128,128]{1,0:T(8,128)(2,1)} %gate_weight.3) | copy-start | bytes 98308
  82.6 5.4 %collective-permute-start.14 = (bf16[32,768]{1,0:T(8,128)(2,1)S(1)}, bf16[32,768]{1,0:T(8,128)(2,1)S(1)}, u32[]{:S(2)}, u32[]{:S(2)}) collective-permute-start(bf16[32,768]{1,0:T(8,128)(2,1)S(1)} %combine.2.refs_0_), channel_id=1, source_target_pairs={{0,6},{2,0},{4,2},{6,4},{1,7},{3,1},{5,3},{7,5},{8,14},{10,8},{12,... | collective-permute-start | bytes 147464 | tf_op jit(solution)/shard_map/ppermute | solution.py:333
  86.3 5.0 %collective-permute-start.13 = (bf16[32,768]{1,0:T(8,128)(2,1)S(1)}, bf16[32,768]{1,0:T(8,128)(2,1)S(1)}, u32[]{:S(2)}, u32[]{:S(2)}) collective-permute-start(bf16[32,768]{1,0:T(8,128)(2,1)S(1)} %combine.2.refs_0_), channel_id=1, source_target_pairs={{0,4},{2,6},{4,0},{6,2},{1,5},{3,7},{5,1},{7,3},{8,12},{10,14},{12... | collective-permute-start | bytes 147464 | tf_op jit(solution)/shard_map/ppermute | solution.py:333
  86.3 5.9 %collective-permute-start.12 = (bf16[32,768]{1,0:T(8,128)(2,1)S(1)}, bf16[32,768]{1,0:T(8,128)(2,1)S(1)}, u32[]{:S(2)}, u32[]{:S(2)}) collective-permute-start(bf16[32,768]{1,0:T(8,128)(2,1)S(1)} %combine.2.refs_0_), channel_id=1, source_target_pairs={{0,2},{2,4},{4,6},{6,0},{1,3},{3,5},{5,7},{7,1},{8,10},{10,12},{12... | collective-permute-start | bytes 147464 | tf_op jit(solution)/shard_map/ppermute | solution.py:333
  92.2 9.3 %collective-permute-start.17 = (bf16[32,768]{1,0:T(8,128)(2,1)S(1)}, bf16[32,768]{1,0:T(8,128)(2,1)S(1)}, u32[]{:S(2)}, u32[]{:S(2)}) collective-permute-start(bf16[32,768]{1,0:T(8,128)(2,1)S(1)} %combine.3.refs_0_), channel_id=1, source_target_pairs={{0,24},{8,0},{16,8},{24,16},{1,25},{9,1},{17,9},{25,17},{2,26},{10... | collective-permute-start | bytes 147464 | tf_op jit(solution)/shard_map/ppermute | solution.py:333
  95.2 6.4 %collective-permute-start.16 = (bf16[32,768]{1,0:T(8,128)(2,1)S(1)}, bf16[32,768]{1,0:T(8,128)(2,1)S(1)}, u32[]{:S(2)}, u32[]{:S(2)}) collective-permute-start(bf16[32,768]{1,0:T(8,128)(2,1)S(1)} %combine.3.refs_0_), channel_id=1, source_target_pairs={{0,16},{8,24},{16,0},{24,8},{1,17},{9,25},{17,1},{25,9},{2,18},{10... | collective-permute-start | bytes 147464 | tf_op jit(solution)/shard_map/ppermute | solution.py:333
  96.2 5.4 %collective-permute-start.15 = (bf16[32,768]{1,0:T(8,128)(2,1)S(1)}, bf16[32,768]{1,0:T(8,128)(2,1)S(1)}, u32[]{:S(2)}, u32[]{:S(2)}) collective-permute-start(bf16[32,768]{1,0:T(8,128)(2,1)S(1)} %combine.3.refs_0_), channel_id=1, source_target_pairs={{0,8},{8,16},{16,24},{24,0},{1,9},{9,17},{17,25},{25,1},{2,10},{10... | collective-permute-start | bytes 147464 | tf_op jit(solution)/shard_map/ppermute | solution.py:333
  96.2 2.5 %copy-start.18 = (bf16[32,16,128]{2,1,0:T(8,128)(2,1)S(1)}, bf16[32,16,128]{2,1,0:T(8,128)(2,1)}, u32[]{:S(2)}) copy-start(bf16[32,16,128]{2,1,0:T(8,128)(2,1)} %copy-done.17) | copy-start | bytes 393220
  96.2 2.5 %copy-start.20 = (bf16[32,16,128]{2,1,0:T(8,128)(2,1)S(1)}, bf16[32,16,128]{2,1,0:T(8,128)(2,1)}, u32[]{:S(2)}) copy-start(bf16[32,16,128]{2,1,0:T(8,128)(2,1)} %refs_1_.1) | copy-start | bytes 393220
  (14 other events, 10.7 us)

commit v4 on v3

--- a/solution.py
+++ b/solution.py
@@ -52,9 +52,19 @@
     return jnp.concatenate([back * sw, back * lin * sw * (1.0 - sw)], axis=-1).astype(bf16)
 
 
-def middle_kernel(middle, cotangent, gate_weight, output_weight, gate, middle_in, head_back, tri_up):
+def middle_kernel(*refs):
+    sources, refs = refs[:4], refs[4:]
+    gate, middle_in, head_back, tri_up, middle, cotangent, gate_weight, output_weight, arrived = refs
     n_i, n_j, width = middle.shape
     step = 8
+    copies = [
+        pltpu.make_async_copy(source, target, arrived.at[at])
+        for at, (source, target) in enumerate(zip(sources, (middle, cotangent, gate_weight, output_weight)))
+    ]
+    for copy in copies:
+        copy.start()
+    for copy in copies:
+        copy.wait()
 
     def body(at, _):
         rows = pl.ds(at * step, step)
@@ -71,7 +81,7 @@
     lax.fori_loop(0, n_i // step, body, 0, unroll=2)
 
 
-def right_kernel(n_rows, n_blk, k_left, ids, *refs):
+def right_kernel(n_rows, n_blk, k_left, *refs):
     raw, (weight, act_out, in_out, *flip_out) = refs[:n_rows], refs[n_rows:]
     n_j, k_right, width = raw[0].shape
     n_k = k_left * n_blk
@@ -87,7 +97,7 @@
             lin, sw = gated(inputs, weight[...])
             act = (sw * lin).astype(bf16).astype(f32).reshape(step, k_right, width)
             for part in range(k_right // unit):
-                at_k = place(ids, n_rows, n_blk, k_left, k_right, s, part)
+                at_k = place(n_rows, n_blk, k_left, k_right, s, part)
                 for j in range(step):
                     start = pl.multiple_of((at * step + j) * n_k + at_k, unit)
                     act_out[pl.ds(start, unit), :] = act[j, part * unit : (part + 1) * unit]
@@ -104,11 +114,11 @@
         lax.fori_loop(0, k_left, flip, 0, unroll=True)
 
 
-def place(ids, n_rows, n_blk, k_left, k_right, piece, part):
+def place(n_rows, n_blk, k_left, k_right, piece, part):
     unit = math.gcd(k_left, k_right)
-    vertex = lax.rem(ids[0] - piece + n_rows, n_rows) * k_right + part * unit
+    vertex = lax.rem(lax.axis_index("rows") - piece + n_rows, n_rows) * k_right + part * unit
     block = vertex // k_left
-    at = lax.rem(ids[1] - block + n_blk, n_blk) * k_left + vertex - block * k_left
+    at = lax.rem(lax.axis_index("blk") - block + n_blk, n_blk) * k_left + vertex - block * k_left
     return pl.multiple_of(at, unit)
 
 
@@ -128,8 +138,9 @@
     lax.fori_loop(0, n_i // step, body, 0, unroll=2)
 
 
-def add_vertices(total, rows, act, flip):
-    for k in range(act.shape[1]):
+def add_vertices(rows, act, flip):
+    total = act[rows, 0:1, :] * flip[0][None]
+    for k in range(1, act.shape[1]):
         total = total + act[rows, k : k + 1, :] * flip[k][None]
     return total
 
@@ -142,8 +153,8 @@
 
     def body(at, _):
         rows = pl.ds(at * step, step)
-        total = jnp.zeros((step, n_j, width), f32) if first else total_in[0][rows]
-        total_out[rows] = add_vertices(total, rows, act_out, flip)
+        total = add_vertices(rows, act_out, flip)
+        total_out[rows] = total if first else total_in[0][rows] + total
         return 0
 
     lax.fori_loop(0, n_i // step, body, 0)
@@ -162,8 +173,9 @@
 
     def triangle_rows(at, _):
         rows = pl.ds(at * step, step)
-        total = total_in[0][rows] if has_total else jnp.zeros((step, n_j, width), f32)
-        total = add_vertices(total, rows, act_out, flip)
+        total = add_vertices(rows, act_out, flip)
+        if has_total:
+            total = total + total_in[0][rows]
         flat = step * n_j
         normed, inverse = normalize(total.reshape(flat, width))
         tri_in = normed.astype(bf16)
@@ -189,10 +201,10 @@
     return size
 
 
-def left_back_kernel(ids, tri_back, right_act, left_out):
+def left_back_kernel(tri_back, right_act, *left_out):
     n_i, n_j, width = tri_back.shape
-    n_blk, _, k_left, _ = left_out.shape
-    n_k = k_left * n_blk
+    k_left = left_out[0].shape[1]
+    n_k = k_left * len(left_out)
     few = 4
     k_step = vertex_step(n_k, k_left)
     for k0 in range(0, n_k, k_step):
@@ -205,17 +217,13 @@
                 total = total + tri_back[rows, j : j + 1, :] * right_act[start : start + k_step, :][None]
             total = total.astype(bf16)
             for s in range(k0 // k_left, (k0 + k_step) // k_left):
-                left_out[owner(ids, n_blk, s), rows] = total[:, s * k_left - k0 : (s + 1) * k_left - k0]
+                left_out[s][rows] = total[:, s * k_left - k0 : (s + 1) * k_left - k0]
             return 0
 
         lax.fori_loop(0, n_i // few, rows_sum, 0)
 
 
-def owner(ids, n_blk, piece):
-    return lax.rem(ids[1] - piece + n_blk, n_blk)
-
-
-def right_back_kernel(n_rows, n_blk, ids, tri_back, *refs):
+def right_back_kernel(n_rows, n_blk, tri_back, *refs):
     left_act, refs = refs[:n_blk], refs[n_blk + 1 :]
     right_out, (right_sum,) = refs[:n_rows], refs[n_rows:]
     n_i, n_j, width = tri_back.shape
@@ -248,21 +256,21 @@
     for s in range(n_rows):
         for part in range(k_right // unit):
             right_out[s][:, part * unit : (part + 1) * unit, :] = right_sum[
-                :, pl.ds(place(ids, n_rows, n_blk, k_left, k_right, s, part), unit), :
+                :, pl.ds(place(n_rows, n_blk, k_left, k_right, s, part), unit), :
             ]
 
 
-def weights_kernel(n_rows, n_blk, ids, right_in, left_w, right_w, gate_part, output_part, *refs):
+def weights_kernel(n_rows, n_blk, right_in, left_w, right_w, gate_part, output_part, *refs):
     left_in, refs = refs[:n_blk], refs[n_blk:]
-    left_out, right_out, refs = refs[0], refs[1 : 1 + n_rows], refs[1 + n_rows :]
+    left_out, refs = refs[:n_blk], refs[n_blk:]
+    right_out, refs = refs[:n_rows], refs[n_rows:]
     pieces, (total,) = refs[:n_rows], refs[n_rows:]
-    left_backs = [left_out.at[owner(ids, n_blk, s)] for s in range(n_blk)]
     right_ins = [right_in.at[s] for s in range(n_rows)]
     width = gate_part.shape[0]
     total[:, 4 * width : 5 * width] = gate_part[...]
     total[:, 5 * width :] = output_part[...]
     for inputs_refs, weight, backs, first in (
-        (left_in, left_w, left_backs, 0),
+        (left_in, left_w, left_out, 0),
         (right_ins, right_w, right_out, 2 * width),
     ):
         columns = slice(first, first + 2 * width)
@@ -283,7 +291,7 @@
             lax.fori_loop(0, n // step, body, 0, unroll=2)
     size = width // n_rows
     for s, piece in enumerate(pieces):
-        start = pl.multiple_of(lax.rem(ids[0] + s, n_rows) * size, size)
+        start = pl.multiple_of(lax.rem(lax.axis_index("rows") + s, n_rows) * size, size)
         piece[...] = total[pl.ds(start, size), :].astype(bf16)
 
 
@@ -302,10 +310,9 @@
     lax.fori_loop(0, n_i // step, body, 0, unroll=2)
 
 
-def side_kernel(n_right, *refs):
-    left, right, left_w, right_w, left_backs = refs[:5]
-    refs = refs[5:]
-    left_back = [left_backs.at[s] for s in range(left_backs.shape[0])]
+def side_kernel(n_left, n_right, *refs):
+    left, right, left_w, right_w = refs[:4]
+    left_back, refs = refs[4 : 4 + n_left], refs[4 + n_left :]
     right_back, refs = refs[:n_right], refs[n_right:]
     for raw, weight, backs, grad in (
         (left, left_w, left_back, refs[0]),
@@ -350,11 +357,11 @@
     return total
 
 
-def deltas_kernel(n_rows, ids, *refs):
+def deltas_kernel(n_rows, *refs):
     pieces, outs = refs[:n_rows], refs[n_rows:]
     size = pieces[0].shape[0]
     for s, piece in enumerate(pieces):
-        start = pl.multiple_of(lax.rem(ids[0] - s + n_rows, n_rows) * size, size)
+        start = pl.multiple_of(lax.rem(lax.axis_index("rows") - s + n_rows, n_rows) * size, size)
         first = 0
         for out in outs:
             last = first + out.shape[1]
@@ -366,10 +373,10 @@
     return jax.ShapeDtypeStruct(tuple(dims), kind)
 
 
-def call(kernel, name, outs, scalars=0, scratch=(), after=0):
+def call(kernel, name, outs, scratch=(), after=0):
     def run(*operands):
-        spaces = [pltpu.SMEM] * scalars + [pltpu.VMEM] * (len(operands) - scalars - after) + [pl.ANY] * after
-        held = sum(math.prod(x.shape) * x.dtype.itemsize for x in scratch)
+        spaces = [pltpu.VMEM] * (len(operands) - after) + [pl.ANY] * after
+        held = sum(math.prod(x.shape) * 4 for x in scratch)
         return pl.pallas_call(
             kernel,
             in_specs=[pl.BlockSpec(memory_space=space) for space in spaces],
@@ -406,15 +413,18 @@
         middle_kernel,
         "middle",
         [shape(middle_shape, f32), shape(middle_shape, bf16), shape(middle_shape, bf16), shape(middle_shape, f32)],
+        scratch=[
+            *(pltpu.VMEM(x.shape, bf16) for x in (pair_middle, cotangent, gate_weight, output_weight)),
+            pltpu.SemaphoreType.DMA((4,)),
+        ],
+        after=4,
     )(pair_middle, cotangent, gate_weight, output_weight)
-    ids = jnp.stack([lax.axis_index("rows"), lax.axis_index("blk")]).astype(jnp.int32)
     right_act, right_in, *right_flip = call(
         functools.partial(right_kernel, n_rows, n_blk, k_left),
         "right",
         [shape((n_j * n_k, width), f32), shape((n_rows, n_j, k_right, width), bf16)]
         + [shape((k_left, n_j, width), f32)] * n_blk,
-        scalars=1,
-    )(ids, *right_raw, right_weight)
+    )(*right_raw, right_weight)
     left_act, left_in, total = [], [], []
     act_shape = shape(pair_left.shape, f32)
     in_shape = shape(pair_left.shape, bf16)
@@ -453,18 +463,17 @@
     )
     left_act.append(act)
     left_in.append(inputs)
-    (left_out,) = call(
-        left_back_kernel, "left_back", [shape((n_blk,) + pair_left.shape, bf16)], scalars=1
-    )(ids, tri_back, right_act)
-    left_back = lax.all_to_all(left_out, "blk", 0, 0)
+    left_out = call(left_back_kernel, "left_back", [shape(pair_left.shape, bf16)] * n_blk)(
+        tri_back, right_act
+    )
+    left_back = [left_out[0]] + [shift(left_out[s], "blk", n_blk, n_blk - s) for s in range(1, n_blk)]
     right_out = call(
         functools.partial(right_back_kernel, n_rows, n_blk),
         "right_back",
         [shape(pair_right.shape, bf16)] * n_rows,
-        scalars=1,
         scratch=[pltpu.VMEM((n_j, n_k, width), bf16)],
         after=1,
-    )(ids, tri_back, *left_act, left_out)
+    )(tri_back, *left_act, left_out[0])
     right_back = [right_out[0]] + [
         shift(right_out[s], "rows", n_rows, n_rows - s) for s in range(1, n_rows)
     ]
@@ -472,27 +481,25 @@
         functools.partial(weights_kernel, n_rows, n_blk),
         "weights",
         [shape((width // n_rows, 6 * width), bf16)] * n_rows,
-        scalars=1,
         scratch=[pltpu.VMEM((width, 6 * width), f32)],
-    )(ids, right_in, left_weight, right_weight, gate_part, output_part, *left_in, left_out, *right_out)
+    )(right_in, left_weight, right_weight, gate_part, output_part, *left_in, *left_out, *right_out)
     pieces = [pieces[0]] + [shift(pieces[s], "rows", n_rows, s) for s in range(1, n_rows)]
-    part = combine(pieces, (left_back, *right_back[1:]))
+    part = combine(pieces, (*left_back[1:], *right_back[1:]))
     part = combine([part] + [shift(part, "blk", n_blk, s) for s in range(1, n_blk)])
     pieces = [part] + [shift(part, "rows", n_rows, s) for s in range(1, n_rows)]
     deltas = call(
         functools.partial(deltas_kernel, n_rows),
         "deltas",
         [shape(x.shape, f32) for x in (left_weight, right_weight, gate_weight, output_weight)],
-        scalars=1,
-    )(ids, *pieces)
+    )(*pieces)
     (grad_middle,) = call(grad_middle_kernel, "grad_middle", [shape(middle_shape, bf16)])(
         pair_middle, pre_back, gate_weight
     )
     grad_left, grad_right = call(
-        functools.partial(side_kernel, n_rows),
+        functools.partial(side_kernel, n_blk, n_rows),
         "sides",
         [shape(pair_left.shape, bf16), shape(pair_right.shape, bf16)],
-    )(pair_left, pair_right, left_weight, right_weight, left_back, *right_back)
+    )(pair_left, pair_right, left_weight, right_weight, *left_back, *right_back)
     return (
         update,
         grad_left,

time: 104 us -> 97.5 us (0.938)
  waiting for transfers between devices: 8.61 us -> 21.9 us
  local copies, waits for them, and re-layouts: 14 us -> 3.63 us
  Pallas kernels: 46.9 us -> 39.5 us
  starting transfers between devices: 32.4 us -> 31.3 us
    ppermute x18 -> x21, waiting for transfers between devices: 8.6 us -> 21.9 us  [shift(): return lax.ppermute(x, axis, [(a, (a + step) % n) for a in range(n)])]
    unnamed x86 -> x22, local copies, waits for them, and re-layouts: 14 us -> 3.63 us
    pallas_call x14, Pallas kernels: 46.9 us -> 39.5 us  [run(): pl.pallas_call(kernel, in_specs=[pl.BlockSpec(memory_space=space) for spa...]
    all_to_all x1 -> x0, starting transfers between devices: 4.09 us -> none  [per_device(): left_back = lax.all_to_all(left_out, 'blk', 0, 0)]
    ppermute x18 -> x21, starting transfers between devices: 28.3 us -> 31.3 us  [shift(): return lax.ppermute(x, axis, [(a, (a + step) % n) for a in range(n)])]
  transfers between devices with their start and end apart: 19 -> 21, of which waited for: 5 -> 8; matrix products, arithmetic and copies ran while one was open for 0% -> 0% of each run, Pallas kernels for 32% -> 19%
where the time goes in v4:
time: 97.5 us; the launch traced here: 97.1 us
  Pallas kernels  39.5 us (41%)
  starting transfers between devices  31.3 us (32%)
  waiting for transfers between devices  21.9 us (22%)
  local copies, waits for them, and re-layouts  3.63 us (4%)
    pallas_call x14, Pallas kernels, run(): pl.pallas_call(kernel, in_specs=[pl.BlockSpec(memory_space=space) for spa...  39.5 us
    ppermute x21, starting transfers between devices, shift(): return lax.ppermute(x, axis, [(a, (a + step) % n) for a in range(n)])  31.3 us
    ppermute x21, waiting for transfers between devices, shift(): return lax.ppermute(x, axis, [(a, (a + step) % n) for a in range(n)])  21.9 us
    unnamed x22, local copies, waits for them, and re-layouts  3.63 us
  transfers between devices with their start and end apart: 21, of which 8 were waited for; matrix products, arithmetic and copies ran while one was open for 0% of the time, Pallas kernels for 19%

profile of v4, /device:TPU:0, one launch (start us, length us, event | category | flops | bytes accessed | tf_op | source)
XLA Modules:
  0.0 97.1 jit_solution(14934944150712506576)
XLA Ops:
  0.6 3.9 %collective-permute-start.3 = (bf16[32,16,128]{2,1,0:T(8,128)(2,1)}, bf16[32,16,128]{2,1,0:T(8,128)(2,1)S(1)}, u32[]{:S(2)}, u32[]{:S(2)}) collective-permute-start(bf16[32,16,128]{2,1,0:T(8,128)(2,1)} %refs_1_.3), channel_id=1, source_target_pairs={{0,24},{8,0},{16,8},{24,16},{1,25},{9,1},{17,9},{25,17},{2,26},{10... | collective-permute-start | bytes 393224 | tf_op jit(solution)/shard_map/ppermute | solution.py:340
  4.6 1.6 %collective-permute-start.5 = (bf16[64,16,128]{2,1,0:T(8,128)(2,1)}, bf16[64,16,128]{2,1,0:T(8,128)(2,1)S(1)}, u32[]{:S(2)}, u32[]{:S(2)}) collective-permute-start(bf16[64,16,128]{2,1,0:T(8,128)(2,1)} %refs_0_.5), channel_id=1, source_target_pairs={{0,2},{2,4},{4,6},{6,0},{1,3},{3,5},{5,7},{7,1},{8,10},{10,12},{12... | collective-permute-start | bytes 786440 | tf_op jit(solution)/shard_map/ppermute | solution.py:340
  6.2 2.6 %collective-permute-start.4 = (bf16[64,16,128]{2,1,0:T(8,128)(2,1)}, bf16[64,16,128]{2,1,0:T(8,128)(2,1)S(1)}, u32[]{:S(2)}, u32[]{:S(2)}) collective-permute-start(bf16[64,16,128]{2,1,0:T(8,128)(2,1)} %refs_0_.5), channel_id=1, source_target_pairs={{0,4},{2,6},{4,0},{6,2},{1,5},{3,7},{5,1},{7,3},{8,12},{10,14},{12... | collective-permute-start | bytes 786440 | tf_op jit(solution)/shard_map/ppermute | solution.py:340
  8.7 1.3 %collective-permute-start = (bf16[64,16,128]{2,1,0:T(8,128)(2,1)}, bf16[64,16,128]{2,1,0:T(8,128)(2,1)S(1)}, u32[]{:S(2)}, u32[]{:S(2)}) collective-permute-start(bf16[64,16,128]{2,1,0:T(8,128)(2,1)} %refs_0_.5), channel_id=1, source_target_pairs={{0,6},{2,0},{4,2},{6,4},{1,7},{3,1},{5,3},{7,5},{8,14},{10,8},{12,... | collective-permute-start | bytes 786440 | tf_op jit(solution)/shard_map/ppermute | solution.py:340
  10.1 0.5 collective-permute-start.2
  10.6 0.6 collective-permute-start.1
  11.2 1.0 %copy-done.1 = bf16[64,32,128]{2,1,0:T(8,128)(2,1)S(1)} copy-done((bf16[64,32,128]{2,1,0:T(8,128)(2,1)S(1)}, bf16[64,32,128]{2,1,0:T(8,128)(2,1)}, u32[]{:S(2)}) %copy-start.1) | copy-done | bytes 524312
  12.2 1.0 %copy-done.3 = bf16[64,32,128]{2,1,0:T(8,128)(2,1)S(1)} copy-done((bf16[64,32,128]{2,1,0:T(8,128)(2,1)S(1)}, bf16[64,32,128]{2,1,0:T(8,128)(2,1)}, u32[]{:S(2)}) %copy-start.3) | copy-done | bytes 524312
  13.3 0.8 copy-done.8
  14.0 0.8 copy-done.9
  14.8 2.3 %middle.2 = (f32[64,32,128]{2,1,0:T(8,128)S(1)}, bf16[64,32,128]{2,1,0:T(8,128)(2,1)S(1)}, bf16[64,32,128]{2,1,0:T(8,128)(2,1)S(1)}, f32[64,32,128]{2,1,0:T(8,128)S(1)}) custom-call(bf16[64,32,128]{2,1,0:T(8,128)(2,1)S(1)} %copy-done.1, bf16[64,32,128]{2,1,0:T(8,128)(2,1)S(1)} %copy-done.3, bf16[128,128]{1,0:T(8,128)(2,1)S(1)} %copy-done.9, ...), custom_call_target="tpu_custom_call" | custom-call | flops 1000 | bytes 1000 | tf_op jit(solution)/shard_map/middle/pallas_call | solution.py:380
  17.1 0.0 copy-start
  17.1 0.0 copy-start.5
  17.1 0.1 collective-permute-done.2.refs_2_
  17.2 3.3 %right.1 = (f32[2048,128]{1,0:T(8,128)S(1)}, bf16[4,32,16,128]{3,2,1,0:T(8,128)(2,1)S(1)}, f32[16,32,128]{2,1,0:T(8,128)S(1)}, f32[16,32,128]{2,1,0:T(8,128)S(1)...) custom-call(bf16[32,16,128]{2,1,0:T(8,128)(2,1)S(1)} %copy-done.7, ...), custom_call_target="tpu_custom_call" | custom-call | flops 1000 | bytes 1000 | tf_op jit(solution)/shard_map/right/pallas_call | solution.py:380
  20.6 2.5 %left.3 = (f32[64,16,128]{2,1,0:T(8,128)S(1)}, bf16[64,16,128]{2,1,0:T(8,128)(2,1)S(1)}, f32[64,32,128]{2,1,0:T(8,128)S(1)}) custom-call(bf16[64,16,128]{2,1,0:T(8,128)(2,1)S(1)} %copy-done.5, bf16[128,256]{1,0:T(8,128)(2,1)S(1)} %copy-done, f32[16,32,128]{2,1,0:T(8,128)S(1)} %get-tuple-element.59.flip), custom_call_target="tpu_custom_call" | custom-call | flops 1000 | bytes 1000 | tf_op jit(solution)/shard_map/left/pallas_call | solution.py:380
  23.2 2.6 %left.4 = (f32[64,16,128]{2,1,0:T(8,128)S(1)}, bf16[64,16,128]{2,1,0:T(8,128)(2,1)S(1)}, f32[64,32,128]{2,1,0:T(8,128)S(1)}) custom-call(bf16[64,16,128]{2,1,0:T(8,128)(2,1)S(1)} %collective-permute-done.5.raw, bf16[128,256]{1,0:T(8,128)(2,1)S(1)} %copy-done, f32[16,32,128]{2,1,0:T(8,128)S(1)} %get-tuple-element.58.flip, ...), custom_call_target="tpu_custom_call" | custom-call | flops 1000 | bytes 1000 | tf_op jit(solution)/shard_map/left/pallas_call | solution.py:380
  25.7 0.0 collective-permute-done.4.raw
  25.8 2.6 %left.5 = (f32[64,16,128]{2,1,0:T(8,128)S(1)}, bf16[64,16,128]{2,1,0:T(8,128)(2,1)S(1)}, f32[64,32,128]{2,1,0:T(8,128)S(1)}) custom-call(bf16[64,16,128]{2,1,0:T(8,128)(2,1)S(1)} %collective-permute-done.4.raw, bf16[128,256]{1,0:T(8,128)(2,1)S(1)} %copy-done, f32[16,32,128]{2,1,0:T(8,128)S(1)} %get-tuple-element.57.flip, ...), custom_call_target="tpu_custom_call" | custom-call | flops 1000 | bytes 1000 | tf_op jit(solution)/shard_map/left/pallas_call | solution.py:380
  28.4 5.5 %triangle.1 = (f32[64,16,128]{2,1,0:T(8,128)S(1)}, bf16[64,16,128]{2,1,0:T(8,128)(2,1)S(1)}, bf16[64,32,128]{2,1,0:T(8,128)(2,1)}, bf16[64,32,128]{2,1,0:T(8,128...) custom-call(bf16[64,16,128]{2,1,0:T(8,128)(2,1)S(1)} %collective-permute-done.raw, ...), custom_call_target="tpu_custom_call" | custom-call | flops 1000 | bytes 1000 | tf_op jit(solution)/shard_map/triangle/pallas_call | solution.py:380
  33.9 4.7 %left_back.1 = (bf16[64,16,128]{2,1,0:T(8,128)(2,1)S(1)}, bf16[64,16,128]{2,1,0:T(8,128)(2,1)S(1)}, bf16[64,16,128]{2,1,0:T(8,128)(2,1)S(1)}, bf16[64,16,128]{2,1,0:T(8,128)(2,1)S(1)}) custom-call(f32[64,32,128]{2,1,0:T(8,128)S(1)} %get-tuple-element.64.tri_back, f32[2048,128]{1,0:T(8,128)S(1)} %get-tuple-element.65.right_act), custom_call_target="tpu_custom_call" | custom-call | flops 1000 | bytes 1000 | tf_op jit(solution)/shard_map/left_back/pallas_call | solution.py:380
  38.6 5.5 %right_back.1 = (bf16[32,16,128]{2,1,0:T(8,128)(2,1)S(1)}, bf16[32,16,128]{2,1,0:T(8,128)(2,1)S(1)}, bf16[32,16,128]{2,1,0:T(8,128)(2,1)S(1)}, bf16[32,16,128]{2,1,0:T(8,128)(2,1)S(1)}) custom-call(f32[64,32,128]{2,1,0:T(8,128)S(1)} %get-tuple-element.64.tri_back, f32[64,16,128]{2,1,0:T(8,128)S(1)} %get-tuple-element.70.refs_0_, ...), custom_call_target="tpu_custom_call" | custom-call | flops 1000 | bytes 1000 | tf_op jit(solution)/shard_map/right_back/pallas_call | solution.py:380
  44.1 4.3 %weights.1 = (bf16[32,768]{1,0:T(8,128)(2,1)S(1)}, bf16[32,768]{1,0:T(8,128)(2,1)S(1)}, bf16[32,768]{1,0:T(8,128)(2,1)S(1)}, bf16[32,768]{1,0:T(8,128)(2,1)S(1)}) custom-call(bf16[4,32,16,128]{3,2,1,0:T(8,128)(2,1)S(1)} %get-tuple-element.81.right_in, bf16[128,256]{1,0:T(8,128)(2,1)S(1)} %copy-done, bf16[128,256]{1,0:T(8,128)(2,1)S(1)} %copy-done.6, ...), custom_call_target="tpu_custom_call" | custom-call | flops 1000 | bytes 1000 | tf_op jit(solution)/shard_map/weights/pallas_call | solution.py:380
  48.5 2.3 %collective-permute-start.12 = (bf16[32,768]{1,0:T(8,128)(2,1)S(1)}, bf16[32,768]{1,0:T(8,128)(2,1)S(1)}, u32[]{:S(2)}, u32[]{:S(2)}) collective-permute-start(bf16[32,768]{1,0:T(8,128)(2,1)S(1)} %get-tuple-element.89), channel_id=1, source_target_pairs={{0,8},{8,16},{16,24},{24,0},{1,9},{9,17},{17,25},{25,1},{2,10},{10... | collective-permute-start | bytes 147464 | tf_op jit(solution)/shard_map/ppermute | solution.py:340
  50.8 0.6 collective-permute-start.9
  51.5 7.1 %collective-permute-start.6 = (bf16[64,16,128]{2,1,0:T(8,128)(2,1)S(1)}, bf16[64,16,128]{2,1,0:T(8,128)(2,1)S(1)}, u32[]{:S(2)}, u32[]{:S(2)}) collective-permute-start(bf16[64,16,128]{2,1,0:T(8,128)(2,1)S(1)} %get-tuple-element.67.refs_5_), channel_id=1, source_target_pairs={{0,6},{2,0},{4,2},{6,4},{1,7},{3,1},{5,3},{7,5},{8,14},{10,8},{12,... | collective-permute-start | bytes 786440 | tf_op jit(solution)/shard_map/ppermute | solution.py:340
  58.6 0.6 collective-permute-start.8
  59.1 0.5 collective-permute-start.13
  59.7 3.6 %collective-permute-done.13.refs_2_ = bf16[32,768]{1,0:T(8,128)(2,1)S(1)} collective-permute-done((bf16[32,768]{1,0:T(8,128)(2,1)S(1)}, bf16[32,768]{1,0:T(8,128)(2,1)S(1)}, u32[]{:S(2)}, u32[]{:S(2)}) %collective-permute-start.13) | collective-permute-done | bytes 49184 | tf_op jit(solution)/shard_map/ppermute | solution.py:340
  63.2 0.0 collective-permute-start.14
  63.2 4.5 %collective-permute-done.14.refs_3_ = bf16[32,768]{1,0:T(8,128)(2,1)S(1)} collective-permute-done((bf16[32,768]{1,0:T(8,128)(2,1)S(1)}, bf16[32,768]{1,0:T(8,128)(2,1)S(1)}, u32[]{:S(2)}, u32[]{:S(2)}) %collective-permute-start.14) | collective-permute-done | bytes 49184 | tf_op jit(solution)/shard_map/ppermute | solution.py:340
  67.7 0.5 collective-permute-start.10
  68.2 1.0 %collective-permute-start.11 = (bf16[32,16,128]{2,1,0:T(8,128)(2,1)S(1)}, bf16[32,16,128]{2,1,0:T(8,128)(2,1)S(1)}, u32[]{:S(2)}, u32[]{:S(2)}) collective-permute-start(bf16[32,16,128]{2,1,0:T(8,128)(2,1)S(1)} %get-tuple-element.77.refs_11_), channel_id=1, source_target_pairs={{0,8},{8,16},{16,24},{24,0},{1,9},{9,17},{17,25},{25,1},{2,10},{10... | collective-permute-start | bytes 393224 | tf_op jit(solution)/shard_map/ppermute | solution.py:340
  69.2 3.5 %collective-permute-done.10.refs_10_.refs_8_ = bf16[32,16,128]{2,1,0:T(8,128)(2,1)S(1)} collective-permute-done((bf16[32,16,128]{2,1,0:T(8,128)(2,1)S(1)}, bf16[32,16,128]{2,1,0:T(8,128)(2,1)S(1)}, u32[]{:S(2)}, u32[]{:S(2)}) %collective-permute-start.10) | collective-permute-done | bytes 131104 | tf_op jit(solution)/shard_map/ppermute | solution.py:340
  72.7 1.4 %collective-permute-done.11.refs_11_.refs_9_ = bf16[32,16,128]{2,1,0:T(8,128)(2,1)S(1)} collective-permute-done((bf16[32,16,128]{2,1,0:T(8,128)(2,1)S(1)}, bf16[32,16,128]{2,1,0:T(8,128)(2,1)S(1)}, u32[]{:S(2)}, u32[]{:S(2)}) %collective-permute-start.11) | collective-permute-done | bytes 131104 | tf_op jit(solution)/shard_map/ppermute | solution.py:340
  74.1 4.8 %collective-permute-done.7.refs_6_.refs_5_ = bf16[64,16,128]{2,1,0:T(8,128)(2,1)S(1)} collective-permute-done((bf16[64,16,128]{2,1,0:T(8,128)(2,1)S(1)}, bf16[64,16,128]{2,1,0:T(8,128)(2,1)S(1)}, u32[]{:S(2)}, u32[]{:S(2)}) %collective-permute-start.7) | collective-permute-done | bytes 262176 | tf_op jit(solution)/shard_map/ppermute | solution.py:340
  78.9 0.0 copy-start.10
  78.9 0.1 collective-permute-start.17
  79.0 3.5 %collective-permute-start.16 = (bf16[32,768]{1,0:T(8,128)(2,1)S(1)}, bf16[32,768]{1,0:T(8,128)(2,1)S(1)}, u32[]{:S(2)}, u32[]{:S(2)}) collective-permute-start(bf16[32,768]{1,0:T(8,128)(2,1)S(1)} %combine.2.refs_0_), channel_id=1, source_target_pairs={{0,4},{2,6},{4,0},{6,2},{1,5},{3,7},{5,1},{7,3},{8,12},{10,14},{12... | collective-permute-start | bytes 147464 | tf_op jit(solution)/shard_map/ppermute | solution.py:340
  82.5 1.9 %collective-permute-start.15 = (bf16[32,768]{1,0:T(8,128)(2,1)S(1)}, bf16[32,768]{1,0:T(8,128)(2,1)S(1)}, u32[]{:S(2)}, u32[]{:S(2)}) collective-permute-start(bf16[32,768]{1,0:T(8,128)(2,1)S(1)} %combine.2.refs_0_), channel_id=1, source_target_pairs={{0,2},{2,4},{4,6},{6,0},{1,3},{3,5},{5,7},{7,1},{8,10},{10,12},{12... | collective-permute-start | bytes 147464 | tf_op jit(solution)/shard_map/ppermute | solution.py:340
  84.4 0.6 collective-permute-done.16.refs_2_
  85.1 3.3 %collective-permute-done.15.refs_1_ = bf16[32,768]{1,0:T(8,128)(2,1)S(1)} collective-permute-done((bf16[32,768]{1,0:T(8,128)(2,1)S(1)}, bf16[32,768]{1,0:T(8,128)(2,1)S(1)}, u32[]{:S(2)}, u32[]{:S(2)}) %collective-permute-start.15) | collective-permute-done | bytes 49184 | tf_op jit(solution)/shard_map/ppermute | solution.py:340
  88.4 0.3 collective-permute-start.20
  88.7 0.6 collective-permute-start.19
  89.4 1.6 %collective-permute-start.18 = (bf16[32,768]{1,0:T(8,128)(2,1)S(1)}, bf16[32,768]{1,0:T(8,128)(2,1)S(1)}, u32[]{:S(2)}, u32[]{:S(2)}) collective-permute-start(bf16[32,768]{1,0:T(8,128)(2,1)S(1)} %combine.3.refs_0_), channel_id=1, source_target_pairs={{0,8},{8,16},{16,24},{24,0},{1,9},{9,17},{17,25},{25,1},{2,10},{10... | collective-permute-start | bytes 147464 | tf_op jit(solution)/shard_map/ppermute | solution.py:340
  91.0 2.4 %grad_middle.1 = bf16[64,32,128]{2,1,0:T(8,128)(2,1)} custom-call(bf16[64,32,128]{2,1,0:T(8,128)(2,1)S(1)} %copy-done.2, bf16[64,32,128]{2,1,0:T(8,128)(2,1)S(1)} %get-tuple-element.80.pre_back, bf16[128,128]{1,0:T(8,128)(2,1)S(1)} %copy-done.10), custom_call_target="tpu_custom_call" | custom-call | flops 1000 | bytes 1000 | tf_op jit(solution)/shard_map/grad_middle/pallas_call | solution.py:380
  93.4 2.9 %sides.1 = (bf16[64,16,128]{2,1,0:T(8,128)(2,1)}, bf16[32,16,128]{2,1,0:T(8,128)(2,1)}) custom-call(bf16[64,16,128]{2,1,0:T(8,128)(2,1)S(1)} %copy-done.5, bf16[32,16,128]{2,1,0:T(8,128)(2,1)S(1)} %copy-done.7, bf16[128,256]{1,0:T(8,128)(2,1)S(1)} %copy-done, bf16[128,256]{1,0:T(8,128)(2,1)S(1)} %copy-done.6, ...), custom_call_target="tpu_custom_call" | custom-call | flops 1000 | bytes 1000 | tf_op jit(solution)/shard_map/sides/pallas_call | solution.py:380
  96.3 0.8 deltas.1
  (30 shorter events, 0.1 us)
Async XLA Ops:
  0.6 10.0 %collective-permute-start.3 = (bf16[32,16,128]{2,1,0:T(8,128)(2,1)}, bf16[32,16,128]{2,1,0:T(8,128)(2,1)S(1)}, u32[]{:S(2)}, u32[]{:S(2)}) collective-permute-start(bf16[32,16,128]{2,1,0:T(8,128)(2,1)} %refs_1_.3), channel_id=1, source_target_pairs={{0,24},{8,0},{16,8},{24,16},{1,25},{9,1},{17,9},{25,17},{2,26},{10... | collective-permute-start | bytes 393224 | tf_op jit(solution)/shard_map/ppermute | solution.py:340
  4.6 18.6 %collective-permute-start.5 = (bf16[64,16,128]{2,1,0:T(8,128)(2,1)}, bf16[64,16,128]{2,1,0:T(8,128)(2,1)S(1)}, u32[]{:S(2)}, u32[]{:S(2)}) collective-permute-start(bf16[64,16,128]{2,1,0:T(8,128)(2,1)} %refs_0_.5), channel_id=1, source_target_pairs={{0,2},{2,4},{4,6},{6,0},{1,3},{3,5},{5,7},{7,1},{8,10},{10,12},{12... | collective-permute-start | bytes 786440 | tf_op jit(solution)/shard_map/ppermute | solution.py:340
  6.2 19.6 %collective-permute-start.4 = (bf16[64,16,128]{2,1,0:T(8,128)(2,1)}, bf16[64,16,128]{2,1,0:T(8,128)(2,1)S(1)}, u32[]{:S(2)}, u32[]{:S(2)}) collective-permute-start(bf16[64,16,128]{2,1,0:T(8,128)(2,1)} %refs_0_.5), channel_id=1, source_target_pairs={{0,4},{2,6},{4,0},{6,2},{1,5},{3,7},{5,1},{7,3},{8,12},{10,14},{12... | collective-permute-start | bytes 786440 | tf_op jit(solution)/shard_map/ppermute | solution.py:340
  8.7 19.6 %collective-permute-start = (bf16[64,16,128]{2,1,0:T(8,128)(2,1)}, bf16[64,16,128]{2,1,0:T(8,128)(2,1)S(1)}, u32[]{:S(2)}, u32[]{:S(2)}) collective-permute-start(bf16[64,16,128]{2,1,0:T(8,128)(2,1)} %refs_0_.5), channel_id=1, source_target_pairs={{0,6},{2,0},{4,2},{6,4},{1,7},{3,1},{5,3},{7,5},{8,14},{10,8},{12,... | collective-permute-start | bytes 786440 | tf_op jit(solution)/shard_map/ppermute | solution.py:340
  10.1 7.1 %collective-permute-start.2 = (bf16[32,16,128]{2,1,0:T(8,128)(2,1)}, bf16[32,16,128]{2,1,0:T(8,128)(2,1)S(1)}, u32[]{:S(2)}, u32[]{:S(2)}) collective-permute-start(bf16[32,16,128]{2,1,0:T(8,128)(2,1)} %refs_1_.3), channel_id=1, source_target_pairs={{0,16},{8,24},{16,0},{24,8},{1,17},{9,25},{17,1},{25,9},{2,18},{10... | collective-permute-start | bytes 393224 | tf_op jit(solution)/shard_map/ppermute | solution.py:340
  10.6 6.6 %collective-permute-start.1 = (bf16[32,16,128]{2,1,0:T(8,128)(2,1)}, bf16[32,16,128]{2,1,0:T(8,128)(2,1)S(1)}, u32[]{:S(2)}, u32[]{:S(2)}) collective-permute-start(bf16[32,16,128]{2,1,0:T(8,128)(2,1)} %refs_1_.3), channel_id=1, source_target_pairs={{0,8},{8,16},{16,24},{24,0},{1,9},{9,17},{17,25},{25,1},{2,10},{10... | collective-permute-start | bytes 393224 | tf_op jit(solution)/shard_map/ppermute | solution.py:340
  11.2 1.0 %copy-start.1 = (bf16[64,32,128]{2,1,0:T(8,128)(2,1)S(1)}, bf16[64,32,128]{2,1,0:T(8,128)(2,1)}, u32[]{:S(2)}) copy-start(bf16[64,32,128]{2,1,0:T(8,128)(2,1)} %middle.3) | copy-start | bytes 1572868
  12.2 1.0 %copy-start.3 = (bf16[64,32,128]{2,1,0:T(8,128)(2,1)S(1)}, bf16[64,32,128]{2,1,0:T(8,128)(2,1)}, u32[]{:S(2)}) copy-start(bf16[64,32,128]{2,1,0:T(8,128)(2,1)} %cotangent.1) | copy-start | bytes 1572868
  13.3 0.8 copy-start.8
  14.0 0.8 copy-start.9
  14.8 2.4 %copy-start.6 = (bf16[128,256]{1,0:T(8,128)(2,1)S(1)}, bf16[128,256]{1,0:T(8,128)(2,1)}, u32[]{:S(2)}) copy-start(bf16[128,256]{1,0:T(8,128)(2,1)} %right_w.1) | copy-start | bytes 196612
  14.8 2.4 %copy-start.7 = (bf16[32,16,128]{2,1,0:T(8,128)(2,1)S(1)}, bf16[32,16,128]{2,1,0:T(8,128)(2,1)}, u32[]{:S(2)}) copy-start(bf16[32,16,128]{2,1,0:T(8,128)(2,1)} %refs_1_.3) | copy-start | bytes 393220
  17.1 3.5 %copy-start = (bf16[128,256]{1,0:T(8,128)(2,1)S(1)}, bf16[128,256]{1,0:T(8,128)(2,1)}, u32[]{:S(2)}) copy-start(bf16[128,256]{1,0:T(8,128)(2,1)} %left_w.3) | copy-start | bytes 196612
  17.1 3.5 %copy-start.5 = (bf16[64,16,128]{2,1,0:T(8,128)(2,1)S(1)}, bf16[64,16,128]{2,1,0:T(8,128)(2,1)}, u32[]{:S(2)}) copy-start(bf16[64,16,128]{2,1,0:T(8,128)(2,1)} %refs_0_.5) | copy-start | bytes 786436
  25.8 2.6 %copy-start.4 = (bf16[64,32,128]{2,1,0:T(8,128)(2,1)S(1)}, bf16[64,32,128]{2,1,0:T(8,128)(2,1)}, u32[]{:S(2)}) copy-start(bf16[64,32,128]{2,1,0:T(8,128)(2,1)} %cotangent.1) | copy-start | bytes 1572868
  48.5 10.7 %collective-permute-start.12 = (bf16[32,768]{1,0:T(8,128)(2,1)S(1)}, bf16[32,768]{1,0:T(8,128)(2,1)S(1)}, u32[]{:S(2)}, u32[]{:S(2)}) collective-permute-start(bf16[32,768]{1,0:T(8,128)(2,1)S(1)} %get-tuple-element.89), channel_id=1, source_target_pairs={{0,8},{8,16},{16,24},{24,0},{1,9},{9,17},{17,25},{25,1},{2,10},{10... | collective-permute-start | bytes 147464 | tf_op jit(solution)/shard_map/ppermute | solution.py:340
  50.8 17.4 %collective-permute-start.9 = (bf16[32,16,128]{2,1,0:T(8,128)(2,1)S(1)}, bf16[32,16,128]{2,1,0:T(8,128)(2,1)S(1)}, u32[]{:S(2)}, u32[]{:S(2)}) collective-permute-start(bf16[32,16,128]{2,1,0:T(8,128)(2,1)S(1)} %get-tuple-element.75.refs_9_), channel_id=1, source_target_pairs={{0,24},{8,0},{16,8},{24,16},{1,25},{9,1},{17,9},{25,17},{2,26},{10... | collective-permute-start | bytes 393224 | tf_op jit(solution)/shard_map/ppermute | solution.py:340
  51.5 22.7 %collective-permute-start.6 = (bf16[64,16,128]{2,1,0:T(8,128)(2,1)S(1)}, bf16[64,16,128]{2,1,0:T(8,128)(2,1)S(1)}, u32[]{:S(2)}, u32[]{:S(2)}) collective-permute-start(bf16[64,16,128]{2,1,0:T(8,128)(2,1)S(1)} %get-tuple-element.67.refs_5_), channel_id=1, source_target_pairs={{0,6},{2,0},{4,2},{6,4},{1,7},{3,1},{5,3},{7,5},{8,14},{10,8},{12,... | collective-permute-start | bytes 786440 | tf_op jit(solution)/shard_map/ppermute | solution.py:340
  58.6 20.3 %collective-permute-start.7 = (bf16[64,16,128]{2,1,0:T(8,128)(2,1)S(1)}, bf16[64,16,128]{2,1,0:T(8,128)(2,1)S(1)}, u32[]{:S(2)}, u32[]{:S(2)}) collective-permute-start(bf16[64,16,128]{2,1,0:T(8,128)(2,1)S(1)} %get-tuple-element.68.refs_6_), channel_id=1, source_target_pairs={{0,4},{2,6},{4,0},{6,2},{1,5},{3,7},{5,1},{7,3},{8,12},{10,14},{12... | collective-permute-start | bytes 786440 | tf_op jit(solution)/shard_map/ppermute | solution.py:340
  58.6 20.3 %collective-permute-start.8 = (bf16[64,16,128]{2,1,0:T(8,128)(2,1)S(1)}, bf16[64,16,128]{2,1,0:T(8,128)(2,1)S(1)}, u32[]{:S(2)}, u32[]{:S(2)}) collective-permute-start(bf16[64,16,128]{2,1,0:T(8,128)(2,1)S(1)} %get-tuple-element.69.refs_7_), channel_id=1, source_target_pairs={{0,2},{2,4},{4,6},{6,0},{1,3},{3,5},{5,7},{7,1},{8,10},{10,12},{12... | collective-permute-start | bytes 786440 | tf_op jit(solution)/shard_map/ppermute | solution.py:340
  59.1 4.1 %collective-permute-start.13 = (bf16[32,768]{1,0:T(8,128)(2,1)S(1)}, bf16[32,768]{1,0:T(8,128)(2,1)S(1)}, u32[]{:S(2)}, u32[]{:S(2)}) collective-permute-start(bf16[32,768]{1,0:T(8,128)(2,1)S(1)} %get-tuple-element.90), channel_id=1, source_target_pairs={{0,16},{8,24},{16,0},{24,8},{1,17},{9,25},{17,1},{25,9},{2,18},{10... | collective-permute-start | bytes 147464 | tf_op jit(solution)/shard_map/ppermute | solution.py:340
  63.2 4.5 %collective-permute-start.14 = (bf16[32,768]{1,0:T(8,128)(2,1)S(1)}, bf16[32,768]{1,0:T(8,128)(2,1)S(1)}, u32[]{:S(2)}, u32[]{:S(2)}) collective-permute-start(bf16[32,768]{1,0:T(8,128)(2,1)S(1)} %get-tuple-element.91), channel_id=1, source_target_pairs={{0,24},{8,0},{16,8},{24,16},{1,25},{9,1},{17,9},{25,17},{2,26},{10... | collective-permute-start | bytes 147464 | tf_op jit(solution)/shard_map/ppermute | solution.py:340
  67.7 5.0 %collective-permute-start.10 = (bf16[32,16,128]{2,1,0:T(8,128)(2,1)S(1)}, bf16[32,16,128]{2,1,0:T(8,128)(2,1)S(1)}, u32[]{:S(2)}, u32[]{:S(2)}) collective-permute-start(bf16[32,16,128]{2,1,0:T(8,128)(2,1)S(1)} %get-tuple-element.76.refs_10_), channel_id=1, source_target_pairs={{0,16},{8,24},{16,0},{24,8},{1,17},{9,25},{17,1},{25,9},{2,18},{10... | collective-permute-start | bytes 393224 | tf_op jit(solution)/shard_map/ppermute | solution.py:340
  68.2 5.9 %collective-permute-start.11 = (bf16[32,16,128]{2,1,0:T(8,128)(2,1)S(1)}, bf16[32,16,128]{2,1,0:T(8,128)(2,1)S(1)}, u32[]{:S(2)}, u32[]{:S(2)}) collective-permute-start(bf16[32,16,128]{2,1,0:T(8,128)(2,1)S(1)} %get-tuple-element.77.refs_11_), channel_id=1, source_target_pairs={{0,8},{8,16},{16,24},{24,0},{1,9},{9,17},{17,25},{25,1},{2,10},{10... | collective-permute-start | bytes 393224 | tf_op jit(solution)/shard_map/ppermute | solution.py:340
  78.9 12.1 %copy-start.2 = (bf16[64,32,128]{2,1,0:T(8,128)(2,1)S(1)}, bf16[64,32,128]{2,1,0:T(8,128)(2,1)}, u32[]{:S(2)}) copy-start(bf16[64,32,128]{2,1,0:T(8,128)(2,1)} %middle.3) | copy-start | bytes 1572868
  78.9 12.1 %copy-start.10 = (bf16[128,128]{1,0:T(8,128)(2,1)S(1)}, bf16[128,128]{1,0:T(8,128)(2,1)}, u32[]{:S(2)}) copy-start(bf16[128,128]{1,0:T(8,128)(2,1)} %gate_weight.1) | copy-start | bytes 98308
  78.9 5.5 %collective-permute-start.17 = (bf16[32,768]{1,0:T(8,128)(2,1)S(1)}, bf16[32,768]{1,0:T(8,128)(2,1)S(1)}, u32[]{:S(2)}, u32[]{:S(2)}) collective-permute-start(bf16[32,768]{1,0:T(8,128)(2,1)S(1)} %combine.2.refs_0_), channel_id=1, source_target_pairs={{0,6},{2,0},{4,2},{6,4},{1,7},{3,1},{5,3},{7,5},{8,14},{10,8},{12,... | collective-permute-start | bytes 147464 | tf_op jit(solution)/shard_map/ppermute | solution.py:340
  79.0 6.1 %collective-permute-start.16 = (bf16[32,768]{1,0:T(8,128)(2,1)S(1)}, bf16[32,768]{1,0:T(8,128)(2,1)S(1)}, u32[]{:S(2)}, u32[]{:S(2)}) collective-permute-start(bf16[32,768]{1,0:T(8,128)(2,1)S(1)} %combine.2.refs_0_), channel_id=1, source_target_pairs={{0,4},{2,6},{4,0},{6,2},{1,5},{3,7},{5,1},{7,3},{8,12},{10,14},{12... | collective-permute-start | bytes 147464 | tf_op jit(solution)/shard_map/ppermute | solution.py:340
  82.5 5.9 %collective-permute-start.15 = (bf16[32,768]{1,0:T(8,128)(2,1)S(1)}, bf16[32,768]{1,0:T(8,128)(2,1)S(1)}, u32[]{:S(2)}, u32[]{:S(2)}) collective-permute-start(bf16[32,768]{1,0:T(8,128)(2,1)S(1)} %combine.2.refs_0_), channel_id=1, source_target_pairs={{0,2},{2,4},{4,6},{6,0},{1,3},{3,5},{5,7},{7,1},{8,10},{10,12},{12... | collective-permute-start | bytes 147464 | tf_op jit(solution)/shard_map/ppermute | solution.py:340
  88.4 7.9 %collective-permute-start.20 = (bf16[32,768]{1,0:T(8,128)(2,1)S(1)}, bf16[32,768]{1,0:T(8,128)(2,1)S(1)}, u32[]{:S(2)}, u32[]{:S(2)}) collective-permute-start(bf16[32,768]{1,0:T(8,128)(2,1)S(1)} %combine.3.refs_0_), channel_id=1, source_target_pairs={{0,24},{8,0},{16,8},{24,16},{1,25},{9,1},{17,9},{25,17},{2,26},{10... | collective-permute-start | bytes 147464 | tf_op jit(solution)/shard_map/ppermute | solution.py:340
  88.7 7.6 %collective-permute-start.19 = (bf16[32,768]{1,0:T(8,128)(2,1)S(1)}, bf16[32,768]{1,0:T(8,128)(2,1)S(1)}, u32[]{:S(2)}, u32[]{:S(2)}) collective-permute-start(bf16[32,768]{1,0:T(8,128)(2,1)S(1)} %combine.3.refs_0_), channel_id=1, source_target_pairs={{0,16},{8,24},{16,0},{24,8},{1,17},{9,25},{17,1},{25,9},{2,18},{10... | collective-permute-start | bytes 147464 | tf_op jit(solution)/shard_map/ppermute | solution.py:340
  89.4 7.0 %collective-permute-start.18 = (bf16[32,768]{1,0:T(8,128)(2,1)S(1)}, bf16[32,768]{1,0:T(8,128)(2,1)S(1)}, u32[]{:S(2)}, u32[]{:S(2)}) collective-permute-start(bf16[32,768]{1,0:T(8,128)(2,1)S(1)} %combine.3.refs_0_), channel_id=1, source_target_pairs={{0,8},{8,16},{16,24},{24,0},{1,9},{9,17},{17,25},{25,1},{2,10},{10... | collective-permute-start | bytes 147464 | tf_op jit(solution)/shard_map/ppermute | solution.py:340

commit v5 on v4

--- a/solution.py
+++ b/solution.py
@@ -97,7 +97,7 @@
             lin, sw = gated(inputs, weight[...])
             act = (sw * lin).astype(bf16).astype(f32).reshape(step, k_right, width)
             for part in range(k_right // unit):
-                at_k = place(n_rows, n_blk, k_left, k_right, s, part)
+                at_k = place(n_blk, k_left, k_right, s, part)
                 for j in range(step):
                     start = pl.multiple_of((at * step + j) * n_k + at_k, unit)
                     act_out[pl.ds(start, unit), :] = act[j, part * unit : (part + 1) * unit]
@@ -114,9 +114,9 @@
         lax.fori_loop(0, k_left, flip, 0, unroll=True)
 
 
-def place(n_rows, n_blk, k_left, k_right, piece, part):
+def place(n_blk, k_left, k_right, piece, part):
     unit = math.gcd(k_left, k_right)
-    vertex = lax.rem(lax.axis_index("rows") - piece + n_rows, n_rows) * k_right + part * unit
+    vertex = lax.bitwise_xor(lax.axis_index("rows"), piece) * k_right + part * unit
     block = vertex // k_left
     at = lax.rem(lax.axis_index("blk") - block + n_blk, n_blk) * k_left + vertex - block * k_left
     return pl.multiple_of(at, unit)
@@ -225,11 +225,11 @@
 
 def right_back_kernel(n_rows, n_blk, tri_back, *refs):
     left_act, refs = refs[:n_blk], refs[n_blk + 1 :]
-    right_out, (right_sum,) = refs[:n_rows], refs[n_rows:]
+    keep, send, right_sum = refs
     n_i, n_j, width = tri_back.shape
     k_left = left_act[0].shape[1]
     n_k = k_left * n_blk
-    k_right = right_out[0].shape[1]
+    k_right = keep.shape[2]
     unit = math.gcd(k_left, k_right)
     few = 4
     k_step = vertex_step(n_k, k_left)
@@ -255,16 +255,17 @@
         lax.fori_loop(0, n_j // 8, rows_sum, 0)
     for s in range(n_rows):
         for part in range(k_right // unit):
-            right_out[s][:, part * unit : (part + 1) * unit, :] = right_sum[
-                :, pl.ds(place(n_rows, n_blk, k_left, k_right, s, part), unit), :
+            out = send if s % 2 else keep
+            out[s // 2, :, part * unit : (part + 1) * unit, :] = right_sum[
+                :, pl.ds(place(n_blk, k_left, k_right, s, part), unit), :
             ]
 
 
 def weights_kernel(n_rows, n_blk, right_in, left_w, right_w, gate_part, output_part, *refs):
     left_in, refs = refs[:n_blk], refs[n_blk:]
     left_out, refs = refs[:n_blk], refs[n_blk:]
-    right_out, refs = refs[:n_rows], refs[n_rows:]
-    pieces, (total,) = refs[:n_rows], refs[n_rows:]
+    keep, send, parts, total = refs
+    right_out = [(send if s % 2 else keep).at[s // 2] for s in range(n_rows)]
     right_ins = [right_in.at[s] for s in range(n_rows)]
     width = gate_part.shape[0]
     total[:, 4 * width : 5 * width] = gate_part[...]
@@ -289,10 +290,7 @@
                 return 0
 
             lax.fori_loop(0, n // step, body, 0, unroll=2)
-    size = width // n_rows
-    for s, piece in enumerate(pieces):
-        start = pl.multiple_of(lax.rem(lax.axis_index("rows") + s, n_rows) * size, size)
-        piece[...] = total[pl.ds(start, size), :].astype(bf16)
+    parts[...] = total[...].astype(bf16)
 
 
 def grad_middle_kernel(middle, pre_back, gate_weight, grad_middle):
@@ -310,10 +308,10 @@
     lax.fori_loop(0, n_i // step, body, 0, unroll=2)
 
 
-def side_kernel(n_left, n_right, *refs):
+def side_kernel(n_left, *refs):
     left, right, left_w, right_w = refs[:4]
     left_back, refs = refs[4 : 4 + n_left], refs[4 + n_left :]
-    right_back, refs = refs[:n_right], refs[n_right:]
+    right_back, refs = [ref.at[0] for ref in refs[:2]], refs[2:]
     for raw, weight, backs, grad in (
         (left, left_w, left_back, refs[0]),
         (right, right_w, right_back, refs[1]),
@@ -340,28 +338,66 @@
     return lax.ppermute(x, axis, [(a, (a + step) % n) for a in range(n)])
 
 
+def exchange(x, axis, n, bit):
+    return lax.ppermute(x, axis, [(a, a ^ bit) for a in range(n)])
+
+
+def halve_kernel(keep, came, *refs):
+    kept, send = refs[-2:]
+    for at in range(keep.shape[0]):
+        total = keep[at].astype(f32) + came[at].astype(f32)
+        if at % 2:
+            send[at // 2] = total.astype(bf16)
+        else:
+            kept[at // 2] = total
+
+
+def halving_sum(keep, send, axis, n, after):
+    came = exchange(send, axis, n, 1)
+    bit = 2
+    while bit < n:
+        half = (keep.shape[0] // 2,) + keep.shape[1:]
+        keep, send = call(halve_kernel, "halve", [shape(half, f32), shape(half, bf16)], after=len(after))(
+            keep, came, *after
+        )
+        came = exchange(send, axis, n, bit)
+        bit *= 2
+    return keep, came, send
+
+
+def order_kernel(*refs):
+    refs[-1][...] = jnp.zeros_like(refs[-1])
+
+
+def behind(*arrays):
+    (mark,) = call(order_kernel, "order", [shape((8, 128), f32)], after=len(arrays), cost=2 * 10**10)(*arrays)
+    return mark
+
+
 def combine_kernel(n, *refs):
-    total = refs[0][...].astype(f32)
+    total = refs[0][0].astype(f32)
+    for at in range(1, refs[0].shape[0]):
+        total = total + refs[0][at].astype(f32)
     for other in refs[1:n]:
-        total = total + other[...].astype(f32)
-    refs[-1][...] = total.astype(bf16)
+        total = total + other[0].astype(f32)
+    refs[-1][0] = total.astype(bf16)
 
 
 def combine(pieces, after=()):
     (total,) = call(
         functools.partial(combine_kernel, len(pieces)),
         "combine",
-        [shape(pieces[0].shape, bf16)],
+        [shape((1,) + pieces[0].shape[1:], bf16)],
         after=len(after),
     )(*pieces, *after)
     return total
 
 
 def deltas_kernel(n_rows, *refs):
-    pieces, outs = refs[:n_rows], refs[n_rows:]
+    pieces, outs = [ref.at[0] for ref in refs[:n_rows]], refs[n_rows:]
     size = pieces[0].shape[0]
     for s, piece in enumerate(pieces):
-        start = pl.multiple_of(lax.rem(lax.axis_index("rows") - s + n_rows, n_rows) * size, size)
+        start = pl.multiple_of(lax.bitwise_xor(lax.axis_index("rows"), s) * size, size)
         first = 0
         for out in outs:
             last = first + out.shape[1]
@@ -373,7 +409,7 @@
     return jax.ShapeDtypeStruct(tuple(dims), kind)
 
 
-def call(kernel, name, outs, scratch=(), after=0):
+def call(kernel, name, outs, scratch=(), after=0, cost=1000):
     def run(*operands):
         spaces = [pltpu.VMEM] * (len(operands) - after) + [pl.ANY] * after
         held = sum(math.prod(x.shape) * 4 for x in scratch)
@@ -384,7 +420,7 @@
             out_shape=outs,
             scratch_shapes=list(scratch),
             compiler_params=pltpu.CompilerParams(vmem_limit_bytes=held + SCOPED),
-            cost_estimate=pl.CostEstimate(flops=1000, bytes_accessed=1000, transcendentals=0),
+            cost_estimate=pl.CostEstimate(flops=cost, bytes_accessed=1000, transcendentals=0),
             name=name,
         )(*operands)
 
@@ -407,7 +443,7 @@
     n_j, k_right, _ = pair_right.shape
     n_k = k_left * n_blk
     left_raw = [pair_left] + [shift(pair_left, "blk", n_blk, s) for s in range(1, n_blk)]
-    right_raw = [pair_right] + [shift(pair_right, "rows", n_rows, s) for s in range(1, n_rows)]
+    right_raw = [pair_right] + [exchange(pair_right, "rows", n_rows, s) for s in range(1, n_rows)]
     middle_shape = (n_i, n_j, width)
     gate, middle_in, head_back, tri_up = call(
         middle_kernel,
@@ -467,26 +503,25 @@
         tri_back, right_act
     )
     left_back = [left_out[0]] + [shift(left_out[s], "blk", n_blk, n_blk - s) for s in range(1, n_blk)]
-    right_out = call(
+    right_stack = shape((n_rows // 2,) + pair_right.shape, bf16)
+    keep, send = call(
         functools.partial(right_back_kernel, n_rows, n_blk),
         "right_back",
-        [shape(pair_right.shape, bf16)] * n_rows,
+        [right_stack, right_stack],
         scratch=[pltpu.VMEM((n_j, n_k, width), bf16)],
         after=1,
     )(tri_back, *left_act, left_out[0])
-    right_back = [right_out[0]] + [
-        shift(right_out[s], "rows", n_rows, n_rows - s) for s in range(1, n_rows)
-    ]
-    pieces = call(
+    kept, came, sent = halving_sum(keep, send, "rows", n_rows, (behind(*left_back[1:]),))
+    (parts,) = call(
         functools.partial(weights_kernel, n_rows, n_blk),
         "weights",
-        [shape((width // n_rows, 6 * width), bf16)] * n_rows,
+        [shape((width, 6 * width), bf16)],
         scratch=[pltpu.VMEM((width, 6 * width), f32)],
-    )(right_in, left_weight, right_weight, gate_part, output_part, *left_in, *left_out, *right_out)
-    pieces = [pieces[0]] + [shift(pieces[s], "rows", n_rows, s) for s in range(1, n_rows)]
-    part = combine(pieces, (*left_back[1:], *right_back[1:]))
+    )(right_in, left_weight, right_weight, gate_part, output_part, *left_in, *left_out, keep, send)
+    parts = lax.all_to_all(parts.reshape(n_rows, width // n_rows, 6 * width), "rows", 0, 0)
+    part = combine([parts], (behind(sent),))
     part = combine([part] + [shift(part, "blk", n_blk, s) for s in range(1, n_blk)])
-    pieces = [part] + [shift(part, "rows", n_rows, s) for s in range(1, n_rows)]
+    pieces = [part] + [exchange(part, "rows", n_rows, s) for s in range(1, n_rows)]
     deltas = call(
         functools.partial(deltas_kernel, n_rows),
         "deltas",
@@ -496,10 +531,10 @@
         pair_middle, pre_back, gate_weight
     )
     grad_left, grad_right = call(
-        functools.partial(side_kernel, n_blk, n_rows),
+        functools.partial(side_kernel, n_blk),
         "sides",
         [shape(pair_left.shape, bf16), shape(pair_right.shape, bf16)],
-    )(pair_left, pair_right, left_weight, right_weight, *left_back, *right_back)
+    )(pair_left, pair_right, left_weight, right_weight, *left_back, kept, came)
     return (
         update,
         grad_left,

time: 97.5 us -> 90 us (0.923)
  waiting for transfers between devices: 21.9 us -> 10.5 us
  Pallas kernels: 39.5 us -> 43.6 us
    ppermute x21 -> x9, starting transfers between devices: 31.3 us -> 17.9 us  [shift(): return lax.ppermute(x, axis, [(a, (a + step) % n) for a in range(n)])]
    ppermute x21 -> x9, waiting for transfers between devices: 21.9 us -> 9.36 us  [shift(): return lax.ppermute(x, axis, [(a, (a + step) % n) for a in range(n)])]
    ppermute x0 -> x8, starting transfers between devices: none -> 9.66 us  [exchange(): return lax.ppermute(x, axis, [(a, a ^ bit) for a in range(n)])]
    pallas_call x14 -> x17, Pallas kernels: 39.5 us -> 43.6 us  [run(): pl.pallas_call(kernel, in_specs=[pl.BlockSpec(memory_space=space) for spa...]
    all_to_all x0 -> x1, starting transfers between devices: none -> 3.36 us  [per_device(): lax.all_to_all(parts.reshape(n_rows, width // n_rows, 6 * width), 'rows',...]
    ppermute x0 -> x8, waiting for transfers between devices: none -> 1.11 us  [exchange(): return lax.ppermute(x, axis, [(a, a ^ bit) for a in range(n)])]
    unnamed x22 -> x24, local copies, waits for them, and re-layouts: 3.63 us -> 3.63 us
  transfers between devices with their start and end apart: 21 -> 18, of which waited for: 8 -> 5; matrix products, arithmetic and copies ran while one was open for 0% -> 0% of each run, Pallas kernels for 19% -> 33%
where the time goes in v5:
time: 90 us; the launch traced here: 89.5 us
  Pallas kernels  43.6 us (48%)
  starting transfers between devices  31 us (34%)
  waiting for transfers between devices  10.5 us (12%)
  local copies, waits for them, and re-layouts  3.63 us (4%)
    pallas_call x17, Pallas kernels, run(): pl.pallas_call(kernel, in_specs=[pl.BlockSpec(memory_space=space) for spa...  43.6 us
    ppermute x9, starting transfers between devices, shift(): return lax.ppermute(x, axis, [(a, (a + step) % n) for a in range(n)])  17.9 us
    ppermute x8, starting transfers between devices, exchange(): return lax.ppermute(x, axis, [(a, a ^ bit) for a in range(n)])  9.66 us
    ppermute x9, waiting for transfers between devices, shift(): return lax.ppermute(x, axis, [(a, (a + step) % n) for a in range(n)])  9.36 us
    unnamed x24, local copies, waits for them, and re-layouts  3.63 us
    all_to_all x1, starting transfers between devices, per_device(): lax.all_to_all(parts.reshape(n_rows, width // n_rows, 6 * width), 'rows',...  3.36 us
  transfers between devices with their start and end apart: 18, of which 5 were waited for; matrix products, arithmetic and copies ran while one was open for 0% of the time, Pallas kernels for 33%

profile of v5, /device:TPU:0, one launch (start us, length us, event | category | flops | bytes accessed | tf_op | source)
XLA Modules:
  0.0 89.5 jit_solution(16415206118854295023)
XLA Ops:
  0.6 4.0 %collective-permute-start.3 = (bf16[32,16,128]{2,1,0:T(8,128)(2,1)}, bf16[32,16,128]{2,1,0:T(8,128)(2,1)S(1)}, u32[]{:S(2)}, u32[]{:S(2)}) collective-permute-start(bf16[32,16,128]{2,1,0:T(8,128)(2,1)} %refs_1_.3), channel_id=1, source_target_pairs={{0,24},{8,16},{16,8},{24,0},{1,25},{9,17},{17,9},{25,1},{2,26},{10... | collective-permute-start | bytes 393224 | tf_op jit(solution)/shard_map/ppermute | solution.py:342
  4.6 1.6 %collective-permute-start.5 = (bf16[64,16,128]{2,1,0:T(8,128)(2,1)}, bf16[64,16,128]{2,1,0:T(8,128)(2,1)S(1)}, u32[]{:S(2)}, u32[]{:S(2)}) collective-permute-start(bf16[64,16,128]{2,1,0:T(8,128)(2,1)} %refs_0_.5), channel_id=1, source_target_pairs={{0,2},{2,4},{4,6},{6,0},{1,3},{3,5},{5,7},{7,1},{8,10},{10,12},{12... | collective-permute-start | bytes 786440 | tf_op jit(solution)/shard_map/ppermute | solution.py:338
  6.2 2.6 %collective-permute-start.4 = (bf16[64,16,128]{2,1,0:T(8,128)(2,1)}, bf16[64,16,128]{2,1,0:T(8,128)(2,1)S(1)}, u32[]{:S(2)}, u32[]{:S(2)}) collective-permute-start(bf16[64,16,128]{2,1,0:T(8,128)(2,1)} %refs_0_.5), channel_id=1, source_target_pairs={{0,4},{2,6},{4,0},{6,2},{1,5},{3,7},{5,1},{7,3},{8,12},{10,14},{12... | collective-permute-start | bytes 786440 | tf_op jit(solution)/shard_map/ppermute | solution.py:338
  8.8 1.3 %collective-permute-start = (bf16[64,16,128]{2,1,0:T(8,128)(2,1)}, bf16[64,16,128]{2,1,0:T(8,128)(2,1)S(1)}, u32[]{:S(2)}, u32[]{:S(2)}) collective-permute-start(bf16[64,16,128]{2,1,0:T(8,128)(2,1)} %refs_0_.5), channel_id=1, source_target_pairs={{0,6},{2,0},{4,2},{6,4},{1,7},{3,1},{5,3},{7,5},{8,14},{10,8},{12,... | collective-permute-start | bytes 786440 | tf_op jit(solution)/shard_map/ppermute | solution.py:338
  10.1 0.5 collective-permute-start.2
  10.6 0.0 collective-permute-done.3.refs_3_
  10.6 0.5 collective-permute-start.1
  11.2 1.0 %copy-done.1 = bf16[64,32,128]{2,1,0:T(8,128)(2,1)S(1)} copy-done((bf16[64,32,128]{2,1,0:T(8,128)(2,1)S(1)}, bf16[64,32,128]{2,1,0:T(8,128)(2,1)}, u32[]{:S(2)}) %copy-start.1) | copy-done | bytes 524312
  12.2 1.0 %copy-done.3 = bf16[64,32,128]{2,1,0:T(8,128)(2,1)S(1)} copy-done((bf16[64,32,128]{2,1,0:T(8,128)(2,1)S(1)}, bf16[64,32,128]{2,1,0:T(8,128)(2,1)}, u32[]{:S(2)}) %copy-start.3) | copy-done | bytes 524312
  13.2 0.8 copy-done.8
  14.0 0.8 copy-done.10
  14.8 2.3 %middle.2 = (f32[64,32,128]{2,1,0:T(8,128)S(1)}, bf16[64,32,128]{2,1,0:T(8,128)(2,1)S(1)}, bf16[64,32,128]{2,1,0:T(8,128)(2,1)S(1)}, f32[64,32,128]{2,1,0:T(8,128)S(1)}) custom-call(bf16[64,32,128]{2,1,0:T(8,128)(2,1)S(1)} %copy-done.1, bf16[64,32,128]{2,1,0:T(8,128)(2,1)S(1)} %copy-done.3, bf16[128,128]{1,0:T(8,128)(2,1)S(1)} %copy-done.10, ...), custom_call_target="tpu_custom_call" | custom-call | flops 1000 | bytes 1000 | tf_op jit(solution)/shard_map/middle/pallas_call | solution.py:416
  17.0 0.0 copy-start
  17.0 0.0 copy-start.5
  17.1 3.3 %right.1 = (f32[2048,128]{1,0:T(8,128)S(1)}, bf16[4,32,16,128]{3,2,1,0:T(8,128)(2,1)S(1)}, f32[16,32,128]{2,1,0:T(8,128)S(1)}, f32[16,32,128]{2,1,0:T(8,128)S(1)...) custom-call(bf16[32,16,128]{2,1,0:T(8,128)(2,1)S(1)} %copy-done.7, ...), custom_call_target="tpu_custom_call" | custom-call | flops 1000 | bytes 1000 | tf_op jit(solution)/shard_map/right/pallas_call | solution.py:416
  20.4 2.5 %left.3 = (f32[64,16,128]{2,1,0:T(8,128)S(1)}, bf16[64,16,128]{2,1,0:T(8,128)(2,1)S(1)}, f32[64,32,128]{2,1,0:T(8,128)S(1)}) custom-call(bf16[64,16,128]{2,1,0:T(8,128)(2,1)S(1)} %copy-done.5, bf16[128,256]{1,0:T(8,128)(2,1)S(1)} %copy-done, f32[16,32,128]{2,1,0:T(8,128)S(1)} %get-tuple-element.55.flip), custom_call_target="tpu_custom_call" | custom-call | flops 1000 | bytes 1000 | tf_op jit(solution)/shard_map/left/pallas_call | solution.py:416
  23.0 2.6 %left.4 = (f32[64,16,128]{2,1,0:T(8,128)S(1)}, bf16[64,16,128]{2,1,0:T(8,128)(2,1)S(1)}, f32[64,32,128]{2,1,0:T(8,128)S(1)}) custom-call(bf16[64,16,128]{2,1,0:T(8,128)(2,1)S(1)} %collective-permute-done.5.raw, bf16[128,256]{1,0:T(8,128)(2,1)S(1)} %copy-done, f32[16,32,128]{2,1,0:T(8,128)S(1)} %get-tuple-element.54.flip, ...), custom_call_target="tpu_custom_call" | custom-call | flops 1000 | bytes 1000 | tf_op jit(solution)/shard_map/left/pallas_call | solution.py:416
  25.6 0.2 collective-permute-done.4.raw
  25.8 2.6 %left.5 = (f32[64,16,128]{2,1,0:T(8,128)S(1)}, bf16[64,16,128]{2,1,0:T(8,128)(2,1)S(1)}, f32[64,32,128]{2,1,0:T(8,128)S(1)}) custom-call(bf16[64,16,128]{2,1,0:T(8,128)(2,1)S(1)} %collective-permute-done.4.raw, bf16[128,256]{1,0:T(8,128)(2,1)S(1)} %copy-done, f32[16,32,128]{2,1,0:T(8,128)S(1)} %get-tuple-element.53.flip, ...), custom_call_target="tpu_custom_call" | custom-call | flops 1000 | bytes 1000 | tf_op jit(solution)/shard_map/left/pallas_call | solution.py:416
  28.4 0.0 collective-permute-done.raw
  28.4 5.5 %triangle.1 = (f32[64,16,128]{2,1,0:T(8,128)S(1)}, bf16[64,16,128]{2,1,0:T(8,128)(2,1)S(1)}, bf16[64,32,128]{2,1,0:T(8,128)(2,1)}, bf16[64,32,128]{2,1,0:T(8,128...) custom-call(bf16[64,16,128]{2,1,0:T(8,128)(2,1)S(1)} %collective-permute-done.raw, ...), custom_call_target="tpu_custom_call" | custom-call | flops 1000 | bytes 1000 | tf_op jit(solution)/shard_map/triangle/pallas_call | solution.py:416
  33.9 5.4 %left_back.1 = (bf16[64,16,128]{2,1,0:T(8,128)(2,1)S(1)}, bf16[64,16,128]{2,1,0:T(8,128)(2,1)}, bf16[64,16,128]{2,1,0:T(8,128)(2,1)S(1)}, bf16[64,16,128]{2,1,0:T(8,128)(2,1)S(1)}) custom-call(f32[64,32,128]{2,1,0:T(8,128)S(1)} %get-tuple-element.60.tri_back, f32[2048,128]{1,0:T(8,128)S(1)} %get-tuple-element.61.right_act), custom_call_target="tpu_custom_call" | custom-call | flops 1000 | bytes 1000 | tf_op jit(solution)/shard_map/left_back/pallas_call | solution.py:416
  39.3 7.1 %collective-permute-start.6 = (bf16[64,16,128]{2,1,0:T(8,128)(2,1)}, bf16[64,16,128]{2,1,0:T(8,128)(2,1)S(1)}, u32[]{:S(2)}, u32[]{:S(2)}) collective-permute-start(bf16[64,16,128]{2,1,0:T(8,128)(2,1)} %get-tuple-element.63.refs_5_), channel_id=1, source_target_pairs={{0,6},{2,0},{4,2},{6,4},{1,7},{3,1},{5,3},{7,5},{8,14},{10,8},{12,... | collective-permute-start | bytes 786440 | tf_op jit(solution)/shard_map/ppermute | solution.py:338
  46.4 0.0 collective-permute-start.7
  46.4 0.6 collective-permute-start.8
  47.0 6.2 %right_back.1 = (bf16[2,32,16,128]{3,2,1,0:T(8,128)(2,1)S(1)}, bf16[2,32,16,128]{3,2,1,0:T(8,128)(2,1)}) custom-call(f32[64,32,128]{2,1,0:T(8,128)S(1)} %get-tuple-element.60.tri_back, f32[64,16,128]{2,1,0:T(8,128)S(1)} %get-tuple-element.66.refs_0_, f32[64,16,128]{2,1,0:T(8,128)S(1)} %get-tuple-element.67.refs_1_, ...), custom_call_target="tpu_custom_call" | custom-call | flops 1000 | bytes 1000 | tf_op jit(solution)/shard_map/right_back/pallas_call | solution.py:416
  53.2 0.5 collective-permute-start.9
  53.7 6.0 %weights.1 = bf16[128,768]{1,0:T(8,128)(2,1)} custom-call(bf16[4,32,16,128]{3,2,1,0:T(8,128)(2,1)S(1)} %get-tuple-element.77.right_in, bf16[128,256]{1,0:T(8,128)(2,1)S(1)} %copy-done, bf16[128,256]{1,0:T(8,128)(2,1)S(1)} %copy-done.6, f32[128,128]{1,0:T(8,128)S(1)} %get-tuple-element.78.gate_part, f32[128,128]{1,0:T(8,128)S(1)} %get-tuple-element.79.output_part, ...), custom_call_target="tpu_custom_call" | custom-call | flops 1000 | bytes 1000 | tf_op jit(solution)/shard_map/weights/pallas_call | solution.py:416
  59.7 3.4 %all-to-all-start = ((bf16[4,32,768]{2,1,0:T(8,128)(2,1)}), bf16[4,32,768]{2,1,0:T(8,128)(2,1)S(1)}, u32[]{:S(2)}, u32[]{:S(2)}) async-start(bf16[4,32,768]{2,1,0:T(8,128)(2,1)} %bitcast), calls=%async_computation | async-start | bytes 393216 | tf_op jit(solution)/shard_map/all_to_all | solution.py:521
  63.1 0.0 collective-permute-done.6.refs_0_.refs_5_
  63.1 4.4 %collective-permute-done.7.refs_1_.refs_6_ = bf16[64,16,128]{2,1,0:T(8,128)(2,1)S(1)} collective-permute-done((bf16[64,16,128]{2,1,0:T(8,128)(2,1)S(1)}, bf16[64,16,128]{2,1,0:T(8,128)(2,1)S(1)}, u32[]{:S(2)}, u32[]{:S(2)}) %collective-permute-start.7) | collective-permute-done | bytes 262176 | tf_op jit(solution)/shard_map/ppermute | solution.py:338
  67.5 0.0 collective-permute-done.8.refs_2_.refs_7_
  67.5 0.0 collective-permute-done.9.came
  67.5 1.0 %halve.1 = (f32[1,32,16,128]{3,2,1,0:T(8,128)S(1)}, bf16[1,32,16,128]{3,2,1,0:T(8,128)(2,1)S(1)}) custom-call(bf16[2,32,16,128]{3,2,1,0:T(8,128)(2,1)S(1)} %get-tuple-element.70.keep.refs_8_, bf16[2,32,16,128]{3,2,1,0:T(8,128)(2,1)} %collective-permute-done.9.came, f32[8,128]{1,0:T(8,128)S(1)} %order.2.refs_0_), custom_call_target="tpu_custom_call" | custom-call | flops 1000 | bytes 1000 | tf_op jit(solution)/shard_map/halve/pallas_call | solution.py:416
  68.5 0.6 collective-permute-start.10
  69.1 0.0 copy-start.11
  69.1 2.5 %collective-permute-start.13 = (bf16[1,32,768]{2,1,0:T(8,128)(2,1)S(1)}, bf16[1,32,768]{2,1,0:T(8,128)(2,1)S(1)}, u32[]{:S(2)}, u32[]{:S(2)}) collective-permute-start(bf16[1,32,768]{2,1,0:T(8,128)(2,1)S(1)} %combine.2.refs_0_), channel_id=1, source_target_pairs={{0,6},{2,0},{4,2},{6,4},{1,7},{3,1},{5,3},{7,5},{8,14},{10,8},{12,... | collective-permute-start | bytes 147464 | tf_op jit(solution)/shard_map/ppermute | solution.py:338
  71.6 1.2 %collective-permute-start.12 = (bf16[1,32,768]{2,1,0:T(8,128)(2,1)S(1)}, bf16[1,32,768]{2,1,0:T(8,128)(2,1)S(1)}, u32[]{:S(2)}, u32[]{:S(2)}) collective-permute-start(bf16[1,32,768]{2,1,0:T(8,128)(2,1)S(1)} %combine.2.refs_0_), channel_id=1, source_target_pairs={{0,4},{2,6},{4,0},{6,2},{1,5},{3,7},{5,1},{7,3},{8,12},{10,14},{12... | collective-permute-start | bytes 147464 | tf_op jit(solution)/shard_map/ppermute | solution.py:338
  72.8 1.1 %collective-permute-start.11 = (bf16[1,32,768]{2,1,0:T(8,128)(2,1)S(1)}, bf16[1,32,768]{2,1,0:T(8,128)(2,1)S(1)}, u32[]{:S(2)}, u32[]{:S(2)}) collective-permute-start(bf16[1,32,768]{2,1,0:T(8,128)(2,1)S(1)} %combine.2.refs_0_), channel_id=1, source_target_pairs={{0,2},{2,4},{4,6},{6,0},{1,3},{3,5},{5,7},{7,1},{8,10},{10,12},{12... | collective-permute-start | bytes 147464 | tf_op jit(solution)/shard_map/ppermute | solution.py:338
  73.9 2.8 %collective-permute-done.12.refs_2_ = bf16[1,32,768]{2,1,0:T(8,128)(2,1)S(1)} collective-permute-done((bf16[1,32,768]{2,1,0:T(8,128)(2,1)S(1)}, bf16[1,32,768]{2,1,0:T(8,128)(2,1)S(1)}, u32[]{:S(2)}, u32[]{:S(2)}) %collective-permute-start.12) | collective-permute-done | bytes 49184 | tf_op jit(solution)/shard_map/ppermute | solution.py:338
  76.7 1.9 %collective-permute-done.11.refs_1_ = bf16[1,32,768]{2,1,0:T(8,128)(2,1)S(1)} collective-permute-done((bf16[1,32,768]{2,1,0:T(8,128)(2,1)S(1)}, bf16[1,32,768]{2,1,0:T(8,128)(2,1)S(1)}, u32[]{:S(2)}, u32[]{:S(2)}) %collective-permute-start.11) | collective-permute-done | bytes 49184 | tf_op jit(solution)/shard_map/ppermute | solution.py:338
  78.7 1.6 %collective-permute-start.16 = (bf16[1,32,768]{2,1,0:T(8,128)(2,1)S(1)}, bf16[1,32,768]{2,1,0:T(8,128)(2,1)S(1)}, u32[]{:S(2)}, u32[]{:S(2)}) collective-permute-start(bf16[1,32,768]{2,1,0:T(8,128)(2,1)S(1)} %combine.3.refs_0_), channel_id=1, source_target_pairs={{0,24},{8,16},{16,8},{24,0},{1,25},{9,17},{17,9},{25,1},{2,26},{10... | collective-permute-start | bytes 147464 | tf_op jit(solution)/shard_map/ppermute | solution.py:342
  80.3 1.4 %collective-permute-start.15 = (bf16[1,32,768]{2,1,0:T(8,128)(2,1)S(1)}, bf16[1,32,768]{2,1,0:T(8,128)(2,1)S(1)}, u32[]{:S(2)}, u32[]{:S(2)}) collective-permute-start(bf16[1,32,768]{2,1,0:T(8,128)(2,1)S(1)} %combine.3.refs_0_), channel_id=1, source_target_pairs={{0,16},{8,24},{16,0},{24,8},{1,17},{9,25},{17,1},{25,9},{2,18},{10... | collective-permute-start | bytes 147464 | tf_op jit(solution)/shard_map/ppermute | solution.py:342
  81.7 0.5 collective-permute-start.14
  82.3 2.4 %grad_middle.1 = bf16[64,32,128]{2,1,0:T(8,128)(2,1)} custom-call(bf16[64,32,128]{2,1,0:T(8,128)(2,1)S(1)} %copy-done.2, bf16[64,32,128]{2,1,0:T(8,128)(2,1)S(1)} %get-tuple-element.76.pre_back, bf16[128,128]{1,0:T(8,128)(2,1)S(1)} %copy-done.11), custom_call_target="tpu_custom_call" | custom-call | flops 1000 | bytes 1000 | tf_op jit(solution)/shard_map/grad_middle/pallas_call | solution.py:416
  84.7 1.1 %collective-permute-done.14.refs_1_ = bf16[1,32,768]{2,1,0:T(8,128)(2,1)S(1)} collective-permute-done((bf16[1,32,768]{2,1,0:T(8,128)(2,1)S(1)}, bf16[1,32,768]{2,1,0:T(8,128)(2,1)S(1)}, u32[]{:S(2)}, u32[]{:S(2)}) %collective-permute-start.14) | collective-permute-done | bytes 49184 | tf_op jit(solution)/shard_map/ppermute | solution.py:342
  85.8 0.8 deltas.1
  86.6 2.9 %sides.1 = (bf16[64,16,128]{2,1,0:T(8,128)(2,1)}, bf16[32,16,128]{2,1,0:T(8,128)(2,1)}) custom-call(bf16[64,16,128]{2,1,0:T(8,128)(2,1)S(1)} %copy-done.5, bf16[32,16,128]{2,1,0:T(8,128)(2,1)S(1)} %copy-done.7, bf16[128,256]{1,0:T(8,128)(2,1)S(1)} %copy-done, bf16[128,256]{1,0:T(8,128)(2,1)S(1)} %copy-done.6, ...), custom_call_target="tpu_custom_call" | custom-call | flops 1000 | bytes 1000 | tf_op jit(solution)/shard_map/sides/pallas_call | solution.py:416
  (29 shorter events, 0.1 us)
Async XLA Ops:
  0.6 10.0 %collective-permute-start.3 = (bf16[32,16,128]{2,1,0:T(8,128)(2,1)}, bf16[32,16,128]{2,1,0:T(8,128)(2,1)S(1)}, u32[]{:S(2)}, u32[]{:S(2)}) collective-permute-start(bf16[32,16,128]{2,1,0:T(8,128)(2,1)} %refs_1_.3), channel_id=1, source_target_pairs={{0,24},{8,16},{16,8},{24,0},{1,25},{9,17},{17,9},{25,1},{2,26},{10... | collective-permute-start | bytes 393224 | tf_op jit(solution)/shard_map/ppermute | solution.py:342
  4.6 18.4 %collective-permute-start.5 = (bf16[64,16,128]{2,1,0:T(8,128)(2,1)}, bf16[64,16,128]{2,1,0:T(8,128)(2,1)S(1)}, u32[]{:S(2)}, u32[]{:S(2)}) collective-permute-start(bf16[64,16,128]{2,1,0:T(8,128)(2,1)} %refs_0_.5), channel_id=1, source_target_pairs={{0,2},{2,4},{4,6},{6,0},{1,3},{3,5},{5,7},{7,1},{8,10},{10,12},{12... | collective-permute-start | bytes 786440 | tf_op jit(solution)/shard_map/ppermute | solution.py:338
  6.2 19.6 %collective-permute-start.4 = (bf16[64,16,128]{2,1,0:T(8,128)(2,1)}, bf16[64,16,128]{2,1,0:T(8,128)(2,1)S(1)}, u32[]{:S(2)}, u32[]{:S(2)}) collective-permute-start(bf16[64,16,128]{2,1,0:T(8,128)(2,1)} %refs_0_.5), channel_id=1, source_target_pairs={{0,4},{2,6},{4,0},{6,2},{1,5},{3,7},{5,1},{7,3},{8,12},{10,14},{12... | collective-permute-start | bytes 786440 | tf_op jit(solution)/shard_map/ppermute | solution.py:338
  8.8 19.6 %collective-permute-start = (bf16[64,16,128]{2,1,0:T(8,128)(2,1)}, bf16[64,16,128]{2,1,0:T(8,128)(2,1)S(1)}, u32[]{:S(2)}, u32[]{:S(2)}) collective-permute-start(bf16[64,16,128]{2,1,0:T(8,128)(2,1)} %refs_0_.5), channel_id=1, source_target_pairs={{0,6},{2,0},{4,2},{6,4},{1,7},{3,1},{5,3},{7,5},{8,14},{10,8},{12,... | collective-permute-start | bytes 786440 | tf_op jit(solution)/shard_map/ppermute | solution.py:338
  10.1 7.0 %collective-permute-start.2 = (bf16[32,16,128]{2,1,0:T(8,128)(2,1)}, bf16[32,16,128]{2,1,0:T(8,128)(2,1)S(1)}, u32[]{:S(2)}, u32[]{:S(2)}) collective-permute-start(bf16[32,16,128]{2,1,0:T(8,128)(2,1)} %refs_1_.3), channel_id=1, source_target_pairs={{0,16},{8,24},{16,0},{24,8},{1,17},{9,25},{17,1},{25,9},{2,18},{10... | collective-permute-start | bytes 393224 | tf_op jit(solution)/shard_map/ppermute | solution.py:342
  10.6 6.5 %collective-permute-start.1 = (bf16[32,16,128]{2,1,0:T(8,128)(2,1)}, bf16[32,16,128]{2,1,0:T(8,128)(2,1)S(1)}, u32[]{:S(2)}, u32[]{:S(2)}) collective-permute-start(bf16[32,16,128]{2,1,0:T(8,128)(2,1)} %refs_1_.3), channel_id=1, source_target_pairs={{0,8},{8,0},{16,24},{24,16},{1,9},{9,1},{17,25},{25,17},{2,10},{10... | collective-permute-start | bytes 393224 | tf_op jit(solution)/shard_map/ppermute | solution.py:342
  11.2 1.0 %copy-start.1 = (bf16[64,32,128]{2,1,0:T(8,128)(2,1)S(1)}, bf16[64,32,128]{2,1,0:T(8,128)(2,1)}, u32[]{:S(2)}) copy-start(bf16[64,32,128]{2,1,0:T(8,128)(2,1)} %middle.3) | copy-start | bytes 1572868
  12.2 1.0 %copy-start.3 = (bf16[64,32,128]{2,1,0:T(8,128)(2,1)S(1)}, bf16[64,32,128]{2,1,0:T(8,128)(2,1)}, u32[]{:S(2)}) copy-start(bf16[64,32,128]{2,1,0:T(8,128)(2,1)} %cotangent.1) | copy-start | bytes 1572868
  13.2 0.8 copy-start.8
  14.0 0.8 copy-start.10
  14.8 2.3 %copy-start.6 = (bf16[128,256]{1,0:T(8,128)(2,1)S(1)}, bf16[128,256]{1,0:T(8,128)(2,1)}, u32[]{:S(2)}) copy-start(bf16[128,256]{1,0:T(8,128)(2,1)} %right_w.1) | copy-start | bytes 196612
  14.8 2.3 %copy-start.7 = (bf16[32,16,128]{2,1,0:T(8,128)(2,1)S(1)}, bf16[32,16,128]{2,1,0:T(8,128)(2,1)}, u32[]{:S(2)}) copy-start(bf16[32,16,128]{2,1,0:T(8,128)(2,1)} %refs_1_.3) | copy-start | bytes 393220
  17.0 3.4 %copy-start = (bf16[128,256]{1,0:T(8,128)(2,1)S(1)}, bf16[128,256]{1,0:T(8,128)(2,1)}, u32[]{:S(2)}) copy-start(bf16[128,256]{1,0:T(8,128)(2,1)} %left_w.3) | copy-start | bytes 196612
  17.0 3.4 %copy-start.5 = (bf16[64,16,128]{2,1,0:T(8,128)(2,1)S(1)}, bf16[64,16,128]{2,1,0:T(8,128)(2,1)}, u32[]{:S(2)}) copy-start(bf16[64,16,128]{2,1,0:T(8,128)(2,1)} %refs_0_.5) | copy-start | bytes 786436
  25.8 2.6 %copy-start.4 = (bf16[64,32,128]{2,1,0:T(8,128)(2,1)S(1)}, bf16[64,32,128]{2,1,0:T(8,128)(2,1)}, u32[]{:S(2)}) copy-start(bf16[64,32,128]{2,1,0:T(8,128)(2,1)} %cotangent.1) | copy-start | bytes 1572868
  25.8 2.6 %copy-start.9 = (bf16[128,128]{1,0:T(8,128)(2,1)S(1)}, bf16[128,128]{1,0:T(8,128)(2,1)}, u32[]{:S(2)}) copy-start(bf16[128,128]{1,0:T(8,128)(2,1)} %out_w.1) | copy-start | bytes 98308
  39.3 23.8 %collective-permute-start.6 = (bf16[64,16,128]{2,1,0:T(8,128)(2,1)}, bf16[64,16,128]{2,1,0:T(8,128)(2,1)S(1)}, u32[]{:S(2)}, u32[]{:S(2)}) collective-permute-start(bf16[64,16,128]{2,1,0:T(8,128)(2,1)} %get-tuple-element.63.refs_5_), channel_id=1, source_target_pairs={{0,6},{2,0},{4,2},{6,4},{1,7},{3,1},{5,3},{7,5},{8,14},{10,8},{12,... | collective-permute-start | bytes 786440 | tf_op jit(solution)/shard_map/ppermute | solution.py:338
  46.4 21.1 %collective-permute-start.7 = (bf16[64,16,128]{2,1,0:T(8,128)(2,1)S(1)}, bf16[64,16,128]{2,1,0:T(8,128)(2,1)S(1)}, u32[]{:S(2)}, u32[]{:S(2)}) collective-permute-start(bf16[64,16,128]{2,1,0:T(8,128)(2,1)S(1)} %get-tuple-element.64.refs_6_), channel_id=1, source_target_pairs={{0,4},{2,6},{4,0},{6,2},{1,5},{3,7},{5,1},{7,3},{8,12},{10,14},{12... | collective-permute-start | bytes 786440 | tf_op jit(solution)/shard_map/ppermute | solution.py:338
  46.4 21.1 %collective-permute-start.8 = (bf16[64,16,128]{2,1,0:T(8,128)(2,1)S(1)}, bf16[64,16,128]{2,1,0:T(8,128)(2,1)S(1)}, u32[]{:S(2)}, u32[]{:S(2)}) collective-permute-start(bf16[64,16,128]{2,1,0:T(8,128)(2,1)S(1)} %get-tuple-element.65.refs_7_), channel_id=1, source_target_pairs={{0,2},{2,4},{4,6},{6,0},{1,3},{3,5},{5,7},{7,1},{8,10},{10,12},{12... | collective-permute-start | bytes 786440 | tf_op jit(solution)/shard_map/ppermute | solution.py:338
  53.2 14.3 %collective-permute-start.9 = (bf16[2,32,16,128]{3,2,1,0:T(8,128)(2,1)}, bf16[2,32,16,128]{3,2,1,0:T(8,128)(2,1)}, u32[]{:S(2)}, u32[]{:S(2)}) collective-permute-start(bf16[2,32,16,128]{3,2,1,0:T(8,128)(2,1)} %get-tuple-element.71.refs_9_), channel_id=1, source_target_pairs={{0,8},{8,0},{16,24},{24,16},{1,9},{9,1},{17,25},{25,17},{2,10},{10... | collective-permute-start | bytes 786440 | tf_op jit(solution)/shard_map/ppermute | solution.py:342
  59.7 9.4 %all-to-all-start = ((bf16[4,32,768]{2,1,0:T(8,128)(2,1)}), bf16[4,32,768]{2,1,0:T(8,128)(2,1)S(1)}, u32[]{:S(2)}, u32[]{:S(2)}) async-start(bf16[4,32,768]{2,1,0:T(8,128)(2,1)} %bitcast), calls=%async_computation | async-start | bytes 393216 | tf_op jit(solution)/shard_map/all_to_all | solution.py:521
  68.5 18.1 %collective-permute-start.10 = (bf16[1,32,16,128]{3,2,1,0:T(8,128)(2,1)S(1)}, bf16[1,32,16,128]{3,2,1,0:T(8,128)(2,1)S(1)}, u32[]{:S(2)}, u32[]{:S(2)}) collective-permute-start(bf16[1,32,16,128]{3,2,1,0:T(8,128)(2,1)S(1)} %get-tuple-element.73.refs_0_), channel_id=1, source_target_pairs={{0,16},{8,24},{16,0},{24,8},{1,17},{9,25},{17,1},{25,9},{2,18},{10... | collective-permute-start | bytes 393224 | tf_op jit(solution)/shard_map/ppermute | solution.py:342
  69.1 13.2 %copy-start.2 = (bf16[64,32,128]{2,1,0:T(8,128)(2,1)S(1)}, bf16[64,32,128]{2,1,0:T(8,128)(2,1)}, u32[]{:S(2)}) copy-start(bf16[64,32,128]{2,1,0:T(8,128)(2,1)} %middle.3) | copy-start | bytes 1572868
  69.1 13.1 %copy-start.11 = (bf16[128,128]{1,0:T(8,128)(2,1)S(1)}, bf16[128,128]{1,0:T(8,128)(2,1)}, u32[]{:S(2)}) copy-start(bf16[128,128]{1,0:T(8,128)(2,1)} %gate_weight.1) | copy-start | bytes 98308
  69.1 4.8 %collective-permute-start.13 = (bf16[1,32,768]{2,1,0:T(8,128)(2,1)S(1)}, bf16[1,32,768]{2,1,0:T(8,128)(2,1)S(1)}, u32[]{:S(2)}, u32[]{:S(2)}) collective-permute-start(bf16[1,32,768]{2,1,0:T(8,128)(2,1)S(1)} %combine.2.refs_0_), channel_id=1, source_target_pairs={{0,6},{2,0},{4,2},{6,4},{1,7},{3,1},{5,3},{7,5},{8,14},{10,8},{12,... | collective-permute-start | bytes 147464 | tf_op jit(solution)/shard_map/ppermute | solution.py:338
  71.6 5.1 %collective-permute-start.12 = (bf16[1,32,768]{2,1,0:T(8,128)(2,1)S(1)}, bf16[1,32,768]{2,1,0:T(8,128)(2,1)S(1)}, u32[]{:S(2)}, u32[]{:S(2)}) collective-permute-start(bf16[1,32,768]{2,1,0:T(8,128)(2,1)S(1)} %combine.2.refs_0_), channel_id=1, source_target_pairs={{0,4},{2,6},{4,0},{6,2},{1,5},{3,7},{5,1},{7,3},{8,12},{10,14},{12... | collective-permute-start | bytes 147464 | tf_op jit(solution)/shard_map/ppermute | solution.py:338
  72.8 5.9 %collective-permute-start.11 = (bf16[1,32,768]{2,1,0:T(8,128)(2,1)S(1)}, bf16[1,32,768]{2,1,0:T(8,128)(2,1)S(1)}, u32[]{:S(2)}, u32[]{:S(2)}) collective-permute-start(bf16[1,32,768]{2,1,0:T(8,128)(2,1)S(1)} %combine.2.refs_0_), channel_id=1, source_target_pairs={{0,2},{2,4},{4,6},{6,0},{1,3},{3,5},{5,7},{7,1},{8,10},{10,12},{12... | collective-permute-start | bytes 147464 | tf_op jit(solution)/shard_map/ppermute | solution.py:338
  78.7 6.0 %collective-permute-start.16 = (bf16[1,32,768]{2,1,0:T(8,128)(2,1)S(1)}, bf16[1,32,768]{2,1,0:T(8,128)(2,1)S(1)}, u32[]{:S(2)}, u32[]{:S(2)}) collective-permute-start(bf16[1,32,768]{2,1,0:T(8,128)(2,1)S(1)} %combine.3.refs_0_), channel_id=1, source_target_pairs={{0,24},{8,16},{16,8},{24,0},{1,25},{9,17},{17,9},{25,1},{2,26},{10... | collective-permute-start | bytes 147464 | tf_op jit(solution)/shard_map/ppermute | solution.py:342
  80.3 4.4 %collective-permute-start.15 = (bf16[1,32,768]{2,1,0:T(8,128)(2,1)S(1)}, bf16[1,32,768]{2,1,0:T(8,128)(2,1)S(1)}, u32[]{:S(2)}, u32[]{:S(2)}) collective-permute-start(bf16[1,32,768]{2,1,0:T(8,128)(2,1)S(1)} %combine.3.refs_0_), channel_id=1, source_target_pairs={{0,16},{8,24},{16,0},{24,8},{1,17},{9,25},{17,1},{25,9},{2,18},{10... | collective-permute-start | bytes 147464 | tf_op jit(solution)/shard_map/ppermute | solution.py:342
  81.7 4.1 %collective-permute-start.14 = (bf16[1,32,768]{2,1,0:T(8,128)(2,1)S(1)}, bf16[1,32,768]{2,1,0:T(8,128)(2,1)S(1)}, u32[]{:S(2)}, u32[]{:S(2)}) collective-permute-start(bf16[1,32,768]{2,1,0:T(8,128)(2,1)S(1)} %combine.3.refs_0_), channel_id=1, source_target_pairs={{0,8},{8,0},{16,24},{24,16},{1,9},{9,1},{17,25},{25,17},{2,10},{10... | collective-permute-start | bytes 147464 | tf_op jit(solution)/shard_map/ppermute | solution.py:342

commit v6 on v5

--- a/solution.py
+++ b/solution.py
@@ -75,7 +75,8 @@
         gate[rows] = opened.reshape(step, n_j, width)
         middle_in[rows] = inputs.reshape(step, n_j, width)
         head_back[rows] = back.reshape(step, n_j, width)
-        tri_up[rows] = dot_nt(back, output_weight[...]).reshape(step, n_j, width)
+        up = dot_nt(back, output_weight[...])
+        tri_up[rows] = (up - jnp.mean(up, axis=-1, keepdims=True)).reshape(step, n_j, width)
         return 0
 
     lax.fori_loop(0, n_i // step, body, 0, unroll=2)
@@ -160,16 +161,12 @@
     lax.fori_loop(0, n_i // step, body, 0)
 
 
-def triangle_kernel(
-    has_total, raw, left_w, flip, out_w, gate, middle_in, head_back, tri_up, cotangent, *refs
-):
+def triangle_kernel(has_total, raw, left_w, flip, tri_up, *refs):
     total_in, refs = refs[: 1 if has_total else 0], refs[1 if has_total else 0 :]
-    act_out, in_out, update, pre_back, tri_back, gate_part, output_part = refs
-    n_i, n_j, width = update.shape
+    act_out, in_out, tri_in, tri_back = refs
+    n_i, n_j, width = tri_in.shape
     step = 8
     project_left(raw, left_w, act_out, in_out)
-    gate_part[...] = jnp.zeros_like(gate_part)
-    output_part[...] = jnp.zeros_like(output_part)
 
     def triangle_rows(at, _):
         rows = pl.ds(at * step, step)
@@ -178,20 +175,38 @@
             total = total + total_in[0][rows]
         flat = step * n_j
         normed, inverse = normalize(total.reshape(flat, width))
-        tri_in = normed.astype(bf16)
-        head = dot(tri_in, out_w[...])
+        tri_in[rows] = normed.astype(bf16).reshape(step, n_j, width)
+        up = tri_up[rows].reshape(flat, width)
+        second = jnp.mean(up * normed, axis=-1, keepdims=True)
+        back = inverse * (up - normed * second)
+        tri_back[rows] = back.astype(bf16).astype(f32).reshape(step, n_j, width)
+        return 0
+
+    lax.fori_loop(0, n_i // step, triangle_rows, 0, unroll=2)
+
+
+def heads_kernel(tri_in, out_w, gate, middle_in, head_back, cotangent, _, *refs):
+    update, pre_back, gate_part, output_part = refs
+    n_i, n_j, width = update.shape
+    step = 8
+    gate_part[...] = jnp.zeros_like(gate_part)
+    output_part[...] = jnp.zeros_like(output_part)
+
+    def body(at, _):
+        rows = pl.ds(at * step, step)
+        flat = step * n_j
+        inputs = tri_in[rows].reshape(flat, width)
+        head = dot(inputs, out_w[...])
         opened = gate[rows].reshape(flat, width)
         update[rows] = (opened * head).astype(bf16).reshape(step, n_j, width)
         upstream = cotangent[rows].astype(f32).reshape(flat, width)
         pre = (upstream * head * opened * (1.0 - opened)).astype(bf16)
         pre_back[rows] = pre.reshape(step, n_j, width)
         gate_part[...] += dot_tn(middle_in[rows].reshape(flat, width), pre)
-        output_part[...] += dot_tn(tri_in, head_back[rows].reshape(flat, width))
-        back = normalize_back(normed, inverse, tri_up[rows].reshape(flat, width))
-        tri_back[rows] = back.astype(bf16).astype(f32).reshape(step, n_j, width)
+        output_part[...] += dot_tn(inputs, head_back[rows].reshape(flat, width))
         return 0
 
-    lax.fori_loop(0, n_i // step, triangle_rows, 0, unroll=2)
+    lax.fori_loop(0, n_i // step, body, 0, unroll=2)
 
 
 def vertex_step(n_k, unit):
@@ -264,7 +279,7 @@
 def weights_kernel(n_rows, n_blk, right_in, left_w, right_w, gate_part, output_part, *refs):
     left_in, refs = refs[:n_blk], refs[n_blk:]
     left_out, refs = refs[:n_blk], refs[n_blk:]
-    keep, send, parts, total = refs
+    keep, send, keep_out, send_out, total = refs
     right_out = [(send if s % 2 else keep).at[s // 2] for s in range(n_rows)]
     right_ins = [right_in.at[s] for s in range(n_rows)]
     width = gate_part.shape[0]
@@ -290,7 +305,14 @@
                 return 0
 
             lax.fori_loop(0, n // step, body, 0, unroll=2)
-    parts[...] = total[...].astype(bf16)
+    size = width // n_rows
+    for s in range(n_rows):
+        start = pl.multiple_of(lax.bitwise_xor(lax.axis_index("rows"), s) * size, size)
+        piece = total[pl.ds(start, size), :]
+        if s % 2:
+            send_out[s // 2] = piece.astype(bf16)
+        else:
+            keep_out[s // 2] = piece
 
 
 def grad_middle_kernel(middle, pre_back, gate_weight, grad_middle):
@@ -394,7 +416,7 @@
 
 
 def deltas_kernel(n_rows, *refs):
-    pieces, outs = [ref.at[0] for ref in refs[:n_rows]], refs[n_rows:]
+    pieces, outs = [ref.at[0] for ref in refs[:n_rows]], refs[n_rows + 1 :]
     size = pieces[0].shape[0]
     for s, piece in enumerate(pieces):
         start = pl.multiple_of(lax.bitwise_xor(lax.axis_index("rows"), s) * size, size)
@@ -409,9 +431,9 @@
     return jax.ShapeDtypeStruct(tuple(dims), kind)
 
 
-def call(kernel, name, outs, scratch=(), after=0, cost=1000):
+def call(kernel, name, outs, scratch=(), after=0, space=pl.ANY, cost=1000):
     def run(*operands):
-        spaces = [pltpu.VMEM] * (len(operands) - after) + [pl.ANY] * after
+        spaces = [pltpu.VMEM] * (len(operands) - after) + [space] * after
         held = sum(math.prod(x.shape) * 4 for x in scratch)
         return pl.pallas_call(
             kernel,
@@ -454,6 +476,7 @@
             pltpu.SemaphoreType.DMA((4,)),
         ],
         after=4,
+        space=pltpu.HBM,
     )(pair_middle, cotangent, gate_weight, output_weight)
     right_act, right_in, *right_flip = call(
         functools.partial(right_kernel, n_rows, n_blk, k_left),
@@ -473,30 +496,11 @@
         left_act.append(act)
         left_in.append(inputs)
         total = [total]
-    act, inputs, update, pre_back, tri_back, gate_part, output_part = call(
+    act, inputs, tri_in, tri_back = call(
         functools.partial(triangle_kernel, n_blk > 1),
         "triangle",
-        [
-            act_shape,
-            in_shape,
-            shape(middle_shape, bf16),
-            shape(middle_shape, bf16),
-            shape(middle_shape, f32),
-            shape(gate_weight.shape, f32),
-            shape(output_weight.shape, f32),
-        ],
-    )(
-        left_raw[-1],
-        left_weight,
-        right_flip[-1],
-        output_weight,
-        gate,
-        middle_in,
-        head_back,
-        tri_up,
-        cotangent,
-        *total,
-    )
+        [act_shape, in_shape, shape(middle_shape, bf16), shape(middle_shape, f32)],
+    )(left_raw[-1], left_weight, right_flip[-1], tri_up, *total)
     left_act.append(act)
     left_in.append(inputs)
     left_out = call(left_back_kernel, "left_back", [shape(pair_left.shape, bf16)] * n_blk)(
@@ -512,29 +516,42 @@
         after=1,
     )(tri_back, *left_act, left_out[0])
     kept, came, sent = halving_sum(keep, send, "rows", n_rows, (behind(*left_back[1:]),))
-    (parts,) = call(
+    update, pre_back, gate_part, output_part = call(
+        heads_kernel,
+        "heads",
+        [
+            shape(middle_shape, bf16),
+            shape(middle_shape, bf16),
+            shape(gate_weight.shape, f32),
+            shape(output_weight.shape, f32),
+        ],
+        after=1,
+    )(tri_in, output_weight, gate, middle_in, head_back, cotangent, left_out[0])
+    parts = (n_rows // 2, width // n_rows, 6 * width)
+    keep, send = call(
         functools.partial(weights_kernel, n_rows, n_blk),
         "weights",
-        [shape((width, 6 * width), bf16)],
+        [shape(parts, f32), shape(parts, bf16)],
         scratch=[pltpu.VMEM((width, 6 * width), f32)],
     )(right_in, left_weight, right_weight, gate_part, output_part, *left_in, *left_out, keep, send)
-    parts = lax.all_to_all(parts.reshape(n_rows, width // n_rows, 6 * width), "rows", 0, 0)
-    part = combine([parts], (behind(sent),))
-    part = combine([part] + [shift(part, "blk", n_blk, s) for s in range(1, n_blk)])
-    pieces = [part] + [exchange(part, "rows", n_rows, s) for s in range(1, n_rows)]
-    deltas = call(
-        functools.partial(deltas_kernel, n_rows),
-        "deltas",
-        [shape(x.shape, f32) for x in (left_weight, right_weight, gate_weight, output_weight)],
-    )(*pieces)
+    keep, part, _ = halving_sum(keep, send, "rows", n_rows, (behind(sent),))
+    part = combine([keep, part])
     (grad_middle,) = call(grad_middle_kernel, "grad_middle", [shape(middle_shape, bf16)])(
         pair_middle, pre_back, gate_weight
     )
+    part = combine([part] + [shift(part, "blk", n_blk, s) for s in range(1, n_blk)], (grad_middle,))
+    pieces = [part] + [exchange(part, "rows", n_rows, s) for s in range(1, n_rows)]
     grad_left, grad_right = call(
         functools.partial(side_kernel, n_blk),
         "sides",
         [shape(pair_left.shape, bf16), shape(pair_right.shape, bf16)],
     )(pair_left, pair_right, left_weight, right_weight, *left_back, kept, came)
+    deltas = call(
+        functools.partial(deltas_kernel, n_rows),
+        "deltas",
+        [shape(x.shape, f32) for x in (left_weight, right_weight, gate_weight, output_weight)],
+        after=1,
+    )(*pieces, grad_left)
     return (
         update,
         grad_left,

time: 90 us -> 87.7 us (0.974)
  Pallas kernels: 43.6 us -> 40.7 us
  local copies, waits for them, and re-layouts: 3.63 us -> 5.61 us
  waiting for transfers between devices: 10.5 us -> 9.13 us
    all_to_all x1 -> x0, starting transfers between devices: 3.36 us -> none  [per_device(): lax.all_to_all(parts.reshape(n_rows, width // n_rows, 6 * width), 'rows',...]
    ppermute x8 -> x10, starting transfers between devices: 9.66 us -> 12.8 us  [exchange(): return lax.ppermute(x, axis, [(a, a ^ bit) for a in range(n)])]
    pallas_call x17 -> x19, Pallas kernels: 43.6 us -> 40.7 us  [run(): pl.pallas_call(kernel, in_specs=[pl.BlockSpec(memory_space=space) for spa...]
    ppermute x9, waiting for transfers between devices: 9.36 us -> 7.04 us  [shift(): return lax.ppermute(x, axis, [(a, (a + step) % n) for a in range(n)])]
    unnamed x24, local copies, waits for them, and re-layouts: 3.63 us -> 5.61 us
    ppermute x8 -> x10, waiting for transfers between devices: 1.11 us -> 2.09 us  [exchange(): return lax.ppermute(x, axis, [(a, a ^ bit) for a in range(n)])]
  transfers between devices with their start and end apart: 18 -> 19, of which waited for: 5 -> 3; matrix products, arithmetic and copies ran while one was open for 0% -> 0% of each run, Pallas kernels for 33% -> 36%
where the time goes in v6:
time: 87.7 us; the launch traced here: 87.3 us
  Pallas kernels  40.7 us (46%)
  starting transfers between devices  31 us (35%)
  waiting for transfers between devices  9.13 us (10%)
  local copies, waits for them, and re-layouts  5.61 us (6%)
    pallas_call x19, Pallas kernels, run(): pl.pallas_call(kernel, in_specs=[pl.BlockSpec(memory_space=space) for spa...  40.7 us
    ppermute x9, starting transfers between devices, shift(): return lax.ppermute(x, axis, [(a, (a + step) % n) for a in range(n)])  18.2 us
    ppermute x10, starting transfers between devices, exchange(): return lax.ppermute(x, axis, [(a, a ^ bit) for a in range(n)])  12.8 us
    ppermute x9, waiting for transfers between devices, shift(): return lax.ppermute(x, axis, [(a, (a + step) % n) for a in range(n)])  7.04 us
    unnamed x24, local copies, waits for them, and re-layouts  5.61 us
    ppermute x10, waiting for transfers between devices, exchange(): return lax.ppermute(x, axis, [(a, a ^ bit) for a in range(n)])  2.09 us
  transfers between devices with their start and end apart: 19, of which 3 were waited for; matrix products, arithmetic and copies ran while one was open for 0% of the time, Pallas kernels for 36%

profile of v6, /device:TPU:0, one launch (start us, length us, event | category | flops | bytes accessed | tf_op | source)
XLA Modules:
  0.0 87.3 jit_solution(7227071270986938544)
XLA Ops:
  0.6 4.0 %collective-permute-start.3 = (bf16[32,16,128]{2,1,0:T(8,128)(2,1)}, bf16[32,16,128]{2,1,0:T(8,128)(2,1)S(1)}, u32[]{:S(2)}, u32[]{:S(2)}) collective-permute-start(bf16[32,16,128]{2,1,0:T(8,128)(2,1)} %refs_1_.3), channel_id=1, source_target_pairs={{0,24},{8,16},{16,8},{24,0},{1,25},{9,17},{17,9},{25,1},{2,26},{10... | collective-permute-start | bytes 393224 | tf_op jit(solution)/shard_map/ppermute | solution.py:364
  4.6 1.6 %collective-permute-start.5 = (bf16[64,16,128]{2,1,0:T(8,128)(2,1)}, bf16[64,16,128]{2,1,0:T(8,128)(2,1)S(1)}, u32[]{:S(2)}, u32[]{:S(2)}) collective-permute-start(bf16[64,16,128]{2,1,0:T(8,128)(2,1)} %refs_0_.5), channel_id=1, source_target_pairs={{0,2},{2,4},{4,6},{6,0},{1,3},{3,5},{5,7},{7,1},{8,10},{10,12},{12... | collective-permute-start | bytes 786440 | tf_op jit(solution)/shard_map/ppermute | solution.py:360
  6.2 2.6 %collective-permute-start.4 = (bf16[64,16,128]{2,1,0:T(8,128)(2,1)}, bf16[64,16,128]{2,1,0:T(8,128)(2,1)S(1)}, u32[]{:S(2)}, u32[]{:S(2)}) collective-permute-start(bf16[64,16,128]{2,1,0:T(8,128)(2,1)} %refs_0_.5), channel_id=1, source_target_pairs={{0,4},{2,6},{4,0},{6,2},{1,5},{3,7},{5,1},{7,3},{8,12},{10,14},{12... | collective-permute-start | bytes 786440 | tf_op jit(solution)/shard_map/ppermute | solution.py:360
  8.8 1.3 %collective-permute-start = (bf16[64,16,128]{2,1,0:T(8,128)(2,1)}, bf16[64,16,128]{2,1,0:T(8,128)(2,1)S(1)}, u32[]{:S(2)}, u32[]{:S(2)}) collective-permute-start(bf16[64,16,128]{2,1,0:T(8,128)(2,1)} %refs_0_.5), channel_id=1, source_target_pairs={{0,6},{2,0},{4,2},{6,4},{1,7},{3,1},{5,3},{7,5},{8,14},{10,8},{12,... | collective-permute-start | bytes 786440 | tf_op jit(solution)/shard_map/ppermute | solution.py:360
  10.1 0.5 collective-permute-start.2
  10.6 0.0 collective-permute-done.3.refs_3_
  10.6 0.5 collective-permute-start.1
  11.2 1.0 %copy-done.1 = bf16[64,32,128]{2,1,0:T(8,128)(2,1)S(1)} copy-done((bf16[64,32,128]{2,1,0:T(8,128)(2,1)S(1)}, bf16[64,32,128]{2,1,0:T(8,128)(2,1)}, u32[]{:S(2)}) %copy-start.1) | copy-done | bytes 524312
  12.2 1.0 %copy-done.4 = bf16[64,32,128]{2,1,0:T(8,128)(2,1)S(1)} copy-done((bf16[64,32,128]{2,1,0:T(8,128)(2,1)S(1)}, bf16[64,32,128]{2,1,0:T(8,128)(2,1)}, u32[]{:S(2)}) %copy-start.4) | copy-done | bytes 524312
  13.2 0.8 copy-done.10
  14.0 0.8 copy-done.11
  14.8 2.6 %middle.2 = (f32[64,32,128]{2,1,0:T(8,128)S(1)}, bf16[64,32,128]{2,1,0:T(8,128)(2,1)S(1)}, bf16[64,32,128]{2,1,0:T(8,128)(2,1)S(1)}, f32[64,32,128]{2,1,0:T(8,128)S(1)}) custom-call(bf16[64,32,128]{2,1,0:T(8,128)(2,1)S(1)} %copy-done.1, bf16[64,32,128]{2,1,0:T(8,128)(2,1)S(1)} %copy-done.4, bf16[128,128]{1,0:T(8,128)(2,1)S(1)} %copy-done.11, ...), custom_call_target="tpu_custom_call" | custom-call | flops 1000 | bytes 1000 | tf_op jit(solution)/shard_map/middle/pallas_call | solution.py:438
  17.4 0.0 copy-start
  17.4 0.0 copy-start.6
  17.4 0.0 collective-permute-done.2.refs_2_
  17.4 3.3 %right.1 = (f32[2048,128]{1,0:T(8,128)S(1)}, bf16[4,32,16,128]{3,2,1,0:T(8,128)(2,1)S(1)}, f32[16,32,128]{2,1,0:T(8,128)S(1)}, f32[16,32,128]{2,1,0:T(8,128)S(1)...) custom-call(bf16[32,16,128]{2,1,0:T(8,128)(2,1)S(1)} %copy-done.8, ...), custom_call_target="tpu_custom_call" | custom-call | flops 1000 | bytes 1000 | tf_op jit(solution)/shard_map/right/pallas_call | solution.py:438
  20.8 2.6 %left.3 = (f32[64,16,128]{2,1,0:T(8,128)S(1)}, bf16[64,16,128]{2,1,0:T(8,128)(2,1)S(1)}, f32[64,32,128]{2,1,0:T(8,128)S(1)}) custom-call(bf16[64,16,128]{2,1,0:T(8,128)(2,1)S(1)} %copy-done.6, bf16[128,256]{1,0:T(8,128)(2,1)S(1)} %copy-done, f32[16,32,128]{2,1,0:T(8,128)S(1)} %get-tuple-element.57.flip), custom_call_target="tpu_custom_call" | custom-call | flops 1000 | bytes 1000 | tf_op jit(solution)/shard_map/left/pallas_call | solution.py:438
  23.4 2.6 %left.4 = (f32[64,16,128]{2,1,0:T(8,128)S(1)}, bf16[64,16,128]{2,1,0:T(8,128)(2,1)S(1)}, f32[64,32,128]{2,1,0:T(8,128)S(1)}) custom-call(bf16[64,16,128]{2,1,0:T(8,128)(2,1)S(1)} %collective-permute-done.5.raw, bf16[128,256]{1,0:T(8,128)(2,1)S(1)} %copy-done, f32[16,32,128]{2,1,0:T(8,128)S(1)} %get-tuple-element.56.flip, ...), custom_call_target="tpu_custom_call" | custom-call | flops 1000 | bytes 1000 | tf_op jit(solution)/shard_map/left/pallas_call | solution.py:438
  26.0 0.0 collective-permute-done.4.raw
  26.0 2.6 %left.5 = (f32[64,16,128]{2,1,0:T(8,128)S(1)}, bf16[64,16,128]{2,1,0:T(8,128)(2,1)S(1)}, f32[64,32,128]{2,1,0:T(8,128)S(1)}) custom-call(bf16[64,16,128]{2,1,0:T(8,128)(2,1)S(1)} %collective-permute-done.4.raw, bf16[128,256]{1,0:T(8,128)(2,1)S(1)} %copy-done, f32[16,32,128]{2,1,0:T(8,128)S(1)} %get-tuple-element.55.flip, ...), custom_call_target="tpu_custom_call" | custom-call | flops 1000 | bytes 1000 | tf_op jit(solution)/shard_map/left/pallas_call | solution.py:438
  28.6 3.5 %triangle.1 = (f32[64,16,128]{2,1,0:T(8,128)S(1)}, bf16[64,16,128]{2,1,0:T(8,128)(2,1)S(1)}, bf16[64,32,128]{2,1,0:T(8,128)(2,1)S(1)}, f32[64,32,128]{2,1,0:T(8,128)S(1)}) custom-call(bf16[64,16,128]{2,1,0:T(8,128)(2,1)S(1)} %collective-permute-done.raw, bf16[128,256]{1,0:T(8,128)(2,1)S(1)} %copy-done, f32[16,32,128]{2,1,0:T(8,128)S(1)} %get-tuple-element.53.flip, ...), custom_call_target="tpu_custom_call" | custom-call | flops 1000 | bytes 1000 | tf_op jit(solution)/shard_map/triangle/pallas_call | solution.py:438
  32.1 4.7 %left_back.1 = (bf16[64,16,128]{2,1,0:T(8,128)(2,1)S(1)}, bf16[64,16,128]{2,1,0:T(8,128)(2,1)S(1)}, bf16[64,16,128]{2,1,0:T(8,128)(2,1)S(1)}, bf16[64,16,128]{2,1,0:T(8,128)(2,1)S(1)}) custom-call(f32[64,32,128]{2,1,0:T(8,128)S(1)} %get-tuple-element.65.tri_back, f32[2048,128]{1,0:T(8,128)S(1)} %get-tuple-element.66.right_act), custom_call_target="tpu_custom_call" | custom-call | flops 1000 | bytes 1000 | tf_op jit(solution)/shard_map/left_back/pallas_call | solution.py:438
  36.8 7.0 %collective-permute-start.6 = (bf16[64,16,128]{2,1,0:T(8,128)(2,1)S(1)}, bf16[64,16,128]{2,1,0:T(8,128)(2,1)S(1)}, u32[]{:S(2)}, u32[]{:S(2)}) collective-permute-start(bf16[64,16,128]{2,1,0:T(8,128)(2,1)S(1)} %get-tuple-element.69.refs_5_), channel_id=1, source_target_pairs={{0,6},{2,0},{4,2},{6,4},{1,7},{3,1},{5,3},{7,5},{8,14},{10,8},{12,... | collective-permute-start | bytes 786440 | tf_op jit(solution)/shard_map/ppermute | solution.py:360
  43.8 0.6 collective-permute-start.8
  44.4 5.5 %right_back.1 = (bf16[2,32,16,128]{3,2,1,0:T(8,128)(2,1)S(1)}, bf16[2,32,16,128]{3,2,1,0:T(8,128)(2,1)S(1)}) custom-call(f32[64,32,128]{2,1,0:T(8,128)S(1)} %get-tuple-element.65.tri_back, f32[64,16,128]{2,1,0:T(8,128)S(1)} %get-tuple-element.72.refs_0_, f32[64,16,128]{2,1,0:T(8,128)S(1)} %get-tuple-element.73.refs_1_, ...), custom_call_target="tpu_custom_call" | custom-call | flops 1000 | bytes 1000 | tf_op jit(solution)/shard_map/right_back/pallas_call | solution.py:438
  50.0 0.6 collective-permute-start.9
  50.6 2.7 %heads.1 = (bf16[64,32,128]{2,1,0:T(8,128)(2,1)}, bf16[64,32,128]{2,1,0:T(8,128)(2,1)S(1)}, f32[128,128]{1,0:T(8,128)S(1)}, f32[128,128]{1,0:T(8,128)S(1)}) custom-call(bf16[64,32,128]{2,1,0:T(8,128)(2,1)S(1)} %get-tuple-element.61.tri_in, bf16[128,128]{1,0:T(8,128)(2,1)S(1)} %copy-done.10, f32[64,32,128]{2,1,0:T(8,128)S(1)} %get-tuple-element.62.gate, ...), custom_call_target="tpu_custom_call" | custom-call | flops 1000 | bytes 1000 | tf_op jit(solution)/shard_map/heads/pallas_call | solution.py:438
  53.3 4.3 %weights.1 = (f32[2,32,768]{2,1,0:T(8,128)S(1)}, bf16[2,32,768]{2,1,0:T(8,128)(2,1)S(1)}) custom-call(bf16[4,32,16,128]{3,2,1,0:T(8,128)(2,1)S(1)} %get-tuple-element.83.right_in, bf16[128,256]{1,0:T(8,128)(2,1)S(1)} %copy-done, bf16[128,256]{1,0:T(8,128)(2,1)S(1)} %copy-done.7, f32[128,128]{1,0:T(8,128)S(1)} %get-tuple-element.84.gate_part, ...), custom_call_target="tpu_custom_call" | custom-call | flops 1000 | bytes 1000 | tf_op jit(solution)/shard_map/weights/pallas_call | solution.py:438
  57.6 1.6 %collective-permute-start.11 = (bf16[2,32,768]{2,1,0:T(8,128)(2,1)S(1)}, bf16[2,32,768]{2,1,0:T(8,128)(2,1)S(1)}, u32[]{:S(2)}, u32[]{:S(2)}) collective-permute-start(bf16[2,32,768]{2,1,0:T(8,128)(2,1)S(1)} %get-tuple-element.91), channel_id=1, source_target_pairs={{0,8},{8,0},{16,24},{24,16},{1,9},{9,1},{17,25},{25,17},{2,10},{10... | collective-permute-start | bytes 294920 | tf_op jit(solution)/shard_map/ppermute | solution.py:364
  59.1 5.5 %collective-permute-done.7.refs_1_.refs_6_ = bf16[64,16,128]{2,1,0:T(8,128)(2,1)S(1)} collective-permute-done((bf16[64,16,128]{2,1,0:T(8,128)(2,1)S(1)}, bf16[64,16,128]{2,1,0:T(8,128)(2,1)S(1)}, u32[]{:S(2)}, u32[]{:S(2)}) %collective-permute-start.7) | collective-permute-done | bytes 262176 | tf_op jit(solution)/shard_map/ppermute | solution.py:360
  64.7 0.1 halve.2
  64.7 0.0 copy-start.2
  64.8 0.6 collective-permute-start.12
  65.4 1.5 %collective-permute-start.10 = (bf16[1,32,16,128]{3,2,1,0:T(8,128)(2,1)S(1)}, bf16[1,32,16,128]{3,2,1,0:T(8,128)(2,1)S(1)}, u32[]{:S(2)}, u32[]{:S(2)}) collective-permute-start(bf16[1,32,16,128]{3,2,1,0:T(8,128)(2,1)S(1)} %get-tuple-element.79.refs_0_), channel_id=1, source_target_pairs={{0,16},{8,24},{16,0},{24,8},{1,17},{9,25},{17,1},{25,9},{2,18},{10... | collective-permute-start | bytes 393224 | tf_op jit(solution)/shard_map/ppermute | solution.py:364
  66.9 2.1 %collective-permute-done.12.refs_1_ = bf16[1,32,768]{2,1,0:T(8,128)(2,1)S(1)} collective-permute-done((bf16[1,32,768]{2,1,0:T(8,128)(2,1)S(1)}, bf16[1,32,768]{2,1,0:T(8,128)(2,1)S(1)}, u32[]{:S(2)}, u32[]{:S(2)}) %collective-permute-start.12) | collective-permute-done | bytes 49184 | tf_op jit(solution)/shard_map/ppermute | solution.py:364
  69.0 0.7 collective-permute-start.15
  69.7 2.4 %collective-permute-start.14 = (bf16[1,32,768]{2,1,0:T(8,128)(2,1)S(1)}, bf16[1,32,768]{2,1,0:T(8,128)(2,1)S(1)}, u32[]{:S(2)}, u32[]{:S(2)}) collective-permute-start(bf16[1,32,768]{2,1,0:T(8,128)(2,1)S(1)} %combine.2.refs_0_), channel_id=1, source_target_pairs={{0,4},{2,6},{4,0},{6,2},{1,5},{3,7},{5,1},{7,3},{8,12},{10,14},{12... | collective-permute-start | bytes 147464 | tf_op jit(solution)/shard_map/ppermute | solution.py:360
  72.1 1.9 %collective-permute-start.13 = (bf16[1,32,768]{2,1,0:T(8,128)(2,1)S(1)}, bf16[1,32,768]{2,1,0:T(8,128)(2,1)S(1)}, u32[]{:S(2)}, u32[]{:S(2)}) collective-permute-start(bf16[1,32,768]{2,1,0:T(8,128)(2,1)S(1)} %combine.2.refs_0_), channel_id=1, source_target_pairs={{0,2},{2,4},{4,6},{6,0},{1,3},{3,5},{5,7},{7,1},{8,10},{10,12},{12... | collective-permute-start | bytes 147464 | tf_op jit(solution)/shard_map/ppermute | solution.py:360
  74.1 2.4 %grad_middle.1.refs_4_ = bf16[64,32,128]{2,1,0:T(8,128)(2,1)} custom-call(bf16[64,32,128]{2,1,0:T(8,128)(2,1)S(1)} %copy-done.2, bf16[64,32,128]{2,1,0:T(8,128)(2,1)S(1)} %get-tuple-element.82.pre_back, bf16[128,128]{1,0:T(8,128)(2,1)S(1)} %copy-done.11), custom_call_target="tpu_custom_call" | custom-call | flops 1000 | bytes 1000 | tf_op jit(solution)/shard_map/grad_middle/pallas_call | solution.py:438
  76.5 1.5 %collective-permute-done.13.refs_1_ = bf16[1,32,768]{2,1,0:T(8,128)(2,1)S(1)} collective-permute-done((bf16[1,32,768]{2,1,0:T(8,128)(2,1)S(1)}, bf16[1,32,768]{2,1,0:T(8,128)(2,1)S(1)}, u32[]{:S(2)}, u32[]{:S(2)}) %collective-permute-start.13) | collective-permute-done | bytes 49184 | tf_op jit(solution)/shard_map/ppermute | solution.py:360
  78.0 1.0 %copy-done.3 = bf16[64,32,128]{2,1,0:T(8,128)(2,1)S(1)} copy-done((bf16[64,32,128]{2,1,0:T(8,128)(2,1)S(1)}, bf16[64,32,128]{2,1,0:T(8,128)(2,1)}, u32[]{:S(2)}) %copy-start.3) | copy-done | bytes 524312
  79.1 0.9 %collective-permute-start.18 = (bf16[1,32,768]{2,1,0:T(8,128)(2,1)S(1)}, bf16[1,32,768]{2,1,0:T(8,128)(2,1)S(1)}, u32[]{:S(2)}, u32[]{:S(2)}) collective-permute-start(bf16[1,32,768]{2,1,0:T(8,128)(2,1)S(1)} %combine.3.refs_0_), channel_id=1, source_target_pairs={{0,24},{8,16},{16,8},{24,0},{1,25},{9,17},{17,9},{25,1},{2,26},{10... | collective-permute-start | bytes 147464 | tf_op jit(solution)/shard_map/ppermute | solution.py:364
  80.0 1.1 %collective-permute-start.17 = (bf16[1,32,768]{2,1,0:T(8,128)(2,1)S(1)}, bf16[1,32,768]{2,1,0:T(8,128)(2,1)S(1)}, u32[]{:S(2)}, u32[]{:S(2)}) collective-permute-start(bf16[1,32,768]{2,1,0:T(8,128)(2,1)S(1)} %combine.3.refs_0_), channel_id=1, source_target_pairs={{0,16},{8,24},{16,0},{24,8},{1,17},{9,25},{17,1},{25,9},{2,18},{10... | collective-permute-start | bytes 147464 | tf_op jit(solution)/shard_map/ppermute | solution.py:364
  81.1 1.5 %collective-permute-start.16 = (bf16[1,32,768]{2,1,0:T(8,128)(2,1)S(1)}, bf16[1,32,768]{2,1,0:T(8,128)(2,1)S(1)}, u32[]{:S(2)}, u32[]{:S(2)}) collective-permute-start(bf16[1,32,768]{2,1,0:T(8,128)(2,1)S(1)} %combine.3.refs_0_), channel_id=1, source_target_pairs={{0,8},{8,0},{16,24},{24,16},{1,9},{9,1},{17,25},{25,17},{2,10},{10... | collective-permute-start | bytes 147464 | tf_op jit(solution)/shard_map/ppermute | solution.py:364
  82.6 2.9 %sides.1 = (bf16[64,16,128]{2,1,0:T(8,128)(2,1)}, bf16[32,16,128]{2,1,0:T(8,128)(2,1)}) custom-call(bf16[64,16,128]{2,1,0:T(8,128)(2,1)S(1)} %copy-done.6, bf16[32,16,128]{2,1,0:T(8,128)(2,1)S(1)} %copy-done.8, bf16[128,256]{1,0:T(8,128)(2,1)S(1)} %copy-done, bf16[128,256]{1,0:T(8,128)(2,1)S(1)} %copy-done.7, ...), custom_call_target="tpu_custom_call" | custom-call | flops 1000 | bytes 1000 | tf_op jit(solution)/shard_map/sides/pallas_call | solution.py:438
  85.6 0.0 copy-start.9
  85.6 0.9 %copy-done.9 = bf16[64,16,128]{2,1,0:T(8,128)(2,1)S(1)} copy-done((bf16[64,16,128]{2,1,0:T(8,128)(2,1)S(1)}, bf16[64,16,128]{2,1,0:T(8,128)(2,1)}, u32[]{:S(2)}) %copy-start.9) | copy-done | bytes 262168
  86.5 0.8 deltas.1
  (33 shorter events, 0.1 us)
Async XLA Ops:
  0.6 10.0 %collective-permute-start.3 = (bf16[32,16,128]{2,1,0:T(8,128)(2,1)}, bf16[32,16,128]{2,1,0:T(8,128)(2,1)S(1)}, u32[]{:S(2)}, u32[]{:S(2)}) collective-permute-start(bf16[32,16,128]{2,1,0:T(8,128)(2,1)} %refs_1_.3), channel_id=1, source_target_pairs={{0,24},{8,16},{16,8},{24,0},{1,25},{9,17},{17,9},{25,1},{2,26},{10... | collective-permute-start | bytes 393224 | tf_op jit(solution)/shard_map/ppermute | solution.py:364
  4.6 18.8 %collective-permute-start.5 = (bf16[64,16,128]{2,1,0:T(8,128)(2,1)}, bf16[64,16,128]{2,1,0:T(8,128)(2,1)S(1)}, u32[]{:S(2)}, u32[]{:S(2)}) collective-permute-start(bf16[64,16,128]{2,1,0:T(8,128)(2,1)} %refs_0_.5), channel_id=1, source_target_pairs={{0,2},{2,4},{4,6},{6,0},{1,3},{3,5},{5,7},{7,1},{8,10},{10,12},{12... | collective-permute-start | bytes 786440 | tf_op jit(solution)/shard_map/ppermute | solution.py:360
  6.2 19.8 %collective-permute-start.4 = (bf16[64,16,128]{2,1,0:T(8,128)(2,1)}, bf16[64,16,128]{2,1,0:T(8,128)(2,1)S(1)}, u32[]{:S(2)}, u32[]{:S(2)}) collective-permute-start(bf16[64,16,128]{2,1,0:T(8,128)(2,1)} %refs_0_.5), channel_id=1, source_target_pairs={{0,4},{2,6},{4,0},{6,2},{1,5},{3,7},{5,1},{7,3},{8,12},{10,14},{12... | collective-permute-start | bytes 786440 | tf_op jit(solution)/shard_map/ppermute | solution.py:360
  8.8 19.8 %collective-permute-start = (bf16[64,16,128]{2,1,0:T(8,128)(2,1)}, bf16[64,16,128]{2,1,0:T(8,128)(2,1)S(1)}, u32[]{:S(2)}, u32[]{:S(2)}) collective-permute-start(bf16[64,16,128]{2,1,0:T(8,128)(2,1)} %refs_0_.5), channel_id=1, source_target_pairs={{0,6},{2,0},{4,2},{6,4},{1,7},{3,1},{5,3},{7,5},{8,14},{10,8},{12,... | collective-permute-start | bytes 786440 | tf_op jit(solution)/shard_map/ppermute | solution.py:360
  10.1 7.3 %collective-permute-start.2 = (bf16[32,16,128]{2,1,0:T(8,128)(2,1)}, bf16[32,16,128]{2,1,0:T(8,128)(2,1)S(1)}, u32[]{:S(2)}, u32[]{:S(2)}) collective-permute-start(bf16[32,16,128]{2,1,0:T(8,128)(2,1)} %refs_1_.3), channel_id=1, source_target_pairs={{0,16},{8,24},{16,0},{24,8},{1,17},{9,25},{17,1},{25,9},{2,18},{10... | collective-permute-start | bytes 393224 | tf_op jit(solution)/shard_map/ppermute | solution.py:364
  10.6 6.8 %collective-permute-start.1 = (bf16[32,16,128]{2,1,0:T(8,128)(2,1)}, bf16[32,16,128]{2,1,0:T(8,128)(2,1)S(1)}, u32[]{:S(2)}, u32[]{:S(2)}) collective-permute-start(bf16[32,16,128]{2,1,0:T(8,128)(2,1)} %refs_1_.3), channel_id=1, source_target_pairs={{0,8},{8,0},{16,24},{24,16},{1,9},{9,1},{17,25},{25,17},{2,10},{10... | collective-permute-start | bytes 393224 | tf_op jit(solution)/shard_map/ppermute | solution.py:364
  11.2 1.0 %copy-start.1 = (bf16[64,32,128]{2,1,0:T(8,128)(2,1)S(1)}, bf16[64,32,128]{2,1,0:T(8,128)(2,1)}, u32[]{:S(2)}) copy-start(bf16[64,32,128]{2,1,0:T(8,128)(2,1)} %middle.3) | copy-start | bytes 1572868
  12.2 1.0 %copy-start.4 = (bf16[64,32,128]{2,1,0:T(8,128)(2,1)S(1)}, bf16[64,32,128]{2,1,0:T(8,128)(2,1)}, u32[]{:S(2)}) copy-start(bf16[64,32,128]{2,1,0:T(8,128)(2,1)} %cotangent.1) | copy-start | bytes 1572868
  13.2 0.8 copy-start.10
  14.0 0.8 copy-start.11
  14.8 2.6 %copy-start.7 = (bf16[128,256]{1,0:T(8,128)(2,1)S(1)}, bf16[128,256]{1,0:T(8,128)(2,1)}, u32[]{:S(2)}) copy-start(bf16[128,256]{1,0:T(8,128)(2,1)} %right_w.1) | copy-start | bytes 196612
  14.8 2.7 %copy-start.8 = (bf16[32,16,128]{2,1,0:T(8,128)(2,1)S(1)}, bf16[32,16,128]{2,1,0:T(8,128)(2,1)}, u32[]{:S(2)}) copy-start(bf16[32,16,128]{2,1,0:T(8,128)(2,1)} %refs_1_.3) | copy-start | bytes 393220
  17.4 3.4 %copy-start = (bf16[128,256]{1,0:T(8,128)(2,1)S(1)}, bf16[128,256]{1,0:T(8,128)(2,1)}, u32[]{:S(2)}) copy-start(bf16[128,256]{1,0:T(8,128)(2,1)} %left_w.3) | copy-start | bytes 196612
  17.4 3.4 %copy-start.6 = (bf16[64,16,128]{2,1,0:T(8,128)(2,1)S(1)}, bf16[64,16,128]{2,1,0:T(8,128)(2,1)}, u32[]{:S(2)}) copy-start(bf16[64,16,128]{2,1,0:T(8,128)(2,1)} %refs_0_.5) | copy-start | bytes 786436
  36.8 22.3 %collective-permute-start.6 = (bf16[64,16,128]{2,1,0:T(8,128)(2,1)S(1)}, bf16[64,16,128]{2,1,0:T(8,128)(2,1)S(1)}, u32[]{:S(2)}, u32[]{:S(2)}) collective-permute-start(bf16[64,16,128]{2,1,0:T(8,128)(2,1)S(1)} %get-tuple-element.69.refs_5_), channel_id=1, source_target_pairs={{0,6},{2,0},{4,2},{6,4},{1,7},{3,1},{5,3},{7,5},{8,14},{10,8},{12,... | collective-permute-start | bytes 786440 | tf_op jit(solution)/shard_map/ppermute | solution.py:360
  43.8 20.9 %collective-permute-start.7 = (bf16[64,16,128]{2,1,0:T(8,128)(2,1)S(1)}, bf16[64,16,128]{2,1,0:T(8,128)(2,1)S(1)}, u32[]{:S(2)}, u32[]{:S(2)}) collective-permute-start(bf16[64,16,128]{2,1,0:T(8,128)(2,1)S(1)} %get-tuple-element.70.refs_6_), channel_id=1, source_target_pairs={{0,4},{2,6},{4,0},{6,2},{1,5},{3,7},{5,1},{7,3},{8,12},{10,14},{12... | collective-permute-start | bytes 786440 | tf_op jit(solution)/shard_map/ppermute | solution.py:360
  43.8 20.9 %collective-permute-start.8 = (bf16[64,16,128]{2,1,0:T(8,128)(2,1)S(1)}, bf16[64,16,128]{2,1,0:T(8,128)(2,1)S(1)}, u32[]{:S(2)}, u32[]{:S(2)}) collective-permute-start(bf16[64,16,128]{2,1,0:T(8,128)(2,1)S(1)} %get-tuple-element.71.refs_7_), channel_id=1, source_target_pairs={{0,2},{2,4},{4,6},{6,0},{1,3},{3,5},{5,7},{7,1},{8,10},{10,12},{12... | collective-permute-start | bytes 786440 | tf_op jit(solution)/shard_map/ppermute | solution.py:360
  44.4 6.1 %copy-start.5 = (bf16[64,32,128]{2,1,0:T(8,128)(2,1)S(1)}, bf16[64,32,128]{2,1,0:T(8,128)(2,1)}, u32[]{:S(2)}) copy-start(bf16[64,32,128]{2,1,0:T(8,128)(2,1)} %cotangent.1) | copy-start | bytes 1572868
  50.0 14.7 %collective-permute-start.9 = (bf16[2,32,16,128]{3,2,1,0:T(8,128)(2,1)S(1)}, bf16[2,32,16,128]{3,2,1,0:T(8,128)(2,1)S(1)}, u32[]{:S(2)}, u32[]{:S(2)}) collective-permute-start(bf16[2,32,16,128]{3,2,1,0:T(8,128)(2,1)S(1)} %get-tuple-element.77.refs_9_), channel_id=1, source_target_pairs={{0,8},{8,0},{16,24},{24,16},{1,9},{9,1},{17,25},{25,17},{2,10},{10... | collective-permute-start | bytes 786440 | tf_op jit(solution)/shard_map/ppermute | solution.py:364
  57.6 7.2 %collective-permute-start.11 = (bf16[2,32,768]{2,1,0:T(8,128)(2,1)S(1)}, bf16[2,32,768]{2,1,0:T(8,128)(2,1)S(1)}, u32[]{:S(2)}, u32[]{:S(2)}) collective-permute-start(bf16[2,32,768]{2,1,0:T(8,128)(2,1)S(1)} %get-tuple-element.91), channel_id=1, source_target_pairs={{0,8},{8,0},{16,24},{24,16},{1,9},{9,1},{17,25},{25,17},{2,10},{10... | collective-permute-start | bytes 294920 | tf_op jit(solution)/shard_map/ppermute | solution.py:364
  64.7 9.3 %copy-start.2 = (bf16[64,32,128]{2,1,0:T(8,128)(2,1)S(1)}, bf16[64,32,128]{2,1,0:T(8,128)(2,1)}, u32[]{:S(2)}) copy-start(bf16[64,32,128]{2,1,0:T(8,128)(2,1)} %middle.3) | copy-start | bytes 1572868
  64.8 4.2 %collective-permute-start.12 = (bf16[1,32,768]{2,1,0:T(8,128)(2,1)S(1)}, bf16[1,32,768]{2,1,0:T(8,128)(2,1)S(1)}, u32[]{:S(2)}, u32[]{:S(2)}) collective-permute-start(bf16[1,32,768]{2,1,0:T(8,128)(2,1)S(1)} %get-tuple-element.93), channel_id=1, source_target_pairs={{0,16},{8,24},{16,0},{24,8},{1,17},{9,25},{17,1},{25,9},{2,18},{10... | collective-permute-start | bytes 147464 | tf_op jit(solution)/shard_map/ppermute | solution.py:364
  65.4 17.3 %collective-permute-start.10 = (bf16[1,32,16,128]{3,2,1,0:T(8,128)(2,1)S(1)}, bf16[1,32,16,128]{3,2,1,0:T(8,128)(2,1)S(1)}, u32[]{:S(2)}, u32[]{:S(2)}) collective-permute-start(bf16[1,32,16,128]{3,2,1,0:T(8,128)(2,1)S(1)} %get-tuple-element.79.refs_0_), channel_id=1, source_target_pairs={{0,16},{8,24},{16,0},{24,8},{1,17},{9,25},{17,1},{25,9},{2,18},{10... | collective-permute-start | bytes 393224 | tf_op jit(solution)/shard_map/ppermute | solution.py:364
  69.0 7.6 %collective-permute-start.15 = (bf16[1,32,768]{2,1,0:T(8,128)(2,1)S(1)}, bf16[1,32,768]{2,1,0:T(8,128)(2,1)S(1)}, u32[]{:S(2)}, u32[]{:S(2)}) collective-permute-start(bf16[1,32,768]{2,1,0:T(8,128)(2,1)S(1)} %combine.2.refs_0_), channel_id=1, source_target_pairs={{0,6},{2,0},{4,2},{6,4},{1,7},{3,1},{5,3},{7,5},{8,14},{10,8},{12,... | collective-permute-start | bytes 147464 | tf_op jit(solution)/shard_map/ppermute | solution.py:360
  69.7 6.9 %collective-permute-start.14 = (bf16[1,32,768]{2,1,0:T(8,128)(2,1)S(1)}, bf16[1,32,768]{2,1,0:T(8,128)(2,1)S(1)}, u32[]{:S(2)}, u32[]{:S(2)}) collective-permute-start(bf16[1,32,768]{2,1,0:T(8,128)(2,1)S(1)} %combine.2.refs_0_), channel_id=1, source_target_pairs={{0,4},{2,6},{4,0},{6,2},{1,5},{3,7},{5,1},{7,3},{8,12},{10,14},{12... | collective-permute-start | bytes 147464 | tf_op jit(solution)/shard_map/ppermute | solution.py:360
  72.1 5.9 %collective-permute-start.13 = (bf16[1,32,768]{2,1,0:T(8,128)(2,1)S(1)}, bf16[1,32,768]{2,1,0:T(8,128)(2,1)S(1)}, u32[]{:S(2)}, u32[]{:S(2)}) collective-permute-start(bf16[1,32,768]{2,1,0:T(8,128)(2,1)S(1)} %combine.2.refs_0_), channel_id=1, source_target_pairs={{0,2},{2,4},{4,6},{6,0},{1,3},{3,5},{5,7},{7,1},{8,10},{10,12},{12... | collective-permute-start | bytes 147464 | tf_op jit(solution)/shard_map/ppermute | solution.py:360
  78.0 1.0 %copy-start.3 = (bf16[64,32,128]{2,1,0:T(8,128)(2,1)S(1)}, bf16[64,32,128]{2,1,0:T(8,128)(2,1)}, u32[]{:S(2)}) copy-start(bf16[64,32,128]{2,1,0:T(8,128)(2,1)} %grad_middle.1.refs_4_) | copy-start | bytes 1572868
  79.1 6.5 %collective-permute-start.18 = (bf16[1,32,768]{2,1,0:T(8,128)(2,1)S(1)}, bf16[1,32,768]{2,1,0:T(8,128)(2,1)S(1)}, u32[]{:S(2)}, u32[]{:S(2)}) collective-permute-start(bf16[1,32,768]{2,1,0:T(8,128)(2,1)S(1)} %combine.3.refs_0_), channel_id=1, source_target_pairs={{0,24},{8,16},{16,8},{24,0},{1,25},{9,17},{17,9},{25,1},{2,26},{10... | collective-permute-start | bytes 147464 | tf_op jit(solution)/shard_map/ppermute | solution.py:364
  80.0 5.5 %collective-permute-start.17 = (bf16[1,32,768]{2,1,0:T(8,128)(2,1)S(1)}, bf16[1,32,768]{2,1,0:T(8,128)(2,1)S(1)}, u32[]{:S(2)}, u32[]{:S(2)}) collective-permute-start(bf16[1,32,768]{2,1,0:T(8,128)(2,1)S(1)} %combine.3.refs_0_), channel_id=1, source_target_pairs={{0,16},{8,24},{16,0},{24,8},{1,17},{9,25},{17,1},{25,9},{2,18},{10... | collective-permute-start | bytes 147464 | tf_op jit(solution)/shard_map/ppermute | solution.py:364
  81.1 4.4 %collective-permute-start.16 = (bf16[1,32,768]{2,1,0:T(8,128)(2,1)S(1)}, bf16[1,32,768]{2,1,0:T(8,128)(2,1)S(1)}, u32[]{:S(2)}, u32[]{:S(2)}) collective-permute-start(bf16[1,32,768]{2,1,0:T(8,128)(2,1)S(1)} %combine.3.refs_0_), channel_id=1, source_target_pairs={{0,8},{8,0},{16,24},{24,16},{1,9},{9,1},{17,25},{25,17},{2,10},{10... | collective-permute-start | bytes 147464 | tf_op jit(solution)/shard_map/ppermute | solution.py:364
  85.6 1.0 %copy-start.9 = (bf16[64,16,128]{2,1,0:T(8,128)(2,1)S(1)}, bf16[64,16,128]{2,1,0:T(8,128)(2,1)}, u32[]{:S(2)}) copy-start(bf16[64,16,128]{2,1,0:T(8,128)(2,1)} %get-tuple-element.46.refs_4_) | copy-start | bytes 786436

commit v7 on v6

--- a/solution.py
+++ b/solution.py
@@ -12,6 +12,7 @@
 f32 = jnp.float32
 bf16 = jnp.bfloat16
 SCOPED = 6 * 1024 * 1024
+MARK = jax.ShapeDtypeStruct((8, 128), jnp.float32)
 
 
 def normalize(values):
@@ -52,19 +53,9 @@
     return jnp.concatenate([back * sw, back * lin * sw * (1.0 - sw)], axis=-1).astype(bf16)
 
 
-def middle_kernel(*refs):
-    sources, refs = refs[:4], refs[4:]
-    gate, middle_in, head_back, tri_up, middle, cotangent, gate_weight, output_weight, arrived = refs
+def middle_kernel(middle, cotangent, gate_weight, output_weight, _, gate, middle_in, head_back, tri_up):
     n_i, n_j, width = middle.shape
     step = 8
-    copies = [
-        pltpu.make_async_copy(source, target, arrived.at[at])
-        for at, (source, target) in enumerate(zip(sources, (middle, cotangent, gate_weight, output_weight)))
-    ]
-    for copy in copies:
-        copy.start()
-    for copy in copies:
-        copy.wait()
 
     def body(at, _):
         rows = pl.ds(at * step, step)
@@ -279,7 +270,7 @@
 def weights_kernel(n_rows, n_blk, right_in, left_w, right_w, gate_part, output_part, *refs):
     left_in, refs = refs[:n_blk], refs[n_blk:]
     left_out, refs = refs[:n_blk], refs[n_blk:]
-    keep, send, keep_out, send_out, total = refs
+    keep, send, _, keep_out, send_out, total = refs
     right_out = [(send if s % 2 else keep).at[s // 2] for s in range(n_rows)]
     right_ins = [right_in.at[s] for s in range(n_rows)]
     width = gate_part.shape[0]
@@ -315,7 +306,8 @@
             keep_out[s // 2] = piece
 
 
-def grad_middle_kernel(middle, pre_back, gate_weight, grad_middle):
+def grad_middle_kernel(middle, pre_back, gate_weight, grad_middle, mark):
+    mark[...] = jnp.zeros_like(mark)
     n_i, n_j, width = middle.shape
     step = 8
 
@@ -331,6 +323,8 @@
 
 
 def side_kernel(n_left, *refs):
+    *refs, mark = refs
+    mark[...] = jnp.zeros_like(mark)
     left, right, left_w, right_w = refs[:4]
     left_back, refs = refs[4 : 4 + n_left], refs[4 + n_left :]
     right_back, refs = [ref.at[0] for ref in refs[:2]], refs[2:]
@@ -392,7 +386,7 @@
 
 
 def behind(*arrays):
-    (mark,) = call(order_kernel, "order", [shape((8, 128), f32)], after=len(arrays), cost=2 * 10**10)(*arrays)
+    (mark,) = call(order_kernel, "order", [MARK], after=len(arrays), cost=2 * 10**10)(*arrays)
     return mark
 
 
@@ -416,7 +410,7 @@
 
 
 def deltas_kernel(n_rows, *refs):
-    pieces, outs = [ref.at[0] for ref in refs[:n_rows]], refs[n_rows + 1 :]
+    pieces, outs = [ref.at[0] for ref in refs[:n_rows]], refs[n_rows:]
     size = pieces[0].shape[0]
     for s, piece in enumerate(pieces):
         start = pl.multiple_of(lax.bitwise_xor(lax.axis_index("rows"), s) * size, size)
@@ -431,9 +425,9 @@
     return jax.ShapeDtypeStruct(tuple(dims), kind)
 
 
-def call(kernel, name, outs, scratch=(), after=0, space=pl.ANY, cost=1000):
+def call(kernel, name, outs, scratch=(), after=0, cost=1000):
     def run(*operands):
-        spaces = [pltpu.VMEM] * (len(operands) - after) + [space] * after
+        spaces = [pltpu.VMEM] * (len(operands) - after) + [pl.ANY] * after
         held = sum(math.prod(x.shape) * 4 for x in scratch)
         return pl.pallas_call(
             kernel,
@@ -471,13 +465,8 @@
         middle_kernel,
         "middle",
         [shape(middle_shape, f32), shape(middle_shape, bf16), shape(middle_shape, bf16), shape(middle_shape, f32)],
-        scratch=[
-            *(pltpu.VMEM(x.shape, bf16) for x in (pair_middle, cotangent, gate_weight, output_weight)),
-            pltpu.SemaphoreType.DMA((4,)),
-        ],
-        after=4,
-        space=pltpu.HBM,
-    )(pair_middle, cotangent, gate_weight, output_weight)
+        after=1,
+    )(pair_middle, cotangent, gate_weight, output_weight, behind())
     right_act, right_in, *right_flip = call(
         functools.partial(right_kernel, n_rows, n_blk, k_left),
         "right",
@@ -527,31 +516,31 @@
         ],
         after=1,
     )(tri_in, output_weight, gate, middle_in, head_back, cotangent, left_out[0])
+    grad_middle, done_middle = call(
+        grad_middle_kernel, "grad_middle", [shape(middle_shape, bf16), MARK]
+    )(pair_middle, pre_back, gate_weight)
     parts = (n_rows // 2, width // n_rows, 6 * width)
     keep, send = call(
         functools.partial(weights_kernel, n_rows, n_blk),
         "weights",
         [shape(parts, f32), shape(parts, bf16)],
         scratch=[pltpu.VMEM((width, 6 * width), f32)],
-    )(right_in, left_weight, right_weight, gate_part, output_part, *left_in, *left_out, keep, send)
-    keep, part, _ = halving_sum(keep, send, "rows", n_rows, (behind(sent),))
-    part = combine([keep, part])
-    (grad_middle,) = call(grad_middle_kernel, "grad_middle", [shape(middle_shape, bf16)])(
-        pair_middle, pre_back, gate_weight
-    )
-    part = combine([part] + [shift(part, "blk", n_blk, s) for s in range(1, n_blk)], (grad_middle,))
-    pieces = [part] + [exchange(part, "rows", n_rows, s) for s in range(1, n_rows)]
-    grad_left, grad_right = call(
+        after=1,
+    )(right_in, left_weight, right_weight, gate_part, output_part, *left_in, *left_out, keep, send, done_middle)
+    keep, part, _ = halving_sum(keep, send, "rows", n_rows, ())
+    part = combine([keep, part], (behind(sent),))
+    grad_left, grad_right, done_sides = call(
         functools.partial(side_kernel, n_blk),
         "sides",
-        [shape(pair_left.shape, bf16), shape(pair_right.shape, bf16)],
+        [shape(pair_left.shape, bf16), shape(pair_right.shape, bf16), MARK],
     )(pair_left, pair_right, left_weight, right_weight, *left_back, kept, came)
+    part = combine([part] + [shift(part, "blk", n_blk, s) for s in range(1, n_blk)], (done_sides,))
+    pieces = [part] + [exchange(part, "rows", n_rows, s) for s in range(1, n_rows)]
     deltas = call(
         functools.partial(deltas_kernel, n_rows),
         "deltas",
         [shape(x.shape, f32) for x in (left_weight, right_weight, gate_weight, output_weight)],
-        after=1,
-    )(*pieces, grad_left)
+    )(*pieces)
     return (
         update,
         grad_left,

time: 87.7 us -> 87.6 us (level)
  local copies, waits for them, and re-layouts: 5.61 us -> 0.04 us
  waiting for transfers between devices: 9.13 us -> 13.3 us
  starting transfers between devices: 31 us -> 32.8 us
    unnamed x24 -> x16, local copies, waits for them, and re-layouts: 5.61 us -> 0.04 us
    ppermute x10, waiting for transfers between devices: 2.09 us -> 7.55 us  [exchange(): return lax.ppermute(x, axis, [(a, a ^ bit) for a in range(n)])]
    ppermute x9, waiting for transfers between devices: 7.04 us -> 5.71 us  [shift(): return lax.ppermute(x, axis, [(a, (a + step) % n) for a in range(n)])]
    ppermute x9, starting transfers between devices: 18.2 us -> 19.3 us  [shift(): return lax.ppermute(x, axis, [(a, (a + step) % n) for a in range(n)])]
    pallas_call x19 -> x20, Pallas kernels: 40.7 us -> 40.5 us  [run(): pl.pallas_call(kernel, in_specs=[pl.BlockSpec(memory_space=space) for spa...]
  transfers between devices with their start and end apart: 19 -> 19, of which waited for: 3 -> 8; matrix products, arithmetic and copies ran while one was open for 0% -> 0% of each run, Pallas kernels for 36% -> 36%
where the time goes in v7:
time: 87.6 us; the launch traced here: 87.5 us
  Pallas kernels  40.5 us (46%)
  starting transfers between devices  32.8 us (37%)
  waiting for transfers between devices  13.3 us (15%)
    pallas_call x20, Pallas kernels, run(): pl.pallas_call(kernel, in_specs=[pl.BlockSpec(memory_space=space) for spa...  40.5 us
    ppermute x9, starting transfers between devices, shift(): return lax.ppermute(x, axis, [(a, (a + step) % n) for a in range(n)])  19.3 us
    ppermute x10, starting transfers between devices, exchange(): return lax.ppermute(x, axis, [(a, a ^ bit) for a in range(n)])  13.4 us
    ppermute x10, waiting for transfers between devices, exchange(): return lax.ppermute(x, axis, [(a, a ^ bit) for a in range(n)])  7.55 us
    ppermute x9, waiting for transfers between devices, shift(): return lax.ppermute(x, axis, [(a, (a + step) % n) for a in range(n)])  5.71 us
  transfers between devices with their start and end apart: 19, of which 8 were waited for; matrix products, arithmetic and copies ran while one was open for 0% of the time, Pallas kernels for 36%

profile of v7, /device:TPU:0, one launch (start us, length us, event | category | flops | bytes accessed | tf_op | source)
XLA Modules:
  0.0 87.5 jit_solution(3296234004694687277)
XLA Ops:
  0.7 4.0 %collective-permute-start.3 = (bf16[32,16,128]{2,1,0:T(8,128)(2,1)}, bf16[32,16,128]{2,1,0:T(8,128)(2,1)S(1)}, u32[]{:S(2)}, u32[]{:S(2)}) collective-permute-start(bf16[32,16,128]{2,1,0:T(8,128)(2,1)} %refs_1_.1), channel_id=1, source_target_pairs={{0,24},{8,16},{16,8},{24,0},{1,25},{9,17},{17,9},{25,1},{2,26},{10... | collective-permute-start | bytes 393224 | tf_op jit(solution)/shard_map/ppermute | solution.py:358
  4.6 0.5 collective-permute-start.2
  5.1 0.1 collective-permute-start.1
  5.3 2.0 %collective-permute-start.5 = (bf16[64,16,128]{2,1,0:T(8,128)(2,1)}, bf16[64,16,128]{2,1,0:T(8,128)(2,1)S(1)}, u32[]{:S(2)}, u32[]{:S(2)}) collective-permute-start(bf16[64,16,128]{2,1,0:T(8,128)(2,1)} %refs_0_.3), channel_id=1, source_target_pairs={{0,2},{2,4},{4,6},{6,0},{1,3},{3,5},{5,7},{7,1},{8,10},{10,12},{12... | collective-permute-start | bytes 786440 | tf_op jit(solution)/shard_map/ppermute | solution.py:354
  7.3 2.6 %collective-permute-start.4 = (bf16[64,16,128]{2,1,0:T(8,128)(2,1)}, bf16[64,16,128]{2,1,0:T(8,128)(2,1)S(1)}, u32[]{:S(2)}, u32[]{:S(2)}) collective-permute-start(bf16[64,16,128]{2,1,0:T(8,128)(2,1)} %refs_0_.3), channel_id=1, source_target_pairs={{0,4},{2,6},{4,0},{6,2},{1,5},{3,7},{5,1},{7,3},{8,12},{10,14},{12... | collective-permute-start | bytes 786440 | tf_op jit(solution)/shard_map/ppermute | solution.py:354
  9.8 2.6 %collective-permute-start = (bf16[64,16,128]{2,1,0:T(8,128)(2,1)}, bf16[64,16,128]{2,1,0:T(8,128)(2,1)S(1)}, u32[]{:S(2)}, u32[]{:S(2)}) collective-permute-start(bf16[64,16,128]{2,1,0:T(8,128)(2,1)} %refs_0_.3), channel_id=1, source_target_pairs={{0,6},{2,0},{4,2},{6,4},{1,7},{3,1},{5,3},{7,5},{8,14},{10,8},{12,... | collective-permute-start | bytes 786440 | tf_op jit(solution)/shard_map/ppermute | solution.py:354
  12.5 0.0 copy-start.4
  12.5 0.0 copy-start.5
  12.5 2.4 %middle.3 = (f32[64,32,128]{2,1,0:T(8,128)S(1)}, bf16[64,32,128]{2,1,0:T(8,128)(2,1)S(1)}, bf16[64,32,128]{2,1,0:T(8,128)(2,1)S(1)}, f32[64,32,128]{2,1,0:T(8,128)S(1)}) custom-call(bf16[64,32,128]{2,1,0:T(8,128)(2,1)S(1)} %copy-done.1, bf16[64,32,128]{2,1,0:T(8,128)(2,1)S(1)} %copy-done.2, bf16[128,128]{1,0:T(8,128)(2,1)S(1)} %copy-done.7, ...), custom_call_target="tpu_custom_call" | custom-call | flops 1000 | bytes 1000 | tf_op jit(solution)/shard_map/middle/pallas_call | solution.py:432
  14.9 0.0 copy-start
  14.9 0.0 copy-start.3
  14.9 0.0 collective-permute-done.2.refs_2_
  15.0 3.3 %right.1 = (f32[2048,128]{1,0:T(8,128)S(1)}, bf16[4,32,16,128]{3,2,1,0:T(8,128)(2,1)S(1)}, f32[16,32,128]{2,1,0:T(8,128)S(1)}, f32[16,32,128]{2,1,0:T(8,128)S(1)...) custom-call(bf16[32,16,128]{2,1,0:T(8,128)(2,1)S(1)} %copy-done.5, ...), custom_call_target="tpu_custom_call" | custom-call | flops 1000 | bytes 1000 | tf_op jit(solution)/shard_map/right/pallas_call | solution.py:432
  18.3 2.6 %left.3 = (f32[64,16,128]{2,1,0:T(8,128)S(1)}, bf16[64,16,128]{2,1,0:T(8,128)(2,1)S(1)}, f32[64,32,128]{2,1,0:T(8,128)S(1)}) custom-call(bf16[64,16,128]{2,1,0:T(8,128)(2,1)S(1)} %copy-done.3, bf16[128,256]{1,0:T(8,128)(2,1)S(1)} %copy-done, f32[16,32,128]{2,1,0:T(8,128)S(1)} %get-tuple-element.60.flip), custom_call_target="tpu_custom_call" | custom-call | flops 1000 | bytes 1000 | tf_op jit(solution)/shard_map/left/pallas_call | solution.py:432
  20.9 0.0 collective-permute-done.5.raw
  20.9 2.6 %left.4 = (f32[64,16,128]{2,1,0:T(8,128)S(1)}, bf16[64,16,128]{2,1,0:T(8,128)(2,1)S(1)}, f32[64,32,128]{2,1,0:T(8,128)S(1)}) custom-call(bf16[64,16,128]{2,1,0:T(8,128)(2,1)S(1)} %collective-permute-done.5.raw, bf16[128,256]{1,0:T(8,128)(2,1)S(1)} %copy-done, f32[16,32,128]{2,1,0:T(8,128)S(1)} %get-tuple-element.59.flip, ...), custom_call_target="tpu_custom_call" | custom-call | flops 1000 | bytes 1000 | tf_op jit(solution)/shard_map/left/pallas_call | solution.py:432
  23.5 2.8 %collective-permute-done.4.raw = bf16[64,16,128]{2,1,0:T(8,128)(2,1)S(1)} collective-permute-done((bf16[64,16,128]{2,1,0:T(8,128)(2,1)}, bf16[64,16,128]{2,1,0:T(8,128)(2,1)S(1)}, u32[]{:S(2)}, u32[]{:S(2)}) %collective-permute-start.4) | collective-permute-done | bytes 262176 | tf_op jit(solution)/shard_map/ppermute | solution.py:354
  26.3 2.7 %left.5 = (f32[64,16,128]{2,1,0:T(8,128)S(1)}, bf16[64,16,128]{2,1,0:T(8,128)(2,1)S(1)}, f32[64,32,128]{2,1,0:T(8,128)S(1)}) custom-call(bf16[64,16,128]{2,1,0:T(8,128)(2,1)S(1)} %collective-permute-done.4.raw, bf16[128,256]{1,0:T(8,128)(2,1)S(1)} %copy-done, f32[16,32,128]{2,1,0:T(8,128)S(1)} %get-tuple-element.58.flip, ...), custom_call_target="tpu_custom_call" | custom-call | flops 1000 | bytes 1000 | tf_op jit(solution)/shard_map/left/pallas_call | solution.py:432
  29.0 0.0 collective-permute-done.raw
  29.0 3.5 %triangle.1 = (f32[64,16,128]{2,1,0:T(8,128)S(1)}, bf16[64,16,128]{2,1,0:T(8,128)(2,1)S(1)}, bf16[64,32,128]{2,1,0:T(8,128)(2,1)S(1)}, f32[64,32,128]{2,1,0:T(8,128)S(1)}) custom-call(bf16[64,16,128]{2,1,0:T(8,128)(2,1)S(1)} %collective-permute-done.raw, bf16[128,256]{1,0:T(8,128)(2,1)S(1)} %copy-done, f32[16,32,128]{2,1,0:T(8,128)S(1)} %get-tuple-element.56.flip, ...), custom_call_target="tpu_custom_call" | custom-call | flops 1000 | bytes 1000 | tf_op jit(solution)/shard_map/triangle/pallas_call | solution.py:432
  32.5 4.7 %left_back.1 = (bf16[64,16,128]{2,1,0:T(8,128)(2,1)S(1)}, bf16[64,16,128]{2,1,0:T(8,128)(2,1)S(1)}, bf16[64,16,128]{2,1,0:T(8,128)(2,1)S(1)}, bf16[64,16,128]{2,1,0:T(8,128)(2,1)S(1)}) custom-call(f32[64,32,128]{2,1,0:T(8,128)S(1)} %get-tuple-element.68.tri_back, f32[2048,128]{1,0:T(8,128)S(1)} %get-tuple-element.69.right_act), custom_call_target="tpu_custom_call" | custom-call | flops 1000 | bytes 1000 | tf_op jit(solution)/shard_map/left_back/pallas_call | solution.py:432
  37.2 7.2 %collective-permute-start.6 = (bf16[64,16,128]{2,1,0:T(8,128)(2,1)S(1)}, bf16[64,16,128]{2,1,0:T(8,128)(2,1)S(1)}, u32[]{:S(2)}, u32[]{:S(2)}) collective-permute-start(bf16[64,16,128]{2,1,0:T(8,128)(2,1)S(1)} %get-tuple-element.72.refs_5_), channel_id=1, source_target_pairs={{0,6},{2,0},{4,2},{6,4},{1,7},{3,1},{5,3},{7,5},{8,14},{10,8},{12,... | collective-permute-start | bytes 786440 | tf_op jit(solution)/shard_map/ppermute | solution.py:354
  44.4 0.0 collective-permute-start.7
  44.4 0.6 collective-permute-start.8
  45.0 2.7 %heads.1 = (bf16[64,32,128]{2,1,0:T(8,128)(2,1)}, bf16[64,32,128]{2,1,0:T(8,128)(2,1)S(1)}, f32[128,128]{1,0:T(8,128)S(1)}, f32[128,128]{1,0:T(8,128)S(1)}) custom-call(bf16[64,32,128]{2,1,0:T(8,128)(2,1)S(1)} %get-tuple-element.64.tri_in, bf16[128,128]{1,0:T(8,128)(2,1)S(1)} %copy-done.6, f32[64,32,128]{2,1,0:T(8,128)S(1)} %get-tuple-element.65.gate, ...), custom_call_target="tpu_custom_call" | custom-call | flops 1000 | bytes 1000 | tf_op jit(solution)/shard_map/heads/pallas_call | solution.py:432
  47.7 2.4 %grad_middle.1 = (bf16[64,32,128]{2,1,0:T(8,128)(2,1)}, f32[8,128]{1,0:T(8,128)S(1)}) custom-call(bf16[64,32,128]{2,1,0:T(8,128)(2,1)S(1)} %copy-done.1, bf16[64,32,128]{2,1,0:T(8,128)(2,1)S(1)} %get-tuple-element.85.pre_back, bf16[128,128]{1,0:T(8,128)(2,1)S(1)} %copy-done.7), custom_call_target="tpu_custom_call" | custom-call | flops 1000 | bytes 1000 | tf_op jit(solution)/shard_map/grad_middle/pallas_call | solution.py:432
  50.2 5.5 %right_back.1 = (bf16[2,32,16,128]{3,2,1,0:T(8,128)(2,1)S(1)}, bf16[2,32,16,128]{3,2,1,0:T(8,128)(2,1)S(1)}) custom-call(f32[64,32,128]{2,1,0:T(8,128)S(1)} %get-tuple-element.68.tri_back, f32[64,16,128]{2,1,0:T(8,128)S(1)} %get-tuple-element.75.refs_0_, f32[64,16,128]{2,1,0:T(8,128)S(1)} %get-tuple-element.76.refs_1_, ...), custom_call_target="tpu_custom_call" | custom-call | flops 1000 | bytes 1000 | tf_op jit(solution)/shard_map/right_back/pallas_call | solution.py:432
  55.7 4.3 %weights.1 = (f32[2,32,768]{2,1,0:T(8,128)S(1)}, bf16[2,32,768]{2,1,0:T(8,128)(2,1)S(1)}) custom-call(bf16[4,32,16,128]{3,2,1,0:T(8,128)(2,1)S(1)} %get-tuple-element.87.right_in, bf16[128,256]{1,0:T(8,128)(2,1)S(1)} %copy-done, bf16[128,256]{1,0:T(8,128)(2,1)S(1)} %copy-done.4, f32[128,128]{1,0:T(8,128)S(1)} %get-tuple-element.88.gate_part, ...), custom_call_target="tpu_custom_call" | custom-call | flops 1000 | bytes 1000 | tf_op jit(solution)/shard_map/weights/pallas_call | solution.py:432
  60.0 1.6 %collective-permute-start.11 = (bf16[2,32,768]{2,1,0:T(8,128)(2,1)S(1)}, bf16[2,32,768]{2,1,0:T(8,128)(2,1)S(1)}, u32[]{:S(2)}, u32[]{:S(2)}) collective-permute-start(bf16[2,32,768]{2,1,0:T(8,128)(2,1)S(1)} %get-tuple-element.96), channel_id=1, source_target_pairs={{0,8},{8,0},{16,24},{24,16},{1,9},{9,1},{17,25},{25,17},{2,10},{10... | collective-permute-start | bytes 294920 | tf_op jit(solution)/shard_map/ppermute | solution.py:358
  61.6 0.5 collective-permute-start.9
  62.1 3.1 %collective-permute-done.11.came = bf16[2,32,768]{2,1,0:T(8,128)(2,1)S(1)} collective-permute-done((bf16[2,32,768]{2,1,0:T(8,128)(2,1)S(1)}, bf16[2,32,768]{2,1,0:T(8,128)(2,1)S(1)}, u32[]{:S(2)}, u32[]{:S(2)}) %collective-permute-start.11) | collective-permute-done | bytes 98336 | tf_op jit(solution)/shard_map/ppermute | solution.py:358
  65.3 1.6 %collective-permute-start.12 = (bf16[1,32,768]{2,1,0:T(8,128)(2,1)S(1)}, bf16[1,32,768]{2,1,0:T(8,128)(2,1)S(1)}, u32[]{:S(2)}, u32[]{:S(2)}) collective-permute-start(bf16[1,32,768]{2,1,0:T(8,128)(2,1)S(1)} %get-tuple-element.98), channel_id=1, source_target_pairs={{0,16},{8,24},{16,0},{24,8},{1,17},{9,25},{17,1},{25,9},{2,18},{10... | collective-permute-start | bytes 147464 | tf_op jit(solution)/shard_map/ppermute | solution.py:358
  66.9 1.2 %collective-permute-done.9.came = bf16[2,32,16,128]{3,2,1,0:T(8,128)(2,1)S(1)} collective-permute-done((bf16[2,32,16,128]{3,2,1,0:T(8,128)(2,1)S(1)}, bf16[2,32,16,128]{3,2,1,0:T(8,128)(2,1)S(1)}, u32[]{:S(2)}, u32[]{:S(2)}) %collective-permute-start.9) | collective-permute-done | bytes 262176 | tf_op jit(solution)/shard_map/ppermute | solution.py:358
  68.1 0.1 halve.2
  68.2 1.6 %collective-permute-start.10 = (bf16[1,32,16,128]{3,2,1,0:T(8,128)(2,1)S(1)}, bf16[1,32,16,128]{3,2,1,0:T(8,128)(2,1)S(1)}, u32[]{:S(2)}, u32[]{:S(2)}) collective-permute-start(bf16[1,32,16,128]{3,2,1,0:T(8,128)(2,1)S(1)} %get-tuple-element.82.refs_0_), channel_id=1, source_target_pairs={{0,16},{8,24},{16,0},{24,8},{1,17},{9,25},{17,1},{25,9},{2,18},{10... | collective-permute-start | bytes 393224 | tf_op jit(solution)/shard_map/ppermute | solution.py:358
  69.8 3.2 %collective-permute-start.15 = (bf16[1,32,768]{2,1,0:T(8,128)(2,1)S(1)}, bf16[1,32,768]{2,1,0:T(8,128)(2,1)S(1)}, u32[]{:S(2)}, u32[]{:S(2)}) collective-permute-start(bf16[1,32,768]{2,1,0:T(8,128)(2,1)S(1)} %combine.2.refs_0_), channel_id=1, source_target_pairs={{0,6},{2,0},{4,2},{6,4},{1,7},{3,1},{5,3},{7,5},{8,14},{10,8},{12,... | collective-permute-start | bytes 147464 | tf_op jit(solution)/shard_map/ppermute | solution.py:354
  73.0 1.0 %collective-permute-start.14 = (bf16[1,32,768]{2,1,0:T(8,128)(2,1)S(1)}, bf16[1,32,768]{2,1,0:T(8,128)(2,1)S(1)}, u32[]{:S(2)}, u32[]{:S(2)}) collective-permute-start(bf16[1,32,768]{2,1,0:T(8,128)(2,1)S(1)} %combine.2.refs_0_), channel_id=1, source_target_pairs={{0,4},{2,6},{4,0},{6,2},{1,5},{3,7},{5,1},{7,3},{8,12},{10,14},{12... | collective-permute-start | bytes 147464 | tf_op jit(solution)/shard_map/ppermute | solution.py:354
  74.0 0.1 collective-permute-start.13
  74.1 2.9 %sides.1 = (bf16[64,16,128]{2,1,0:T(8,128)(2,1)}, bf16[32,16,128]{2,1,0:T(8,128)(2,1)}, f32[8,128]{1,0:T(8,128)S(1)}) custom-call(bf16[64,16,128]{2,1,0:T(8,128)(2,1)S(1)} %copy-done.3, bf16[32,16,128]{2,1,0:T(8,128)(2,1)S(1)} %copy-done.5, bf16[128,256]{1,0:T(8,128)(2,1)S(1)} %copy-done, bf16[128,256]{1,0:T(8,128)(2,1)S(1)} %copy-done.4, ...), custom_call_target="tpu_custom_call" | custom-call | flops 1000 | bytes 1000 | tf_op jit(solution)/shard_map/sides/pallas_call | solution.py:432
  77.0 1.0 %collective-permute-done.14.refs_2_ = bf16[1,32,768]{2,1,0:T(8,128)(2,1)S(1)} collective-permute-done((bf16[1,32,768]{2,1,0:T(8,128)(2,1)S(1)}, bf16[1,32,768]{2,1,0:T(8,128)(2,1)S(1)}, u32[]{:S(2)}, u32[]{:S(2)}) %collective-permute-start.14) | collective-permute-done | bytes 49184 | tf_op jit(solution)/shard_map/ppermute | solution.py:354
  78.0 1.9 %collective-permute-done.13.refs_1_ = bf16[1,32,768]{2,1,0:T(8,128)(2,1)S(1)} collective-permute-done((bf16[1,32,768]{2,1,0:T(8,128)(2,1)S(1)}, bf16[1,32,768]{2,1,0:T(8,128)(2,1)S(1)}, u32[]{:S(2)}, u32[]{:S(2)}) %collective-permute-start.13) | collective-permute-done | bytes 49184 | tf_op jit(solution)/shard_map/ppermute | solution.py:354
  79.9 1.9 %collective-permute-start.18 = (bf16[1,32,768]{2,1,0:T(8,128)(2,1)S(1)}, bf16[1,32,768]{2,1,0:T(8,128)(2,1)S(1)}, u32[]{:S(2)}, u32[]{:S(2)}) collective-permute-start(bf16[1,32,768]{2,1,0:T(8,128)(2,1)S(1)} %combine.3.refs_0_), channel_id=1, source_target_pairs={{0,24},{8,16},{16,8},{24,0},{1,25},{9,17},{17,9},{25,1},{2,26},{10... | collective-permute-start | bytes 147464 | tf_op jit(solution)/shard_map/ppermute | solution.py:358
  81.8 0.8 collective-permute-start.17
  82.6 0.9 collective-permute-start.16
  83.5 1.5 %collective-permute-done.18.refs_3_ = bf16[1,32,768]{2,1,0:T(8,128)(2,1)S(1)} collective-permute-done((bf16[1,32,768]{2,1,0:T(8,128)(2,1)S(1)}, bf16[1,32,768]{2,1,0:T(8,128)(2,1)S(1)}, u32[]{:S(2)}, u32[]{:S(2)}) %collective-permute-start.18) | collective-permute-done | bytes 49184 | tf_op jit(solution)/shard_map/ppermute | solution.py:358
  85.0 0.9 %collective-permute-done.17.refs_2_ = bf16[1,32,768]{2,1,0:T(8,128)(2,1)S(1)} collective-permute-done((bf16[1,32,768]{2,1,0:T(8,128)(2,1)S(1)}, bf16[1,32,768]{2,1,0:T(8,128)(2,1)S(1)}, u32[]{:S(2)}, u32[]{:S(2)}) %collective-permute-start.17) | collective-permute-done | bytes 49184 | tf_op jit(solution)/shard_map/ppermute | solution.py:358
  85.9 0.8 collective-permute-done.16.refs_1_
  86.7 0.8 deltas.1
  (26 shorter events, 0.1 us)
Async XLA Ops:
  0.6 11.8 %copy-start.6 = (bf16[128,128]{1,0:T(8,128)(2,1)S(1)}, bf16[128,128]{1,0:T(8,128)(2,1)}, u32[]{:S(2)}) copy-start(bf16[128,128]{1,0:T(8,128)(2,1)} %out_w.1) | copy-start | bytes 98308
  0.6 11.8 %copy-start.7 = (bf16[128,128]{1,0:T(8,128)(2,1)S(1)}, bf16[128,128]{1,0:T(8,128)(2,1)}, u32[]{:S(2)}) copy-start(bf16[128,128]{1,0:T(8,128)(2,1)} %gate_weight.3) | copy-start | bytes 98308
  0.7 11.8 %copy-start.2 = (bf16[64,32,128]{2,1,0:T(8,128)(2,1)S(1)}, bf16[64,32,128]{2,1,0:T(8,128)(2,1)}, u32[]{:S(2)}) copy-start(bf16[64,32,128]{2,1,0:T(8,128)(2,1)} %cotangent.3) | copy-start | bytes 1572868
  0.7 11.8 %copy-start.1 = (bf16[64,32,128]{2,1,0:T(8,128)(2,1)S(1)}, bf16[64,32,128]{2,1,0:T(8,128)(2,1)}, u32[]{:S(2)}) copy-start(bf16[64,32,128]{2,1,0:T(8,128)(2,1)} %middle.5) | copy-start | bytes 1572868
  0.7 9.2 %collective-permute-start.3 = (bf16[32,16,128]{2,1,0:T(8,128)(2,1)}, bf16[32,16,128]{2,1,0:T(8,128)(2,1)S(1)}, u32[]{:S(2)}, u32[]{:S(2)}) collective-permute-start(bf16[32,16,128]{2,1,0:T(8,128)(2,1)} %refs_1_.1), channel_id=1, source_target_pairs={{0,24},{8,16},{16,8},{24,0},{1,25},{9,17},{17,9},{25,1},{2,26},{10... | collective-permute-start | bytes 393224 | tf_op jit(solution)/shard_map/ppermute | solution.py:358
  4.6 10.3 %collective-permute-start.2 = (bf16[32,16,128]{2,1,0:T(8,128)(2,1)}, bf16[32,16,128]{2,1,0:T(8,128)(2,1)S(1)}, u32[]{:S(2)}, u32[]{:S(2)}) collective-permute-start(bf16[32,16,128]{2,1,0:T(8,128)(2,1)} %refs_1_.1), channel_id=1, source_target_pairs={{0,16},{8,24},{16,0},{24,8},{1,17},{9,25},{17,1},{25,9},{2,18},{10... | collective-permute-start | bytes 393224 | tf_op jit(solution)/shard_map/ppermute | solution.py:358
  5.1 9.8 %collective-permute-start.1 = (bf16[32,16,128]{2,1,0:T(8,128)(2,1)}, bf16[32,16,128]{2,1,0:T(8,128)(2,1)S(1)}, u32[]{:S(2)}, u32[]{:S(2)}) collective-permute-start(bf16[32,16,128]{2,1,0:T(8,128)(2,1)} %refs_1_.1), channel_id=1, source_target_pairs={{0,8},{8,0},{16,24},{24,16},{1,9},{9,1},{17,25},{25,17},{2,10},{10... | collective-permute-start | bytes 393224 | tf_op jit(solution)/shard_map/ppermute | solution.py:358
  5.3 15.6 %collective-permute-start.5 = (bf16[64,16,128]{2,1,0:T(8,128)(2,1)}, bf16[64,16,128]{2,1,0:T(8,128)(2,1)S(1)}, u32[]{:S(2)}, u32[]{:S(2)}) collective-permute-start(bf16[64,16,128]{2,1,0:T(8,128)(2,1)} %refs_0_.3), channel_id=1, source_target_pairs={{0,2},{2,4},{4,6},{6,0},{1,3},{3,5},{5,7},{7,1},{8,10},{10,12},{12... | collective-permute-start | bytes 786440 | tf_op jit(solution)/shard_map/ppermute | solution.py:354
  7.3 19.1 %collective-permute-start.4 = (bf16[64,16,128]{2,1,0:T(8,128)(2,1)}, bf16[64,16,128]{2,1,0:T(8,128)(2,1)S(1)}, u32[]{:S(2)}, u32[]{:S(2)}) collective-permute-start(bf16[64,16,128]{2,1,0:T(8,128)(2,1)} %refs_0_.3), channel_id=1, source_target_pairs={{0,4},{2,6},{4,0},{6,2},{1,5},{3,7},{5,1},{7,3},{8,12},{10,14},{12... | collective-permute-start | bytes 786440 | tf_op jit(solution)/shard_map/ppermute | solution.py:354
  9.8 19.1 %collective-permute-start = (bf16[64,16,128]{2,1,0:T(8,128)(2,1)}, bf16[64,16,128]{2,1,0:T(8,128)(2,1)S(1)}, u32[]{:S(2)}, u32[]{:S(2)}) collective-permute-start(bf16[64,16,128]{2,1,0:T(8,128)(2,1)} %refs_0_.3), channel_id=1, source_target_pairs={{0,6},{2,0},{4,2},{6,4},{1,7},{3,1},{5,3},{7,5},{8,14},{10,8},{12,... | collective-permute-start | bytes 786440 | tf_op jit(solution)/shard_map/ppermute | solution.py:354
  12.5 2.5 %copy-start.4 = (bf16[128,256]{1,0:T(8,128)(2,1)S(1)}, bf16[128,256]{1,0:T(8,128)(2,1)}, u32[]{:S(2)}) copy-start(bf16[128,256]{1,0:T(8,128)(2,1)} %right_w.1) | copy-start | bytes 196612
  12.5 2.5 %copy-start.5 = (bf16[32,16,128]{2,1,0:T(8,128)(2,1)S(1)}, bf16[32,16,128]{2,1,0:T(8,128)(2,1)}, u32[]{:S(2)}) copy-start(bf16[32,16,128]{2,1,0:T(8,128)(2,1)} %refs_1_.1) | copy-start | bytes 393220
  14.9 3.4 %copy-start = (bf16[128,256]{1,0:T(8,128)(2,1)S(1)}, bf16[128,256]{1,0:T(8,128)(2,1)}, u32[]{:S(2)}) copy-start(bf16[128,256]{1,0:T(8,128)(2,1)} %left_w.3) | copy-start | bytes 196612
  14.9 3.4 %copy-start.3 = (bf16[64,16,128]{2,1,0:T(8,128)(2,1)S(1)}, bf16[64,16,128]{2,1,0:T(8,128)(2,1)}, u32[]{:S(2)}) copy-start(bf16[64,16,128]{2,1,0:T(8,128)(2,1)} %refs_0_.3) | copy-start | bytes 786436
  37.2 29.7 %collective-permute-start.6 = (bf16[64,16,128]{2,1,0:T(8,128)(2,1)S(1)}, bf16[64,16,128]{2,1,0:T(8,128)(2,1)S(1)}, u32[]{:S(2)}, u32[]{:S(2)}) collective-permute-start(bf16[64,16,128]{2,1,0:T(8,128)(2,1)S(1)} %get-tuple-element.72.refs_5_), channel_id=1, source_target_pairs={{0,6},{2,0},{4,2},{6,4},{1,7},{3,1},{5,3},{7,5},{8,14},{10,8},{12,... | collective-permute-start | bytes 786440 | tf_op jit(solution)/shard_map/ppermute | solution.py:354
  44.4 22.5 %collective-permute-start.7 = (bf16[64,16,128]{2,1,0:T(8,128)(2,1)S(1)}, bf16[64,16,128]{2,1,0:T(8,128)(2,1)S(1)}, u32[]{:S(2)}, u32[]{:S(2)}) collective-permute-start(bf16[64,16,128]{2,1,0:T(8,128)(2,1)S(1)} %get-tuple-element.73.refs_6_), channel_id=1, source_target_pairs={{0,4},{2,6},{4,0},{6,2},{1,5},{3,7},{5,1},{7,3},{8,12},{10,14},{12... | collective-permute-start | bytes 786440 | tf_op jit(solution)/shard_map/ppermute | solution.py:354
  44.4 22.5 %collective-permute-start.8 = (bf16[64,16,128]{2,1,0:T(8,128)(2,1)S(1)}, bf16[64,16,128]{2,1,0:T(8,128)(2,1)S(1)}, u32[]{:S(2)}, u32[]{:S(2)}) collective-permute-start(bf16[64,16,128]{2,1,0:T(8,128)(2,1)S(1)} %get-tuple-element.74.refs_7_), channel_id=1, source_target_pairs={{0,2},{2,4},{4,6},{6,0},{1,3},{3,5},{5,7},{7,1},{8,10},{10,12},{12... | collective-permute-start | bytes 786440 | tf_op jit(solution)/shard_map/ppermute | solution.py:354
  60.0 5.2 %collective-permute-start.11 = (bf16[2,32,768]{2,1,0:T(8,128)(2,1)S(1)}, bf16[2,32,768]{2,1,0:T(8,128)(2,1)S(1)}, u32[]{:S(2)}, u32[]{:S(2)}) collective-permute-start(bf16[2,32,768]{2,1,0:T(8,128)(2,1)S(1)} %get-tuple-element.96), channel_id=1, source_target_pairs={{0,8},{8,0},{16,24},{24,16},{1,9},{9,1},{17,25},{25,17},{2,10},{10... | collective-permute-start | bytes 294920 | tf_op jit(solution)/shard_map/ppermute | solution.py:358
  61.6 6.5 %collective-permute-start.9 = (bf16[2,32,16,128]{3,2,1,0:T(8,128)(2,1)S(1)}, bf16[2,32,16,128]{3,2,1,0:T(8,128)(2,1)S(1)}, u32[]{:S(2)}, u32[]{:S(2)}) collective-permute-start(bf16[2,32,16,128]{3,2,1,0:T(8,128)(2,1)S(1)} %get-tuple-element.80.refs_9_), channel_id=1, source_target_pairs={{0,8},{8,0},{16,24},{24,16},{1,9},{9,1},{17,25},{25,17},{2,10},{10... | collective-permute-start | bytes 786440 | tf_op jit(solution)/shard_map/ppermute | solution.py:358
  65.3 4.4 %collective-permute-start.12 = (bf16[1,32,768]{2,1,0:T(8,128)(2,1)S(1)}, bf16[1,32,768]{2,1,0:T(8,128)(2,1)S(1)}, u32[]{:S(2)}, u32[]{:S(2)}) collective-permute-start(bf16[1,32,768]{2,1,0:T(8,128)(2,1)S(1)} %get-tuple-element.98), channel_id=1, source_target_pairs={{0,16},{8,24},{16,0},{24,8},{1,17},{9,25},{17,1},{25,9},{2,18},{10... | collective-permute-start | bytes 147464 | tf_op jit(solution)/shard_map/ppermute | solution.py:358
  68.2 6.0 %collective-permute-start.10 = (bf16[1,32,16,128]{3,2,1,0:T(8,128)(2,1)S(1)}, bf16[1,32,16,128]{3,2,1,0:T(8,128)(2,1)S(1)}, u32[]{:S(2)}, u32[]{:S(2)}) collective-permute-start(bf16[1,32,16,128]{3,2,1,0:T(8,128)(2,1)S(1)} %get-tuple-element.82.refs_0_), channel_id=1, source_target_pairs={{0,16},{8,24},{16,0},{24,8},{1,17},{9,25},{17,1},{25,9},{2,18},{10... | collective-permute-start | bytes 393224 | tf_op jit(solution)/shard_map/ppermute | solution.py:358
  69.8 7.3 %collective-permute-start.15 = (bf16[1,32,768]{2,1,0:T(8,128)(2,1)S(1)}, bf16[1,32,768]{2,1,0:T(8,128)(2,1)S(1)}, u32[]{:S(2)}, u32[]{:S(2)}) collective-permute-start(bf16[1,32,768]{2,1,0:T(8,128)(2,1)S(1)} %combine.2.refs_0_), channel_id=1, source_target_pairs={{0,6},{2,0},{4,2},{6,4},{1,7},{3,1},{5,3},{7,5},{8,14},{10,8},{12,... | collective-permute-start | bytes 147464 | tf_op jit(solution)/shard_map/ppermute | solution.py:354
  73.0 5.0 %collective-permute-start.14 = (bf16[1,32,768]{2,1,0:T(8,128)(2,1)S(1)}, bf16[1,32,768]{2,1,0:T(8,128)(2,1)S(1)}, u32[]{:S(2)}, u32[]{:S(2)}) collective-permute-start(bf16[1,32,768]{2,1,0:T(8,128)(2,1)S(1)} %combine.2.refs_0_), channel_id=1, source_target_pairs={{0,4},{2,6},{4,0},{6,2},{1,5},{3,7},{5,1},{7,3},{8,12},{10,14},{12... | collective-permute-start | bytes 147464 | tf_op jit(solution)/shard_map/ppermute | solution.py:354
  74.0 5.9 %collective-permute-start.13 = (bf16[1,32,768]{2,1,0:T(8,128)(2,1)S(1)}, bf16[1,32,768]{2,1,0:T(8,128)(2,1)S(1)}, u32[]{:S(2)}, u32[]{:S(2)}) collective-permute-start(bf16[1,32,768]{2,1,0:T(8,128)(2,1)S(1)} %combine.2.refs_0_), channel_id=1, source_target_pairs={{0,2},{2,4},{4,6},{6,0},{1,3},{3,5},{5,7},{7,1},{8,10},{10,12},{12... | collective-permute-start | bytes 147464 | tf_op jit(solution)/shard_map/ppermute | solution.py:354
  79.9 5.1 %collective-permute-start.18 = (bf16[1,32,768]{2,1,0:T(8,128)(2,1)S(1)}, bf16[1,32,768]{2,1,0:T(8,128)(2,1)S(1)}, u32[]{:S(2)}, u32[]{:S(2)}) collective-permute-start(bf16[1,32,768]{2,1,0:T(8,128)(2,1)S(1)} %combine.3.refs_0_), channel_id=1, source_target_pairs={{0,24},{8,16},{16,8},{24,0},{1,25},{9,17},{17,9},{25,1},{2,26},{10... | collective-permute-start | bytes 147464 | tf_op jit(solution)/shard_map/ppermute | solution.py:358
  81.8 4.1 %collective-permute-start.17 = (bf16[1,32,768]{2,1,0:T(8,128)(2,1)S(1)}, bf16[1,32,768]{2,1,0:T(8,128)(2,1)S(1)}, u32[]{:S(2)}, u32[]{:S(2)}) collective-permute-start(bf16[1,32,768]{2,1,0:T(8,128)(2,1)S(1)} %combine.3.refs_0_), channel_id=1, source_target_pairs={{0,16},{8,24},{16,0},{24,8},{1,17},{9,25},{17,1},{25,9},{2,18},{10... | collective-permute-start | bytes 147464 | tf_op jit(solution)/shard_map/ppermute | solution.py:358
  82.6 4.1 %collective-permute-start.16 = (bf16[1,32,768]{2,1,0:T(8,128)(2,1)S(1)}, bf16[1,32,768]{2,1,0:T(8,128)(2,1)S(1)}, u32[]{:S(2)}, u32[]{:S(2)}) collective-permute-start(bf16[1,32,768]{2,1,0:T(8,128)(2,1)S(1)} %combine.3.refs_0_), channel_id=1, source_target_pairs={{0,8},{8,0},{16,24},{24,16},{1,9},{9,1},{17,25},{25,17},{2,10},{10... | collective-permute-start | bytes 147464 | tf_op jit(solution)/shard_map/ppermute | solution.py:358

commit v8 on v7

--- a/solution.py
+++ b/solution.py
@@ -12,6 +12,7 @@
 f32 = jnp.float32
 bf16 = jnp.bfloat16
 SCOPED = 6 * 1024 * 1024
+LEFT_COST = 2 * 10**8
 MARK = jax.ShapeDtypeStruct((8, 128), jnp.float32)
 
 
@@ -110,17 +111,20 @@
     unit = math.gcd(k_left, k_right)
     vertex = lax.bitwise_xor(lax.axis_index("rows"), piece) * k_right + part * unit
     block = vertex // k_left
-    at = lax.rem(lax.axis_index("blk") - block + n_blk, n_blk) * k_left + vertex - block * k_left
+    at = lax.bitwise_xor(lax.axis_index("blk"), block) * k_left + vertex - block * k_left
     return pl.multiple_of(at, unit)
 
 
-def project_left(raw, weight, act_out, in_out):
-    n_i, k_left, width = raw.shape
+def project_left(raws, weight, act_out, in_out):
+    n_i, k_left, width = raws[0].shape
     step = 8
 
     def body(at, _):
         rows = pl.ds(at * step, step)
-        normed, _ = normalize(raw[rows].astype(f32).reshape(step * k_left, width))
+        raw = raws[0][rows].astype(f32)
+        for other in raws[1:]:
+            raw = raw + other[rows].astype(f32)
+        normed, _ = normalize(raw.reshape(step * k_left, width))
         inputs = normed.astype(bf16)
         in_out[rows] = inputs.reshape(step, k_left, width)
         lin, sw = gated(inputs, weight[...])
@@ -137,7 +141,8 @@
     return total
 
 
-def left_kernel(first, raw, weight, flip, *refs):
+def left_kernel(n_raw, first, *refs):
+    raw, (weight, flip, *refs) = refs[:n_raw], refs[n_raw:]
     total_in, (act_out, in_out, total_out) = refs[: 0 if first else 1], refs[0 if first else 1 :]
     n_i, n_j, width = total_out.shape
     step = 8
@@ -152,7 +157,8 @@
     lax.fori_loop(0, n_i // step, body, 0)
 
 
-def triangle_kernel(has_total, raw, left_w, flip, tri_up, *refs):
+def triangle_kernel(n_raw, has_total, *refs):
+    raw, (left_w, flip, tri_up, *refs) = refs[:n_raw], refs[n_raw:]
     total_in, refs = refs[: 1 if has_total else 0], refs[1 if has_total else 0 :]
     act_out, in_out, tri_in, tri_back = refs
     n_i, n_j, width = tri_in.shape
@@ -207,13 +213,14 @@
     return size
 
 
-def left_back_kernel(tri_back, right_act, *left_out):
+def left_back_kernel(first, n_blk, tri_back, right_act, *left_out):
     n_i, n_j, width = tri_back.shape
     k_left = left_out[0].shape[1]
-    n_k = k_left * len(left_out)
-    few = 4
-    k_step = vertex_step(n_k, k_left)
-    for k0 in range(0, n_k, k_step):
+    n_k = k_left * n_blk
+    last = (first + len(left_out)) * k_left
+    k_step = k_left * math.gcd(len(left_out), max(1, 64 // k_left))
+    few = max(1, 256 // k_step)
+    for k0 in range(first * k_left, last, k_step):
 
         def rows_sum(at, _, k0=k0):
             rows = pl.ds(at * few, few)
@@ -222,8 +229,8 @@
                 start = j * n_k + k0
                 total = total + tri_back[rows, j : j + 1, :] * right_act[start : start + k_step, :][None]
             total = total.astype(bf16)
-            for s in range(k0 // k_left, (k0 + k_step) // k_left):
-                left_out[s][rows] = total[:, s * k_left - k0 : (s + 1) * k_left - k0]
+            for s in range(k_step // k_left):
+                left_out[k0 // k_left - first + s][rows] = total[:, s * k_left : (s + 1) * k_left]
             return 0
 
         lax.fori_loop(0, n_i // few, rows_sum, 0)
@@ -270,7 +277,7 @@
 def weights_kernel(n_rows, n_blk, right_in, left_w, right_w, gate_part, output_part, *refs):
     left_in, refs = refs[:n_blk], refs[n_blk:]
     left_out, refs = refs[:n_blk], refs[n_blk:]
-    keep, send, _, keep_out, send_out, total = refs
+    keep, send, keep_out, send_out, total = refs
     right_out = [(send if s % 2 else keep).at[s // 2] for s in range(n_rows)]
     right_ins = [right_in.at[s] for s in range(n_rows)]
     width = gate_part.shape[0]
@@ -306,7 +313,7 @@
             keep_out[s // 2] = piece
 
 
-def grad_middle_kernel(middle, pre_back, gate_weight, grad_middle, mark):
+def grad_middle_kernel(middle, pre_back, gate_weight, _, grad_middle, mark):
     mark[...] = jnp.zeros_like(mark)
     n_i, n_j, width = middle.shape
     step = 8
@@ -350,10 +357,6 @@
         lax.fori_loop(0, n // step, body, 0, unroll=2)
 
 
-def shift(x, axis, n, step):
-    return lax.ppermute(x, axis, [(a, (a + step) % n) for a in range(n)])
-
-
 def exchange(x, axis, n, bit):
     return lax.ppermute(x, axis, [(a, a ^ bit) for a in range(n)])
 
@@ -381,12 +384,28 @@
     return keep, came, send
 
 
+def forward_kernel(*refs):
+    for source, target in zip(refs[:2], refs[-2:]):
+        target[...] = source[...]
+
+
+def gather_left(block, n, after):
+    if n != 4:
+        return [(block,)] + [(exchange(block, "blk", n, s),) for s in range(1, n)]
+    across = exchange(block, "blk", n, 2)
+    beside = exchange(block, "blk", n, 1)
+    passed, own = call(forward_kernel, "forward", [shape(block.shape, block.dtype)] * 2, after=len(after))(across, block, *after)
+    outer = lax.ppermute(passed, "blk", [(1, 0), (2, 3)])
+    inner = lax.ppermute(own, "blk", [(1, 2), (2, 1)])
+    return [(block,), (beside,), (across,), (outer, inner)]
+
+
 def order_kernel(*refs):
     refs[-1][...] = jnp.zeros_like(refs[-1])
 
 
-def behind(*arrays):
-    (mark,) = call(order_kernel, "order", [MARK], after=len(arrays), cost=2 * 10**10)(*arrays)
+def behind(*arrays, cost=2 * 10**10):
+    (mark,) = call(order_kernel, "order", [MARK], after=len(arrays), cost=cost)(*arrays)
     return mark
 
 
@@ -458,7 +477,6 @@
     n_i, k_left, width = pair_left.shape
     n_j, k_right, _ = pair_right.shape
     n_k = k_left * n_blk
-    left_raw = [pair_left] + [shift(pair_left, "blk", n_blk, s) for s in range(1, n_blk)]
     right_raw = [pair_right] + [exchange(pair_right, "rows", n_rows, s) for s in range(1, n_rows)]
     middle_shape = (n_i, n_j, width)
     gate, middle_in, head_back, tri_up = call(
@@ -466,36 +484,44 @@
         "middle",
         [shape(middle_shape, f32), shape(middle_shape, bf16), shape(middle_shape, bf16), shape(middle_shape, f32)],
         after=1,
-    )(pair_middle, cotangent, gate_weight, output_weight, behind())
+    )(pair_middle, cotangent, gate_weight, output_weight, behind(cost=10**9))
     right_act, right_in, *right_flip = call(
         functools.partial(right_kernel, n_rows, n_blk, k_left),
         "right",
         [shape((n_j * n_k, width), f32), shape((n_rows, n_j, k_right, width), bf16)]
         + [shape((k_left, n_j, width), f32)] * n_blk,
     )(*right_raw, right_weight)
+    left_raw = gather_left(pair_left, n_blk, (right_in, middle_in))
     left_act, left_in, total = [], [], []
     act_shape = shape(pair_left.shape, f32)
     in_shape = shape(pair_left.shape, bf16)
     for s in range(n_blk - 1):
         act, inputs, total = call(
-            functools.partial(left_kernel, s == 0),
+            functools.partial(left_kernel, len(left_raw[s]), s == 0),
             "left",
             [act_shape, in_shape, shape(middle_shape, f32)],
-        )(left_raw[s], left_weight, right_flip[s], *total)
+        )(*left_raw[s], left_weight, right_flip[s], *total)
         left_act.append(act)
         left_in.append(inputs)
         total = [total]
     act, inputs, tri_in, tri_back = call(
-        functools.partial(triangle_kernel, n_blk > 1),
+        functools.partial(triangle_kernel, len(left_raw[-1]), n_blk > 1),
         "triangle",
         [act_shape, in_shape, shape(middle_shape, bf16), shape(middle_shape, f32)],
-    )(left_raw[-1], left_weight, right_flip[-1], tri_up, *total)
+    )(*left_raw[-1], left_weight, right_flip[-1], tri_up, *total)
     left_act.append(act)
     left_in.append(inputs)
-    left_out = call(left_back_kernel, "left_back", [shape(pair_left.shape, bf16)] * n_blk)(
-        tri_back, right_act
-    )
-    left_back = [left_out[0]] + [shift(left_out[s], "blk", n_blk, n_blk - s) for s in range(1, n_blk)]
+    half = n_blk // 2
+    left_out = []
+    for first in (half, 0):
+        some = call(
+            functools.partial(left_back_kernel, first, n_blk),
+            "left_back",
+            [shape(pair_left.shape, bf16)] * half,
+            after=0,
+        )(tri_back, right_act)
+        left_out = [*some, *left_out]
+    left_back = [left_out[0]] + [exchange(left_out[s], "blk", n_blk, s) for s in range(1, n_blk)]
     right_stack = shape((n_rows // 2,) + pair_right.shape, bf16)
     keep, send = call(
         functools.partial(right_back_kernel, n_rows, n_blk),
@@ -504,7 +530,7 @@
         scratch=[pltpu.VMEM((n_j, n_k, width), bf16)],
         after=1,
     )(tri_back, *left_act, left_out[0])
-    kept, came, sent = halving_sum(keep, send, "rows", n_rows, (behind(*left_back[1:]),))
+    kept, came, sent = halving_sum(keep, send, "rows", n_rows, (behind(*left_back[1:], cost=LEFT_COST),))
     update, pre_back, gate_part, output_part = call(
         heads_kernel,
         "heads",
@@ -516,25 +542,24 @@
         ],
         after=1,
     )(tri_in, output_weight, gate, middle_in, head_back, cotangent, left_out[0])
-    grad_middle, done_middle = call(
-        grad_middle_kernel, "grad_middle", [shape(middle_shape, bf16), MARK]
-    )(pair_middle, pre_back, gate_weight)
     parts = (n_rows // 2, width // n_rows, 6 * width)
     keep, send = call(
         functools.partial(weights_kernel, n_rows, n_blk),
         "weights",
         [shape(parts, f32), shape(parts, bf16)],
         scratch=[pltpu.VMEM((width, 6 * width), f32)],
-        after=1,
-    )(right_in, left_weight, right_weight, gate_part, output_part, *left_in, *left_out, keep, send, done_middle)
-    keep, part, _ = halving_sum(keep, send, "rows", n_rows, ())
+    )(right_in, left_weight, right_weight, gate_part, output_part, *left_in, *left_out, keep, send)
+    grad_middle, done_middle = call(
+        grad_middle_kernel, "grad_middle", [shape(middle_shape, bf16), MARK], after=1
+    )(pair_middle, pre_back, gate_weight, send)
+    keep, part, _ = halving_sum(keep, send, "rows", n_rows, (done_middle,))
     part = combine([keep, part], (behind(sent),))
     grad_left, grad_right, done_sides = call(
         functools.partial(side_kernel, n_blk),
         "sides",
         [shape(pair_left.shape, bf16), shape(pair_right.shape, bf16), MARK],
     )(pair_left, pair_right, left_weight, right_weight, *left_back, kept, came)
-    part = combine([part] + [shift(part, "blk", n_blk, s) for s in range(1, n_blk)], (done_sides,))
+    part = combine([part] + [exchange(part, "blk", n_blk, s) for s in range(1, n_blk)], (done_sides,))
     pieces = [part] + [exchange(part, "rows", n_rows, s) for s in range(1, n_rows)]
     deltas = call(
         functools.partial(deltas_kernel, n_rows),

time: 87.6 us -> 81.9 us (0.935)
  waiting for transfers between devices: 13.3 us -> 8.05 us
    ppermute x9 -> x2, starting transfers between devices: 19.3 us -> 1.97 us  [the longest x1 1.29 us: gather_left(): outer = lax.ppermute(passed, 'blk', [(1, 0), (2, 3)])]
    ppermute x10 -> x18, starting transfers between devices: 13.4 us -> 30.3 us  [exchange(): return lax.ppermute(x, axis, [(a, a ^ bit) for a in range(n)])]
    ppermute x9 -> x2, waiting for transfers between devices: 5.71 us -> 0.14 us  [the longest x1 0.14 us: gather_left(): outer = lax.ppermute(passed, 'blk', [(1, 0), (2, 3)])]
    ppermute x10 -> x18, waiting for transfers between devices: 7.55 us -> 7.91 us  [exchange(): return lax.ppermute(x, axis, [(a, a ^ bit) for a in range(n)])]
    pallas_call x20 -> x22, Pallas kernels: 40.5 us -> 40.4 us  [run(): pl.pallas_call(kernel, in_specs=[pl.BlockSpec(memory_space=space) for spa...]
  transfers between devices with their start and end apart: 19 -> 20, of which waited for: 8 -> 9; matrix products, arithmetic and copies ran while one was open for 0% -> 0% of each run, Pallas kernels for 36% -> 41%
where the time goes in v8:
time: 81.9 us; the launch traced here: 81.7 us
  Pallas kernels  40.4 us (49%)
  starting transfers between devices  32.3 us (39%)
  waiting for transfers between devices  8.05 us (10%)
  between operations  0.89 us (1%)
    pallas_call x22, Pallas kernels, run(): pl.pallas_call(kernel, in_specs=[pl.BlockSpec(memory_space=space) for spa...  40.4 us
    ppermute x18, starting transfers between devices, exchange(): return lax.ppermute(x, axis, [(a, a ^ bit) for a in range(n)])  30.3 us
    ppermute x18, waiting for transfers between devices, exchange(): return lax.ppermute(x, axis, [(a, a ^ bit) for a in range(n)])  7.91 us
  transfers between devices with their start and end apart: 20, of which 9 were waited for; matrix products, arithmetic and copies ran while one was open for 0% of the time, Pallas kernels for 41%

profile of v8, /device:TPU:0, one launch (start us, length us, event | category | flops | bytes accessed | tf_op | source)
XLA Modules:
  0.0 81.7 jit_solution(4622352047409248846)
XLA Ops:
  0.7 4.1 %collective-permute-start = (bf16[64,16,128]{2,1,0:T(8,128)(2,1)}, bf16[64,16,128]{2,1,0:T(8,128)(2,1)S(1)}, u32[]{:S(2)}, u32[]{:S(2)}) collective-permute-start(bf16[64,16,128]{2,1,0:T(8,128)(2,1)} %refs_0_.5), channel_id=1, source_target_pairs={{0,4},{2,6},{4,0},{6,2},{1,5},{3,7},{5,1},{7,3},{8,12},{10,14},{12... | collective-permute-start | bytes 786440 | tf_op jit(solution)/shard_map/ppermute | solution.py:361
  4.8 2.4 %collective-permute-start.3 = (bf16[32,16,128]{2,1,0:T(8,128)(2,1)}, bf16[32,16,128]{2,1,0:T(8,128)(2,1)S(1)}, u32[]{:S(2)}, u32[]{:S(2)}) collective-permute-start(bf16[32,16,128]{2,1,0:T(8,128)(2,1)} %refs_1_.9), channel_id=1, source_target_pairs={{0,24},{8,16},{16,8},{24,0},{1,25},{9,17},{17,9},{25,1},{2,26},{10... | collective-permute-start | bytes 393224 | tf_op jit(solution)/shard_map/ppermute | solution.py:361
  7.2 0.5 collective-permute-start.2
  7.7 0.5 collective-permute-start.1
  8.3 1.6 %collective-permute-start.6 = (bf16[64,16,128]{2,1,0:T(8,128)(2,1)}, bf16[64,16,128]{2,1,0:T(8,128)(2,1)S(1)}, u32[]{:S(2)}, u32[]{:S(2)}) collective-permute-start(bf16[64,16,128]{2,1,0:T(8,128)(2,1)} %refs_0_.5), channel_id=1, source_target_pairs={{0,2},{2,0},{4,6},{6,4},{1,3},{3,1},{5,7},{7,5},{8,10},{10,8},{12,... | collective-permute-start | bytes 786440 | tf_op jit(solution)/shard_map/ppermute | solution.py:361
  9.9 0.0 copy-start.4
  9.9 0.0 copy-start.5
  9.9 2.4 %middle.3 = (f32[64,32,128]{2,1,0:T(8,128)S(1)}, bf16[64,32,128]{2,1,0:T(8,128)(2,1)S(1)}, bf16[64,32,128]{2,1,0:T(8,128)(2,1)S(1)}, f32[64,32,128]{2,1,0:T(8,128)S(1)}) custom-call(bf16[64,32,128]{2,1,0:T(8,128)(2,1)S(1)} %copy-done.2, bf16[64,32,128]{2,1,0:T(8,128)(2,1)S(1)} %copy-done.3, bf16[128,128]{1,0:T(8,128)(2,1)S(1)} %copy-done.7, ...), custom_call_target="tpu_custom_call" | custom-call | flops 1000 | bytes 1000 | tf_op jit(solution)/shard_map/middle/pallas_call | solution.py:451
  12.3 0.0 copy-start
  12.3 1.3 %collective-permute-done.2.refs_2_ = bf16[32,16,128]{2,1,0:T(8,128)(2,1)S(1)} collective-permute-done((bf16[32,16,128]{2,1,0:T(8,128)(2,1)}, bf16[32,16,128]{2,1,0:T(8,128)(2,1)S(1)}, u32[]{:S(2)}, u32[]{:S(2)}) %collective-permute-start.2) | collective-permute-done | bytes 131104 | tf_op jit(solution)/shard_map/ppermute | solution.py:361
  13.7 0.1 collective-permute-done.1.refs_1_
  13.7 3.3 %right.1 = (f32[2048,128]{1,0:T(8,128)S(1)}, bf16[4,32,16,128]{3,2,1,0:T(8,128)(2,1)S(1)}, f32[16,32,128]{2,1,0:T(8,128)S(1)}, f32[16,32,128]{2,1,0:T(8,128)S(1)...) custom-call(bf16[32,16,128]{2,1,0:T(8,128)(2,1)S(1)} %copy-done.5, ...), custom_call_target="tpu_custom_call" | custom-call | flops 1000 | bytes 1000 | tf_op jit(solution)/shard_map/right/pallas_call | solution.py:451
  17.1 0.0 copy-start.1
  17.1 1.3 %collective-permute-start.4 = (bf16[64,16,128]{2,1,0:T(8,128)(2,1)S(1)}, bf16[64,16,128]{2,1,0:T(8,128)(2,1)S(1)}, u32[]{:S(2)}, u32[]{:S(2)}) collective-permute-start(bf16[64,16,128]{2,1,0:T(8,128)(2,1)S(1)} %get-tuple-element.60), channel_id=1, source_target_pairs={{2,0},{4,6},{3,1},{5,7},{10,8},{12,14},{11,9},{13,15},{18,16},{20,... | collective-permute-start | bytes 786440 | tf_op jit(solution)/shard_map/ppermute | solution.py:398
  18.4 0.7 collective-permute-start.5
  19.1 2.5 %left.3 = (f32[64,16,128]{2,1,0:T(8,128)S(1)}, bf16[64,16,128]{2,1,0:T(8,128)(2,1)S(1)}, f32[64,32,128]{2,1,0:T(8,128)S(1)}) custom-call(bf16[64,16,128]{2,1,0:T(8,128)(2,1)S(1)} %copy-done, bf16[128,256]{1,0:T(8,128)(2,1)S(1)} %copy-done.1, f32[16,32,128]{2,1,0:T(8,128)S(1)} %get-tuple-element.66.refs_2_), custom_call_target="tpu_custom_call" | custom-call | flops 1000 | bytes 1000 | tf_op jit(solution)/shard_map/left/pallas_call | solution.py:451
  21.7 2.6 %left.4 = (f32[64,16,128]{2,1,0:T(8,128)S(1)}, bf16[64,16,128]{2,1,0:T(8,128)(2,1)S(1)}, f32[64,32,128]{2,1,0:T(8,128)S(1)}) custom-call(bf16[64,16,128]{2,1,0:T(8,128)(2,1)S(1)} %collective-permute-done.6.refs_0_, bf16[128,256]{1,0:T(8,128)(2,1)S(1)} %copy-done.1, f32[16,32,128]{2,1,0:T(8,128)S(1)} %get-tuple-element.65.refs_2_, ...), custom_call_target="tpu_custom_call" | custom-call | flops 1000 | bytes 1000 | tf_op jit(solution)/shard_map/left/pallas_call | solution.py:451
  24.3 2.6 %left.5 = (f32[64,16,128]{2,1,0:T(8,128)S(1)}, bf16[64,16,128]{2,1,0:T(8,128)(2,1)S(1)}, f32[64,32,128]{2,1,0:T(8,128)S(1)}) custom-call(bf16[64,16,128]{2,1,0:T(8,128)(2,1)S(1)} %collective-permute-done.refs_0_, bf16[128,256]{1,0:T(8,128)(2,1)S(1)} %copy-done.1, f32[16,32,128]{2,1,0:T(8,128)S(1)} %get-tuple-element.64.refs_2_, ...), custom_call_target="tpu_custom_call" | custom-call | flops 1000 | bytes 1000 | tf_op jit(solution)/shard_map/left/pallas_call | solution.py:451
  26.9 0.1 collective-permute-done.4.refs_0_
  27.0 3.5 %triangle.1 = (f32[64,16,128]{2,1,0:T(8,128)S(1)}, bf16[64,16,128]{2,1,0:T(8,128)(2,1)S(1)}, bf16[64,32,128]{2,1,0:T(8,128)(2,1)S(1)}, f32[64,32,128]{2,1,0:T(8,128)S(1)}) custom-call(bf16[64,16,128]{2,1,0:T(8,128)(2,1)S(1)} %collective-permute-done.4.refs_0_, bf16[64,16,128]{2,1,0:T(8,128)(2,1)S(1)} %collective-permute-done.5.refs_1_, ...), custom_call_target="tpu_custom_call" | custom-call | flops 1000 | bytes 1000 | tf_op jit(solution)/shard_map/triangle/pallas_call | solution.py:451
  30.5 2.3 %left_back.3 = (bf16[64,16,128]{2,1,0:T(8,128)(2,1)S(1)}, bf16[64,16,128]{2,1,0:T(8,128)(2,1)S(1)}) custom-call(f32[64,32,128]{2,1,0:T(8,128)S(1)} %get-tuple-element.73.tri_back, f32[2048,128]{1,0:T(8,128)S(1)} %get-tuple-element.74.right_act), custom_call_target="tpu_custom_call" | custom-call | flops 1000 | bytes 1000 | tf_op jit(solution)/shard_map/left_back/pallas_call | solution.py:451
  32.9 5.9 %collective-permute-start.8 = (bf16[64,16,128]{2,1,0:T(8,128)(2,1)S(1)}, bf16[64,16,128]{2,1,0:T(8,128)(2,1)S(1)}, u32[]{:S(2)}, u32[]{:S(2)}) collective-permute-start(bf16[64,16,128]{2,1,0:T(8,128)(2,1)S(1)} %get-tuple-element.78.refs_6_), channel_id=1, source_target_pairs={{0,4},{2,6},{4,0},{6,2},{1,5},{3,7},{5,1},{7,3},{8,12},{10,14},{12... | collective-permute-start | bytes 786440 | tf_op jit(solution)/shard_map/ppermute | solution.py:361
  38.8 2.9 %collective-permute-start.9 = (bf16[64,16,128]{2,1,0:T(8,128)(2,1)S(1)}, bf16[64,16,128]{2,1,0:T(8,128)(2,1)S(1)}, u32[]{:S(2)}, u32[]{:S(2)}) collective-permute-start(bf16[64,16,128]{2,1,0:T(8,128)(2,1)S(1)} %get-tuple-element.79.refs_7_), channel_id=1, source_target_pairs={{0,6},{2,4},{4,2},{6,0},{1,7},{3,5},{5,3},{7,1},{8,14},{10,12},{12... | collective-permute-start | bytes 786440 | tf_op jit(solution)/shard_map/ppermute | solution.py:361
  41.7 2.3 %left_back.2 = (bf16[64,16,128]{2,1,0:T(8,128)(2,1)S(1)}, bf16[64,16,128]{2,1,0:T(8,128)(2,1)S(1)}) custom-call(f32[64,32,128]{2,1,0:T(8,128)S(1)} %get-tuple-element.73.tri_back, f32[2048,128]{1,0:T(8,128)S(1)} %get-tuple-element.74.right_act), custom_call_target="tpu_custom_call" | custom-call | flops 1000 | bytes 1000 | tf_op jit(solution)/shard_map/left_back/pallas_call | solution.py:451
  44.0 0.1 collective-permute-start.7
  44.1 5.5 %right_back.1 = (bf16[2,32,16,128]{3,2,1,0:T(8,128)(2,1)S(1)}, bf16[2,32,16,128]{3,2,1,0:T(8,128)(2,1)S(1)}) custom-call(f32[64,32,128]{2,1,0:T(8,128)S(1)} %get-tuple-element.73.tri_back, f32[64,16,128]{2,1,0:T(8,128)S(1)} %get-tuple-element.80.refs_0_, f32[64,16,128]{2,1,0:T(8,128)S(1)} %get-tuple-element.81.refs_1_, ...), custom_call_target="tpu_custom_call" | custom-call | flops 1000 | bytes 1000 | tf_op jit(solution)/shard_map/right_back/pallas_call | solution.py:451
  49.6 1.6 %collective-permute-start.10 = (bf16[2,32,16,128]{3,2,1,0:T(8,128)(2,1)S(1)}, bf16[2,32,16,128]{3,2,1,0:T(8,128)(2,1)S(1)}, u32[]{:S(2)}, u32[]{:S(2)}) collective-permute-start(bf16[2,32,16,128]{3,2,1,0:T(8,128)(2,1)S(1)} %get-tuple-element.85.refs_9_), channel_id=1, source_target_pairs={{0,8},{8,0},{16,24},{24,16},{1,9},{9,1},{17,25},{25,17},{2,10},{10... | collective-permute-start | bytes 786440 | tf_op jit(solution)/shard_map/ppermute | solution.py:361
  51.2 2.7 %heads.1 = (bf16[64,32,128]{2,1,0:T(8,128)(2,1)}, bf16[64,32,128]{2,1,0:T(8,128)(2,1)S(1)}, f32[128,128]{1,0:T(8,128)S(1)}, f32[128,128]{1,0:T(8,128)S(1)}) custom-call(bf16[64,32,128]{2,1,0:T(8,128)(2,1)S(1)} %get-tuple-element.70.tri_in, bf16[128,128]{1,0:T(8,128)(2,1)S(1)} %copy-done.6, f32[64,32,128]{2,1,0:T(8,128)S(1)} %get-tuple-element.71.gate, ...), custom_call_target="tpu_custom_call" | custom-call | flops 1000 | bytes 1000 | tf_op jit(solution)/shard_map/heads/pallas_call | solution.py:451
  53.9 4.3 %weights.1 = (f32[2,32,768]{2,1,0:T(8,128)S(1)}, bf16[2,32,768]{2,1,0:T(8,128)(2,1)S(1)}) custom-call(bf16[4,32,16,128]{3,2,1,0:T(8,128)(2,1)S(1)} %get-tuple-element.58.refs_2_.right_in, bf16[128,256]{1,0:T(8,128)(2,1)S(1)} %copy-done.1, bf16[128,256]{1,0:T(8,128)(2,1)S(1)} %copy-done.4, f32[128,128]{1,0:T(8,128)S(1)} %get-tuple-element.91.gate_part, ...), custom_call_target="tpu_custom_call" | custom-call | flops 1000 | bytes 1000 | tf_op jit(solution)/shard_map/weights/pallas_call | solution.py:451
  58.2 0.6 collective-permute-start.12
  58.8 2.4 %grad_middle.1 = (bf16[64,32,128]{2,1,0:T(8,128)(2,1)}, f32[8,128]{1,0:T(8,128)S(1)}) custom-call(bf16[64,32,128]{2,1,0:T(8,128)(2,1)S(1)} %copy-done.2, bf16[64,32,128]{2,1,0:T(8,128)(2,1)S(1)} %get-tuple-element.90.pre_back, bf16[128,128]{1,0:T(8,128)(2,1)S(1)} %copy-done.7, bf16[2,32,768]{2,1,0:T(8,128)(2,1)S(1)} %get-tuple-element.97._), custom_call_target="tpu_custom_call" | custom-call | flops 1000 | bytes 1000 | tf_op jit(solution)/shard_map/grad_middle/pallas_call | solution.py:451
  61.2 1.6 %collective-permute-done.12.came = bf16[2,32,768]{2,1,0:T(8,128)(2,1)S(1)} collective-permute-done((bf16[2,32,768]{2,1,0:T(8,128)(2,1)S(1)}, bf16[2,32,768]{2,1,0:T(8,128)(2,1)S(1)}, u32[]{:S(2)}, u32[]{:S(2)}) %collective-permute-start.12) | collective-permute-done | bytes 98336 | tf_op jit(solution)/shard_map/ppermute | solution.py:361
  62.9 1.6 %collective-permute-start.13 = (bf16[1,32,768]{2,1,0:T(8,128)(2,1)S(1)}, bf16[1,32,768]{2,1,0:T(8,128)(2,1)S(1)}, u32[]{:S(2)}, u32[]{:S(2)}) collective-permute-start(bf16[1,32,768]{2,1,0:T(8,128)(2,1)S(1)} %get-tuple-element.102), channel_id=1, source_target_pairs={{0,16},{8,24},{16,0},{24,8},{1,17},{9,25},{17,1},{25,9},{2,18},{10... | collective-permute-start | bytes 147464 | tf_op jit(solution)/shard_map/ppermute | solution.py:361
  64.5 0.1 halve.2
  64.6 0.6 collective-permute-start.11
  65.1 1.9 %collective-permute-done.13.refs_1_ = bf16[1,32,768]{2,1,0:T(8,128)(2,1)S(1)} collective-permute-done((bf16[1,32,768]{2,1,0:T(8,128)(2,1)S(1)}, bf16[1,32,768]{2,1,0:T(8,128)(2,1)S(1)}, u32[]{:S(2)}, u32[]{:S(2)}) %collective-permute-start.13) | collective-permute-done | bytes 49184 | tf_op jit(solution)/shard_map/ppermute | solution.py:361
  67.0 1.0 %collective-permute-start.16 = (bf16[1,32,768]{2,1,0:T(8,128)(2,1)S(1)}, bf16[1,32,768]{2,1,0:T(8,128)(2,1)S(1)}, u32[]{:S(2)}, u32[]{:S(2)}) collective-permute-start(bf16[1,32,768]{2,1,0:T(8,128)(2,1)S(1)} %combine.2.refs_0_), channel_id=1, source_target_pairs={{0,6},{2,4},{4,2},{6,0},{1,7},{3,5},{5,3},{7,1},{8,14},{10,12},{12... | collective-permute-start | bytes 147464 | tf_op jit(solution)/shard_map/ppermute | solution.py:361
  68.1 2.5 %collective-permute-start.15 = (bf16[1,32,768]{2,1,0:T(8,128)(2,1)S(1)}, bf16[1,32,768]{2,1,0:T(8,128)(2,1)S(1)}, u32[]{:S(2)}, u32[]{:S(2)}) collective-permute-start(bf16[1,32,768]{2,1,0:T(8,128)(2,1)S(1)} %combine.2.refs_0_), channel_id=1, source_target_pairs={{0,4},{2,6},{4,0},{6,2},{1,5},{3,7},{5,1},{7,3},{8,12},{10,14},{12... | collective-permute-start | bytes 147464 | tf_op jit(solution)/shard_map/ppermute | solution.py:361
  70.6 0.9 %collective-permute-start.14 = (bf16[1,32,768]{2,1,0:T(8,128)(2,1)S(1)}, bf16[1,32,768]{2,1,0:T(8,128)(2,1)S(1)}, u32[]{:S(2)}, u32[]{:S(2)}) collective-permute-start(bf16[1,32,768]{2,1,0:T(8,128)(2,1)S(1)} %combine.2.refs_0_), channel_id=1, source_target_pairs={{0,2},{2,0},{4,6},{6,4},{1,3},{3,1},{5,7},{7,5},{8,10},{10,8},{12,... | collective-permute-start | bytes 147464 | tf_op jit(solution)/shard_map/ppermute | solution.py:361
  71.5 2.9 %sides.1 = (bf16[64,16,128]{2,1,0:T(8,128)(2,1)}, bf16[32,16,128]{2,1,0:T(8,128)(2,1)}, f32[8,128]{1,0:T(8,128)S(1)}) custom-call(bf16[64,16,128]{2,1,0:T(8,128)(2,1)S(1)} %copy-done, bf16[32,16,128]{2,1,0:T(8,128)(2,1)S(1)} %copy-done.5, bf16[128,256]{1,0:T(8,128)(2,1)S(1)} %copy-done.1, bf16[128,256]{1,0:T(8,128)(2,1)S(1)} %copy-done.4, ...), custom_call_target="tpu_custom_call" | custom-call | flops 1000 | bytes 1000 | tf_op jit(solution)/shard_map/sides/pallas_call | solution.py:451
  74.4 0.3 collective-permute-done.14.refs_1_
  74.8 1.6 %collective-permute-start.19 = (bf16[1,32,768]{2,1,0:T(8,128)(2,1)S(1)}, bf16[1,32,768]{2,1,0:T(8,128)(2,1)S(1)}, u32[]{:S(2)}, u32[]{:S(2)}) collective-permute-start(bf16[1,32,768]{2,1,0:T(8,128)(2,1)S(1)} %combine.3.refs_0_), channel_id=1, source_target_pairs={{0,24},{8,16},{16,8},{24,0},{1,25},{9,17},{17,9},{25,1},{2,26},{10... | collective-permute-start | bytes 147464 | tf_op jit(solution)/shard_map/ppermute | solution.py:361
  76.3 0.5 collective-permute-start.18
  76.8 1.5 %collective-permute-start.17 = (bf16[1,32,768]{2,1,0:T(8,128)(2,1)S(1)}, bf16[1,32,768]{2,1,0:T(8,128)(2,1)S(1)}, u32[]{:S(2)}, u32[]{:S(2)}) collective-permute-start(bf16[1,32,768]{2,1,0:T(8,128)(2,1)S(1)} %combine.3.refs_0_), channel_id=1, source_target_pairs={{0,8},{8,0},{16,24},{24,16},{1,9},{9,1},{17,25},{25,17},{2,10},{10... | collective-permute-start | bytes 147464 | tf_op jit(solution)/shard_map/ppermute | solution.py:361
  78.3 1.5 %collective-permute-done.19.refs_3_ = bf16[1,32,768]{2,1,0:T(8,128)(2,1)S(1)} collective-permute-done((bf16[1,32,768]{2,1,0:T(8,128)(2,1)S(1)}, bf16[1,32,768]{2,1,0:T(8,128)(2,1)S(1)}, u32[]{:S(2)}, u32[]{:S(2)}) %collective-permute-start.19) | collective-permute-done | bytes 49184 | tf_op jit(solution)/shard_map/ppermute | solution.py:361
  79.8 0.6 collective-permute-done.18.refs_2_
  80.4 0.5 collective-permute-done.17.refs_1_
  80.9 0.8 deltas.1
  (30 shorter events, 0.2 us)
Async XLA Ops:
  0.6 9.2 %copy-start.6 = (bf16[128,128]{1,0:T(8,128)(2,1)S(1)}, bf16[128,128]{1,0:T(8,128)(2,1)}, u32[]{:S(2)}) copy-start(bf16[128,128]{1,0:T(8,128)(2,1)} %out_w.1) | copy-start | bytes 98308
  0.6 9.2 %copy-start.7 = (bf16[128,128]{1,0:T(8,128)(2,1)S(1)}, bf16[128,128]{1,0:T(8,128)(2,1)}, u32[]{:S(2)}) copy-start(bf16[128,128]{1,0:T(8,128)(2,1)} %gate_weight.3) | copy-start | bytes 98308
  0.7 9.2 %copy-start.3 = (bf16[64,32,128]{2,1,0:T(8,128)(2,1)S(1)}, bf16[64,32,128]{2,1,0:T(8,128)(2,1)}, u32[]{:S(2)}) copy-start(bf16[64,32,128]{2,1,0:T(8,128)(2,1)} %cotangent.3) | copy-start | bytes 1572868
  0.7 9.2 %copy-start.2 = (bf16[64,32,128]{2,1,0:T(8,128)(2,1)S(1)}, bf16[64,32,128]{2,1,0:T(8,128)(2,1)}, u32[]{:S(2)}) copy-start(bf16[64,32,128]{2,1,0:T(8,128)(2,1)} %middle.5) | copy-start | bytes 1572868
  0.7 16.4 %collective-permute-start = (bf16[64,16,128]{2,1,0:T(8,128)(2,1)}, bf16[64,16,128]{2,1,0:T(8,128)(2,1)S(1)}, u32[]{:S(2)}, u32[]{:S(2)}) collective-permute-start(bf16[64,16,128]{2,1,0:T(8,128)(2,1)} %refs_0_.5), channel_id=1, source_target_pairs={{0,4},{2,6},{4,0},{6,2},{1,5},{3,7},{5,1},{7,3},{8,12},{10,14},{12... | collective-permute-start | bytes 786440 | tf_op jit(solution)/shard_map/ppermute | solution.py:361
  4.8 7.5 %collective-permute-start.3 = (bf16[32,16,128]{2,1,0:T(8,128)(2,1)}, bf16[32,16,128]{2,1,0:T(8,128)(2,1)S(1)}, u32[]{:S(2)}, u32[]{:S(2)}) collective-permute-start(bf16[32,16,128]{2,1,0:T(8,128)(2,1)} %refs_1_.9), channel_id=1, source_target_pairs={{0,24},{8,16},{16,8},{24,0},{1,25},{9,17},{17,9},{25,1},{2,26},{10... | collective-permute-start | bytes 393224 | tf_op jit(solution)/shard_map/ppermute | solution.py:361
  7.2 6.4 %collective-permute-start.2 = (bf16[32,16,128]{2,1,0:T(8,128)(2,1)}, bf16[32,16,128]{2,1,0:T(8,128)(2,1)S(1)}, u32[]{:S(2)}, u32[]{:S(2)}) collective-permute-start(bf16[32,16,128]{2,1,0:T(8,128)(2,1)} %refs_1_.9), channel_id=1, source_target_pairs={{0,16},{8,24},{16,0},{24,8},{1,17},{9,25},{17,1},{25,9},{2,18},{10... | collective-permute-start | bytes 393224 | tf_op jit(solution)/shard_map/ppermute | solution.py:361
  7.7 6.0 %collective-permute-start.1 = (bf16[32,16,128]{2,1,0:T(8,128)(2,1)}, bf16[32,16,128]{2,1,0:T(8,128)(2,1)S(1)}, u32[]{:S(2)}, u32[]{:S(2)}) collective-permute-start(bf16[32,16,128]{2,1,0:T(8,128)(2,1)} %refs_1_.9), channel_id=1, source_target_pairs={{0,8},{8,0},{16,24},{24,16},{1,9},{9,1},{17,25},{25,17},{2,10},{10... | collective-permute-start | bytes 393224 | tf_op jit(solution)/shard_map/ppermute | solution.py:361
  8.3 13.4 %collective-permute-start.6 = (bf16[64,16,128]{2,1,0:T(8,128)(2,1)}, bf16[64,16,128]{2,1,0:T(8,128)(2,1)S(1)}, u32[]{:S(2)}, u32[]{:S(2)}) collective-permute-start(bf16[64,16,128]{2,1,0:T(8,128)(2,1)} %refs_0_.5), channel_id=1, source_target_pairs={{0,2},{2,0},{4,6},{6,4},{1,3},{3,1},{5,7},{7,5},{8,10},{10,8},{12,... | collective-permute-start | bytes 786440 | tf_op jit(solution)/shard_map/ppermute | solution.py:361
  9.9 3.9 %copy-start.4 = (bf16[128,256]{1,0:T(8,128)(2,1)S(1)}, bf16[128,256]{1,0:T(8,128)(2,1)}, u32[]{:S(2)}) copy-start(bf16[128,256]{1,0:T(8,128)(2,1)} %right_w.1) | copy-start | bytes 196612
  9.9 3.8 %copy-start.5 = (bf16[32,16,128]{2,1,0:T(8,128)(2,1)S(1)}, bf16[32,16,128]{2,1,0:T(8,128)(2,1)}, u32[]{:S(2)}) copy-start(bf16[32,16,128]{2,1,0:T(8,128)(2,1)} %refs_1_.9) | copy-start | bytes 393220
  12.3 4.8 %copy-start = (bf16[64,16,128]{2,1,0:T(8,128)(2,1)S(1)}, bf16[64,16,128]{2,1,0:T(8,128)(2,1)}, u32[]{:S(2)}) copy-start(bf16[64,16,128]{2,1,0:T(8,128)(2,1)} %refs_0_.5) | copy-start | bytes 786436
  17.1 2.0 %copy-start.1 = (bf16[128,256]{1,0:T(8,128)(2,1)S(1)}, bf16[128,256]{1,0:T(8,128)(2,1)}, u32[]{:S(2)}) copy-start(bf16[128,256]{1,0:T(8,128)(2,1)} %left_w.1) | copy-start | bytes 196612
  17.1 9.9 %collective-permute-start.4 = (bf16[64,16,128]{2,1,0:T(8,128)(2,1)S(1)}, bf16[64,16,128]{2,1,0:T(8,128)(2,1)S(1)}, u32[]{:S(2)}, u32[]{:S(2)}) collective-permute-start(bf16[64,16,128]{2,1,0:T(8,128)(2,1)S(1)} %get-tuple-element.60), channel_id=1, source_target_pairs={{2,0},{4,6},{3,1},{5,7},{10,8},{12,14},{11,9},{13,15},{18,16},{20,... | collective-permute-start | bytes 786440 | tf_op jit(solution)/shard_map/ppermute | solution.py:398
  18.4 8.6 %collective-permute-start.5 = (bf16[64,16,128]{2,1,0:T(8,128)(2,1)S(1)}, bf16[64,16,128]{2,1,0:T(8,128)(2,1)S(1)}, u32[]{:S(2)}, u32[]{:S(2)}) collective-permute-start(bf16[64,16,128]{2,1,0:T(8,128)(2,1)S(1)} %get-tuple-element.61), channel_id=1, source_target_pairs={{2,4},{4,2},{3,5},{5,3},{10,12},{12,10},{11,13},{13,11},{18,20},{2... | collective-permute-start | bytes 786440 | tf_op jit(solution)/shard_map/ppermute | solution.py:399
  32.9 31.6 %collective-permute-start.8 = (bf16[64,16,128]{2,1,0:T(8,128)(2,1)S(1)}, bf16[64,16,128]{2,1,0:T(8,128)(2,1)S(1)}, u32[]{:S(2)}, u32[]{:S(2)}) collective-permute-start(bf16[64,16,128]{2,1,0:T(8,128)(2,1)S(1)} %get-tuple-element.78.refs_6_), channel_id=1, source_target_pairs={{0,4},{2,6},{4,0},{6,2},{1,5},{3,7},{5,1},{7,3},{8,12},{10,14},{12... | collective-permute-start | bytes 786440 | tf_op jit(solution)/shard_map/ppermute | solution.py:361
  38.8 25.7 %collective-permute-start.9 = (bf16[64,16,128]{2,1,0:T(8,128)(2,1)S(1)}, bf16[64,16,128]{2,1,0:T(8,128)(2,1)S(1)}, u32[]{:S(2)}, u32[]{:S(2)}) collective-permute-start(bf16[64,16,128]{2,1,0:T(8,128)(2,1)S(1)} %get-tuple-element.79.refs_7_), channel_id=1, source_target_pairs={{0,6},{2,4},{4,2},{6,0},{1,7},{3,5},{5,3},{7,1},{8,14},{10,12},{12... | collective-permute-start | bytes 786440 | tf_op jit(solution)/shard_map/ppermute | solution.py:361
  44.0 20.5 %collective-permute-start.7 = (bf16[64,16,128]{2,1,0:T(8,128)(2,1)S(1)}, bf16[64,16,128]{2,1,0:T(8,128)(2,1)S(1)}, u32[]{:S(2)}, u32[]{:S(2)}) collective-permute-start(bf16[64,16,128]{2,1,0:T(8,128)(2,1)S(1)} %get-tuple-element.77.refs_5_), channel_id=1, source_target_pairs={{0,2},{2,0},{4,6},{6,4},{1,3},{3,1},{5,7},{7,5},{8,10},{10,8},{12,... | collective-permute-start | bytes 786440 | tf_op jit(solution)/shard_map/ppermute | solution.py:361
  49.6 14.9 %collective-permute-start.10 = (bf16[2,32,16,128]{3,2,1,0:T(8,128)(2,1)S(1)}, bf16[2,32,16,128]{3,2,1,0:T(8,128)(2,1)S(1)}, u32[]{:S(2)}, u32[]{:S(2)}) collective-permute-start(bf16[2,32,16,128]{3,2,1,0:T(8,128)(2,1)S(1)} %get-tuple-element.85.refs_9_), channel_id=1, source_target_pairs={{0,8},{8,0},{16,24},{24,16},{1,9},{9,1},{17,25},{25,17},{2,10},{10... | collective-permute-start | bytes 786440 | tf_op jit(solution)/shard_map/ppermute | solution.py:361
  58.2 4.7 %collective-permute-start.12 = (bf16[2,32,768]{2,1,0:T(8,128)(2,1)S(1)}, bf16[2,32,768]{2,1,0:T(8,128)(2,1)S(1)}, u32[]{:S(2)}, u32[]{:S(2)}) collective-permute-start(bf16[2,32,768]{2,1,0:T(8,128)(2,1)S(1)} %get-tuple-element.97._), channel_id=1, source_target_pairs={{0,8},{8,0},{16,24},{24,16},{1,9},{9,1},{17,25},{25,17},{2,10},{10... | collective-permute-start | bytes 294920 | tf_op jit(solution)/shard_map/ppermute | solution.py:361
  62.9 4.2 %collective-permute-start.13 = (bf16[1,32,768]{2,1,0:T(8,128)(2,1)S(1)}, bf16[1,32,768]{2,1,0:T(8,128)(2,1)S(1)}, u32[]{:S(2)}, u32[]{:S(2)}) collective-permute-start(bf16[1,32,768]{2,1,0:T(8,128)(2,1)S(1)} %get-tuple-element.102), channel_id=1, source_target_pairs={{0,16},{8,24},{16,0},{24,8},{1,17},{9,25},{17,1},{25,9},{2,18},{10... | collective-permute-start | bytes 147464 | tf_op jit(solution)/shard_map/ppermute | solution.py:361
  64.6 6.9 %collective-permute-start.11 = (bf16[1,32,16,128]{3,2,1,0:T(8,128)(2,1)S(1)}, bf16[1,32,16,128]{3,2,1,0:T(8,128)(2,1)S(1)}, u32[]{:S(2)}, u32[]{:S(2)}) collective-permute-start(bf16[1,32,16,128]{3,2,1,0:T(8,128)(2,1)S(1)} %get-tuple-element.87.refs_0_), channel_id=1, source_target_pairs={{0,16},{8,24},{16,0},{24,8},{1,17},{9,25},{17,1},{25,9},{2,18},{10... | collective-permute-start | bytes 393224 | tf_op jit(solution)/shard_map/ppermute | solution.py:361
  67.0 7.4 %collective-permute-start.16 = (bf16[1,32,768]{2,1,0:T(8,128)(2,1)S(1)}, bf16[1,32,768]{2,1,0:T(8,128)(2,1)S(1)}, u32[]{:S(2)}, u32[]{:S(2)}) collective-permute-start(bf16[1,32,768]{2,1,0:T(8,128)(2,1)S(1)} %combine.2.refs_0_), channel_id=1, source_target_pairs={{0,6},{2,4},{4,2},{6,0},{1,7},{3,5},{5,3},{7,1},{8,14},{10,12},{12... | collective-permute-start | bytes 147464 | tf_op jit(solution)/shard_map/ppermute | solution.py:361
  68.1 6.3 %collective-permute-start.15 = (bf16[1,32,768]{2,1,0:T(8,128)(2,1)S(1)}, bf16[1,32,768]{2,1,0:T(8,128)(2,1)S(1)}, u32[]{:S(2)}, u32[]{:S(2)}) collective-permute-start(bf16[1,32,768]{2,1,0:T(8,128)(2,1)S(1)} %combine.2.refs_0_), channel_id=1, source_target_pairs={{0,4},{2,6},{4,0},{6,2},{1,5},{3,7},{5,1},{7,3},{8,12},{10,14},{12... | collective-permute-start | bytes 147464 | tf_op jit(solution)/shard_map/ppermute | solution.py:361
  70.6 4.2 %collective-permute-start.14 = (bf16[1,32,768]{2,1,0:T(8,128)(2,1)S(1)}, bf16[1,32,768]{2,1,0:T(8,128)(2,1)S(1)}, u32[]{:S(2)}, u32[]{:S(2)}) collective-permute-start(bf16[1,32,768]{2,1,0:T(8,128)(2,1)S(1)} %combine.2.refs_0_), channel_id=1, source_target_pairs={{0,2},{2,0},{4,6},{6,4},{1,3},{3,1},{5,7},{7,5},{8,10},{10,8},{12,... | collective-permute-start | bytes 147464 | tf_op jit(solution)/shard_map/ppermute | solution.py:361
  74.8 5.1 %collective-permute-start.19 = (bf16[1,32,768]{2,1,0:T(8,128)(2,1)S(1)}, bf16[1,32,768]{2,1,0:T(8,128)(2,1)S(1)}, u32[]{:S(2)}, u32[]{:S(2)}) collective-permute-start(bf16[1,32,768]{2,1,0:T(8,128)(2,1)S(1)} %combine.3.refs_0_), channel_id=1, source_target_pairs={{0,24},{8,16},{16,8},{24,0},{1,25},{9,17},{17,9},{25,1},{2,26},{10... | collective-permute-start | bytes 147464 | tf_op jit(solution)/shard_map/ppermute | solution.py:361
  76.3 4.1 %collective-permute-start.18 = (bf16[1,32,768]{2,1,0:T(8,128)(2,1)S(1)}, bf16[1,32,768]{2,1,0:T(8,128)(2,1)S(1)}, u32[]{:S(2)}, u32[]{:S(2)}) collective-permute-start(bf16[1,32,768]{2,1,0:T(8,128)(2,1)S(1)} %combine.3.refs_0_), channel_id=1, source_target_pairs={{0,16},{8,24},{16,0},{24,8},{1,17},{9,25},{17,1},{25,9},{2,18},{10... | collective-permute-start | bytes 147464 | tf_op jit(solution)/shard_map/ppermute | solution.py:361
  76.8 4.1 %collective-permute-start.17 = (bf16[1,32,768]{2,1,0:T(8,128)(2,1)S(1)}, bf16[1,32,768]{2,1,0:T(8,128)(2,1)S(1)}, u32[]{:S(2)}, u32[]{:S(2)}) collective-permute-start(bf16[1,32,768]{2,1,0:T(8,128)(2,1)S(1)} %combine.3.refs_0_), channel_id=1, source_target_pairs={{0,8},{8,0},{16,24},{24,16},{1,9},{9,1},{17,25},{25,17},{2,10},{10... | collective-permute-start | bytes 147464 | tf_op jit(solution)/shard_map/ppermute | solution.py:361

commit v9 on v8

--- a/solution.py
+++ b/solution.py
@@ -16,18 +16,6 @@
 MARK = jax.ShapeDtypeStruct((8, 128), jnp.float32)
 
 
-def normalize(values):
-    centred = values - jnp.mean(values, axis=-1, keepdims=True)
-    inverse = lax.rsqrt(jnp.mean(centred * centred, axis=-1, keepdims=True) + epsilon)
-    return (centred * inverse, inverse)
-
-
-def normalize_back(normed, inverse, upstream):
-    first = jnp.mean(upstream, axis=-1, keepdims=True)
-    second = jnp.mean(upstream * normed, axis=-1, keepdims=True)
-    return inverse * (upstream - first - normed * second)
-
-
 def sigmoid(x):
     return 0.5 * jnp.tanh(0.5 * x) + 0.5
 
@@ -42,6 +30,32 @@
 
 def dot_tn(a, b):
     return lax.dot_general(a, b, (((0,), (0,)), ((), ())), preferred_element_type=f32)
+
+
+def split(values):
+    high = values.astype(bf16)
+    return jnp.concatenate([high, (values - high.astype(f32)).astype(bf16)], axis=-1)
+
+
+def row_mean(parts, width):
+    return dot(parts, jnp.full((parts.shape[-1], width), 1.0 / width, bf16))
+
+
+def normalize(values, mean):
+    centred = values - mean
+    inverse = lax.rsqrt(row_mean(split(centred * centred), values.shape[-1]) + epsilon)
+    return (centred * inverse, inverse)
+
+
+def normalize_raw(raw):
+    return normalize(raw.astype(f32), row_mean(raw, raw.shape[-1]))
+
+
+def normalize_back(normed, inverse, upstream):
+    width = upstream.shape[-1]
+    first = row_mean(split(upstream), width)
+    second = row_mean(split(upstream * normed), width)
+    return inverse * (upstream - first - normed * second)
 
 
 def gated(inputs, weight):
@@ -56,11 +70,11 @@
 
 def middle_kernel(middle, cotangent, gate_weight, output_weight, _, gate, middle_in, head_back, tri_up):
     n_i, n_j, width = middle.shape
-    step = 8
+    step = 16
 
     def body(at, _):
         rows = pl.ds(at * step, step)
-        normed, _ = normalize(middle[rows].astype(f32).reshape(step * n_j, width))
+        normed, _ = normalize_raw(middle[rows].reshape(step * n_j, width))
         inputs = normed.astype(bf16)
         opened = sigmoid(dot(inputs, gate_weight[...]))
         back = (cotangent[rows].astype(f32).reshape(step * n_j, width) * opened).astype(bf16)
@@ -68,7 +82,7 @@
         middle_in[rows] = inputs.reshape(step, n_j, width)
         head_back[rows] = back.reshape(step, n_j, width)
         up = dot_nt(back, output_weight[...])
-        tri_up[rows] = (up - jnp.mean(up, axis=-1, keepdims=True)).reshape(step, n_j, width)
+        tri_up[rows] = (up - row_mean(split(up), width)).reshape(step, n_j, width)
         return 0
 
     lax.fori_loop(0, n_i // step, body, 0, unroll=2)
@@ -79,12 +93,12 @@
     n_j, k_right, width = raw[0].shape
     n_k = k_left * n_blk
     unit = math.gcd(k_left, k_right)
-    step = 16
+    step = n_j
     for s in range(n_rows):
 
         def body(at, _, s=s):
             rows = pl.ds(at * step, step)
-            normed, _ = normalize(raw[s][rows].astype(f32).reshape(step * k_right, width))
+            normed, _ = normalize_raw(raw[s][rows].reshape(step * k_right, width))
             inputs = normed.astype(bf16)
             in_out[s, rows] = inputs.reshape(step, k_right, width)
             lin, sw = gated(inputs, weight[...])
@@ -96,7 +110,7 @@
                     act_out[pl.ds(start, unit), :] = act[j, part * unit : (part + 1) * unit]
             return 0
 
-        lax.fori_loop(0, n_j // step, body, 0)
+        lax.fori_loop(0, n_j // step, body, 0, unroll=True)
 
     for s in range(n_blk):
 
@@ -117,14 +131,14 @@
 
 def project_left(raws, weight, act_out, in_out):
     n_i, k_left, width = raws[0].shape
-    step = 8
+    step = 32
 
     def body(at, _):
         rows = pl.ds(at * step, step)
-        raw = raws[0][rows].astype(f32)
+        raw = raws[0][rows]
         for other in raws[1:]:
-            raw = raw + other[rows].astype(f32)
-        normed, _ = normalize(raw.reshape(step * k_left, width))
+            raw = (raw.astype(f32) + other[rows].astype(f32)).astype(bf16)
+        normed, _ = normalize_raw(raw.reshape(step * k_left, width))
         inputs = normed.astype(bf16)
         in_out[rows] = inputs.reshape(step, k_left, width)
         lin, sw = gated(inputs, weight[...])
@@ -171,15 +185,16 @@
         if has_total:
             total = total + total_in[0][rows]
         flat = step * n_j
-        normed, inverse = normalize(total.reshape(flat, width))
+        total = total.reshape(flat, width)
+        normed, inverse = normalize(total, row_mean(split(total), width))
         tri_in[rows] = normed.astype(bf16).reshape(step, n_j, width)
         up = tri_up[rows].reshape(flat, width)
-        second = jnp.mean(up * normed, axis=-1, keepdims=True)
+        second = row_mean(split(up * normed), width)
         back = inverse * (up - normed * second)
         tri_back[rows] = back.astype(bf16).astype(f32).reshape(step, n_j, width)
         return 0
 
-    lax.fori_loop(0, n_i // step, triangle_rows, 0, unroll=2)
+    lax.fori_loop(0, n_i // step, triangle_rows, 0, unroll=4)
 
 
 def heads_kernel(tri_in, out_w, gate, middle_in, head_back, cotangent, _, *refs):
@@ -316,12 +331,12 @@
 def grad_middle_kernel(middle, pre_back, gate_weight, _, grad_middle, mark):
     mark[...] = jnp.zeros_like(mark)
     n_i, n_j, width = middle.shape
-    step = 8
+    step = 16
 
     def body(at, _):
         rows = pl.ds(at * step, step)
         flat = step * n_j
-        normed, inverse = normalize(middle[rows].astype(f32).reshape(flat, width))
+        normed, inverse = normalize_raw(middle[rows].reshape(flat, width))
         up = dot_nt(pre_back[rows].reshape(flat, width), gate_weight[...])
         grad_middle[rows] = normalize_back(normed, inverse, up).astype(bf16).reshape(step, n_j, width)
         return 0
@@ -329,32 +344,25 @@
     lax.fori_loop(0, n_i // step, body, 0, unroll=2)
 
 
-def side_kernel(n_left, *refs):
-    *refs, mark = refs
+def side_kernel(raw, weight, *refs):
+    backs, (grad, mark) = refs[:-2], refs[-2:]
     mark[...] = jnp.zeros_like(mark)
-    left, right, left_w, right_w = refs[:4]
-    left_back, refs = refs[4 : 4 + n_left], refs[4 + n_left :]
-    right_back, refs = [ref.at[0] for ref in refs[:2]], refs[2:]
-    for raw, weight, backs, grad in (
-        (left, left_w, left_back, refs[0]),
-        (right, right_w, right_back, refs[1]),
-    ):
-        n, k, width = raw.shape
-        step = 16
-        flat = step * k
-
-        def body(at, _, raw=raw, weight=weight, backs=backs, grad=grad, step=step, flat=flat, k=k, width=width):
-            rows = pl.ds(at * step, step)
-            normed, inverse = normalize(raw[rows].astype(f32).reshape(flat, width))
-            lin, sw = gated(normed.astype(bf16), weight[...])
-            back = backs[0][rows].astype(f32)
-            for other in backs[1:]:
-                back = back + other[rows].astype(f32)
-            up = dot_nt(joined_grad(back.reshape(flat, width), lin, sw), weight[...])
-            grad[rows] = normalize_back(normed, inverse, up).astype(bf16).reshape(step, k, width)
-            return 0
-
-        lax.fori_loop(0, n // step, body, 0, unroll=2)
+    n, k, width = raw.shape
+    step = 32
+    flat = step * k
+
+    def body(at, _):
+        rows = pl.ds(at * step, step)
+        normed, inverse = normalize_raw(raw[rows].reshape(flat, width))
+        lin, sw = gated(normed.astype(bf16), weight[...])
+        back = backs[0][rows].astype(f32)
+        for other in backs[1:]:
+            back = back + other[rows].astype(f32)
+        up = dot_nt(joined_grad(back.reshape(flat, width), lin, sw), weight[...])
+        grad[rows] = normalize_back(normed, inverse, up).astype(bf16).reshape(step, k, width)
+        return 0
+
+    lax.fori_loop(0, n // step, body, 0, unroll=2 if n // step % 2 == 0 else 1)
 
 
 def exchange(x, axis, n, bit):
@@ -429,7 +437,7 @@
 
 
 def deltas_kernel(n_rows, *refs):
-    pieces, outs = [ref.at[0] for ref in refs[:n_rows]], refs[n_rows:]
+    pieces, outs = [ref.at[0] for ref in refs[:n_rows]], refs[n_rows + 1 :]
     size = pieces[0].shape[0]
     for s, piece in enumerate(pieces):
         start = pl.multiple_of(lax.bitwise_xor(lax.axis_index("rows"), s) * size, size)
@@ -554,18 +562,20 @@
     )(pair_middle, pre_back, gate_weight, send)
     keep, part, _ = halving_sum(keep, send, "rows", n_rows, (done_middle,))
     part = combine([keep, part], (behind(sent),))
-    grad_left, grad_right, done_sides = call(
-        functools.partial(side_kernel, n_blk),
-        "sides",
-        [shape(pair_left.shape, bf16), shape(pair_right.shape, bf16), MARK],
-    )(pair_left, pair_right, left_weight, right_weight, *left_back, kept, came)
-    part = combine([part] + [exchange(part, "blk", n_blk, s) for s in range(1, n_blk)], (done_sides,))
+    grad_left, done_left = call(side_kernel, "left_side", [shape(pair_left.shape, bf16), MARK])(
+        pair_left, left_weight, *left_back
+    )
+    part = combine([part] + [exchange(part, "blk", n_blk, s) for s in range(1, n_blk)], (done_left,))
     pieces = [part] + [exchange(part, "rows", n_rows, s) for s in range(1, n_rows)]
+    grad_right, done_right = call(side_kernel, "right_side", [shape(pair_right.shape, bf16), MARK])(
+        pair_right, right_weight, kept.reshape(pair_right.shape), came.reshape(pair_right.shape)
+    )
     deltas = call(
         functools.partial(deltas_kernel, n_rows),
         "deltas",
         [shape(x.shape, f32) for x in (left_weight, right_weight, gate_weight, output_weight)],
-    )(*pieces)
+        after=1,
+    )(*pieces, done_right)
     return (
         update,
         grad_left,

time: 81.9 us -> 80.6 us (0.984)
  Pallas kernels: 40.4 us -> 38.2 us
  waiting for transfers between devices: 8.05 us -> 9.75 us
    pallas_call x22 -> x23, Pallas kernels: 40.4 us -> 38.2 us  [run(): pl.pallas_call(kernel, in_specs=[pl.BlockSpec(memory_space=space) for spa...]
    ppermute x1, waiting for transfers between devices: 0.14 us -> 1.08 us  [gather_left(): outer = lax.ppermute(passed, 'blk', [(1, 0), (2, 3)])]
    ppermute x18, starting transfers between devices: 30.3 us -> 29.4 us  [exchange(): return lax.ppermute(x, axis, [(a, a ^ bit) for a in range(n)])]
  transfers between devices with their start and end apart: 20 -> 20, of which waited for: 9 -> 10; matrix products, arithmetic and copies ran while one was open for 0% -> 0% of each run, Pallas kernels for 41% -> 39%
where the time goes in v9:
time: 80.6 us; the launch traced here: 80.4 us
  Pallas kernels  38.2 us (47%)
  starting transfers between devices  31.6 us (39%)
  waiting for transfers between devices  9.75 us (12%)
  between operations  0.87 us (1%)
    pallas_call x23, Pallas kernels, run(): pl.pallas_call(kernel, in_specs=[pl.BlockSpec(memory_space=space) for spa...  38.2 us
    ppermute x18, starting transfers between devices, exchange(): return lax.ppermute(x, axis, [(a, a ^ bit) for a in range(n)])  29.4 us
    ppermute x18, waiting for transfers between devices, exchange(): return lax.ppermute(x, axis, [(a, a ^ bit) for a in range(n)])  8.67 us
  transfers between devices with their start and end apart: 20, of which 10 were waited for; matrix products, arithmetic and copies ran while one was open for 0% of the time, Pallas kernels for 39%

profile of v9, /device:TPU:0, one launch (start us, length us, event | category | flops | bytes accessed | tf_op | source)
XLA Modules:
  0.0 80.4 jit_solution(8050920211228306253)
XLA Ops:
  0.7 4.1 %collective-permute-start = (bf16[64,16,128]{2,1,0:T(8,128)(2,1)}, bf16[64,16,128]{2,1,0:T(8,128)(2,1)S(1)}, u32[]{:S(2)}, u32[]{:S(2)}) collective-permute-start(bf16[64,16,128]{2,1,0:T(8,128)(2,1)} %raw.2), channel_id=1, source_target_pairs={{0,4},{2,6},{4,0},{6,2},{1,5},{3,7},{5,1},{7,3},{8,12},{10,14},{12... | collective-permute-start | bytes 786440 | tf_op jit(solution)/shard_map/ppermute | solution.py:369
  4.8 2.4 %collective-permute-start.3 = (bf16[32,16,128]{2,1,0:T(8,128)(2,1)}, bf16[32,16,128]{2,1,0:T(8,128)(2,1)S(1)}, u32[]{:S(2)}, u32[]{:S(2)}) collective-permute-start(bf16[32,16,128]{2,1,0:T(8,128)(2,1)} %raw.3), channel_id=1, source_target_pairs={{0,24},{8,16},{16,8},{24,0},{1,25},{9,17},{17,9},{25,1},{2,26},{10... | collective-permute-start | bytes 393224 | tf_op jit(solution)/shard_map/ppermute | solution.py:369
  7.2 0.5 collective-permute-start.2
  7.7 0.5 collective-permute-start.1
  8.3 1.6 %collective-permute-start.6 = (bf16[64,16,128]{2,1,0:T(8,128)(2,1)}, bf16[64,16,128]{2,1,0:T(8,128)(2,1)S(1)}, u32[]{:S(2)}, u32[]{:S(2)}) collective-permute-start(bf16[64,16,128]{2,1,0:T(8,128)(2,1)} %raw.2), channel_id=1, source_target_pairs={{0,2},{2,0},{4,6},{6,4},{1,3},{3,1},{5,7},{7,5},{8,10},{10,8},{12,... | collective-permute-start | bytes 786440 | tf_op jit(solution)/shard_map/ppermute | solution.py:369
  9.9 0.0 copy-start.4
  9.9 2.6 %middle.3 = (f32[64,32,128]{2,1,0:T(8,128)S(1)}, bf16[64,32,128]{2,1,0:T(8,128)(2,1)S(1)}, bf16[64,32,128]{2,1,0:T(8,128)(2,1)S(1)}, f32[64,32,128]{2,1,0:T(8,128)S(1)}) custom-call(bf16[64,32,128]{2,1,0:T(8,128)(2,1)S(1)} %copy-done.2, bf16[64,32,128]{2,1,0:T(8,128)(2,1)S(1)} %copy-done.3, bf16[128,128]{1,0:T(8,128)(2,1)S(1)} %copy-done.7, ...), custom_call_target="tpu_custom_call" | custom-call | flops 1000 | bytes 1000 | tf_op jit(solution)/shard_map/middle/pallas_call | solution.py:459
  12.5 1.1 %collective-permute-done.2.refs_2_ = bf16[32,16,128]{2,1,0:T(8,128)(2,1)S(1)} collective-permute-done((bf16[32,16,128]{2,1,0:T(8,128)(2,1)}, bf16[32,16,128]{2,1,0:T(8,128)(2,1)S(1)}, u32[]{:S(2)}, u32[]{:S(2)}) %collective-permute-start.2) | collective-permute-done | bytes 131104 | tf_op jit(solution)/shard_map/ppermute | solution.py:369
  13.7 0.1 collective-permute-done.1.refs_1_
  13.7 1.9 %right.1 = (f32[2048,128]{1,0:T(8,128)S(1)}, bf16[4,32,16,128]{3,2,1,0:T(8,128)(2,1)S(1)}, f32[16,32,128]{2,1,0:T(8,128)S(1)}, f32[16,32,128]{2,1,0:T(8,128)S(1)...) custom-call(bf16[32,16,128]{2,1,0:T(8,128)(2,1)S(1)} %copy-done.5, ...), custom_call_target="tpu_custom_call" | custom-call | flops 1000 | bytes 1000 | tf_op jit(solution)/shard_map/right/pallas_call | solution.py:459
  15.6 1.4 %collective-permute-done.refs_0_ = bf16[64,16,128]{2,1,0:T(8,128)(2,1)S(1)} collective-permute-done((bf16[64,16,128]{2,1,0:T(8,128)(2,1)}, bf16[64,16,128]{2,1,0:T(8,128)(2,1)S(1)}, u32[]{:S(2)}, u32[]{:S(2)}) %collective-permute-start) | collective-permute-done | bytes 262176 | tf_op jit(solution)/shard_map/ppermute | solution.py:369
  17.1 1.3 %collective-permute-start.4 = (bf16[64,16,128]{2,1,0:T(8,128)(2,1)S(1)}, bf16[64,16,128]{2,1,0:T(8,128)(2,1)S(1)}, u32[]{:S(2)}, u32[]{:S(2)}) collective-permute-start(bf16[64,16,128]{2,1,0:T(8,128)(2,1)S(1)} %get-tuple-element.61), channel_id=1, source_target_pairs={{2,0},{4,6},{3,1},{5,7},{10,8},{12,14},{11,9},{13,15},{18,16},{20,... | collective-permute-start | bytes 786440 | tf_op jit(solution)/shard_map/ppermute | solution.py:406
  18.4 0.9 %collective-permute-start.5 = (bf16[64,16,128]{2,1,0:T(8,128)(2,1)S(1)}, bf16[64,16,128]{2,1,0:T(8,128)(2,1)S(1)}, u32[]{:S(2)}, u32[]{:S(2)}) collective-permute-start(bf16[64,16,128]{2,1,0:T(8,128)(2,1)S(1)} %get-tuple-element.62), channel_id=1, source_target_pairs={{2,4},{4,2},{3,5},{5,3},{10,12},{12,10},{11,13},{13,11},{18,20},{2... | collective-permute-start | bytes 786440 | tf_op jit(solution)/shard_map/ppermute | solution.py:407
  19.2 2.0 %left.3 = (f32[64,16,128]{2,1,0:T(8,128)S(1)}, bf16[64,16,128]{2,1,0:T(8,128)(2,1)S(1)}, f32[64,32,128]{2,1,0:T(8,128)S(1)}) custom-call(bf16[64,16,128]{2,1,0:T(8,128)(2,1)S(1)} %copy-done, bf16[128,256]{1,0:T(8,128)(2,1)S(1)} %copy-done.1, f32[16,32,128]{2,1,0:T(8,128)S(1)} %get-tuple-element.67.refs_2_), custom_call_target="tpu_custom_call" | custom-call | flops 1000 | bytes 1000 | tf_op jit(solution)/shard_map/left/pallas_call | solution.py:459
  21.2 2.0 %left.4 = (f32[64,16,128]{2,1,0:T(8,128)S(1)}, bf16[64,16,128]{2,1,0:T(8,128)(2,1)S(1)}, f32[64,32,128]{2,1,0:T(8,128)S(1)}) custom-call(bf16[64,16,128]{2,1,0:T(8,128)(2,1)S(1)} %collective-permute-done.6.refs_0_, bf16[128,256]{1,0:T(8,128)(2,1)S(1)} %copy-done.1, f32[16,32,128]{2,1,0:T(8,128)S(1)} %get-tuple-element.66.refs_2_, ...), custom_call_target="tpu_custom_call" | custom-call | flops 1000 | bytes 1000 | tf_op jit(solution)/shard_map/left/pallas_call | solution.py:459
  23.3 2.0 %left.5 = (f32[64,16,128]{2,1,0:T(8,128)S(1)}, bf16[64,16,128]{2,1,0:T(8,128)(2,1)S(1)}, f32[64,32,128]{2,1,0:T(8,128)S(1)}) custom-call(bf16[64,16,128]{2,1,0:T(8,128)(2,1)S(1)} %collective-permute-done.refs_0_, bf16[128,256]{1,0:T(8,128)(2,1)S(1)} %copy-done.1, f32[16,32,128]{2,1,0:T(8,128)S(1)} %get-tuple-element.65.refs_2_, ...), custom_call_target="tpu_custom_call" | custom-call | flops 1000 | bytes 1000 | tf_op jit(solution)/shard_map/left/pallas_call | solution.py:459
  25.3 1.1 %collective-permute-done.4.refs_0_ = bf16[64,16,128]{2,1,0:T(8,128)(2,1)S(1)} collective-permute-done((bf16[64,16,128]{2,1,0:T(8,128)(2,1)S(1)}, bf16[64,16,128]{2,1,0:T(8,128)(2,1)S(1)}, u32[]{:S(2)}, u32[]{:S(2)}) %collective-permute-start.4) | collective-permute-done | bytes 262176 | tf_op jit(solution)/shard_map/ppermute | solution.py:406
  26.4 3.4 %triangle.1 = (f32[64,16,128]{2,1,0:T(8,128)S(1)}, bf16[64,16,128]{2,1,0:T(8,128)(2,1)S(1)}, bf16[64,32,128]{2,1,0:T(8,128)(2,1)S(1)}, f32[64,32,128]{2,1,0:T(8,128)S(1)}) custom-call(bf16[64,16,128]{2,1,0:T(8,128)(2,1)S(1)} %collective-permute-done.4.refs_0_, bf16[64,16,128]{2,1,0:T(8,128)(2,1)S(1)} %collective-permute-done.5.refs_1_, ...), custom_call_target="tpu_custom_call" | custom-call | flops 1000 | bytes 1000 | tf_op jit(solution)/shard_map/triangle/pallas_call | solution.py:459
  29.8 2.3 %left_back.3 = (bf16[64,16,128]{2,1,0:T(8,128)(2,1)S(1)}, bf16[64,16,128]{2,1,0:T(8,128)(2,1)S(1)}) custom-call(f32[64,32,128]{2,1,0:T(8,128)S(1)} %get-tuple-element.74.tri_back, f32[2048,128]{1,0:T(8,128)S(1)} %get-tuple-element.75.right_act), custom_call_target="tpu_custom_call" | custom-call | flops 1000 | bytes 1000 | tf_op jit(solution)/shard_map/left_back/pallas_call | solution.py:459
  32.1 6.5 %collective-permute-start.8 = (bf16[64,16,128]{2,1,0:T(8,128)(2,1)S(1)}, bf16[64,16,128]{2,1,0:T(8,128)(2,1)S(1)}, u32[]{:S(2)}, u32[]{:S(2)}) collective-permute-start(bf16[64,16,128]{2,1,0:T(8,128)(2,1)S(1)} %get-tuple-element.79.refs_6_), channel_id=1, source_target_pairs={{0,4},{2,6},{4,0},{6,2},{1,5},{3,7},{5,1},{7,3},{8,12},{10,14},{12... | collective-permute-start | bytes 786440 | tf_op jit(solution)/shard_map/ppermute | solution.py:369
  38.7 1.3 %collective-permute-start.9 = (bf16[64,16,128]{2,1,0:T(8,128)(2,1)S(1)}, bf16[64,16,128]{2,1,0:T(8,128)(2,1)S(1)}, u32[]{:S(2)}, u32[]{:S(2)}) collective-permute-start(bf16[64,16,128]{2,1,0:T(8,128)(2,1)S(1)} %get-tuple-element.80.refs_7_), channel_id=1, source_target_pairs={{0,6},{2,4},{4,2},{6,0},{1,7},{3,5},{5,3},{7,1},{8,14},{10,12},{12... | collective-permute-start | bytes 786440 | tf_op jit(solution)/shard_map/ppermute | solution.py:369
  40.0 2.3 %left_back.2 = (bf16[64,16,128]{2,1,0:T(8,128)(2,1)S(1)}, bf16[64,16,128]{2,1,0:T(8,128)(2,1)S(1)}) custom-call(f32[64,32,128]{2,1,0:T(8,128)S(1)} %get-tuple-element.74.tri_back, f32[2048,128]{1,0:T(8,128)S(1)} %get-tuple-element.75.right_act), custom_call_target="tpu_custom_call" | custom-call | flops 1000 | bytes 1000 | tf_op jit(solution)/shard_map/left_back/pallas_call | solution.py:459
  42.4 0.1 collective-permute-start.7
  42.4 5.5 %right_back.1 = (bf16[2,32,16,128]{3,2,1,0:T(8,128)(2,1)S(1)}, bf16[2,32,16,128]{3,2,1,0:T(8,128)(2,1)S(1)}) custom-call(f32[64,32,128]{2,1,0:T(8,128)S(1)} %get-tuple-element.74.tri_back, f32[64,16,128]{2,1,0:T(8,128)S(1)} %get-tuple-element.82.refs_0_, f32[64,16,128]{2,1,0:T(8,128)S(1)} %get-tuple-element.83.refs_1_, ...), custom_call_target="tpu_custom_call" | custom-call | flops 1000 | bytes 1000 | tf_op jit(solution)/shard_map/right_back/pallas_call | solution.py:459
  48.0 1.6 %collective-permute-start.10 = (bf16[2,32,16,128]{3,2,1,0:T(8,128)(2,1)S(1)}, bf16[2,32,16,128]{3,2,1,0:T(8,128)(2,1)S(1)}, u32[]{:S(2)}, u32[]{:S(2)}) collective-permute-start(bf16[2,32,16,128]{3,2,1,0:T(8,128)(2,1)S(1)} %get-tuple-element.87.refs_9_), channel_id=1, source_target_pairs={{0,8},{8,0},{16,24},{24,16},{1,9},{9,1},{17,25},{25,17},{2,10},{10... | collective-permute-start | bytes 786440 | tf_op jit(solution)/shard_map/ppermute | solution.py:369
  49.5 2.7 %heads.1 = (bf16[64,32,128]{2,1,0:T(8,128)(2,1)}, bf16[64,32,128]{2,1,0:T(8,128)(2,1)S(1)}, f32[128,128]{1,0:T(8,128)S(1)}, f32[128,128]{1,0:T(8,128)S(1)}) custom-call(bf16[64,32,128]{2,1,0:T(8,128)(2,1)S(1)} %get-tuple-element.71.tri_in, bf16[128,128]{1,0:T(8,128)(2,1)S(1)} %copy-done.6, f32[64,32,128]{2,1,0:T(8,128)S(1)} %get-tuple-element.72.gate, ...), custom_call_target="tpu_custom_call" | custom-call | flops 1000 | bytes 1000 | tf_op jit(solution)/shard_map/heads/pallas_call | solution.py:459
  52.2 4.3 %weights.1 = (f32[2,32,768]{2,1,0:T(8,128)S(1)}, bf16[2,32,768]{2,1,0:T(8,128)(2,1)S(1)}) custom-call(bf16[4,32,16,128]{3,2,1,0:T(8,128)(2,1)S(1)} %get-tuple-element.59.refs_2_.right_in, bf16[128,256]{1,0:T(8,128)(2,1)S(1)} %copy-done.1, bf16[128,256]{1,0:T(8,128)(2,1)S(1)} %copy-done.4, f32[128,128]{1,0:T(8,128)S(1)} %get-tuple-element.92.gate_part, ...), custom_call_target="tpu_custom_call" | custom-call | flops 1000 | bytes 1000 | tf_op jit(solution)/shard_map/weights/pallas_call | solution.py:459
  56.5 0.6 collective-permute-start.12
  57.1 2.5 %grad_middle.1 = (bf16[64,32,128]{2,1,0:T(8,128)(2,1)}, f32[8,128]{1,0:T(8,128)S(1)}) custom-call(bf16[64,32,128]{2,1,0:T(8,128)(2,1)S(1)} %copy-done.2, bf16[64,32,128]{2,1,0:T(8,128)(2,1)S(1)} %get-tuple-element.91.pre_back, bf16[128,128]{1,0:T(8,128)(2,1)S(1)} %copy-done.7, bf16[2,32,768]{2,1,0:T(8,128)(2,1)S(1)} %get-tuple-element.98._), custom_call_target="tpu_custom_call" | custom-call | flops 1000 | bytes 1000 | tf_op jit(solution)/shard_map/grad_middle/pallas_call | solution.py:459
  59.6 1.6 %collective-permute-done.12.came = bf16[2,32,768]{2,1,0:T(8,128)(2,1)S(1)} collective-permute-done((bf16[2,32,768]{2,1,0:T(8,128)(2,1)S(1)}, bf16[2,32,768]{2,1,0:T(8,128)(2,1)S(1)}, u32[]{:S(2)}, u32[]{:S(2)}) %collective-permute-start.12) | collective-permute-done | bytes 98336 | tf_op jit(solution)/shard_map/ppermute | solution.py:369
  61.2 1.6 %collective-permute-start.13 = (bf16[1,32,768]{2,1,0:T(8,128)(2,1)S(1)}, bf16[1,32,768]{2,1,0:T(8,128)(2,1)S(1)}, u32[]{:S(2)}, u32[]{:S(2)}) collective-permute-start(bf16[1,32,768]{2,1,0:T(8,128)(2,1)S(1)} %get-tuple-element.103), channel_id=1, source_target_pairs={{0,16},{8,24},{16,0},{24,8},{1,17},{9,25},{17,1},{25,9},{2,18},{10... | collective-permute-start | bytes 147464 | tf_op jit(solution)/shard_map/ppermute | solution.py:369
  62.9 0.1 halve.2
  62.9 0.6 collective-permute-start.11
  63.5 1.9 %collective-permute-done.13.refs_1_ = bf16[1,32,768]{2,1,0:T(8,128)(2,1)S(1)} collective-permute-done((bf16[1,32,768]{2,1,0:T(8,128)(2,1)S(1)}, bf16[1,32,768]{2,1,0:T(8,128)(2,1)S(1)}, u32[]{:S(2)}, u32[]{:S(2)}) %collective-permute-start.13) | collective-permute-done | bytes 49184 | tf_op jit(solution)/shard_map/ppermute | solution.py:369
  65.4 2.5 %collective-permute-start.16 = (bf16[1,32,768]{2,1,0:T(8,128)(2,1)S(1)}, bf16[1,32,768]{2,1,0:T(8,128)(2,1)S(1)}, u32[]{:S(2)}, u32[]{:S(2)}) collective-permute-start(bf16[1,32,768]{2,1,0:T(8,128)(2,1)S(1)} %combine.2.refs_0_), channel_id=1, source_target_pairs={{0,6},{2,4},{4,2},{6,0},{1,7},{3,5},{5,3},{7,1},{8,14},{10,12},{12... | collective-permute-start | bytes 147464 | tf_op jit(solution)/shard_map/ppermute | solution.py:369
  67.9 1.0 %collective-permute-start.15 = (bf16[1,32,768]{2,1,0:T(8,128)(2,1)S(1)}, bf16[1,32,768]{2,1,0:T(8,128)(2,1)S(1)}, u32[]{:S(2)}, u32[]{:S(2)}) collective-permute-start(bf16[1,32,768]{2,1,0:T(8,128)(2,1)S(1)} %combine.2.refs_0_), channel_id=1, source_target_pairs={{0,4},{2,6},{4,0},{6,2},{1,5},{3,7},{5,1},{7,3},{8,12},{10,14},{12... | collective-permute-start | bytes 147464 | tf_op jit(solution)/shard_map/ppermute | solution.py:369
  68.9 0.9 %collective-permute-start.14 = (bf16[1,32,768]{2,1,0:T(8,128)(2,1)S(1)}, bf16[1,32,768]{2,1,0:T(8,128)(2,1)S(1)}, u32[]{:S(2)}, u32[]{:S(2)}) collective-permute-start(bf16[1,32,768]{2,1,0:T(8,128)(2,1)S(1)} %combine.2.refs_0_), channel_id=1, source_target_pairs={{0,2},{2,0},{4,6},{6,4},{1,3},{3,1},{5,7},{7,5},{8,10},{10,8},{12,... | collective-permute-start | bytes 147464 | tf_op jit(solution)/shard_map/ppermute | solution.py:369
  69.9 2.1 %left_side.1 = (bf16[64,16,128]{2,1,0:T(8,128)(2,1)}, f32[8,128]{1,0:T(8,128)S(1)}) custom-call(bf16[64,16,128]{2,1,0:T(8,128)(2,1)S(1)} %copy-done, bf16[128,256]{1,0:T(8,128)(2,1)S(1)} %copy-done.1, bf16[64,16,128]{2,1,0:T(8,128)(2,1)S(1)} %get-tuple-element.76._.refs_0_.refs_4_, bf16[64,16,128]{2,1,0:T(8,128)(2,1)S(1)} %collective-permute-done.7.refs_1_.refs_0_, ...), custom_call_target="tpu_custom_call" | custom-call | flops 1000 | bytes 1000 | tf_op jit(solution)/shard_map/left_side/pallas_call | solution.py:459
  72.0 1.0 %collective-permute-done.15.refs_2_ = bf16[1,32,768]{2,1,0:T(8,128)(2,1)S(1)} collective-permute-done((bf16[1,32,768]{2,1,0:T(8,128)(2,1)S(1)}, bf16[1,32,768]{2,1,0:T(8,128)(2,1)S(1)}, u32[]{:S(2)}, u32[]{:S(2)}) %collective-permute-start.15) | collective-permute-done | bytes 49184 | tf_op jit(solution)/shard_map/ppermute | solution.py:369
  73.0 0.5 collective-permute-done.14.refs_1_
  73.5 1.6 %collective-permute-start.19 = (bf16[1,32,768]{2,1,0:T(8,128)(2,1)S(1)}, bf16[1,32,768]{2,1,0:T(8,128)(2,1)S(1)}, u32[]{:S(2)}, u32[]{:S(2)}) collective-permute-start(bf16[1,32,768]{2,1,0:T(8,128)(2,1)S(1)} %combine.3.refs_0_), channel_id=1, source_target_pairs={{0,24},{8,16},{16,8},{24,0},{1,25},{9,17},{17,9},{25,1},{2,26},{10... | collective-permute-start | bytes 147464 | tf_op jit(solution)/shard_map/ppermute | solution.py:369
  75.1 0.5 collective-permute-start.18
  75.6 1.5 %collective-permute-start.17 = (bf16[1,32,768]{2,1,0:T(8,128)(2,1)S(1)}, bf16[1,32,768]{2,1,0:T(8,128)(2,1)S(1)}, u32[]{:S(2)}, u32[]{:S(2)}) collective-permute-start(bf16[1,32,768]{2,1,0:T(8,128)(2,1)S(1)} %combine.3.refs_0_), channel_id=1, source_target_pairs={{0,8},{8,0},{16,24},{24,16},{1,9},{9,1},{17,25},{25,17},{2,10},{10... | collective-permute-start | bytes 147464 | tf_op jit(solution)/shard_map/ppermute | solution.py:369
  77.1 1.5 %right_side.1 = (bf16[32,16,128]{2,1,0:T(8,128)(2,1)}, f32[8,128]{1,0:T(8,128)S(1)}) custom-call(bf16[32,16,128]{2,1,0:T(8,128)(2,1)S(1)} %copy-done.5, bf16[128,256]{1,0:T(8,128)(2,1)S(1)} %copy-done.4, f32[32,16,128]{2,1,0:T(8,128)S(1)} %bitcast.2, bf16[32,16,128]{2,1,0:T(8,128)(2,1)S(1)} %bitcast.3), custom_call_target="tpu_custom_call" | custom-call | flops 1000 | bytes 1000 | tf_op jit(solution)/shard_map/right_side/pallas_call | solution.py:459
  78.5 0.0 collective-permute-done.19.refs_3_
  78.5 0.6 collective-permute-done.18.refs_2_
  79.1 0.5 collective-permute-done.17.refs_1_
  79.7 0.8 deltas.1
  (31 shorter events, 0.2 us)
Async XLA Ops:
  0.6 9.2 %copy-start.6 = (bf16[128,128]{1,0:T(8,128)(2,1)S(1)}, bf16[128,128]{1,0:T(8,128)(2,1)}, u32[]{:S(2)}) copy-start(bf16[128,128]{1,0:T(8,128)(2,1)} %out_w.1) | copy-start | bytes 98308
  0.6 9.2 %copy-start.7 = (bf16[128,128]{1,0:T(8,128)(2,1)S(1)}, bf16[128,128]{1,0:T(8,128)(2,1)}, u32[]{:S(2)}) copy-start(bf16[128,128]{1,0:T(8,128)(2,1)} %gate_weight.3) | copy-start | bytes 98308
  0.7 9.2 %copy-start.3 = (bf16[64,32,128]{2,1,0:T(8,128)(2,1)S(1)}, bf16[64,32,128]{2,1,0:T(8,128)(2,1)}, u32[]{:S(2)}) copy-start(bf16[64,32,128]{2,1,0:T(8,128)(2,1)} %cotangent.3) | copy-start | bytes 1572868
  0.7 9.2 %copy-start.2 = (bf16[64,32,128]{2,1,0:T(8,128)(2,1)S(1)}, bf16[64,32,128]{2,1,0:T(8,128)(2,1)}, u32[]{:S(2)}) copy-start(bf16[64,32,128]{2,1,0:T(8,128)(2,1)} %middle.5) | copy-start | bytes 1572868
  0.7 16.3 %collective-permute-start = (bf16[64,16,128]{2,1,0:T(8,128)(2,1)}, bf16[64,16,128]{2,1,0:T(8,128)(2,1)S(1)}, u32[]{:S(2)}, u32[]{:S(2)}) collective-permute-start(bf16[64,16,128]{2,1,0:T(8,128)(2,1)} %raw.2), channel_id=1, source_target_pairs={{0,4},{2,6},{4,0},{6,2},{1,5},{3,7},{5,1},{7,3},{8,12},{10,14},{12... | collective-permute-start | bytes 786440 | tf_op jit(solution)/shard_map/ppermute | solution.py:369
  4.8 7.7 %collective-permute-start.3 = (bf16[32,16,128]{2,1,0:T(8,128)(2,1)}, bf16[32,16,128]{2,1,0:T(8,128)(2,1)S(1)}, u32[]{:S(2)}, u32[]{:S(2)}) collective-permute-start(bf16[32,16,128]{2,1,0:T(8,128)(2,1)} %raw.3), channel_id=1, source_target_pairs={{0,24},{8,16},{16,8},{24,0},{1,25},{9,17},{17,9},{25,1},{2,26},{10... | collective-permute-start | bytes 393224 | tf_op jit(solution)/shard_map/ppermute | solution.py:369
  7.2 6.4 %collective-permute-start.2 = (bf16[32,16,128]{2,1,0:T(8,128)(2,1)}, bf16[32,16,128]{2,1,0:T(8,128)(2,1)S(1)}, u32[]{:S(2)}, u32[]{:S(2)}) collective-permute-start(bf16[32,16,128]{2,1,0:T(8,128)(2,1)} %raw.3), channel_id=1, source_target_pairs={{0,16},{8,24},{16,0},{24,8},{1,17},{9,25},{17,1},{25,9},{2,18},{10... | collective-permute-start | bytes 393224 | tf_op jit(solution)/shard_map/ppermute | solution.py:369
  7.7 6.0 %collective-permute-start.1 = (bf16[32,16,128]{2,1,0:T(8,128)(2,1)}, bf16[32,16,128]{2,1,0:T(8,128)(2,1)S(1)}, u32[]{:S(2)}, u32[]{:S(2)}) collective-permute-start(bf16[32,16,128]{2,1,0:T(8,128)(2,1)} %raw.3), channel_id=1, source_target_pairs={{0,8},{8,0},{16,24},{24,16},{1,9},{9,1},{17,25},{25,17},{2,10},{10... | collective-permute-start | bytes 393224 | tf_op jit(solution)/shard_map/ppermute | solution.py:369
  8.3 13.0 %collective-permute-start.6 = (bf16[64,16,128]{2,1,0:T(8,128)(2,1)}, bf16[64,16,128]{2,1,0:T(8,128)(2,1)S(1)}, u32[]{:S(2)}, u32[]{:S(2)}) collective-permute-start(bf16[64,16,128]{2,1,0:T(8,128)(2,1)} %raw.2), channel_id=1, source_target_pairs={{0,2},{2,0},{4,6},{6,4},{1,3},{3,1},{5,7},{7,5},{8,10},{10,8},{12,... | collective-permute-start | bytes 786440 | tf_op jit(solution)/shard_map/ppermute | solution.py:369
  9.9 3.9 %copy-start.4 = (bf16[128,256]{1,0:T(8,128)(2,1)S(1)}, bf16[128,256]{1,0:T(8,128)(2,1)}, u32[]{:S(2)}) copy-start(bf16[128,256]{1,0:T(8,128)(2,1)} %right_w.1) | copy-start | bytes 196612
  9.9 3.8 %copy-start.5 = (bf16[32,16,128]{2,1,0:T(8,128)(2,1)S(1)}, bf16[32,16,128]{2,1,0:T(8,128)(2,1)}, u32[]{:S(2)}) copy-start(bf16[32,16,128]{2,1,0:T(8,128)(2,1)} %raw.3) | copy-start | bytes 393220
  12.5 4.5 %copy-start = (bf16[64,16,128]{2,1,0:T(8,128)(2,1)S(1)}, bf16[64,16,128]{2,1,0:T(8,128)(2,1)}, u32[]{:S(2)}) copy-start(bf16[64,16,128]{2,1,0:T(8,128)(2,1)} %raw.2) | copy-start | bytes 786436
  17.0 2.2 %copy-start.1 = (bf16[128,256]{1,0:T(8,128)(2,1)S(1)}, bf16[128,256]{1,0:T(8,128)(2,1)}, u32[]{:S(2)}) copy-start(bf16[128,256]{1,0:T(8,128)(2,1)} %left_w.1) | copy-start | bytes 196612
  17.1 9.3 %collective-permute-start.4 = (bf16[64,16,128]{2,1,0:T(8,128)(2,1)S(1)}, bf16[64,16,128]{2,1,0:T(8,128)(2,1)S(1)}, u32[]{:S(2)}, u32[]{:S(2)}) collective-permute-start(bf16[64,16,128]{2,1,0:T(8,128)(2,1)S(1)} %get-tuple-element.61), channel_id=1, source_target_pairs={{2,0},{4,6},{3,1},{5,7},{10,8},{12,14},{11,9},{13,15},{18,16},{20,... | collective-permute-start | bytes 786440 | tf_op jit(solution)/shard_map/ppermute | solution.py:406
  18.4 8.0 %collective-permute-start.5 = (bf16[64,16,128]{2,1,0:T(8,128)(2,1)S(1)}, bf16[64,16,128]{2,1,0:T(8,128)(2,1)S(1)}, u32[]{:S(2)}, u32[]{:S(2)}) collective-permute-start(bf16[64,16,128]{2,1,0:T(8,128)(2,1)S(1)} %get-tuple-element.62), channel_id=1, source_target_pairs={{2,4},{4,2},{3,5},{5,3},{10,12},{12,10},{11,13},{13,11},{18,20},{2... | collective-permute-start | bytes 786440 | tf_op jit(solution)/shard_map/ppermute | solution.py:407
  32.1 30.7 %collective-permute-start.8 = (bf16[64,16,128]{2,1,0:T(8,128)(2,1)S(1)}, bf16[64,16,128]{2,1,0:T(8,128)(2,1)S(1)}, u32[]{:S(2)}, u32[]{:S(2)}) collective-permute-start(bf16[64,16,128]{2,1,0:T(8,128)(2,1)S(1)} %get-tuple-element.79.refs_6_), channel_id=1, source_target_pairs={{0,4},{2,6},{4,0},{6,2},{1,5},{3,7},{5,1},{7,3},{8,12},{10,14},{12... | collective-permute-start | bytes 786440 | tf_op jit(solution)/shard_map/ppermute | solution.py:369
  38.7 24.2 %collective-permute-start.9 = (bf16[64,16,128]{2,1,0:T(8,128)(2,1)S(1)}, bf16[64,16,128]{2,1,0:T(8,128)(2,1)S(1)}, u32[]{:S(2)}, u32[]{:S(2)}) collective-permute-start(bf16[64,16,128]{2,1,0:T(8,128)(2,1)S(1)} %get-tuple-element.80.refs_7_), channel_id=1, source_target_pairs={{0,6},{2,4},{4,2},{6,0},{1,7},{3,5},{5,3},{7,1},{8,14},{10,12},{12... | collective-permute-start | bytes 786440 | tf_op jit(solution)/shard_map/ppermute | solution.py:369
  42.4 20.5 %collective-permute-start.7 = (bf16[64,16,128]{2,1,0:T(8,128)(2,1)S(1)}, bf16[64,16,128]{2,1,0:T(8,128)(2,1)S(1)}, u32[]{:S(2)}, u32[]{:S(2)}) collective-permute-start(bf16[64,16,128]{2,1,0:T(8,128)(2,1)S(1)} %get-tuple-element.78.refs_5_), channel_id=1, source_target_pairs={{0,2},{2,0},{4,6},{6,4},{1,3},{3,1},{5,7},{7,5},{8,10},{10,8},{12,... | collective-permute-start | bytes 786440 | tf_op jit(solution)/shard_map/ppermute | solution.py:369
  48.0 14.9 %collective-permute-start.10 = (bf16[2,32,16,128]{3,2,1,0:T(8,128)(2,1)S(1)}, bf16[2,32,16,128]{3,2,1,0:T(8,128)(2,1)S(1)}, u32[]{:S(2)}, u32[]{:S(2)}) collective-permute-start(bf16[2,32,16,128]{3,2,1,0:T(8,128)(2,1)S(1)} %get-tuple-element.87.refs_9_), channel_id=1, source_target_pairs={{0,8},{8,0},{16,24},{24,16},{1,9},{9,1},{17,25},{25,17},{2,10},{10... | collective-permute-start | bytes 786440 | tf_op jit(solution)/shard_map/ppermute | solution.py:369
  56.5 4.7 %collective-permute-start.12 = (bf16[2,32,768]{2,1,0:T(8,128)(2,1)S(1)}, bf16[2,32,768]{2,1,0:T(8,128)(2,1)S(1)}, u32[]{:S(2)}, u32[]{:S(2)}) collective-permute-start(bf16[2,32,768]{2,1,0:T(8,128)(2,1)S(1)} %get-tuple-element.98._), channel_id=1, source_target_pairs={{0,8},{8,0},{16,24},{24,16},{1,9},{9,1},{17,25},{25,17},{2,10},{10... | collective-permute-start | bytes 294920 | tf_op jit(solution)/shard_map/ppermute | solution.py:369
  61.2 4.2 %collective-permute-start.13 = (bf16[1,32,768]{2,1,0:T(8,128)(2,1)S(1)}, bf16[1,32,768]{2,1,0:T(8,128)(2,1)S(1)}, u32[]{:S(2)}, u32[]{:S(2)}) collective-permute-start(bf16[1,32,768]{2,1,0:T(8,128)(2,1)S(1)} %get-tuple-element.103), channel_id=1, source_target_pairs={{0,16},{8,24},{16,0},{24,8},{1,17},{9,25},{17,1},{25,9},{2,18},{10... | collective-permute-start | bytes 147464 | tf_op jit(solution)/shard_map/ppermute | solution.py:369
  62.9 14.1 %collective-permute-start.11 = (bf16[1,32,16,128]{3,2,1,0:T(8,128)(2,1)S(1)}, bf16[1,32,16,128]{3,2,1,0:T(8,128)(2,1)S(1)}, u32[]{:S(2)}, u32[]{:S(2)}) collective-permute-start(bf16[1,32,16,128]{3,2,1,0:T(8,128)(2,1)S(1)} %get-tuple-element.89.refs_0_), channel_id=1, source_target_pairs={{0,16},{8,24},{16,0},{24,8},{1,17},{9,25},{17,1},{25,9},{2,18},{10... | collective-permute-start | bytes 393224 | tf_op jit(solution)/shard_map/ppermute | solution.py:369
  65.4 6.6 %collective-permute-start.16 = (bf16[1,32,768]{2,1,0:T(8,128)(2,1)S(1)}, bf16[1,32,768]{2,1,0:T(8,128)(2,1)S(1)}, u32[]{:S(2)}, u32[]{:S(2)}) collective-permute-start(bf16[1,32,768]{2,1,0:T(8,128)(2,1)S(1)} %combine.2.refs_0_), channel_id=1, source_target_pairs={{0,6},{2,4},{4,2},{6,0},{1,7},{3,5},{5,3},{7,1},{8,14},{10,12},{12... | collective-permute-start | bytes 147464 | tf_op jit(solution)/shard_map/ppermute | solution.py:369
  67.9 5.0 %collective-permute-start.15 = (bf16[1,32,768]{2,1,0:T(8,128)(2,1)S(1)}, bf16[1,32,768]{2,1,0:T(8,128)(2,1)S(1)}, u32[]{:S(2)}, u32[]{:S(2)}) collective-permute-start(bf16[1,32,768]{2,1,0:T(8,128)(2,1)S(1)} %combine.2.refs_0_), channel_id=1, source_target_pairs={{0,4},{2,6},{4,0},{6,2},{1,5},{3,7},{5,1},{7,3},{8,12},{10,14},{12... | collective-permute-start | bytes 147464 | tf_op jit(solution)/shard_map/ppermute | solution.py:369
  68.9 4.5 %collective-permute-start.14 = (bf16[1,32,768]{2,1,0:T(8,128)(2,1)S(1)}, bf16[1,32,768]{2,1,0:T(8,128)(2,1)S(1)}, u32[]{:S(2)}, u32[]{:S(2)}) collective-permute-start(bf16[1,32,768]{2,1,0:T(8,128)(2,1)S(1)} %combine.2.refs_0_), channel_id=1, source_target_pairs={{0,2},{2,0},{4,6},{6,4},{1,3},{3,1},{5,7},{7,5},{8,10},{10,8},{12,... | collective-permute-start | bytes 147464 | tf_op jit(solution)/shard_map/ppermute | solution.py:369
  73.5 5.1 %collective-permute-start.19 = (bf16[1,32,768]{2,1,0:T(8,128)(2,1)S(1)}, bf16[1,32,768]{2,1,0:T(8,128)(2,1)S(1)}, u32[]{:S(2)}, u32[]{:S(2)}) collective-permute-start(bf16[1,32,768]{2,1,0:T(8,128)(2,1)S(1)} %combine.3.refs_0_), channel_id=1, source_target_pairs={{0,24},{8,16},{16,8},{24,0},{1,25},{9,17},{17,9},{25,1},{2,26},{10... | collective-permute-start | bytes 147464 | tf_op jit(solution)/shard_map/ppermute | solution.py:369
  75.1 4.1 %collective-permute-start.18 = (bf16[1,32,768]{2,1,0:T(8,128)(2,1)S(1)}, bf16[1,32,768]{2,1,0:T(8,128)(2,1)S(1)}, u32[]{:S(2)}, u32[]{:S(2)}) collective-permute-start(bf16[1,32,768]{2,1,0:T(8,128)(2,1)S(1)} %combine.3.refs_0_), channel_id=1, source_target_pairs={{0,16},{8,24},{16,0},{24,8},{1,17},{9,25},{17,1},{25,9},{2,18},{10... | collective-permute-start | bytes 147464 | tf_op jit(solution)/shard_map/ppermute | solution.py:369
  75.6 4.1 %collective-permute-start.17 = (bf16[1,32,768]{2,1,0:T(8,128)(2,1)S(1)}, bf16[1,32,768]{2,1,0:T(8,128)(2,1)S(1)}, u32[]{:S(2)}, u32[]{:S(2)}) collective-permute-start(bf16[1,32,768]{2,1,0:T(8,128)(2,1)S(1)} %combine.3.refs_0_), channel_id=1, source_target_pairs={{0,8},{8,0},{16,24},{24,16},{1,9},{9,1},{17,25},{25,17},{2,10},{10... | collective-permute-start | bytes 147464 | tf_op jit(solution)/shard_map/ppermute | solution.py:369

commit v10 on v9

--- a/solution.py
+++ b/solution.py
@@ -136,8 +136,10 @@
     def body(at, _):
         rows = pl.ds(at * step, step)
         raw = raws[0][rows]
-        for other in raws[1:]:
-            raw = (raw.astype(f32) + other[rows].astype(f32)).astype(bf16)
+        if len(raws) > 1:
+            place = jnp.full(raw.shape, lax.axis_index("blk"), jnp.int32)
+            inner = jnp.logical_or(place == 1, place == 2)
+            raw = jnp.where(inner, raws[1][rows].astype(f32), raw.astype(f32)).astype(bf16)
         normed, _ = normalize_raw(raw.reshape(step * k_left, width))
         inputs = normed.astype(bf16)
         in_out[rows] = inputs.reshape(step, k_left, width)
@@ -200,7 +202,7 @@
 def heads_kernel(tri_in, out_w, gate, middle_in, head_back, cotangent, _, *refs):
     update, pre_back, gate_part, output_part = refs
     n_i, n_j, width = update.shape
-    step = 8
+    step = 16
     gate_part[...] = jnp.zeros_like(gate_part)
     output_part[...] = jnp.zeros_like(output_part)
 
@@ -305,7 +307,7 @@
         columns = slice(first, first + 2 * width)
         total[:, columns] = jnp.zeros((width, 2 * width), f32)
         n, k, _ = inputs_refs[0].shape
-        step = 16
+        step = 32
         flat = step * k
         for inputs_ref, back_ref in zip(inputs_refs, backs):
 
@@ -317,7 +319,7 @@
                 total[:, columns] += dot_tn(inputs, joined_grad(back, lin, sw))
                 return 0
 
-            lax.fori_loop(0, n // step, body, 0, unroll=2)
+            lax.fori_loop(0, n // step, body, 0, unroll=True)
     size = width // n_rows
     for s in range(n_rows):
         start = pl.multiple_of(lax.bitwise_xor(lax.axis_index("rows"), s) * size, size)
@@ -403,8 +405,8 @@
     across = exchange(block, "blk", n, 2)
     beside = exchange(block, "blk", n, 1)
     passed, own = call(forward_kernel, "forward", [shape(block.shape, block.dtype)] * 2, after=len(after))(across, block, *after)
-    outer = lax.ppermute(passed, "blk", [(1, 0), (2, 3)])
-    inner = lax.ppermute(own, "blk", [(1, 2), (2, 1)])
+    outer = exchange(passed, "blk", n, 1)
+    inner = lax.ppermute(own, "blk", [(0, 0), (1, 2), (2, 1), (3, 3)])
     return [(block,), (beside,), (across,), (outer, inner)]
 
 

time: 80.6 us -> 75.8 us (0.940)
  Pallas kernels: 38.2 us -> 34.8 us
  starting transfers between devices: 31.6 us -> 30.6 us
    pallas_call x23, Pallas kernels: 38.2 us -> 34.8 us  [run(): pl.pallas_call(kernel, in_specs=[pl.BlockSpec(memory_space=space) for spa...]
    ppermute x2 -> x1, starting transfers between devices: 2.15 us -> 0.85 us  [gather_left(): inner = lax.ppermute(own, 'blk', [(0, 0), (1, 2), (2, 1), (3, 3)])]
    ppermute x2 -> x1, waiting for transfers between devices: 1.08 us -> 0.01 us  [gather_left(): inner = lax.ppermute(own, 'blk', [(0, 0), (1, 2), (2, 1), (3, 3)])]
    ppermute x18 -> x19, waiting for transfers between devices: 8.67 us -> 9.35 us  [exchange(): return lax.ppermute(x, axis, [(a, a ^ bit) for a in range(n)])]
    ppermute x18 -> x19, starting transfers between devices: 29.4 us -> 29.8 us  [exchange(): return lax.ppermute(x, axis, [(a, a ^ bit) for a in range(n)])]
  transfers between devices with their start and end apart: 20 -> 20, of which waited for: 10 -> 10; matrix products, arithmetic and copies ran while one was open for 0% -> 0% of each run, Pallas kernels for 39% -> 37%
where the time goes in v10:
time: 75.8 us; the launch traced here: 75.7 us
  Pallas kernels  34.8 us (46%)
  starting transfers between devices  30.6 us (40%)
  waiting for transfers between devices  9.36 us (12%)
  between operations  0.86 us (1%)
    pallas_call x23, Pallas kernels, run(): pl.pallas_call(kernel, in_specs=[pl.BlockSpec(memory_space=space) for spa...  34.8 us
    ppermute x19, starting transfers between devices, exchange(): return lax.ppermute(x, axis, [(a, a ^ bit) for a in range(n)])  29.8 us
    ppermute x19, waiting for transfers between devices, exchange(): return lax.ppermute(x, axis, [(a, a ^ bit) for a in range(n)])  9.35 us
  transfers between devices with their start and end apart: 20, of which 10 were waited for; matrix products, arithmetic and copies ran while one was open for 0% of the time, Pallas kernels for 37%

profile of v10, /device:TPU:0, one launch (start us, length us, event | category | flops | bytes accessed | tf_op | source)
XLA Modules:
  0.0 75.7 jit_solution(13267556730711544637)
XLA Ops:
  0.7 4.1 %collective-permute-start = (bf16[64,16,128]{2,1,0:T(8,128)(2,1)}, bf16[64,16,128]{2,1,0:T(8,128)(2,1)S(1)}, u32[]{:S(2)}, u32[]{:S(2)}) collective-permute-start(bf16[64,16,128]{2,1,0:T(8,128)(2,1)} %raw.2), channel_id=1, source_target_pairs={{0,4},{2,6},{4,0},{6,2},{1,5},{3,7},{5,1},{7,3},{8,12},{10,14},{12... | collective-permute-start | bytes 786440 | tf_op jit(solution)/shard_map/ppermute | solution.py:371
  4.8 2.4 %collective-permute-start.3 = (bf16[32,16,128]{2,1,0:T(8,128)(2,1)}, bf16[32,16,128]{2,1,0:T(8,128)(2,1)S(1)}, u32[]{:S(2)}, u32[]{:S(2)}) collective-permute-start(bf16[32,16,128]{2,1,0:T(8,128)(2,1)} %raw.3), channel_id=1, source_target_pairs={{0,24},{8,16},{16,8},{24,0},{1,25},{9,17},{17,9},{25,1},{2,26},{10... | collective-permute-start | bytes 393224 | tf_op jit(solution)/shard_map/ppermute | solution.py:371
  7.2 0.5 collective-permute-start.2
  7.7 0.5 collective-permute-start.1
  8.3 1.6 %collective-permute-start.6 = (bf16[64,16,128]{2,1,0:T(8,128)(2,1)}, bf16[64,16,128]{2,1,0:T(8,128)(2,1)S(1)}, u32[]{:S(2)}, u32[]{:S(2)}) collective-permute-start(bf16[64,16,128]{2,1,0:T(8,128)(2,1)} %raw.2), channel_id=1, source_target_pairs={{0,2},{2,0},{4,6},{6,4},{1,3},{3,1},{5,7},{7,5},{8,10},{10,8},{12,... | collective-permute-start | bytes 786440 | tf_op jit(solution)/shard_map/ppermute | solution.py:371
  9.9 0.0 copy-start.4
  9.9 2.6 %middle.3 = (f32[64,32,128]{2,1,0:T(8,128)S(1)}, bf16[64,32,128]{2,1,0:T(8,128)(2,1)S(1)}, bf16[64,32,128]{2,1,0:T(8,128)(2,1)S(1)}, f32[64,32,128]{2,1,0:T(8,128)S(1)}) custom-call(bf16[64,32,128]{2,1,0:T(8,128)(2,1)S(1)} %copy-done.2, bf16[64,32,128]{2,1,0:T(8,128)(2,1)S(1)} %copy-done.3, bf16[128,128]{1,0:T(8,128)(2,1)S(1)} %copy-done.7, ...), custom_call_target="tpu_custom_call" | custom-call | flops 1000 | bytes 1000 | tf_op jit(solution)/shard_map/middle/pallas_call | solution.py:461
  12.5 1.1 %collective-permute-done.2.refs_2_ = bf16[32,16,128]{2,1,0:T(8,128)(2,1)S(1)} collective-permute-done((bf16[32,16,128]{2,1,0:T(8,128)(2,1)}, bf16[32,16,128]{2,1,0:T(8,128)(2,1)S(1)}, u32[]{:S(2)}, u32[]{:S(2)}) %collective-permute-start.2) | collective-permute-done | bytes 131104 | tf_op jit(solution)/shard_map/ppermute | solution.py:371
  13.7 0.1 collective-permute-done.1.refs_1_
  13.7 1.9 %right.1 = (f32[2048,128]{1,0:T(8,128)S(1)}, bf16[4,32,16,128]{3,2,1,0:T(8,128)(2,1)S(1)}, f32[16,32,128]{2,1,0:T(8,128)S(1)}, f32[16,32,128]{2,1,0:T(8,128)S(1)...) custom-call(bf16[32,16,128]{2,1,0:T(8,128)(2,1)S(1)} %copy-done.5, ...), custom_call_target="tpu_custom_call" | custom-call | flops 1000 | bytes 1000 | tf_op jit(solution)/shard_map/right/pallas_call | solution.py:461
  15.6 1.4 %collective-permute-done.refs_0_ = bf16[64,16,128]{2,1,0:T(8,128)(2,1)S(1)} collective-permute-done((bf16[64,16,128]{2,1,0:T(8,128)(2,1)}, bf16[64,16,128]{2,1,0:T(8,128)(2,1)S(1)}, u32[]{:S(2)}, u32[]{:S(2)}) %collective-permute-start) | collective-permute-done | bytes 262176 | tf_op jit(solution)/shard_map/ppermute | solution.py:371
  17.1 0.8 %collective-permute-start.4 = (bf16[64,16,128]{2,1,0:T(8,128)(2,1)S(1)}, bf16[64,16,128]{2,1,0:T(8,128)(2,1)S(1)}, u32[]{:S(2)}, u32[]{:S(2)}) collective-permute-start(bf16[64,16,128]{2,1,0:T(8,128)(2,1)S(1)} %get-tuple-element.61), channel_id=1, source_target_pairs={{0,2},{2,0},{4,6},{6,4},{1,3},{3,1},{5,7},{7,5},{8,10},{10,8},{12,... | collective-permute-start | bytes 786440 | tf_op jit(solution)/shard_map/ppermute | solution.py:371
  17.9 0.8 %collective-permute-start.5 = (bf16[64,16,128]{2,1,0:T(8,128)(2,1)S(1)}, bf16[64,16,128]{2,1,0:T(8,128)(2,1)S(1)}, u32[]{:S(2)}, u32[]{:S(2)}) collective-permute-start(bf16[64,16,128]{2,1,0:T(8,128)(2,1)S(1)} %get-tuple-element.62), channel_id=1, source_target_pairs={{0,0},{2,4},{4,2},{6,6},{1,1},{3,5},{5,3},{7,7},{8,8},{10,12},{12,... | collective-permute-start | bytes 786440 | tf_op jit(solution)/shard_map/ppermute | solution.py:409
  18.8 2.0 %left.3 = (f32[64,16,128]{2,1,0:T(8,128)S(1)}, bf16[64,16,128]{2,1,0:T(8,128)(2,1)S(1)}, f32[64,32,128]{2,1,0:T(8,128)S(1)}) custom-call(bf16[64,16,128]{2,1,0:T(8,128)(2,1)S(1)} %copy-done, bf16[128,256]{1,0:T(8,128)(2,1)S(1)} %copy-done.1, f32[16,32,128]{2,1,0:T(8,128)S(1)} %get-tuple-element.67.refs_2_), custom_call_target="tpu_custom_call" | custom-call | flops 1000 | bytes 1000 | tf_op jit(solution)/shard_map/left/pallas_call | solution.py:461
  20.8 2.0 %left.4 = (f32[64,16,128]{2,1,0:T(8,128)S(1)}, bf16[64,16,128]{2,1,0:T(8,128)(2,1)S(1)}, f32[64,32,128]{2,1,0:T(8,128)S(1)}) custom-call(bf16[64,16,128]{2,1,0:T(8,128)(2,1)S(1)} %collective-permute-done.6.refs_0_, bf16[128,256]{1,0:T(8,128)(2,1)S(1)} %copy-done.1, f32[16,32,128]{2,1,0:T(8,128)S(1)} %get-tuple-element.66.refs_2_, ...), custom_call_target="tpu_custom_call" | custom-call | flops 1000 | bytes 1000 | tf_op jit(solution)/shard_map/left/pallas_call | solution.py:461
  22.8 2.0 %left.5 = (f32[64,16,128]{2,1,0:T(8,128)S(1)}, bf16[64,16,128]{2,1,0:T(8,128)(2,1)S(1)}, f32[64,32,128]{2,1,0:T(8,128)S(1)}) custom-call(bf16[64,16,128]{2,1,0:T(8,128)(2,1)S(1)} %collective-permute-done.refs_0_, bf16[128,256]{1,0:T(8,128)(2,1)S(1)} %copy-done.1, f32[16,32,128]{2,1,0:T(8,128)S(1)} %get-tuple-element.65.refs_2_, ...), custom_call_target="tpu_custom_call" | custom-call | flops 1000 | bytes 1000 | tf_op jit(solution)/shard_map/left/pallas_call | solution.py:461
  24.8 0.6 collective-permute-done.4.refs_0_
  25.5 3.4 %triangle.1 = (f32[64,16,128]{2,1,0:T(8,128)S(1)}, bf16[64,16,128]{2,1,0:T(8,128)(2,1)S(1)}, bf16[64,32,128]{2,1,0:T(8,128)(2,1)S(1)}, f32[64,32,128]{2,1,0:T(8,128)S(1)}) custom-call(bf16[64,16,128]{2,1,0:T(8,128)(2,1)S(1)} %collective-permute-done.4.refs_0_, bf16[64,16,128]{2,1,0:T(8,128)(2,1)S(1)} %collective-permute-done.5.refs_1_, ...), custom_call_target="tpu_custom_call" | custom-call | flops 1000 | bytes 1000 | tf_op jit(solution)/shard_map/triangle/pallas_call | solution.py:461
  28.9 2.3 %left_back.3 = (bf16[64,16,128]{2,1,0:T(8,128)(2,1)S(1)}, bf16[64,16,128]{2,1,0:T(8,128)(2,1)S(1)}) custom-call(f32[64,32,128]{2,1,0:T(8,128)S(1)} %get-tuple-element.74.tri_back, f32[2048,128]{1,0:T(8,128)S(1)} %get-tuple-element.75.right_act), custom_call_target="tpu_custom_call" | custom-call | flops 1000 | bytes 1000 | tf_op jit(solution)/shard_map/left_back/pallas_call | solution.py:461
  31.2 5.6 %collective-permute-start.8 = (bf16[64,16,128]{2,1,0:T(8,128)(2,1)S(1)}, bf16[64,16,128]{2,1,0:T(8,128)(2,1)S(1)}, u32[]{:S(2)}, u32[]{:S(2)}) collective-permute-start(bf16[64,16,128]{2,1,0:T(8,128)(2,1)S(1)} %get-tuple-element.79.refs_6_), channel_id=1, source_target_pairs={{0,4},{2,6},{4,0},{6,2},{1,5},{3,7},{5,1},{7,3},{8,12},{10,14},{12... | collective-permute-start | bytes 786440 | tf_op jit(solution)/shard_map/ppermute | solution.py:371
  36.8 1.4 %collective-permute-start.9 = (bf16[64,16,128]{2,1,0:T(8,128)(2,1)S(1)}, bf16[64,16,128]{2,1,0:T(8,128)(2,1)S(1)}, u32[]{:S(2)}, u32[]{:S(2)}) collective-permute-start(bf16[64,16,128]{2,1,0:T(8,128)(2,1)S(1)} %get-tuple-element.80.refs_7_), channel_id=1, source_target_pairs={{0,6},{2,4},{4,2},{6,0},{1,7},{3,5},{5,3},{7,1},{8,14},{10,12},{12... | collective-permute-start | bytes 786440 | tf_op jit(solution)/shard_map/ppermute | solution.py:371
  38.1 2.3 %left_back.2 = (bf16[64,16,128]{2,1,0:T(8,128)(2,1)S(1)}, bf16[64,16,128]{2,1,0:T(8,128)(2,1)S(1)}) custom-call(f32[64,32,128]{2,1,0:T(8,128)S(1)} %get-tuple-element.74.tri_back, f32[2048,128]{1,0:T(8,128)S(1)} %get-tuple-element.75.right_act), custom_call_target="tpu_custom_call" | custom-call | flops 1000 | bytes 1000 | tf_op jit(solution)/shard_map/left_back/pallas_call | solution.py:461
  40.5 0.1 collective-permute-start.7
  40.6 5.5 %right_back.1 = (bf16[2,32,16,128]{3,2,1,0:T(8,128)(2,1)S(1)}, bf16[2,32,16,128]{3,2,1,0:T(8,128)(2,1)S(1)}) custom-call(f32[64,32,128]{2,1,0:T(8,128)S(1)} %get-tuple-element.74.tri_back, f32[64,16,128]{2,1,0:T(8,128)S(1)} %get-tuple-element.82.refs_0_, f32[64,16,128]{2,1,0:T(8,128)S(1)} %get-tuple-element.83.refs_1_, ...), custom_call_target="tpu_custom_call" | custom-call | flops 1000 | bytes 1000 | tf_op jit(solution)/shard_map/right_back/pallas_call | solution.py:461
  46.1 1.6 %collective-permute-start.10 = (bf16[2,32,16,128]{3,2,1,0:T(8,128)(2,1)S(1)}, bf16[2,32,16,128]{3,2,1,0:T(8,128)(2,1)S(1)}, u32[]{:S(2)}, u32[]{:S(2)}) collective-permute-start(bf16[2,32,16,128]{3,2,1,0:T(8,128)(2,1)S(1)} %get-tuple-element.87.refs_9_), channel_id=1, source_target_pairs={{0,8},{8,0},{16,24},{24,16},{1,9},{9,1},{17,25},{25,17},{2,10},{10... | collective-permute-start | bytes 786440 | tf_op jit(solution)/shard_map/ppermute | solution.py:371
  47.7 1.6 %heads.1 = (bf16[64,32,128]{2,1,0:T(8,128)(2,1)}, bf16[64,32,128]{2,1,0:T(8,128)(2,1)S(1)}, f32[128,128]{1,0:T(8,128)S(1)}, f32[128,128]{1,0:T(8,128)S(1)}) custom-call(bf16[64,32,128]{2,1,0:T(8,128)(2,1)S(1)} %get-tuple-element.71.tri_in, bf16[128,128]{1,0:T(8,128)(2,1)S(1)} %copy-done.6, f32[64,32,128]{2,1,0:T(8,128)S(1)} %get-tuple-element.72.gate, ...), custom_call_target="tpu_custom_call" | custom-call | flops 1000 | bytes 1000 | tf_op jit(solution)/shard_map/heads/pallas_call | solution.py:461
  49.3 2.0 %weights.1 = (f32[2,32,768]{2,1,0:T(8,128)S(1)}, bf16[2,32,768]{2,1,0:T(8,128)(2,1)S(1)}) custom-call(bf16[4,32,16,128]{3,2,1,0:T(8,128)(2,1)S(1)} %get-tuple-element.59.refs_2_.right_in, bf16[128,256]{1,0:T(8,128)(2,1)S(1)} %copy-done.1, bf16[128,256]{1,0:T(8,128)(2,1)S(1)} %copy-done.4, f32[128,128]{1,0:T(8,128)S(1)} %get-tuple-element.92.gate_part, ...), custom_call_target="tpu_custom_call" | custom-call | flops 1000 | bytes 1000 | tf_op jit(solution)/shard_map/weights/pallas_call | solution.py:461
  51.3 0.6 collective-permute-start.12
  51.9 2.5 %grad_middle.1 = (bf16[64,32,128]{2,1,0:T(8,128)(2,1)}, f32[8,128]{1,0:T(8,128)S(1)}) custom-call(bf16[64,32,128]{2,1,0:T(8,128)(2,1)S(1)} %copy-done.2, bf16[64,32,128]{2,1,0:T(8,128)(2,1)S(1)} %get-tuple-element.91.pre_back, bf16[128,128]{1,0:T(8,128)(2,1)S(1)} %copy-done.7, bf16[2,32,768]{2,1,0:T(8,128)(2,1)S(1)} %get-tuple-element.98._), custom_call_target="tpu_custom_call" | custom-call | flops 1000 | bytes 1000 | tf_op jit(solution)/shard_map/grad_middle/pallas_call | solution.py:461
  54.4 1.6 %collective-permute-done.12.came = bf16[2,32,768]{2,1,0:T(8,128)(2,1)S(1)} collective-permute-done((bf16[2,32,768]{2,1,0:T(8,128)(2,1)S(1)}, bf16[2,32,768]{2,1,0:T(8,128)(2,1)S(1)}, u32[]{:S(2)}, u32[]{:S(2)}) %collective-permute-start.12) | collective-permute-done | bytes 98336 | tf_op jit(solution)/shard_map/ppermute | solution.py:371
  56.0 1.6 %collective-permute-start.13 = (bf16[1,32,768]{2,1,0:T(8,128)(2,1)S(1)}, bf16[1,32,768]{2,1,0:T(8,128)(2,1)S(1)}, u32[]{:S(2)}, u32[]{:S(2)}) collective-permute-start(bf16[1,32,768]{2,1,0:T(8,128)(2,1)S(1)} %get-tuple-element.103), channel_id=1, source_target_pairs={{0,16},{8,24},{16,0},{24,8},{1,17},{9,25},{17,1},{25,9},{2,18},{10... | collective-permute-start | bytes 147464 | tf_op jit(solution)/shard_map/ppermute | solution.py:371
  57.6 0.1 halve.2
  57.7 1.0 %collective-permute-start.11 = (bf16[1,32,16,128]{3,2,1,0:T(8,128)(2,1)S(1)}, bf16[1,32,16,128]{3,2,1,0:T(8,128)(2,1)S(1)}, u32[]{:S(2)}, u32[]{:S(2)}) collective-permute-start(bf16[1,32,16,128]{3,2,1,0:T(8,128)(2,1)S(1)} %get-tuple-element.89.refs_0_), channel_id=1, source_target_pairs={{0,16},{8,24},{16,0},{24,8},{1,17},{9,25},{17,1},{25,9},{2,18},{10... | collective-permute-start | bytes 393224 | tf_op jit(solution)/shard_map/ppermute | solution.py:371
  58.7 1.9 %collective-permute-done.13.refs_1_ = bf16[1,32,768]{2,1,0:T(8,128)(2,1)S(1)} collective-permute-done((bf16[1,32,768]{2,1,0:T(8,128)(2,1)S(1)}, bf16[1,32,768]{2,1,0:T(8,128)(2,1)S(1)}, u32[]{:S(2)}, u32[]{:S(2)}) %collective-permute-start.13) | collective-permute-done | bytes 49184 | tf_op jit(solution)/shard_map/ppermute | solution.py:371
  60.6 2.1 %collective-permute-start.16 = (bf16[1,32,768]{2,1,0:T(8,128)(2,1)S(1)}, bf16[1,32,768]{2,1,0:T(8,128)(2,1)S(1)}, u32[]{:S(2)}, u32[]{:S(2)}) collective-permute-start(bf16[1,32,768]{2,1,0:T(8,128)(2,1)S(1)} %combine.2.refs_0_), channel_id=1, source_target_pairs={{0,6},{2,4},{4,2},{6,0},{1,7},{3,5},{5,3},{7,1},{8,14},{10,12},{12... | collective-permute-start | bytes 147464 | tf_op jit(solution)/shard_map/ppermute | solution.py:371
  62.7 1.3 %collective-permute-start.15 = (bf16[1,32,768]{2,1,0:T(8,128)(2,1)S(1)}, bf16[1,32,768]{2,1,0:T(8,128)(2,1)S(1)}, u32[]{:S(2)}, u32[]{:S(2)}) collective-permute-start(bf16[1,32,768]{2,1,0:T(8,128)(2,1)S(1)} %combine.2.refs_0_), channel_id=1, source_target_pairs={{0,4},{2,6},{4,0},{6,2},{1,5},{3,7},{5,1},{7,3},{8,12},{10,14},{12... | collective-permute-start | bytes 147464 | tf_op jit(solution)/shard_map/ppermute | solution.py:371
  64.0 1.0 %collective-permute-start.14 = (bf16[1,32,768]{2,1,0:T(8,128)(2,1)S(1)}, bf16[1,32,768]{2,1,0:T(8,128)(2,1)S(1)}, u32[]{:S(2)}, u32[]{:S(2)}) collective-permute-start(bf16[1,32,768]{2,1,0:T(8,128)(2,1)S(1)} %combine.2.refs_0_), channel_id=1, source_target_pairs={{0,2},{2,0},{4,6},{6,4},{1,3},{3,1},{5,7},{7,5},{8,10},{10,8},{12,... | collective-permute-start | bytes 147464 | tf_op jit(solution)/shard_map/ppermute | solution.py:371
  65.0 2.1 %left_side.1 = (bf16[64,16,128]{2,1,0:T(8,128)(2,1)}, f32[8,128]{1,0:T(8,128)S(1)}) custom-call(bf16[64,16,128]{2,1,0:T(8,128)(2,1)S(1)} %copy-done, bf16[128,256]{1,0:T(8,128)(2,1)S(1)} %copy-done.1, bf16[64,16,128]{2,1,0:T(8,128)(2,1)S(1)} %get-tuple-element.76._.refs_0_.refs_4_, bf16[64,16,128]{2,1,0:T(8,128)(2,1)S(1)} %collective-permute-done.7.refs_1_.refs_0_, ...), custom_call_target="tpu_custom_call" | custom-call | flops 1000 | bytes 1000 | tf_op jit(solution)/shard_map/left_side/pallas_call | solution.py:461
  67.2 0.5 collective-permute-done.15.refs_2_
  67.7 0.5 collective-permute-done.14.refs_1_
  68.2 2.1 %collective-permute-start.19 = (bf16[1,32,768]{2,1,0:T(8,128)(2,1)S(1)}, bf16[1,32,768]{2,1,0:T(8,128)(2,1)S(1)}, u32[]{:S(2)}, u32[]{:S(2)}) collective-permute-start(bf16[1,32,768]{2,1,0:T(8,128)(2,1)S(1)} %combine.3.refs_0_), channel_id=1, source_target_pairs={{0,24},{8,16},{16,8},{24,0},{1,25},{9,17},{17,9},{25,1},{2,26},{10... | collective-permute-start | bytes 147464 | tf_op jit(solution)/shard_map/ppermute | solution.py:371
  70.3 0.5 collective-permute-start.18
  70.8 1.0 %collective-permute-start.17 = (bf16[1,32,768]{2,1,0:T(8,128)(2,1)S(1)}, bf16[1,32,768]{2,1,0:T(8,128)(2,1)S(1)}, u32[]{:S(2)}, u32[]{:S(2)}) collective-permute-start(bf16[1,32,768]{2,1,0:T(8,128)(2,1)S(1)} %combine.3.refs_0_), channel_id=1, source_target_pairs={{0,8},{8,0},{16,24},{24,16},{1,9},{9,1},{17,25},{25,17},{2,10},{10... | collective-permute-start | bytes 147464 | tf_op jit(solution)/shard_map/ppermute | solution.py:371
  71.8 1.5 %right_side.1 = (bf16[32,16,128]{2,1,0:T(8,128)(2,1)}, f32[8,128]{1,0:T(8,128)S(1)}) custom-call(bf16[32,16,128]{2,1,0:T(8,128)(2,1)S(1)} %copy-done.5, bf16[128,256]{1,0:T(8,128)(2,1)S(1)} %copy-done.4, f32[32,16,128]{2,1,0:T(8,128)S(1)} %bitcast.2, bf16[32,16,128]{2,1,0:T(8,128)(2,1)S(1)} %bitcast.3), custom_call_target="tpu_custom_call" | custom-call | flops 1000 | bytes 1000 | tf_op jit(solution)/shard_map/right_side/pallas_call | solution.py:461
  73.3 0.0 collective-permute-done.19.refs_3_
  73.3 1.1 %collective-permute-done.18.refs_2_ = bf16[1,32,768]{2,1,0:T(8,128)(2,1)S(1)} collective-permute-done((bf16[1,32,768]{2,1,0:T(8,128)(2,1)S(1)}, bf16[1,32,768]{2,1,0:T(8,128)(2,1)S(1)}, u32[]{:S(2)}, u32[]{:S(2)}) %collective-permute-start.18) | collective-permute-done | bytes 49184 | tf_op jit(solution)/shard_map/ppermute | solution.py:371
  74.4 0.5 collective-permute-done.17.refs_1_
  74.9 0.8 %deltas.1 = (f32[128,256]{1,0:T(8,128)}, f32[128,256]{1,0:T(8,128)}, f32[128,128]{1,0:T(8,128)}, f32[128,128]{1,0:T(8,128)}) custom-call(bf16[1,32,768]{2,1,0:T(8,128)(2,1)S(1)} %combine.3.refs_0_, bf16[1,32,768]{2,1,0:T(8,128)(2,1)S(1)} %collective-permute-done.17.refs_1_, bf16[1,32,768]{2,1,0:T(8,128)(2,1)S(1)} %collective-permute-done.18.refs_2_, ...), custom_call_target="tpu_custom_call" | custom-call | flops 1000 | bytes 1000 | tf_op jit(solution)/shard_map/deltas/pallas_call | solution.py:461
  (31 shorter events, 0.2 us)
Async XLA Ops:
  0.6 9.2 %copy-start.6 = (bf16[128,128]{1,0:T(8,128)(2,1)S(1)}, bf16[128,128]{1,0:T(8,128)(2,1)}, u32[]{:S(2)}) copy-start(bf16[128,128]{1,0:T(8,128)(2,1)} %out_w.1) | copy-start | bytes 98308
  0.6 9.2 %copy-start.7 = (bf16[128,128]{1,0:T(8,128)(2,1)S(1)}, bf16[128,128]{1,0:T(8,128)(2,1)}, u32[]{:S(2)}) copy-start(bf16[128,128]{1,0:T(8,128)(2,1)} %gate_weight.3) | copy-start | bytes 98308
  0.7 9.2 %copy-start.3 = (bf16[64,32,128]{2,1,0:T(8,128)(2,1)S(1)}, bf16[64,32,128]{2,1,0:T(8,128)(2,1)}, u32[]{:S(2)}) copy-start(bf16[64,32,128]{2,1,0:T(8,128)(2,1)} %cotangent.3) | copy-start | bytes 1572868
  0.7 9.2 %copy-start.2 = (bf16[64,32,128]{2,1,0:T(8,128)(2,1)S(1)}, bf16[64,32,128]{2,1,0:T(8,128)(2,1)}, u32[]{:S(2)}) copy-start(bf16[64,32,128]{2,1,0:T(8,128)(2,1)} %middle.5) | copy-start | bytes 1572868
  0.7 16.3 %collective-permute-start = (bf16[64,16,128]{2,1,0:T(8,128)(2,1)}, bf16[64,16,128]{2,1,0:T(8,128)(2,1)S(1)}, u32[]{:S(2)}, u32[]{:S(2)}) collective-permute-start(bf16[64,16,128]{2,1,0:T(8,128)(2,1)} %raw.2), channel_id=1, source_target_pairs={{0,4},{2,6},{4,0},{6,2},{1,5},{3,7},{5,1},{7,3},{8,12},{10,14},{12... | collective-permute-start | bytes 786440 | tf_op jit(solution)/shard_map/ppermute | solution.py:371
  4.8 7.7 %collective-permute-start.3 = (bf16[32,16,128]{2,1,0:T(8,128)(2,1)}, bf16[32,16,128]{2,1,0:T(8,128)(2,1)S(1)}, u32[]{:S(2)}, u32[]{:S(2)}) collective-permute-start(bf16[32,16,128]{2,1,0:T(8,128)(2,1)} %raw.3), channel_id=1, source_target_pairs={{0,24},{8,16},{16,8},{24,0},{1,25},{9,17},{17,9},{25,1},{2,26},{10... | collective-permute-start | bytes 393224 | tf_op jit(solution)/shard_map/ppermute | solution.py:371
  7.2 6.4 %collective-permute-start.2 = (bf16[32,16,128]{2,1,0:T(8,128)(2,1)}, bf16[32,16,128]{2,1,0:T(8,128)(2,1)S(1)}, u32[]{:S(2)}, u32[]{:S(2)}) collective-permute-start(bf16[32,16,128]{2,1,0:T(8,128)(2,1)} %raw.3), channel_id=1, source_target_pairs={{0,16},{8,24},{16,0},{24,8},{1,17},{9,25},{17,1},{25,9},{2,18},{10... | collective-permute-start | bytes 393224 | tf_op jit(solution)/shard_map/ppermute | solution.py:371
  7.7 6.0 %collective-permute-start.1 = (bf16[32,16,128]{2,1,0:T(8,128)(2,1)}, bf16[32,16,128]{2,1,0:T(8,128)(2,1)S(1)}, u32[]{:S(2)}, u32[]{:S(2)}) collective-permute-start(bf16[32,16,128]{2,1,0:T(8,128)(2,1)} %raw.3), channel_id=1, source_target_pairs={{0,8},{8,0},{16,24},{24,16},{1,9},{9,1},{17,25},{25,17},{2,10},{10... | collective-permute-start | bytes 393224 | tf_op jit(solution)/shard_map/ppermute | solution.py:371
  8.3 12.5 %collective-permute-start.6 = (bf16[64,16,128]{2,1,0:T(8,128)(2,1)}, bf16[64,16,128]{2,1,0:T(8,128)(2,1)S(1)}, u32[]{:S(2)}, u32[]{:S(2)}) collective-permute-start(bf16[64,16,128]{2,1,0:T(8,128)(2,1)} %raw.2), channel_id=1, source_target_pairs={{0,2},{2,0},{4,6},{6,4},{1,3},{3,1},{5,7},{7,5},{8,10},{10,8},{12,... | collective-permute-start | bytes 786440 | tf_op jit(solution)/shard_map/ppermute | solution.py:371
  9.9 3.9 %copy-start.4 = (bf16[128,256]{1,0:T(8,128)(2,1)S(1)}, bf16[128,256]{1,0:T(8,128)(2,1)}, u32[]{:S(2)}) copy-start(bf16[128,256]{1,0:T(8,128)(2,1)} %right_w.1) | copy-start | bytes 196612
  9.9 3.8 %copy-start.5 = (bf16[32,16,128]{2,1,0:T(8,128)(2,1)S(1)}, bf16[32,16,128]{2,1,0:T(8,128)(2,1)}, u32[]{:S(2)}) copy-start(bf16[32,16,128]{2,1,0:T(8,128)(2,1)} %raw.3) | copy-start | bytes 393220
  12.5 4.5 %copy-start = (bf16[64,16,128]{2,1,0:T(8,128)(2,1)S(1)}, bf16[64,16,128]{2,1,0:T(8,128)(2,1)}, u32[]{:S(2)}) copy-start(bf16[64,16,128]{2,1,0:T(8,128)(2,1)} %raw.2) | copy-start | bytes 786436
  17.0 1.7 %copy-start.1 = (bf16[128,256]{1,0:T(8,128)(2,1)S(1)}, bf16[128,256]{1,0:T(8,128)(2,1)}, u32[]{:S(2)}) copy-start(bf16[128,256]{1,0:T(8,128)(2,1)} %left_w.1) | copy-start | bytes 196612
  17.1 8.4 %collective-permute-start.4 = (bf16[64,16,128]{2,1,0:T(8,128)(2,1)S(1)}, bf16[64,16,128]{2,1,0:T(8,128)(2,1)S(1)}, u32[]{:S(2)}, u32[]{:S(2)}) collective-permute-start(bf16[64,16,128]{2,1,0:T(8,128)(2,1)S(1)} %get-tuple-element.61), channel_id=1, source_target_pairs={{0,2},{2,0},{4,6},{6,4},{1,3},{3,1},{5,7},{7,5},{8,10},{10,8},{12,... | collective-permute-start | bytes 786440 | tf_op jit(solution)/shard_map/ppermute | solution.py:371
  17.9 7.6 %collective-permute-start.5 = (bf16[64,16,128]{2,1,0:T(8,128)(2,1)S(1)}, bf16[64,16,128]{2,1,0:T(8,128)(2,1)S(1)}, u32[]{:S(2)}, u32[]{:S(2)}) collective-permute-start(bf16[64,16,128]{2,1,0:T(8,128)(2,1)S(1)} %get-tuple-element.62), channel_id=1, source_target_pairs={{0,0},{2,4},{4,2},{6,6},{1,1},{3,5},{5,3},{7,7},{8,8},{10,12},{12,... | collective-permute-start | bytes 786440 | tf_op jit(solution)/shard_map/ppermute | solution.py:409
  31.2 26.4 %collective-permute-start.8 = (bf16[64,16,128]{2,1,0:T(8,128)(2,1)S(1)}, bf16[64,16,128]{2,1,0:T(8,128)(2,1)S(1)}, u32[]{:S(2)}, u32[]{:S(2)}) collective-permute-start(bf16[64,16,128]{2,1,0:T(8,128)(2,1)S(1)} %get-tuple-element.79.refs_6_), channel_id=1, source_target_pairs={{0,4},{2,6},{4,0},{6,2},{1,5},{3,7},{5,1},{7,3},{8,12},{10,14},{12... | collective-permute-start | bytes 786440 | tf_op jit(solution)/shard_map/ppermute | solution.py:371
  36.8 20.8 %collective-permute-start.9 = (bf16[64,16,128]{2,1,0:T(8,128)(2,1)S(1)}, bf16[64,16,128]{2,1,0:T(8,128)(2,1)S(1)}, u32[]{:S(2)}, u32[]{:S(2)}) collective-permute-start(bf16[64,16,128]{2,1,0:T(8,128)(2,1)S(1)} %get-tuple-element.80.refs_7_), channel_id=1, source_target_pairs={{0,6},{2,4},{4,2},{6,0},{1,7},{3,5},{5,3},{7,1},{8,14},{10,12},{12... | collective-permute-start | bytes 786440 | tf_op jit(solution)/shard_map/ppermute | solution.py:371
  40.5 17.1 %collective-permute-start.7 = (bf16[64,16,128]{2,1,0:T(8,128)(2,1)S(1)}, bf16[64,16,128]{2,1,0:T(8,128)(2,1)S(1)}, u32[]{:S(2)}, u32[]{:S(2)}) collective-permute-start(bf16[64,16,128]{2,1,0:T(8,128)(2,1)S(1)} %get-tuple-element.78.refs_5_), channel_id=1, source_target_pairs={{0,2},{2,0},{4,6},{6,4},{1,3},{3,1},{5,7},{7,5},{8,10},{10,8},{12,... | collective-permute-start | bytes 786440 | tf_op jit(solution)/shard_map/ppermute | solution.py:371
  46.1 11.5 %collective-permute-start.10 = (bf16[2,32,16,128]{3,2,1,0:T(8,128)(2,1)S(1)}, bf16[2,32,16,128]{3,2,1,0:T(8,128)(2,1)S(1)}, u32[]{:S(2)}, u32[]{:S(2)}) collective-permute-start(bf16[2,32,16,128]{3,2,1,0:T(8,128)(2,1)S(1)} %get-tuple-element.87.refs_9_), channel_id=1, source_target_pairs={{0,8},{8,0},{16,24},{24,16},{1,9},{9,1},{17,25},{25,17},{2,10},{10... | collective-permute-start | bytes 786440 | tf_op jit(solution)/shard_map/ppermute | solution.py:371
  51.3 4.7 %collective-permute-start.12 = (bf16[2,32,768]{2,1,0:T(8,128)(2,1)S(1)}, bf16[2,32,768]{2,1,0:T(8,128)(2,1)S(1)}, u32[]{:S(2)}, u32[]{:S(2)}) collective-permute-start(bf16[2,32,768]{2,1,0:T(8,128)(2,1)S(1)} %get-tuple-element.98._), channel_id=1, source_target_pairs={{0,8},{8,0},{16,24},{24,16},{1,9},{9,1},{17,25},{25,17},{2,10},{10... | collective-permute-start | bytes 294920 | tf_op jit(solution)/shard_map/ppermute | solution.py:371
  56.0 4.6 %collective-permute-start.13 = (bf16[1,32,768]{2,1,0:T(8,128)(2,1)S(1)}, bf16[1,32,768]{2,1,0:T(8,128)(2,1)S(1)}, u32[]{:S(2)}, u32[]{:S(2)}) collective-permute-start(bf16[1,32,768]{2,1,0:T(8,128)(2,1)S(1)} %get-tuple-element.103), channel_id=1, source_target_pairs={{0,16},{8,24},{16,0},{24,8},{1,17},{9,25},{17,1},{25,9},{2,18},{10... | collective-permute-start | bytes 147464 | tf_op jit(solution)/shard_map/ppermute | solution.py:371
  57.7 14.1 %collective-permute-start.11 = (bf16[1,32,16,128]{3,2,1,0:T(8,128)(2,1)S(1)}, bf16[1,32,16,128]{3,2,1,0:T(8,128)(2,1)S(1)}, u32[]{:S(2)}, u32[]{:S(2)}) collective-permute-start(bf16[1,32,16,128]{3,2,1,0:T(8,128)(2,1)S(1)} %get-tuple-element.89.refs_0_), channel_id=1, source_target_pairs={{0,16},{8,24},{16,0},{24,8},{1,17},{9,25},{17,1},{25,9},{2,18},{10... | collective-permute-start | bytes 393224 | tf_op jit(solution)/shard_map/ppermute | solution.py:371
  60.6 6.6 %collective-permute-start.16 = (bf16[1,32,768]{2,1,0:T(8,128)(2,1)S(1)}, bf16[1,32,768]{2,1,0:T(8,128)(2,1)S(1)}, u32[]{:S(2)}, u32[]{:S(2)}) collective-permute-start(bf16[1,32,768]{2,1,0:T(8,128)(2,1)S(1)} %combine.2.refs_0_), channel_id=1, source_target_pairs={{0,6},{2,4},{4,2},{6,0},{1,7},{3,5},{5,3},{7,1},{8,14},{10,12},{12... | collective-permute-start | bytes 147464 | tf_op jit(solution)/shard_map/ppermute | solution.py:371
  62.7 5.0 %collective-permute-start.15 = (bf16[1,32,768]{2,1,0:T(8,128)(2,1)S(1)}, bf16[1,32,768]{2,1,0:T(8,128)(2,1)S(1)}, u32[]{:S(2)}, u32[]{:S(2)}) collective-permute-start(bf16[1,32,768]{2,1,0:T(8,128)(2,1)S(1)} %combine.2.refs_0_), channel_id=1, source_target_pairs={{0,4},{2,6},{4,0},{6,2},{1,5},{3,7},{5,1},{7,3},{8,12},{10,14},{12... | collective-permute-start | bytes 147464 | tf_op jit(solution)/shard_map/ppermute | solution.py:371
  64.0 4.2 %collective-permute-start.14 = (bf16[1,32,768]{2,1,0:T(8,128)(2,1)S(1)}, bf16[1,32,768]{2,1,0:T(8,128)(2,1)S(1)}, u32[]{:S(2)}, u32[]{:S(2)}) collective-permute-start(bf16[1,32,768]{2,1,0:T(8,128)(2,1)S(1)} %combine.2.refs_0_), channel_id=1, source_target_pairs={{0,2},{2,0},{4,6},{6,4},{1,3},{3,1},{5,7},{7,5},{8,10},{10,8},{12,... | collective-permute-start | bytes 147464 | tf_op jit(solution)/shard_map/ppermute | solution.py:371
  68.2 5.1 %collective-permute-start.19 = (bf16[1,32,768]{2,1,0:T(8,128)(2,1)S(1)}, bf16[1,32,768]{2,1,0:T(8,128)(2,1)S(1)}, u32[]{:S(2)}, u32[]{:S(2)}) collective-permute-start(bf16[1,32,768]{2,1,0:T(8,128)(2,1)S(1)} %combine.3.refs_0_), channel_id=1, source_target_pairs={{0,24},{8,16},{16,8},{24,0},{1,25},{9,17},{17,9},{25,1},{2,26},{10... | collective-permute-start | bytes 147464 | tf_op jit(solution)/shard_map/ppermute | solution.py:371
  70.3 4.1 %collective-permute-start.18 = (bf16[1,32,768]{2,1,0:T(8,128)(2,1)S(1)}, bf16[1,32,768]{2,1,0:T(8,128)(2,1)S(1)}, u32[]{:S(2)}, u32[]{:S(2)}) collective-permute-start(bf16[1,32,768]{2,1,0:T(8,128)(2,1)S(1)} %combine.3.refs_0_), channel_id=1, source_target_pairs={{0,16},{8,24},{16,0},{24,8},{1,17},{9,25},{17,1},{25,9},{2,18},{10... | collective-permute-start | bytes 147464 | tf_op jit(solution)/shard_map/ppermute | solution.py:371
  70.8 4.1 %collective-permute-start.17 = (bf16[1,32,768]{2,1,0:T(8,128)(2,1)S(1)}, bf16[1,32,768]{2,1,0:T(8,128)(2,1)S(1)}, u32[]{:S(2)}, u32[]{:S(2)}) collective-permute-start(bf16[1,32,768]{2,1,0:T(8,128)(2,1)S(1)} %combine.3.refs_0_), channel_id=1, source_target_pairs={{0,8},{8,0},{16,24},{24,16},{1,9},{9,1},{17,25},{25,17},{2,10},{10... | collective-permute-start | bytes 147464 | tf_op jit(solution)/shard_map/ppermute | solution.py:371

commit v11 on v10

--- a/solution.py
+++ b/solution.py
@@ -85,7 +85,7 @@
         tri_up[rows] = (up - row_mean(split(up), width)).reshape(step, n_j, width)
         return 0
 
-    lax.fori_loop(0, n_i // step, body, 0, unroll=2)
+    lax.fori_loop(0, n_i // step, body, 0, unroll=True)
 
 
 def right_kernel(n_rows, n_blk, k_left, *refs):
@@ -147,7 +147,7 @@
         act_out[rows] = (sw * lin).astype(bf16).astype(f32).reshape(step, k_left, width)
         return 0
 
-    lax.fori_loop(0, n_i // step, body, 0, unroll=2)
+    lax.fori_loop(0, n_i // step, body, 0, unroll=True)
 
 
 def add_vertices(rows, act, flip):
@@ -170,7 +170,7 @@
         total_out[rows] = total if first else total_in[0][rows] + total
         return 0
 
-    lax.fori_loop(0, n_i // step, body, 0)
+    lax.fori_loop(0, n_i // step, body, 0, unroll=2)
 
 
 def triangle_kernel(n_raw, has_total, *refs):
@@ -196,7 +196,7 @@
         tri_back[rows] = back.astype(bf16).astype(f32).reshape(step, n_j, width)
         return 0
 
-    lax.fori_loop(0, n_i // step, triangle_rows, 0, unroll=4)
+    lax.fori_loop(0, n_i // step, triangle_rows, 0, unroll=True)
 
 
 def heads_kernel(tri_in, out_w, gate, middle_in, head_back, cotangent, _, *refs):
@@ -220,7 +220,7 @@
         output_part[...] += dot_tn(inputs, head_back[rows].reshape(flat, width))
         return 0
 
-    lax.fori_loop(0, n_i // step, body, 0, unroll=2)
+    lax.fori_loop(0, n_i // step, body, 0, unroll=True)
 
 
 def vertex_step(n_k, unit):
@@ -250,7 +250,7 @@
                 left_out[k0 // k_left - first + s][rows] = total[:, s * k_left : (s + 1) * k_left]
             return 0
 
-        lax.fori_loop(0, n_i // few, rows_sum, 0)
+        lax.fori_loop(0, n_i // few, rows_sum, 0, unroll=2)
 
 
 def right_back_kernel(n_rows, n_blk, tri_back, *refs):
@@ -277,7 +277,7 @@
                     )
 
                 zeros = tuple(jnp.zeros((few, k_left, width), f32) for _ in blocks)
-                totals = lax.fori_loop(0, n_i, add, zeros, unroll=16)
+                totals = lax.fori_loop(0, n_i, add, zeros, unroll=32)
                 for s, total in zip(blocks, totals):
                     right_sum[pl.ds(at * 8 + half, few), s * k_left : (s + 1) * k_left, :] = total.astype(bf16)
             return 0
@@ -343,7 +343,7 @@
         grad_middle[rows] = normalize_back(normed, inverse, up).astype(bf16).reshape(step, n_j, width)
         return 0
 
-    lax.fori_loop(0, n_i // step, body, 0, unroll=2)
+    lax.fori_loop(0, n_i // step, body, 0, unroll=True)
 
 
 def side_kernel(raw, weight, *refs):
@@ -364,7 +364,7 @@
         grad[rows] = normalize_back(normed, inverse, up).astype(bf16).reshape(step, k, width)
         return 0
 
-    lax.fori_loop(0, n // step, body, 0, unroll=2 if n // step % 2 == 0 else 1)
+    lax.fori_loop(0, n // step, body, 0, unroll=True)
 
 
 def exchange(x, axis, n, bit):
@@ -438,8 +438,34 @@
     return total
 
 
-def deltas_kernel(n_rows, *refs):
-    pieces, outs = [ref.at[0] for ref in refs[:n_rows]], refs[n_rows + 1 :]
+def everywhere_sum(part, axis, n, after):
+    bit = 1
+    while bit < n:
+        part = combine([part, exchange(part, axis, n, bit)], after[:1])
+        after = after[1:]
+        bit *= 2
+    return part
+
+
+def stack_kernel(own, came, both):
+    both[0 : own.shape[0]] = own[...]
+    both[own.shape[0] :] = came[...]
+
+
+def gather_doubling(part, axis, n):
+    came = exchange(part, axis, n, 1)
+    bit = 2
+    while bit < n:
+        both = shape((2 * part.shape[0],) + part.shape[1:], part.dtype)
+        (part,) = call(stack_kernel, "stack", [both])(part, came)
+        came = exchange(part, axis, n, bit)
+        bit *= 2
+    return part, came
+
+
+def deltas_kernel(*refs):
+    stacks, outs = refs[:2], refs[2:]
+    pieces = [stack.at[at] for stack in stacks for at in range(stack.shape[0])]
     size = pieces[0].shape[0]
     for s, piece in enumerate(pieces):
         start = pl.multiple_of(lax.bitwise_xor(lax.axis_index("rows"), s) * size, size)
@@ -567,17 +593,16 @@
     grad_left, done_left = call(side_kernel, "left_side", [shape(pair_left.shape, bf16), MARK])(
         pair_left, left_weight, *left_back
     )
-    part = combine([part] + [exchange(part, "blk", n_blk, s) for s in range(1, n_blk)], (done_left,))
-    pieces = [part] + [exchange(part, "rows", n_rows, s) for s in range(1, n_rows)]
     grad_right, done_right = call(side_kernel, "right_side", [shape(pair_right.shape, bf16), MARK])(
         pair_right, right_weight, kept.reshape(pair_right.shape), came.reshape(pair_right.shape)
     )
+    part = everywhere_sum(part, "blk", n_blk, (done_left, done_right))
+    pieces = gather_doubling(part, "rows", n_rows)
     deltas = call(
-        functools.partial(deltas_kernel, n_rows),
+        deltas_kernel,
         "deltas",
         [shape(x.shape, f32) for x in (left_weight, right_weight, gate_weight, output_weight)],
-        after=1,
-    )(*pieces, done_right)
+    )(*pieces)
     return (
         update,
         grad_left,

time: 75.8 us -> 78.7 us (1.038)
  waiting for transfers between devices: 9.36 us -> 13.7 us
  Pallas kernels: 34.8 us -> 33.2 us
    ppermute x19 -> x17, waiting for transfers between devices: 9.35 us -> 13.7 us  [exchange(): return lax.ppermute(x, axis, [(a, a ^ bit) for a in range(n)])]
    pallas_call x23 -> x25, Pallas kernels: 34.8 us -> 33.2 us  [run(): pl.pallas_call(kernel, in_specs=[pl.BlockSpec(memory_space=space) for spa...]
    ppermute x19 -> x17, starting transfers between devices: 29.8 us -> 30 us  [exchange(): return lax.ppermute(x, axis, [(a, a ^ bit) for a in range(n)])]
  transfers between devices with their start and end apart: 20 -> 18, of which waited for: 10 -> 9; matrix products, arithmetic and copies ran while one was open for 0% -> 0% of each run, Pallas kernels for 37% -> 35%
where the time goes in v11:
time: 78.7 us; the launch traced here: 78.6 us
  Pallas kernels  33.2 us (42%)
  starting transfers between devices  30.9 us (39%)
  waiting for transfers between devices  13.7 us (17%)
  between operations  0.85 us (1%)
    pallas_call x25, Pallas kernels, run(): pl.pallas_call(kernel, in_specs=[pl.BlockSpec(memory_space=space) for spa...  33.2 us
    ppermute x17, starting transfers between devices, exchange(): return lax.ppermute(x, axis, [(a, a ^ bit) for a in range(n)])  30 us
    ppermute x17, waiting for transfers between devices, exchange(): return lax.ppermute(x, axis, [(a, a ^ bit) for a in range(n)])  13.7 us
  transfers between devices with their start and end apart: 18, of which 9 were waited for; matrix products, arithmetic and copies ran while one was open for 0% of the time, Pallas kernels for 35%

profile of v11, /device:TPU:0, one launch (start us, length us, event | category | flops | bytes accessed | tf_op | source)
XLA Modules:
  0.0 78.6 jit_solution(6092186581479689025)
XLA Ops:
  0.7 4.1 %collective-permute-start = (bf16[64,16,128]{2,1,0:T(8,128)(2,1)}, bf16[64,16,128]{2,1,0:T(8,128)(2,1)S(1)}, u32[]{:S(2)}, u32[]{:S(2)}) collective-permute-start(bf16[64,16,128]{2,1,0:T(8,128)(2,1)} %raw.2), channel_id=1, source_target_pairs={{0,4},{2,6},{4,0},{6,2},{1,5},{3,7},{5,1},{7,3},{8,12},{10,14},{12... | collective-permute-start | bytes 786440 | tf_op jit(solution)/shard_map/ppermute | solution.py:371
  4.8 2.4 %collective-permute-start.3 = (bf16[32,16,128]{2,1,0:T(8,128)(2,1)}, bf16[32,16,128]{2,1,0:T(8,128)(2,1)S(1)}, u32[]{:S(2)}, u32[]{:S(2)}) collective-permute-start(bf16[32,16,128]{2,1,0:T(8,128)(2,1)} %raw.3), channel_id=1, source_target_pairs={{0,24},{8,16},{16,8},{24,0},{1,25},{9,17},{17,9},{25,1},{2,26},{10... | collective-permute-start | bytes 393224 | tf_op jit(solution)/shard_map/ppermute | solution.py:371
  7.2 0.5 collective-permute-start.2
  7.7 0.5 collective-permute-start.1
  8.3 1.6 %collective-permute-start.6 = (bf16[64,16,128]{2,1,0:T(8,128)(2,1)}, bf16[64,16,128]{2,1,0:T(8,128)(2,1)S(1)}, u32[]{:S(2)}, u32[]{:S(2)}) collective-permute-start(bf16[64,16,128]{2,1,0:T(8,128)(2,1)} %raw.2), channel_id=1, source_target_pairs={{0,2},{2,0},{4,6},{6,4},{1,3},{3,1},{5,7},{7,5},{8,10},{10,8},{12,... | collective-permute-start | bytes 786440 | tf_op jit(solution)/shard_map/ppermute | solution.py:371
  9.9 0.0 copy-start.4
  9.9 0.0 copy-start.5
  9.9 2.3 %middle.3 = (f32[64,32,128]{2,1,0:T(8,128)S(1)}, bf16[64,32,128]{2,1,0:T(8,128)(2,1)S(1)}, bf16[64,32,128]{2,1,0:T(8,128)(2,1)S(1)}, f32[64,32,128]{2,1,0:T(8,128)S(1)}) custom-call(bf16[64,32,128]{2,1,0:T(8,128)(2,1)S(1)} %copy-done.2, bf16[64,32,128]{2,1,0:T(8,128)(2,1)S(1)} %copy-done.3, bf16[128,128]{1,0:T(8,128)(2,1)S(1)} %copy-done.7, ...), custom_call_target="tpu_custom_call" | custom-call | flops 1000 | bytes 1000 | tf_op jit(solution)/shard_map/middle/pallas_call | solution.py:487
  12.2 0.0 copy-start
  12.2 0.0 collective-permute-done.3.refs_3_
  12.3 1.4 %collective-permute-done.2.refs_2_ = bf16[32,16,128]{2,1,0:T(8,128)(2,1)S(1)} collective-permute-done((bf16[32,16,128]{2,1,0:T(8,128)(2,1)}, bf16[32,16,128]{2,1,0:T(8,128)(2,1)S(1)}, u32[]{:S(2)}, u32[]{:S(2)}) %collective-permute-start.2) | collective-permute-done | bytes 131104 | tf_op jit(solution)/shard_map/ppermute | solution.py:371
  13.7 0.1 collective-permute-done.1.refs_1_
  13.7 1.9 %right.1 = (f32[2048,128]{1,0:T(8,128)S(1)}, bf16[4,32,16,128]{3,2,1,0:T(8,128)(2,1)S(1)}, f32[16,32,128]{2,1,0:T(8,128)S(1)}, f32[16,32,128]{2,1,0:T(8,128)S(1)...) custom-call(bf16[32,16,128]{2,1,0:T(8,128)(2,1)S(1)} %copy-done.5, ...), custom_call_target="tpu_custom_call" | custom-call | flops 1000 | bytes 1000 | tf_op jit(solution)/shard_map/right/pallas_call | solution.py:487
  15.6 1.4 %collective-permute-done.refs_0_ = bf16[64,16,128]{2,1,0:T(8,128)(2,1)S(1)} collective-permute-done((bf16[64,16,128]{2,1,0:T(8,128)(2,1)}, bf16[64,16,128]{2,1,0:T(8,128)(2,1)S(1)}, u32[]{:S(2)}, u32[]{:S(2)}) %collective-permute-start) | collective-permute-done | bytes 262176 | tf_op jit(solution)/shard_map/ppermute | solution.py:371
  17.1 0.8 %collective-permute-start.4 = (bf16[64,16,128]{2,1,0:T(8,128)(2,1)S(1)}, bf16[64,16,128]{2,1,0:T(8,128)(2,1)S(1)}, u32[]{:S(2)}, u32[]{:S(2)}) collective-permute-start(bf16[64,16,128]{2,1,0:T(8,128)(2,1)S(1)} %get-tuple-element.61), channel_id=1, source_target_pairs={{0,2},{2,0},{4,6},{6,4},{1,3},{3,1},{5,7},{7,5},{8,10},{10,8},{12,... | collective-permute-start | bytes 786440 | tf_op jit(solution)/shard_map/ppermute | solution.py:371
  17.9 0.8 %collective-permute-start.5 = (bf16[64,16,128]{2,1,0:T(8,128)(2,1)S(1)}, bf16[64,16,128]{2,1,0:T(8,128)(2,1)S(1)}, u32[]{:S(2)}, u32[]{:S(2)}) collective-permute-start(bf16[64,16,128]{2,1,0:T(8,128)(2,1)S(1)} %get-tuple-element.62), channel_id=1, source_target_pairs={{0,0},{2,4},{4,2},{6,6},{1,1},{3,5},{5,3},{7,7},{8,8},{10,12},{12,... | collective-permute-start | bytes 786440 | tf_op jit(solution)/shard_map/ppermute | solution.py:409
  18.8 1.9 %left.3 = (f32[64,16,128]{2,1,0:T(8,128)S(1)}, bf16[64,16,128]{2,1,0:T(8,128)(2,1)S(1)}, f32[64,32,128]{2,1,0:T(8,128)S(1)}) custom-call(bf16[64,16,128]{2,1,0:T(8,128)(2,1)S(1)} %copy-done, bf16[128,256]{1,0:T(8,128)(2,1)S(1)} %copy-done.1, f32[16,32,128]{2,1,0:T(8,128)S(1)} %get-tuple-element.67.refs_2_), custom_call_target="tpu_custom_call" | custom-call | flops 1000 | bytes 1000 | tf_op jit(solution)/shard_map/left/pallas_call | solution.py:487
  20.7 0.0 collective-permute-done.6.refs_0_
  20.7 2.0 %left.4 = (f32[64,16,128]{2,1,0:T(8,128)S(1)}, bf16[64,16,128]{2,1,0:T(8,128)(2,1)S(1)}, f32[64,32,128]{2,1,0:T(8,128)S(1)}) custom-call(bf16[64,16,128]{2,1,0:T(8,128)(2,1)S(1)} %collective-permute-done.6.refs_0_, bf16[128,256]{1,0:T(8,128)(2,1)S(1)} %copy-done.1, f32[16,32,128]{2,1,0:T(8,128)S(1)} %get-tuple-element.66.refs_2_, ...), custom_call_target="tpu_custom_call" | custom-call | flops 1000 | bytes 1000 | tf_op jit(solution)/shard_map/left/pallas_call | solution.py:487
  22.7 2.0 %left.5 = (f32[64,16,128]{2,1,0:T(8,128)S(1)}, bf16[64,16,128]{2,1,0:T(8,128)(2,1)S(1)}, f32[64,32,128]{2,1,0:T(8,128)S(1)}) custom-call(bf16[64,16,128]{2,1,0:T(8,128)(2,1)S(1)} %collective-permute-done.refs_0_, bf16[128,256]{1,0:T(8,128)(2,1)S(1)} %copy-done.1, f32[16,32,128]{2,1,0:T(8,128)S(1)} %get-tuple-element.65.refs_2_, ...), custom_call_target="tpu_custom_call" | custom-call | flops 1000 | bytes 1000 | tf_op jit(solution)/shard_map/left/pallas_call | solution.py:487
  24.6 0.8 %collective-permute-done.4.refs_0_ = bf16[64,16,128]{2,1,0:T(8,128)(2,1)S(1)} collective-permute-done((bf16[64,16,128]{2,1,0:T(8,128)(2,1)S(1)}, bf16[64,16,128]{2,1,0:T(8,128)(2,1)S(1)}, u32[]{:S(2)}, u32[]{:S(2)}) %collective-permute-start.4) | collective-permute-done | bytes 262176 | tf_op jit(solution)/shard_map/ppermute | solution.py:371
  25.5 2.9 %triangle.1 = (f32[64,16,128]{2,1,0:T(8,128)S(1)}, bf16[64,16,128]{2,1,0:T(8,128)(2,1)S(1)}, bf16[64,32,128]{2,1,0:T(8,128)(2,1)S(1)}, f32[64,32,128]{2,1,0:T(8,128)S(1)}) custom-call(bf16[64,16,128]{2,1,0:T(8,128)(2,1)S(1)} %collective-permute-done.4.refs_0_, bf16[64,16,128]{2,1,0:T(8,128)(2,1)S(1)} %collective-permute-done.5.refs_1_, ...), custom_call_target="tpu_custom_call" | custom-call | flops 1000 | bytes 1000 | tf_op jit(solution)/shard_map/triangle/pallas_call | solution.py:487
  28.3 2.2 %left_back.3 = (bf16[64,16,128]{2,1,0:T(8,128)(2,1)S(1)}, bf16[64,16,128]{2,1,0:T(8,128)(2,1)S(1)}) custom-call(f32[64,32,128]{2,1,0:T(8,128)S(1)} %get-tuple-element.74.tri_back, f32[2048,128]{1,0:T(8,128)S(1)} %get-tuple-element.75.right_act), custom_call_target="tpu_custom_call" | custom-call | flops 1000 | bytes 1000 | tf_op jit(solution)/shard_map/left_back/pallas_call | solution.py:487
  30.6 5.6 %collective-permute-start.8 = (bf16[64,16,128]{2,1,0:T(8,128)(2,1)S(1)}, bf16[64,16,128]{2,1,0:T(8,128)(2,1)S(1)}, u32[]{:S(2)}, u32[]{:S(2)}) collective-permute-start(bf16[64,16,128]{2,1,0:T(8,128)(2,1)S(1)} %get-tuple-element.79.refs_6_), channel_id=1, source_target_pairs={{0,4},{2,6},{4,0},{6,2},{1,5},{3,7},{5,1},{7,3},{8,12},{10,14},{12... | collective-permute-start | bytes 786440 | tf_op jit(solution)/shard_map/ppermute | solution.py:371
  36.2 1.2 %collective-permute-start.9 = (bf16[64,16,128]{2,1,0:T(8,128)(2,1)S(1)}, bf16[64,16,128]{2,1,0:T(8,128)(2,1)S(1)}, u32[]{:S(2)}, u32[]{:S(2)}) collective-permute-start(bf16[64,16,128]{2,1,0:T(8,128)(2,1)S(1)} %get-tuple-element.80.refs_7_), channel_id=1, source_target_pairs={{0,6},{2,4},{4,2},{6,0},{1,7},{3,5},{5,3},{7,1},{8,14},{10,12},{12... | collective-permute-start | bytes 786440 | tf_op jit(solution)/shard_map/ppermute | solution.py:371
  37.4 2.2 %left_back.2 = (bf16[64,16,128]{2,1,0:T(8,128)(2,1)S(1)}, bf16[64,16,128]{2,1,0:T(8,128)(2,1)S(1)}) custom-call(f32[64,32,128]{2,1,0:T(8,128)S(1)} %get-tuple-element.74.tri_back, f32[2048,128]{1,0:T(8,128)S(1)} %get-tuple-element.75.right_act), custom_call_target="tpu_custom_call" | custom-call | flops 1000 | bytes 1000 | tf_op jit(solution)/shard_map/left_back/pallas_call | solution.py:487
  39.6 0.1 collective-permute-start.7
  39.7 5.5 %right_back.1 = (bf16[2,32,16,128]{3,2,1,0:T(8,128)(2,1)S(1)}, bf16[2,32,16,128]{3,2,1,0:T(8,128)(2,1)S(1)}) custom-call(f32[64,32,128]{2,1,0:T(8,128)S(1)} %get-tuple-element.74.tri_back, f32[64,16,128]{2,1,0:T(8,128)S(1)} %get-tuple-element.82.refs_0_, f32[64,16,128]{2,1,0:T(8,128)S(1)} %get-tuple-element.83.refs_1_, ...), custom_call_target="tpu_custom_call" | custom-call | flops 1000 | bytes 1000 | tf_op jit(solution)/shard_map/right_back/pallas_call | solution.py:487
  45.2 1.6 %collective-permute-start.10 = (bf16[2,32,16,128]{3,2,1,0:T(8,128)(2,1)S(1)}, bf16[2,32,16,128]{3,2,1,0:T(8,128)(2,1)S(1)}, u32[]{:S(2)}, u32[]{:S(2)}) collective-permute-start(bf16[2,32,16,128]{3,2,1,0:T(8,128)(2,1)S(1)} %get-tuple-element.87.refs_9_), channel_id=1, source_target_pairs={{0,8},{8,0},{16,24},{24,16},{1,9},{9,1},{17,25},{25,17},{2,10},{10... | collective-permute-start | bytes 786440 | tf_op jit(solution)/shard_map/ppermute | solution.py:371
  46.8 1.3 %heads.1 = (bf16[64,32,128]{2,1,0:T(8,128)(2,1)}, bf16[64,32,128]{2,1,0:T(8,128)(2,1)S(1)}, f32[128,128]{1,0:T(8,128)S(1)}, f32[128,128]{1,0:T(8,128)S(1)}) custom-call(bf16[64,32,128]{2,1,0:T(8,128)(2,1)S(1)} %get-tuple-element.71.tri_in, bf16[128,128]{1,0:T(8,128)(2,1)S(1)} %copy-done.6, f32[64,32,128]{2,1,0:T(8,128)S(1)} %get-tuple-element.72.gate, ...), custom_call_target="tpu_custom_call" | custom-call | flops 1000 | bytes 1000 | tf_op jit(solution)/shard_map/heads/pallas_call | solution.py:487
  48.1 2.0 %weights.1 = (f32[2,32,768]{2,1,0:T(8,128)S(1)}, bf16[2,32,768]{2,1,0:T(8,128)(2,1)S(1)}) custom-call(bf16[4,32,16,128]{3,2,1,0:T(8,128)(2,1)S(1)} %get-tuple-element.59.refs_2_.right_in, bf16[128,256]{1,0:T(8,128)(2,1)S(1)} %copy-done.1, bf16[128,256]{1,0:T(8,128)(2,1)S(1)} %copy-done.4, f32[128,128]{1,0:T(8,128)S(1)} %get-tuple-element.92.gate_part, ...), custom_call_target="tpu_custom_call" | custom-call | flops 1000 | bytes 1000 | tf_op jit(solution)/shard_map/weights/pallas_call | solution.py:487
  50.1 0.6 collective-permute-start.12
  50.7 2.3 %grad_middle.1 = (bf16[64,32,128]{2,1,0:T(8,128)(2,1)}, f32[8,128]{1,0:T(8,128)S(1)}) custom-call(bf16[64,32,128]{2,1,0:T(8,128)(2,1)S(1)} %copy-done.2, bf16[64,32,128]{2,1,0:T(8,128)(2,1)S(1)} %get-tuple-element.91.pre_back, bf16[128,128]{1,0:T(8,128)(2,1)S(1)} %copy-done.7, bf16[2,32,768]{2,1,0:T(8,128)(2,1)S(1)} %get-tuple-element.98._), custom_call_target="tpu_custom_call" | custom-call | flops 1000 | bytes 1000 | tf_op jit(solution)/shard_map/grad_middle/pallas_call | solution.py:487
  53.0 1.8 %collective-permute-done.12.came = bf16[2,32,768]{2,1,0:T(8,128)(2,1)S(1)} collective-permute-done((bf16[2,32,768]{2,1,0:T(8,128)(2,1)S(1)}, bf16[2,32,768]{2,1,0:T(8,128)(2,1)S(1)}, u32[]{:S(2)}, u32[]{:S(2)}) %collective-permute-start.12) | collective-permute-done | bytes 98336 | tf_op jit(solution)/shard_map/ppermute | solution.py:371
  54.8 1.6 %collective-permute-start.13 = (bf16[1,32,768]{2,1,0:T(8,128)(2,1)S(1)}, bf16[1,32,768]{2,1,0:T(8,128)(2,1)S(1)}, u32[]{:S(2)}, u32[]{:S(2)}) collective-permute-start(bf16[1,32,768]{2,1,0:T(8,128)(2,1)S(1)} %get-tuple-element.103), channel_id=1, source_target_pairs={{0,16},{8,24},{16,0},{24,8},{1,17},{9,25},{17,1},{25,9},{2,18},{10... | collective-permute-start | bytes 147464 | tf_op jit(solution)/shard_map/ppermute | solution.py:371
  56.5 0.1 halve.2
  56.5 1.5 %collective-permute-start.11 = (bf16[1,32,16,128]{3,2,1,0:T(8,128)(2,1)S(1)}, bf16[1,32,16,128]{3,2,1,0:T(8,128)(2,1)S(1)}, u32[]{:S(2)}, u32[]{:S(2)}) collective-permute-start(bf16[1,32,16,128]{3,2,1,0:T(8,128)(2,1)S(1)} %get-tuple-element.89.refs_0_), channel_id=1, source_target_pairs={{0,16},{8,24},{16,0},{24,8},{1,17},{9,25},{17,1},{25,9},{2,18},{10... | collective-permute-start | bytes 393224 | tf_op jit(solution)/shard_map/ppermute | solution.py:371
  58.0 1.5 %collective-permute-done.13.refs_1_ = bf16[1,32,768]{2,1,0:T(8,128)(2,1)S(1)} collective-permute-done((bf16[1,32,768]{2,1,0:T(8,128)(2,1)S(1)}, bf16[1,32,768]{2,1,0:T(8,128)(2,1)S(1)}, u32[]{:S(2)}, u32[]{:S(2)}) %collective-permute-start.13) | collective-permute-done | bytes 49184 | tf_op jit(solution)/shard_map/ppermute | solution.py:371
  59.5 2.0 %collective-permute-start.14 = (bf16[1,32,768]{2,1,0:T(8,128)(2,1)S(1)}, bf16[1,32,768]{2,1,0:T(8,128)(2,1)S(1)}, u32[]{:S(2)}, u32[]{:S(2)}) collective-permute-start(bf16[1,32,768]{2,1,0:T(8,128)(2,1)S(1)} %combine.3.refs_0_), channel_id=1, source_target_pairs={{0,2},{2,0},{4,6},{6,4},{1,3},{3,1},{5,7},{7,5},{8,10},{10,8},{12,... | collective-permute-start | bytes 147464 | tf_op jit(solution)/shard_map/ppermute | solution.py:371
  61.5 2.1 %left_side.1 = (bf16[64,16,128]{2,1,0:T(8,128)(2,1)}, f32[8,128]{1,0:T(8,128)S(1)}) custom-call(bf16[64,16,128]{2,1,0:T(8,128)(2,1)S(1)} %copy-done, bf16[128,256]{1,0:T(8,128)(2,1)S(1)} %copy-done.1, bf16[64,16,128]{2,1,0:T(8,128)(2,1)S(1)} %get-tuple-element.76._.refs_0_.refs_4_, bf16[64,16,128]{2,1,0:T(8,128)(2,1)S(1)} %collective-permute-done.7.refs_1_.refs_0_, ...), custom_call_target="tpu_custom_call" | custom-call | flops 1000 | bytes 1000 | tf_op jit(solution)/shard_map/left_side/pallas_call | solution.py:487
  63.7 3.2 %collective-permute-start.15 = (bf16[1,32,768]{2,1,0:T(8,128)(2,1)S(1)}, bf16[1,32,768]{2,1,0:T(8,128)(2,1)S(1)}, u32[]{:S(2)}, u32[]{:S(2)}) collective-permute-start(bf16[1,32,768]{2,1,0:T(8,128)(2,1)S(1)} %combine.4.refs_0_), channel_id=1, source_target_pairs={{0,4},{2,6},{4,0},{6,2},{1,5},{3,7},{5,1},{7,3},{8,12},{10,14},{12... | collective-permute-start | bytes 147464 | tf_op jit(solution)/shard_map/ppermute | solution.py:371
  66.9 1.5 %right_side.1 = (bf16[32,16,128]{2,1,0:T(8,128)(2,1)}, f32[8,128]{1,0:T(8,128)S(1)}) custom-call(bf16[32,16,128]{2,1,0:T(8,128)(2,1)S(1)} %copy-done.5, bf16[128,256]{1,0:T(8,128)(2,1)S(1)} %copy-done.4, f32[32,16,128]{2,1,0:T(8,128)S(1)} %bitcast.2, bf16[32,16,128]{2,1,0:T(8,128)(2,1)S(1)} %bitcast.3), custom_call_target="tpu_custom_call" | custom-call | flops 1000 | bytes 1000 | tf_op jit(solution)/shard_map/right_side/pallas_call | solution.py:487
  68.3 0.6 collective-permute-done.15.refs_1_
  68.9 1.1 %collective-permute-start.16 = (bf16[1,32,768]{2,1,0:T(8,128)(2,1)S(1)}, bf16[1,32,768]{2,1,0:T(8,128)(2,1)S(1)}, u32[]{:S(2)}, u32[]{:S(2)}) collective-permute-start(bf16[1,32,768]{2,1,0:T(8,128)(2,1)S(1)} %combine.5.own), channel_id=1, source_target_pairs={{0,8},{8,0},{16,24},{24,16},{1,9},{9,1},{17,25},{25,17},{2,10},{10... | collective-permute-start | bytes 147464 | tf_op jit(solution)/shard_map/ppermute | solution.py:371
  70.1 3.0 %collective-permute-done.16.came = bf16[1,32,768]{2,1,0:T(8,128)(2,1)S(1)} collective-permute-done((bf16[1,32,768]{2,1,0:T(8,128)(2,1)S(1)}, bf16[1,32,768]{2,1,0:T(8,128)(2,1)S(1)}, u32[]{:S(2)}, u32[]{:S(2)}) %collective-permute-start.16) | collective-permute-done | bytes 49184 | tf_op jit(solution)/shard_map/ppermute | solution.py:371
  73.1 1.6 %collective-permute-start.17 = (bf16[2,32,768]{2,1,0:T(8,128)(2,1)S(1)}, bf16[2,32,768]{2,1,0:T(8,128)(2,1)S(1)}, u32[]{:S(2)}, u32[]{:S(2)}) collective-permute-start(bf16[2,32,768]{2,1,0:T(8,128)(2,1)S(1)} %stack.1.refs_0_), channel_id=1, source_target_pairs={{0,16},{8,24},{16,0},{24,8},{1,17},{9,25},{17,1},{25,9},{2,18},{10... | collective-permute-start | bytes 294920 | tf_op jit(solution)/shard_map/ppermute | solution.py:371
  74.7 3.1 %collective-permute-done.17.refs_1_ = bf16[2,32,768]{2,1,0:T(8,128)(2,1)S(1)} collective-permute-done((bf16[2,32,768]{2,1,0:T(8,128)(2,1)S(1)}, bf16[2,32,768]{2,1,0:T(8,128)(2,1)S(1)}, u32[]{:S(2)}, u32[]{:S(2)}) %collective-permute-start.17) | collective-permute-done | bytes 98336 | tf_op jit(solution)/shard_map/ppermute | solution.py:371
  77.8 0.8 deltas.1
  (29 shorter events, 0.2 us)
Async XLA Ops:
  0.6 9.2 %copy-start.6 = (bf16[128,128]{1,0:T(8,128)(2,1)S(1)}, bf16[128,128]{1,0:T(8,128)(2,1)}, u32[]{:S(2)}) copy-start(bf16[128,128]{1,0:T(8,128)(2,1)} %out_w.1) | copy-start | bytes 98308
  0.6 9.2 %copy-start.7 = (bf16[128,128]{1,0:T(8,128)(2,1)S(1)}, bf16[128,128]{1,0:T(8,128)(2,1)}, u32[]{:S(2)}) copy-start(bf16[128,128]{1,0:T(8,128)(2,1)} %gate_weight.3) | copy-start | bytes 98308
  0.7 9.2 %copy-start.3 = (bf16[64,32,128]{2,1,0:T(8,128)(2,1)S(1)}, bf16[64,32,128]{2,1,0:T(8,128)(2,1)}, u32[]{:S(2)}) copy-start(bf16[64,32,128]{2,1,0:T(8,128)(2,1)} %cotangent.3) | copy-start | bytes 1572868
  0.7 9.2 %copy-start.2 = (bf16[64,32,128]{2,1,0:T(8,128)(2,1)S(1)}, bf16[64,32,128]{2,1,0:T(8,128)(2,1)}, u32[]{:S(2)}) copy-start(bf16[64,32,128]{2,1,0:T(8,128)(2,1)} %middle.5) | copy-start | bytes 1572868
  0.7 16.3 %collective-permute-start = (bf16[64,16,128]{2,1,0:T(8,128)(2,1)}, bf16[64,16,128]{2,1,0:T(8,128)(2,1)S(1)}, u32[]{:S(2)}, u32[]{:S(2)}) collective-permute-start(bf16[64,16,128]{2,1,0:T(8,128)(2,1)} %raw.2), channel_id=1, source_target_pairs={{0,4},{2,6},{4,0},{6,2},{1,5},{3,7},{5,1},{7,3},{8,12},{10,14},{12... | collective-permute-start | bytes 786440 | tf_op jit(solution)/shard_map/ppermute | solution.py:371
  4.8 7.5 %collective-permute-start.3 = (bf16[32,16,128]{2,1,0:T(8,128)(2,1)}, bf16[32,16,128]{2,1,0:T(8,128)(2,1)S(1)}, u32[]{:S(2)}, u32[]{:S(2)}) collective-permute-start(bf16[32,16,128]{2,1,0:T(8,128)(2,1)} %raw.3), channel_id=1, source_target_pairs={{0,24},{8,16},{16,8},{24,0},{1,25},{9,17},{17,9},{25,1},{2,26},{10... | collective-permute-start | bytes 393224 | tf_op jit(solution)/shard_map/ppermute | solution.py:371
  7.2 6.4 %collective-permute-start.2 = (bf16[32,16,128]{2,1,0:T(8,128)(2,1)}, bf16[32,16,128]{2,1,0:T(8,128)(2,1)S(1)}, u32[]{:S(2)}, u32[]{:S(2)}) collective-permute-start(bf16[32,16,128]{2,1,0:T(8,128)(2,1)} %raw.3), channel_id=1, source_target_pairs={{0,16},{8,24},{16,0},{24,8},{1,17},{9,25},{17,1},{25,9},{2,18},{10... | collective-permute-start | bytes 393224 | tf_op jit(solution)/shard_map/ppermute | solution.py:371
  7.7 6.0 %collective-permute-start.1 = (bf16[32,16,128]{2,1,0:T(8,128)(2,1)}, bf16[32,16,128]{2,1,0:T(8,128)(2,1)S(1)}, u32[]{:S(2)}, u32[]{:S(2)}) collective-permute-start(bf16[32,16,128]{2,1,0:T(8,128)(2,1)} %raw.3), channel_id=1, source_target_pairs={{0,8},{8,0},{16,24},{24,16},{1,9},{9,1},{17,25},{25,17},{2,10},{10... | collective-permute-start | bytes 393224 | tf_op jit(solution)/shard_map/ppermute | solution.py:371
  8.3 12.4 %collective-permute-start.6 = (bf16[64,16,128]{2,1,0:T(8,128)(2,1)}, bf16[64,16,128]{2,1,0:T(8,128)(2,1)S(1)}, u32[]{:S(2)}, u32[]{:S(2)}) collective-permute-start(bf16[64,16,128]{2,1,0:T(8,128)(2,1)} %raw.2), channel_id=1, source_target_pairs={{0,2},{2,0},{4,6},{6,4},{1,3},{3,1},{5,7},{7,5},{8,10},{10,8},{12,... | collective-permute-start | bytes 786440 | tf_op jit(solution)/shard_map/ppermute | solution.py:371
  9.9 3.9 %copy-start.4 = (bf16[128,256]{1,0:T(8,128)(2,1)S(1)}, bf16[128,256]{1,0:T(8,128)(2,1)}, u32[]{:S(2)}) copy-start(bf16[128,256]{1,0:T(8,128)(2,1)} %right_w.1) | copy-start | bytes 196612
  9.9 3.8 %copy-start.5 = (bf16[32,16,128]{2,1,0:T(8,128)(2,1)S(1)}, bf16[32,16,128]{2,1,0:T(8,128)(2,1)}, u32[]{:S(2)}) copy-start(bf16[32,16,128]{2,1,0:T(8,128)(2,1)} %raw.3) | copy-start | bytes 393220
  12.2 4.8 %copy-start = (bf16[64,16,128]{2,1,0:T(8,128)(2,1)S(1)}, bf16[64,16,128]{2,1,0:T(8,128)(2,1)}, u32[]{:S(2)}) copy-start(bf16[64,16,128]{2,1,0:T(8,128)(2,1)} %raw.2) | copy-start | bytes 786436
  17.0 1.7 %copy-start.1 = (bf16[128,256]{1,0:T(8,128)(2,1)S(1)}, bf16[128,256]{1,0:T(8,128)(2,1)}, u32[]{:S(2)}) copy-start(bf16[128,256]{1,0:T(8,128)(2,1)} %left_w.1) | copy-start | bytes 196612
  17.1 8.4 %collective-permute-start.4 = (bf16[64,16,128]{2,1,0:T(8,128)(2,1)S(1)}, bf16[64,16,128]{2,1,0:T(8,128)(2,1)S(1)}, u32[]{:S(2)}, u32[]{:S(2)}) collective-permute-start(bf16[64,16,128]{2,1,0:T(8,128)(2,1)S(1)} %get-tuple-element.61), channel_id=1, source_target_pairs={{0,2},{2,0},{4,6},{6,4},{1,3},{3,1},{5,7},{7,5},{8,10},{10,8},{12,... | collective-permute-start | bytes 786440 | tf_op jit(solution)/shard_map/ppermute | solution.py:371
  17.9 7.6 %collective-permute-start.5 = (bf16[64,16,128]{2,1,0:T(8,128)(2,1)S(1)}, bf16[64,16,128]{2,1,0:T(8,128)(2,1)S(1)}, u32[]{:S(2)}, u32[]{:S(2)}) collective-permute-start(bf16[64,16,128]{2,1,0:T(8,128)(2,1)S(1)} %get-tuple-element.62), channel_id=1, source_target_pairs={{0,0},{2,4},{4,2},{6,6},{1,1},{3,5},{5,3},{7,7},{8,8},{10,12},{12,... | collective-permute-start | bytes 786440 | tf_op jit(solution)/shard_map/ppermute | solution.py:409
  30.6 25.8 %collective-permute-start.8 = (bf16[64,16,128]{2,1,0:T(8,128)(2,1)S(1)}, bf16[64,16,128]{2,1,0:T(8,128)(2,1)S(1)}, u32[]{:S(2)}, u32[]{:S(2)}) collective-permute-start(bf16[64,16,128]{2,1,0:T(8,128)(2,1)S(1)} %get-tuple-element.79.refs_6_), channel_id=1, source_target_pairs={{0,4},{2,6},{4,0},{6,2},{1,5},{3,7},{5,1},{7,3},{8,12},{10,14},{12... | collective-permute-start | bytes 786440 | tf_op jit(solution)/shard_map/ppermute | solution.py:371
  36.2 20.3 %collective-permute-start.9 = (bf16[64,16,128]{2,1,0:T(8,128)(2,1)S(1)}, bf16[64,16,128]{2,1,0:T(8,128)(2,1)S(1)}, u32[]{:S(2)}, u32[]{:S(2)}) collective-permute-start(bf16[64,16,128]{2,1,0:T(8,128)(2,1)S(1)} %get-tuple-element.80.refs_7_), channel_id=1, source_target_pairs={{0,6},{2,4},{4,2},{6,0},{1,7},{3,5},{5,3},{7,1},{8,14},{10,12},{12... | collective-permute-start | bytes 786440 | tf_op jit(solution)/shard_map/ppermute | solution.py:371
  39.6 16.8 %collective-permute-start.7 = (bf16[64,16,128]{2,1,0:T(8,128)(2,1)S(1)}, bf16[64,16,128]{2,1,0:T(8,128)(2,1)S(1)}, u32[]{:S(2)}, u32[]{:S(2)}) collective-permute-start(bf16[64,16,128]{2,1,0:T(8,128)(2,1)S(1)} %get-tuple-element.78.refs_5_), channel_id=1, source_target_pairs={{0,2},{2,0},{4,6},{6,4},{1,3},{3,1},{5,7},{7,5},{8,10},{10,8},{12,... | collective-permute-start | bytes 786440 | tf_op jit(solution)/shard_map/ppermute | solution.py:371
  45.2 11.2 %collective-permute-start.10 = (bf16[2,32,16,128]{3,2,1,0:T(8,128)(2,1)S(1)}, bf16[2,32,16,128]{3,2,1,0:T(8,128)(2,1)S(1)}, u32[]{:S(2)}, u32[]{:S(2)}) collective-permute-start(bf16[2,32,16,128]{3,2,1,0:T(8,128)(2,1)S(1)} %get-tuple-element.87.refs_9_), channel_id=1, source_target_pairs={{0,8},{8,0},{16,24},{24,16},{1,9},{9,1},{17,25},{25,17},{2,10},{10... | collective-permute-start | bytes 786440 | tf_op jit(solution)/shard_map/ppermute | solution.py:371
  50.1 4.7 %collective-permute-start.12 = (bf16[2,32,768]{2,1,0:T(8,128)(2,1)S(1)}, bf16[2,32,768]{2,1,0:T(8,128)(2,1)S(1)}, u32[]{:S(2)}, u32[]{:S(2)}) collective-permute-start(bf16[2,32,768]{2,1,0:T(8,128)(2,1)S(1)} %get-tuple-element.98._), channel_id=1, source_target_pairs={{0,8},{8,0},{16,24},{24,16},{1,9},{9,1},{17,25},{25,17},{2,10},{10... | collective-permute-start | bytes 294920 | tf_op jit(solution)/shard_map/ppermute | solution.py:371
  54.8 4.6 %collective-permute-start.13 = (bf16[1,32,768]{2,1,0:T(8,128)(2,1)S(1)}, bf16[1,32,768]{2,1,0:T(8,128)(2,1)S(1)}, u32[]{:S(2)}, u32[]{:S(2)}) collective-permute-start(bf16[1,32,768]{2,1,0:T(8,128)(2,1)S(1)} %get-tuple-element.103), channel_id=1, source_target_pairs={{0,16},{8,24},{16,0},{24,8},{1,17},{9,25},{17,1},{25,9},{2,18},{10... | collective-permute-start | bytes 147464 | tf_op jit(solution)/shard_map/ppermute | solution.py:371
  56.5 10.3 %collective-permute-start.11 = (bf16[1,32,16,128]{3,2,1,0:T(8,128)(2,1)S(1)}, bf16[1,32,16,128]{3,2,1,0:T(8,128)(2,1)S(1)}, u32[]{:S(2)}, u32[]{:S(2)}) collective-permute-start(bf16[1,32,16,128]{3,2,1,0:T(8,128)(2,1)S(1)} %get-tuple-element.89.refs_0_), channel_id=1, source_target_pairs={{0,16},{8,24},{16,0},{24,8},{1,17},{9,25},{17,1},{25,9},{2,18},{10... | collective-permute-start | bytes 393224 | tf_op jit(solution)/shard_map/ppermute | solution.py:371
  59.5 4.2 %collective-permute-start.14 = (bf16[1,32,768]{2,1,0:T(8,128)(2,1)S(1)}, bf16[1,32,768]{2,1,0:T(8,128)(2,1)S(1)}, u32[]{:S(2)}, u32[]{:S(2)}) collective-permute-start(bf16[1,32,768]{2,1,0:T(8,128)(2,1)S(1)} %combine.3.refs_0_), channel_id=1, source_target_pairs={{0,2},{2,0},{4,6},{6,4},{1,3},{3,1},{5,7},{7,5},{8,10},{10,8},{12,... | collective-permute-start | bytes 147464 | tf_op jit(solution)/shard_map/ppermute | solution.py:371
  63.7 5.3 %collective-permute-start.15 = (bf16[1,32,768]{2,1,0:T(8,128)(2,1)S(1)}, bf16[1,32,768]{2,1,0:T(8,128)(2,1)S(1)}, u32[]{:S(2)}, u32[]{:S(2)}) collective-permute-start(bf16[1,32,768]{2,1,0:T(8,128)(2,1)S(1)} %combine.4.refs_0_), channel_id=1, source_target_pairs={{0,4},{2,6},{4,0},{6,2},{1,5},{3,7},{5,1},{7,3},{8,12},{10,14},{12... | collective-permute-start | bytes 147464 | tf_op jit(solution)/shard_map/ppermute | solution.py:371
  68.9 4.2 %collective-permute-start.16 = (bf16[1,32,768]{2,1,0:T(8,128)(2,1)S(1)}, bf16[1,32,768]{2,1,0:T(8,128)(2,1)S(1)}, u32[]{:S(2)}, u32[]{:S(2)}) collective-permute-start(bf16[1,32,768]{2,1,0:T(8,128)(2,1)S(1)} %combine.5.own), channel_id=1, source_target_pairs={{0,8},{8,0},{16,24},{24,16},{1,9},{9,1},{17,25},{25,17},{2,10},{10... | collective-permute-start | bytes 147464 | tf_op jit(solution)/shard_map/ppermute | solution.py:371
  73.1 4.7 %collective-permute-start.17 = (bf16[2,32,768]{2,1,0:T(8,128)(2,1)S(1)}, bf16[2,32,768]{2,1,0:T(8,128)(2,1)S(1)}, u32[]{:S(2)}, u32[]{:S(2)}) collective-permute-start(bf16[2,32,768]{2,1,0:T(8,128)(2,1)S(1)} %stack.1.refs_0_), channel_id=1, source_target_pairs={{0,16},{8,24},{16,0},{24,8},{1,17},{9,25},{17,1},{25,9},{2,18},{10... | collective-permute-start | bytes 294920 | tf_op jit(solution)/shard_map/ppermute | solution.py:371

commit v12 on v11

--- a/solution.py
+++ b/solution.py
@@ -89,7 +89,8 @@
 
 
 def right_kernel(n_rows, n_blk, k_left, *refs):
-    raw, (weight, act_out, in_out, *flip_out) = refs[:n_rows], refs[n_rows:]
+    raw = [stack.at[at] for stack in refs[:2] for at in range(stack.shape[0])]
+    weight, act_out, in_out, *flip_out = refs[2:]
     n_j, k_right, width = raw[0].shape
     n_k = k_left * n_blk
     unit = math.gcd(k_left, k_right)
@@ -420,12 +421,11 @@
 
 
 def combine_kernel(n, *refs):
-    total = refs[0][0].astype(f32)
-    for at in range(1, refs[0].shape[0]):
-        total = total + refs[0][at].astype(f32)
-    for other in refs[1:n]:
-        total = total + other[0].astype(f32)
-    refs[-1][0] = total.astype(bf16)
+    totals = [ref[0].astype(f32) for ref in refs[:n]]
+    while len(totals) > 1:
+        pairs = [a + b for a, b in zip(totals[::2], totals[1::2])]
+        totals = pairs + totals[2 * len(pairs) :]
+    refs[-1][0] = totals[0].astype(bf16)
 
 
 def combine(pieces, after=()):
@@ -436,15 +436,6 @@
         after=len(after),
     )(*pieces, *after)
     return total
-
-
-def everywhere_sum(part, axis, n, after):
-    bit = 1
-    while bit < n:
-        part = combine([part, exchange(part, axis, n, bit)], after[:1])
-        after = after[1:]
-        bit *= 2
-    return part
 
 
 def stack_kernel(own, came, both):
@@ -463,9 +454,8 @@
     return part, came
 
 
-def deltas_kernel(*refs):
-    stacks, outs = refs[:2], refs[2:]
-    pieces = [stack.at[at] for stack in stacks for at in range(stack.shape[0])]
+def deltas_kernel(n_rows, *refs):
+    pieces, outs = [ref.at[0] for ref in refs[:n_rows]], refs[n_rows + 1 :]
     size = pieces[0].shape[0]
     for s, piece in enumerate(pieces):
         start = pl.multiple_of(lax.bitwise_xor(lax.axis_index("rows"), s) * size, size)
@@ -513,7 +503,7 @@
     n_i, k_left, width = pair_left.shape
     n_j, k_right, _ = pair_right.shape
     n_k = k_left * n_blk
-    right_raw = [pair_right] + [exchange(pair_right, "rows", n_rows, s) for s in range(1, n_rows)]
+    right_raw = gather_doubling(pair_right[None], "rows", n_rows)
     middle_shape = (n_i, n_j, width)
     gate, middle_in, head_back, tri_up = call(
         middle_kernel,
@@ -527,7 +517,7 @@
         [shape((n_j * n_k, width), f32), shape((n_rows, n_j, k_right, width), bf16)]
         + [shape((k_left, n_j, width), f32)] * n_blk,
     )(*right_raw, right_weight)
-    left_raw = gather_left(pair_left, n_blk, (right_in, middle_in))
+    left_raw = gather_left(pair_left, n_blk, (right_raw[0], middle_in))
     left_act, left_in, total = [], [], []
     act_shape = shape(pair_left.shape, f32)
     in_shape = shape(pair_left.shape, bf16)
@@ -593,16 +583,17 @@
     grad_left, done_left = call(side_kernel, "left_side", [shape(pair_left.shape, bf16), MARK])(
         pair_left, left_weight, *left_back
     )
+    part = combine([part] + [exchange(part, "blk", n_blk, s) for s in range(1, n_blk)], (done_left,))
+    pieces = [part] + [exchange(part, "rows", n_rows, s) for s in range(1, n_rows)]
     grad_right, done_right = call(side_kernel, "right_side", [shape(pair_right.shape, bf16), MARK])(
         pair_right, right_weight, kept.reshape(pair_right.shape), came.reshape(pair_right.shape)
     )
-    part = everywhere_sum(part, "blk", n_blk, (done_left, done_right))
-    pieces = gather_doubling(part, "rows", n_rows)
     deltas = call(
-        deltas_kernel,
+        functools.partial(deltas_kernel, n_rows),
         "deltas",
         [shape(x.shape, f32) for x in (left_weight, right_weight, gate_weight, output_weight)],
-    )(*pieces)
+        after=1,
+    )(*pieces, done_right)
     return (
         update,
         grad_left,

time: 78.7 us -> 76.4 us (0.971)
  waiting for transfers between devices: 13.7 us -> 10.6 us
  local copies, waits for them, and re-layouts: 0.04 us -> 0.95 us
    ppermute x17 -> x18, waiting for transfers between devices: 13.7 us -> 10.6 us  [exchange(): return lax.ppermute(x, axis, [(a, a ^ bit) for a in range(n)])]
    unnamed x16 -> x18, local copies, waits for them, and re-layouts: 0.04 us -> 0.95 us
    ppermute x17 -> x18, starting transfers between devices: 30 us -> 29.7 us  [exchange(): return lax.ppermute(x, axis, [(a, a ^ bit) for a in range(n)])]
    pallas_call x25 -> x24, Pallas kernels: 33.2 us -> 33.2 us  [run(): pl.pallas_call(kernel, in_specs=[pl.BlockSpec(memory_space=space) for spa...]
  transfers between devices with their start and end apart: 18 -> 19, of which waited for: 9 -> 8; matrix products, arithmetic and copies ran while one was open for 0% -> 0% of each run, Pallas kernels for 35% -> 36%
where the time goes in v12:
time: 76.4 us; the launch traced here: 76.3 us
  Pallas kernels  33.2 us (43%)
  starting transfers between devices  30.7 us (40%)
  waiting for transfers between devices  10.6 us (14%)
  local copies, waits for them, and re-layouts  0.95 us (1%)
  between operations  0.86 us (1%)
    pallas_call x24, Pallas kernels, run(): pl.pallas_call(kernel, in_specs=[pl.BlockSpec(memory_space=space) for spa...  33.2 us
    ppermute x18, starting transfers between devices, exchange(): return lax.ppermute(x, axis, [(a, a ^ bit) for a in range(n)])  29.7 us
    ppermute x18, waiting for transfers between devices, exchange(): return lax.ppermute(x, axis, [(a, a ^ bit) for a in range(n)])  10.6 us
  transfers between devices with their start and end apart: 19, of which 8 were waited for; matrix products, arithmetic and copies ran while one was open for 0% of the time, Pallas kernels for 36%

profile of v12, /device:TPU:0, one launch (start us, length us, event | category | flops | bytes accessed | tf_op | source)
XLA Modules:
  0.0 76.3 jit_solution(6175419823329706486)
XLA Ops:
  0.6 4.1 %collective-permute-start = (bf16[64,16,128]{2,1,0:T(8,128)(2,1)}, bf16[64,16,128]{2,1,0:T(8,128)(2,1)S(1)}, u32[]{:S(2)}, u32[]{:S(2)}) collective-permute-start(bf16[64,16,128]{2,1,0:T(8,128)(2,1)} %raw.2), channel_id=1, source_target_pairs={{0,4},{2,6},{4,0},{6,2},{1,5},{3,7},{5,1},{7,3},{8,12},{10,14},{12... | collective-permute-start | bytes 786440 | tf_op jit(solution)/shard_map/ppermute | solution.py:372
  4.7 1.5 %collective-permute-start.1 = (bf16[1,32,16,128]{3,2,1,0:T(8,128)(2,1)}, bf16[1,32,16,128]{3,2,1,0:T(8,128)(2,1)S(1)}, u32[]{:S(2)}, u32[]{:S(2)}) collective-permute-start(bf16[1,32,16,128]{3,2,1,0:T(8,128)(2,1)} %bitcast.3), channel_id=1, source_target_pairs={{0,8},{8,0},{16,24},{24,16},{1,9},{9,1},{17,25},{25,17},{2,10},{10... | collective-permute-start | bytes 393224 | tf_op jit(solution)/shard_map/ppermute | solution.py:372
  6.2 1.6 %collective-permute-start.5 = (bf16[64,16,128]{2,1,0:T(8,128)(2,1)}, bf16[64,16,128]{2,1,0:T(8,128)(2,1)S(1)}, u32[]{:S(2)}, u32[]{:S(2)}) collective-permute-start(bf16[64,16,128]{2,1,0:T(8,128)(2,1)} %raw.2), channel_id=1, source_target_pairs={{0,2},{2,0},{4,6},{6,4},{1,3},{3,1},{5,7},{7,5},{8,10},{10,8},{12,... | collective-permute-start | bytes 786440 | tf_op jit(solution)/shard_map/ppermute | solution.py:372
  7.8 2.1 %collective-permute-done.1.came = bf16[1,32,16,128]{3,2,1,0:T(8,128)(2,1)S(1)} collective-permute-done((bf16[1,32,16,128]{3,2,1,0:T(8,128)(2,1)}, bf16[1,32,16,128]{3,2,1,0:T(8,128)(2,1)S(1)}, u32[]{:S(2)}, u32[]{:S(2)}) %collective-permute-start.1) | collective-permute-done | bytes 131104 | tf_op jit(solution)/shard_map/ppermute | solution.py:372
  9.9 0.9 %copy-done.5 = bf16[32,16,128]{2,1,0:T(8,128)(2,1)S(1)} copy-done((bf16[32,16,128]{2,1,0:T(8,128)(2,1)S(1)}, bf16[32,16,128]{2,1,0:T(8,128)(2,1)}, u32[]{:S(2)}) %copy-start.5) | copy-done | bytes 131096
  10.8 0.0 copy-start.2
  10.9 0.0 copy-start.8
  10.9 1.6 %collective-permute-start.4 = (bf16[2,32,16,128]{3,2,1,0:T(8,128)(2,1)S(1)}, bf16[2,32,16,128]{3,2,1,0:T(8,128)(2,1)S(1)}, u32[]{:S(2)}, u32[]{:S(2)}) collective-permute-start(bf16[2,32,16,128]{3,2,1,0:T(8,128)(2,1)S(1)} %stack.1.refs_2_.refs_0_), channel_id=1, source_target_pairs={{0,16},{8,24},{16,0},{24,8},{1,17},{9,25},{17,1},{25,9},{2,18},{10... | collective-permute-start | bytes 786440 | tf_op jit(solution)/shard_map/ppermute | solution.py:372
  12.5 0.0 copy-start
  12.5 2.3 %middle.3 = (f32[64,32,128]{2,1,0:T(8,128)S(1)}, bf16[64,32,128]{2,1,0:T(8,128)(2,1)S(1)}, bf16[64,32,128]{2,1,0:T(8,128)(2,1)S(1)}, f32[64,32,128]{2,1,0:T(8,128)S(1)}) custom-call(bf16[64,32,128]{2,1,0:T(8,128)(2,1)S(1)} %copy-done.2, bf16[64,32,128]{2,1,0:T(8,128)(2,1)S(1)} %copy-done.3, bf16[128,128]{1,0:T(8,128)(2,1)S(1)} %copy-done.8, ...), custom_call_target="tpu_custom_call" | custom-call | flops 1000 | bytes 1000 | tf_op jit(solution)/shard_map/middle/pallas_call | solution.py:477
  14.9 2.1 %collective-permute-done.refs_0_ = bf16[64,16,128]{2,1,0:T(8,128)(2,1)S(1)} collective-permute-done((bf16[64,16,128]{2,1,0:T(8,128)(2,1)}, bf16[64,16,128]{2,1,0:T(8,128)(2,1)S(1)}, u32[]{:S(2)}, u32[]{:S(2)}) %collective-permute-start) | collective-permute-done | bytes 262176 | tf_op jit(solution)/shard_map/ppermute | solution.py:372
  17.0 0.8 %collective-permute-start.2 = (bf16[64,16,128]{2,1,0:T(8,128)(2,1)S(1)}, bf16[64,16,128]{2,1,0:T(8,128)(2,1)S(1)}, u32[]{:S(2)}, u32[]{:S(2)}) collective-permute-start(bf16[64,16,128]{2,1,0:T(8,128)(2,1)S(1)} %get-tuple-element.60), channel_id=1, source_target_pairs={{0,2},{2,0},{4,6},{6,4},{1,3},{3,1},{5,7},{7,5},{8,10},{10,8},{12,... | collective-permute-start | bytes 786440 | tf_op jit(solution)/shard_map/ppermute | solution.py:372
  17.9 1.0 %collective-permute-start.3 = (bf16[64,16,128]{2,1,0:T(8,128)(2,1)S(1)}, bf16[64,16,128]{2,1,0:T(8,128)(2,1)S(1)}, u32[]{:S(2)}, u32[]{:S(2)}) collective-permute-start(bf16[64,16,128]{2,1,0:T(8,128)(2,1)S(1)} %get-tuple-element.61), channel_id=1, source_target_pairs={{0,0},{2,4},{4,2},{6,6},{1,1},{3,5},{5,3},{7,7},{8,8},{10,12},{12,... | collective-permute-start | bytes 786440 | tf_op jit(solution)/shard_map/ppermute | solution.py:410
  18.9 1.9 %right.1 = (f32[2048,128]{1,0:T(8,128)S(1)}, bf16[4,32,16,128]{3,2,1,0:T(8,128)(2,1)S(1)}, f32[16,32,128]{2,1,0:T(8,128)S(1)}, f32[16,32,128]{2,1,0:T(8,128)S(1)...) custom-call(bf16[2,32,16,128]{3,2,1,0:T(8,128)(2,1)S(1)} %stack.1.refs_2_.refs_0_, ...), custom_call_target="tpu_custom_call" | custom-call | flops 1000 | bytes 1000 | tf_op jit(solution)/shard_map/right/pallas_call | solution.py:477
  20.8 1.9 %left.3 = (f32[64,16,128]{2,1,0:T(8,128)S(1)}, bf16[64,16,128]{2,1,0:T(8,128)(2,1)S(1)}, f32[64,32,128]{2,1,0:T(8,128)S(1)}) custom-call(bf16[64,16,128]{2,1,0:T(8,128)(2,1)S(1)} %copy-done, bf16[128,256]{1,0:T(8,128)(2,1)S(1)} %copy-done.1, f32[16,32,128]{2,1,0:T(8,128)S(1)} %get-tuple-element.66.refs_2_), custom_call_target="tpu_custom_call" | custom-call | flops 1000 | bytes 1000 | tf_op jit(solution)/shard_map/left/pallas_call | solution.py:477
  22.7 2.0 %left.4 = (f32[64,16,128]{2,1,0:T(8,128)S(1)}, bf16[64,16,128]{2,1,0:T(8,128)(2,1)S(1)}, f32[64,32,128]{2,1,0:T(8,128)S(1)}) custom-call(bf16[64,16,128]{2,1,0:T(8,128)(2,1)S(1)} %collective-permute-done.5.refs_0_, bf16[128,256]{1,0:T(8,128)(2,1)S(1)} %copy-done.1, f32[16,32,128]{2,1,0:T(8,128)S(1)} %get-tuple-element.65.refs_2_, ...), custom_call_target="tpu_custom_call" | custom-call | flops 1000 | bytes 1000 | tf_op jit(solution)/shard_map/left/pallas_call | solution.py:477
  24.7 2.0 %left.5 = (f32[64,16,128]{2,1,0:T(8,128)S(1)}, bf16[64,16,128]{2,1,0:T(8,128)(2,1)S(1)}, f32[64,32,128]{2,1,0:T(8,128)S(1)}) custom-call(bf16[64,16,128]{2,1,0:T(8,128)(2,1)S(1)} %collective-permute-done.refs_0_, bf16[128,256]{1,0:T(8,128)(2,1)S(1)} %copy-done.1, f32[16,32,128]{2,1,0:T(8,128)S(1)} %get-tuple-element.64.refs_2_, ...), custom_call_target="tpu_custom_call" | custom-call | flops 1000 | bytes 1000 | tf_op jit(solution)/shard_map/left/pallas_call | solution.py:477
  26.7 2.9 %triangle.1 = (f32[64,16,128]{2,1,0:T(8,128)S(1)}, bf16[64,16,128]{2,1,0:T(8,128)(2,1)S(1)}, bf16[64,32,128]{2,1,0:T(8,128)(2,1)S(1)}, f32[64,32,128]{2,1,0:T(8,128)S(1)}) custom-call(bf16[64,16,128]{2,1,0:T(8,128)(2,1)S(1)} %collective-permute-done.2.refs_0_, bf16[64,16,128]{2,1,0:T(8,128)(2,1)S(1)} %collective-permute-done.3.refs_1_, ...), custom_call_target="tpu_custom_call" | custom-call | flops 1000 | bytes 1000 | tf_op jit(solution)/shard_map/triangle/pallas_call | solution.py:477
  29.6 2.2 %left_back.3 = (bf16[64,16,128]{2,1,0:T(8,128)(2,1)S(1)}, bf16[64,16,128]{2,1,0:T(8,128)(2,1)S(1)}) custom-call(f32[64,32,128]{2,1,0:T(8,128)S(1)} %get-tuple-element.73.tri_back, f32[2048,128]{1,0:T(8,128)S(1)} %get-tuple-element.74.right_act), custom_call_target="tpu_custom_call" | custom-call | flops 1000 | bytes 1000 | tf_op jit(solution)/shard_map/left_back/pallas_call | solution.py:477
  31.8 4.6 %collective-permute-start.7 = (bf16[64,16,128]{2,1,0:T(8,128)(2,1)S(1)}, bf16[64,16,128]{2,1,0:T(8,128)(2,1)S(1)}, u32[]{:S(2)}, u32[]{:S(2)}) collective-permute-start(bf16[64,16,128]{2,1,0:T(8,128)(2,1)S(1)} %get-tuple-element.78.refs_6_), channel_id=1, source_target_pairs={{0,4},{2,6},{4,0},{6,2},{1,5},{3,7},{5,1},{7,3},{8,12},{10,14},{12... | collective-permute-start | bytes 786440 | tf_op jit(solution)/shard_map/ppermute | solution.py:372
  36.5 2.9 %collective-permute-start.8 = (bf16[64,16,128]{2,1,0:T(8,128)(2,1)S(1)}, bf16[64,16,128]{2,1,0:T(8,128)(2,1)S(1)}, u32[]{:S(2)}, u32[]{:S(2)}) collective-permute-start(bf16[64,16,128]{2,1,0:T(8,128)(2,1)S(1)} %get-tuple-element.79.refs_7_), channel_id=1, source_target_pairs={{0,6},{2,4},{4,2},{6,0},{1,7},{3,5},{5,3},{7,1},{8,14},{10,12},{12... | collective-permute-start | bytes 786440 | tf_op jit(solution)/shard_map/ppermute | solution.py:372
  39.4 2.2 %left_back.2 = (bf16[64,16,128]{2,1,0:T(8,128)(2,1)S(1)}, bf16[64,16,128]{2,1,0:T(8,128)(2,1)S(1)}) custom-call(f32[64,32,128]{2,1,0:T(8,128)S(1)} %get-tuple-element.73.tri_back, f32[2048,128]{1,0:T(8,128)S(1)} %get-tuple-element.74.right_act), custom_call_target="tpu_custom_call" | custom-call | flops 1000 | bytes 1000 | tf_op jit(solution)/shard_map/left_back/pallas_call | solution.py:477
  41.6 0.1 collective-permute-start.6
  41.7 5.5 %right_back.1 = (bf16[2,32,16,128]{3,2,1,0:T(8,128)(2,1)S(1)}, bf16[2,32,16,128]{3,2,1,0:T(8,128)(2,1)S(1)}) custom-call(f32[64,32,128]{2,1,0:T(8,128)S(1)} %get-tuple-element.73.tri_back, f32[64,16,128]{2,1,0:T(8,128)S(1)} %get-tuple-element.81.refs_0_, f32[64,16,128]{2,1,0:T(8,128)S(1)} %get-tuple-element.82.refs_1_, ...), custom_call_target="tpu_custom_call" | custom-call | flops 1000 | bytes 1000 | tf_op jit(solution)/shard_map/right_back/pallas_call | solution.py:477
  47.2 1.5 %collective-permute-start.9 = (bf16[2,32,16,128]{3,2,1,0:T(8,128)(2,1)S(1)}, bf16[2,32,16,128]{3,2,1,0:T(8,128)(2,1)S(1)}, u32[]{:S(2)}, u32[]{:S(2)}) collective-permute-start(bf16[2,32,16,128]{3,2,1,0:T(8,128)(2,1)S(1)} %get-tuple-element.86.refs_9_), channel_id=1, source_target_pairs={{0,8},{8,0},{16,24},{24,16},{1,9},{9,1},{17,25},{25,17},{2,10},{10... | collective-permute-start | bytes 786440 | tf_op jit(solution)/shard_map/ppermute | solution.py:372
  48.7 1.3 %heads.1 = (bf16[64,32,128]{2,1,0:T(8,128)(2,1)}, bf16[64,32,128]{2,1,0:T(8,128)(2,1)S(1)}, f32[128,128]{1,0:T(8,128)S(1)}, f32[128,128]{1,0:T(8,128)S(1)}) custom-call(bf16[64,32,128]{2,1,0:T(8,128)(2,1)S(1)} %get-tuple-element.70.tri_in, bf16[128,128]{1,0:T(8,128)(2,1)S(1)} %copy-done.7, f32[64,32,128]{2,1,0:T(8,128)S(1)} %get-tuple-element.71.gate, ...), custom_call_target="tpu_custom_call" | custom-call | flops 1000 | bytes 1000 | tf_op jit(solution)/shard_map/heads/pallas_call | solution.py:477
  50.0 2.0 %weights.1 = (f32[2,32,768]{2,1,0:T(8,128)S(1)}, bf16[2,32,768]{2,1,0:T(8,128)(2,1)S(1)}) custom-call(bf16[4,32,16,128]{3,2,1,0:T(8,128)(2,1)S(1)} %get-tuple-element.91.right_in, bf16[128,256]{1,0:T(8,128)(2,1)S(1)} %copy-done.1, bf16[128,256]{1,0:T(8,128)(2,1)S(1)} %copy-done.4, f32[128,128]{1,0:T(8,128)S(1)} %get-tuple-element.92.gate_part, ...), custom_call_target="tpu_custom_call" | custom-call | flops 1000 | bytes 1000 | tf_op jit(solution)/shard_map/weights/pallas_call | solution.py:477
  52.0 0.7 collective-permute-start.11
  52.7 2.3 %grad_middle.1 = (bf16[64,32,128]{2,1,0:T(8,128)(2,1)}, f32[8,128]{1,0:T(8,128)S(1)}) custom-call(bf16[64,32,128]{2,1,0:T(8,128)(2,1)S(1)} %copy-done.2, bf16[64,32,128]{2,1,0:T(8,128)(2,1)S(1)} %get-tuple-element.90.pre_back, bf16[128,128]{1,0:T(8,128)(2,1)S(1)} %copy-done.8, bf16[2,32,768]{2,1,0:T(8,128)(2,1)S(1)} %get-tuple-element.98._), custom_call_target="tpu_custom_call" | custom-call | flops 1000 | bytes 1000 | tf_op jit(solution)/shard_map/grad_middle/pallas_call | solution.py:477
  55.0 1.7 %collective-permute-done.11.came = bf16[2,32,768]{2,1,0:T(8,128)(2,1)S(1)} collective-permute-done((bf16[2,32,768]{2,1,0:T(8,128)(2,1)S(1)}, bf16[2,32,768]{2,1,0:T(8,128)(2,1)S(1)}, u32[]{:S(2)}, u32[]{:S(2)}) %collective-permute-start.11) | collective-permute-done | bytes 98336 | tf_op jit(solution)/shard_map/ppermute | solution.py:372
  56.7 1.6 %collective-permute-start.12 = (bf16[1,32,768]{2,1,0:T(8,128)(2,1)S(1)}, bf16[1,32,768]{2,1,0:T(8,128)(2,1)S(1)}, u32[]{:S(2)}, u32[]{:S(2)}) collective-permute-start(bf16[1,32,768]{2,1,0:T(8,128)(2,1)S(1)} %get-tuple-element.103), channel_id=1, source_target_pairs={{0,16},{8,24},{16,0},{24,8},{1,17},{9,25},{17,1},{25,9},{2,18},{10... | collective-permute-start | bytes 147464 | tf_op jit(solution)/shard_map/ppermute | solution.py:372
  58.3 0.1 halve.2
  58.4 0.8 collective-permute-start.10
  59.2 2.2 %collective-permute-done.12.refs_1_ = bf16[1,32,768]{2,1,0:T(8,128)(2,1)S(1)} collective-permute-done((bf16[1,32,768]{2,1,0:T(8,128)(2,1)S(1)}, bf16[1,32,768]{2,1,0:T(8,128)(2,1)S(1)}, u32[]{:S(2)}, u32[]{:S(2)}) %collective-permute-start.12) | collective-permute-done | bytes 49184 | tf_op jit(solution)/shard_map/ppermute | solution.py:372
  61.4 0.8 %collective-permute-start.15 = (bf16[1,32,768]{2,1,0:T(8,128)(2,1)S(1)}, bf16[1,32,768]{2,1,0:T(8,128)(2,1)S(1)}, u32[]{:S(2)}, u32[]{:S(2)}) collective-permute-start(bf16[1,32,768]{2,1,0:T(8,128)(2,1)S(1)} %combine.2.refs_0_), channel_id=1, source_target_pairs={{0,6},{2,4},{4,2},{6,0},{1,7},{3,5},{5,3},{7,1},{8,14},{10,12},{12... | collective-permute-start | bytes 147464 | tf_op jit(solution)/shard_map/ppermute | solution.py:372
  62.2 2.7 %collective-permute-start.14 = (bf16[1,32,768]{2,1,0:T(8,128)(2,1)S(1)}, bf16[1,32,768]{2,1,0:T(8,128)(2,1)S(1)}, u32[]{:S(2)}, u32[]{:S(2)}) collective-permute-start(bf16[1,32,768]{2,1,0:T(8,128)(2,1)S(1)} %combine.2.refs_0_), channel_id=1, source_target_pairs={{0,4},{2,6},{4,0},{6,2},{1,5},{3,7},{5,1},{7,3},{8,12},{10,14},{12... | collective-permute-start | bytes 147464 | tf_op jit(solution)/shard_map/ppermute | solution.py:372
  64.9 1.0 %collective-permute-start.13 = (bf16[1,32,768]{2,1,0:T(8,128)(2,1)S(1)}, bf16[1,32,768]{2,1,0:T(8,128)(2,1)S(1)}, u32[]{:S(2)}, u32[]{:S(2)}) collective-permute-start(bf16[1,32,768]{2,1,0:T(8,128)(2,1)S(1)} %combine.2.refs_0_), channel_id=1, source_target_pairs={{0,2},{2,0},{4,6},{6,4},{1,3},{3,1},{5,7},{7,5},{8,10},{10,8},{12,... | collective-permute-start | bytes 147464 | tf_op jit(solution)/shard_map/ppermute | solution.py:372
  65.8 2.1 %left_side.1 = (bf16[64,16,128]{2,1,0:T(8,128)(2,1)}, f32[8,128]{1,0:T(8,128)S(1)}) custom-call(bf16[64,16,128]{2,1,0:T(8,128)(2,1)S(1)} %copy-done, bf16[128,256]{1,0:T(8,128)(2,1)S(1)} %copy-done.1, bf16[64,16,128]{2,1,0:T(8,128)(2,1)S(1)} %get-tuple-element.75._.refs_0_.refs_4_, bf16[64,16,128]{2,1,0:T(8,128)(2,1)S(1)} %collective-permute-done.6.refs_1_.refs_0_, ...), custom_call_target="tpu_custom_call" | custom-call | flops 1000 | bytes 1000 | tf_op jit(solution)/shard_map/left_side/pallas_call | solution.py:477
  68.0 0.6 collective-permute-done.14.refs_2_
  68.5 0.5 collective-permute-done.13.refs_1_
  69.1 2.0 %collective-permute-start.18 = (bf16[1,32,768]{2,1,0:T(8,128)(2,1)S(1)}, bf16[1,32,768]{2,1,0:T(8,128)(2,1)S(1)}, u32[]{:S(2)}, u32[]{:S(2)}) collective-permute-start(bf16[1,32,768]{2,1,0:T(8,128)(2,1)S(1)} %combine.3.refs_0_), channel_id=1, source_target_pairs={{0,24},{8,16},{16,8},{24,0},{1,25},{9,17},{17,9},{25,1},{2,26},{10... | collective-permute-start | bytes 147464 | tf_op jit(solution)/shard_map/ppermute | solution.py:372
  71.0 0.4 collective-permute-start.17
  71.4 1.2 %collective-permute-start.16 = (bf16[1,32,768]{2,1,0:T(8,128)(2,1)S(1)}, bf16[1,32,768]{2,1,0:T(8,128)(2,1)S(1)}, u32[]{:S(2)}, u32[]{:S(2)}) collective-permute-start(bf16[1,32,768]{2,1,0:T(8,128)(2,1)S(1)} %combine.3.refs_0_), channel_id=1, source_target_pairs={{0,8},{8,0},{16,24},{24,16},{1,9},{9,1},{17,25},{25,17},{2,10},{10... | collective-permute-start | bytes 147464 | tf_op jit(solution)/shard_map/ppermute | solution.py:372
  72.6 1.5 %right_side.1 = (bf16[32,16,128]{2,1,0:T(8,128)(2,1)}, f32[8,128]{1,0:T(8,128)S(1)}) custom-call(bf16[32,16,128]{2,1,0:T(8,128)(2,1)S(1)} %copy-done.6, bf16[128,256]{1,0:T(8,128)(2,1)S(1)} %copy-done.4, f32[32,16,128]{2,1,0:T(8,128)S(1)} %bitcast.5, bf16[32,16,128]{2,1,0:T(8,128)(2,1)S(1)} %bitcast.6), custom_call_target="tpu_custom_call" | custom-call | flops 1000 | bytes 1000 | tf_op jit(solution)/shard_map/right_side/pallas_call | solution.py:477
  74.1 0.0 collective-permute-done.18.refs_3_
  74.1 1.0 %collective-permute-done.17.refs_2_ = bf16[1,32,768]{2,1,0:T(8,128)(2,1)S(1)} collective-permute-done((bf16[1,32,768]{2,1,0:T(8,128)(2,1)S(1)}, bf16[1,32,768]{2,1,0:T(8,128)(2,1)S(1)}, u32[]{:S(2)}, u32[]{:S(2)}) %collective-permute-start.17) | collective-permute-done | bytes 49184 | tf_op jit(solution)/shard_map/ppermute | solution.py:372
  75.1 0.4 collective-permute-done.16.refs_1_
  75.5 0.8 %deltas.1 = (f32[128,256]{1,0:T(8,128)}, f32[128,256]{1,0:T(8,128)}, f32[128,128]{1,0:T(8,128)}, f32[128,128]{1,0:T(8,128)}) custom-call(bf16[1,32,768]{2,1,0:T(8,128)(2,1)S(1)} %combine.3.refs_0_, bf16[1,32,768]{2,1,0:T(8,128)(2,1)S(1)} %collective-permute-done.16.refs_1_, bf16[1,32,768]{2,1,0:T(8,128)(2,1)S(1)} %collective-permute-done.17.refs_2_, ...), custom_call_target="tpu_custom_call" | custom-call | flops 1000 | bytes 1000 | tf_op jit(solution)/shard_map/deltas/pallas_call | solution.py:477
  (32 shorter events, 0.2 us)
Async XLA Ops:
  0.6 16.3 %collective-permute-start = (bf16[64,16,128]{2,1,0:T(8,128)(2,1)}, bf16[64,16,128]{2,1,0:T(8,128)(2,1)S(1)}, u32[]{:S(2)}, u32[]{:S(2)}) collective-permute-start(bf16[64,16,128]{2,1,0:T(8,128)(2,1)} %raw.2), channel_id=1, source_target_pairs={{0,4},{2,6},{4,0},{6,2},{1,5},{3,7},{5,1},{7,3},{8,12},{10,14},{12... | collective-permute-start | bytes 786440 | tf_op jit(solution)/shard_map/ppermute | solution.py:372
  4.7 5.2 %collective-permute-start.1 = (bf16[1,32,16,128]{3,2,1,0:T(8,128)(2,1)}, bf16[1,32,16,128]{3,2,1,0:T(8,128)(2,1)S(1)}, u32[]{:S(2)}, u32[]{:S(2)}) collective-permute-start(bf16[1,32,16,128]{3,2,1,0:T(8,128)(2,1)} %bitcast.3), channel_id=1, source_target_pairs={{0,8},{8,0},{16,24},{24,16},{1,9},{9,1},{17,25},{25,17},{2,10},{10... | collective-permute-start | bytes 393224 | tf_op jit(solution)/shard_map/ppermute | solution.py:372
  6.2 16.5 %collective-permute-start.5 = (bf16[64,16,128]{2,1,0:T(8,128)(2,1)}, bf16[64,16,128]{2,1,0:T(8,128)(2,1)S(1)}, u32[]{:S(2)}, u32[]{:S(2)}) collective-permute-start(bf16[64,16,128]{2,1,0:T(8,128)(2,1)} %raw.2), channel_id=1, source_target_pairs={{0,2},{2,0},{4,6},{6,4},{1,3},{3,1},{5,7},{7,5},{8,10},{10,8},{12,... | collective-permute-start | bytes 786440 | tf_op jit(solution)/shard_map/ppermute | solution.py:372
  9.9 0.9 %copy-start.5 = (bf16[32,16,128]{2,1,0:T(8,128)(2,1)S(1)}, bf16[32,16,128]{2,1,0:T(8,128)(2,1)}, u32[]{:S(2)}) copy-start(bf16[32,16,128]{2,1,0:T(8,128)(2,1)} %raw.3) | copy-start | bytes 393220
  10.8 1.6 %copy-start.2 = (bf16[64,32,128]{2,1,0:T(8,128)(2,1)S(1)}, bf16[64,32,128]{2,1,0:T(8,128)(2,1)}, u32[]{:S(2)}) copy-start(bf16[64,32,128]{2,1,0:T(8,128)(2,1)} %middle.5) | copy-start | bytes 1572868
  10.9 1.6 %copy-start.3 = (bf16[64,32,128]{2,1,0:T(8,128)(2,1)S(1)}, bf16[64,32,128]{2,1,0:T(8,128)(2,1)}, u32[]{:S(2)}) copy-start(bf16[64,32,128]{2,1,0:T(8,128)(2,1)} %cotangent.3) | copy-start | bytes 1572868
  10.9 1.6 %copy-start.7 = (bf16[128,128]{1,0:T(8,128)(2,1)S(1)}, bf16[128,128]{1,0:T(8,128)(2,1)}, u32[]{:S(2)}) copy-start(bf16[128,128]{1,0:T(8,128)(2,1)} %out_w.1) | copy-start | bytes 98308
  10.9 1.6 %copy-start.8 = (bf16[128,128]{1,0:T(8,128)(2,1)S(1)}, bf16[128,128]{1,0:T(8,128)(2,1)}, u32[]{:S(2)}) copy-start(bf16[128,128]{1,0:T(8,128)(2,1)} %gate_weight.3) | copy-start | bytes 98308
  10.9 8.0 %collective-permute-start.4 = (bf16[2,32,16,128]{3,2,1,0:T(8,128)(2,1)S(1)}, bf16[2,32,16,128]{3,2,1,0:T(8,128)(2,1)S(1)}, u32[]{:S(2)}, u32[]{:S(2)}) collective-permute-start(bf16[2,32,16,128]{3,2,1,0:T(8,128)(2,1)S(1)} %stack.1.refs_2_.refs_0_), channel_id=1, source_target_pairs={{0,16},{8,24},{16,0},{24,8},{1,17},{9,25},{17,1},{25,9},{2,18},{10... | collective-permute-start | bytes 786440 | tf_op jit(solution)/shard_map/ppermute | solution.py:372
  12.5 4.5 %copy-start = (bf16[64,16,128]{2,1,0:T(8,128)(2,1)S(1)}, bf16[64,16,128]{2,1,0:T(8,128)(2,1)}, u32[]{:S(2)}) copy-start(bf16[64,16,128]{2,1,0:T(8,128)(2,1)} %raw.2) | copy-start | bytes 786436
  17.0 1.9 %copy-start.4 = (bf16[128,256]{1,0:T(8,128)(2,1)S(1)}, bf16[128,256]{1,0:T(8,128)(2,1)}, u32[]{:S(2)}) copy-start(bf16[128,256]{1,0:T(8,128)(2,1)} %right_w.1) | copy-start | bytes 196612
  17.0 9.7 %collective-permute-start.2 = (bf16[64,16,128]{2,1,0:T(8,128)(2,1)S(1)}, bf16[64,16,128]{2,1,0:T(8,128)(2,1)S(1)}, u32[]{:S(2)}, u32[]{:S(2)}) collective-permute-start(bf16[64,16,128]{2,1,0:T(8,128)(2,1)S(1)} %get-tuple-element.60), channel_id=1, source_target_pairs={{0,2},{2,0},{4,6},{6,4},{1,3},{3,1},{5,7},{7,5},{8,10},{10,8},{12,... | collective-permute-start | bytes 786440 | tf_op jit(solution)/shard_map/ppermute | solution.py:372
  17.8 2.9 %copy-start.1 = (bf16[128,256]{1,0:T(8,128)(2,1)S(1)}, bf16[128,256]{1,0:T(8,128)(2,1)}, u32[]{:S(2)}) copy-start(bf16[128,256]{1,0:T(8,128)(2,1)} %left_w.1) | copy-start | bytes 196612
  17.9 8.8 %collective-permute-start.3 = (bf16[64,16,128]{2,1,0:T(8,128)(2,1)S(1)}, bf16[64,16,128]{2,1,0:T(8,128)(2,1)S(1)}, u32[]{:S(2)}, u32[]{:S(2)}) collective-permute-start(bf16[64,16,128]{2,1,0:T(8,128)(2,1)S(1)} %get-tuple-element.61), channel_id=1, source_target_pairs={{0,0},{2,4},{4,2},{6,6},{1,1},{3,5},{5,3},{7,7},{8,8},{10,12},{12,... | collective-permute-start | bytes 786440 | tf_op jit(solution)/shard_map/ppermute | solution.py:410
  31.8 26.5 %collective-permute-start.7 = (bf16[64,16,128]{2,1,0:T(8,128)(2,1)S(1)}, bf16[64,16,128]{2,1,0:T(8,128)(2,1)S(1)}, u32[]{:S(2)}, u32[]{:S(2)}) collective-permute-start(bf16[64,16,128]{2,1,0:T(8,128)(2,1)S(1)} %get-tuple-element.78.refs_6_), channel_id=1, source_target_pairs={{0,4},{2,6},{4,0},{6,2},{1,5},{3,7},{5,1},{7,3},{8,12},{10,14},{12... | collective-permute-start | bytes 786440 | tf_op jit(solution)/shard_map/ppermute | solution.py:372
  36.5 21.9 %collective-permute-start.8 = (bf16[64,16,128]{2,1,0:T(8,128)(2,1)S(1)}, bf16[64,16,128]{2,1,0:T(8,128)(2,1)S(1)}, u32[]{:S(2)}, u32[]{:S(2)}) collective-permute-start(bf16[64,16,128]{2,1,0:T(8,128)(2,1)S(1)} %get-tuple-element.79.refs_7_), channel_id=1, source_target_pairs={{0,6},{2,4},{4,2},{6,0},{1,7},{3,5},{5,3},{7,1},{8,14},{10,12},{12... | collective-permute-start | bytes 786440 | tf_op jit(solution)/shard_map/ppermute | solution.py:372
  41.6 16.7 %collective-permute-start.6 = (bf16[64,16,128]{2,1,0:T(8,128)(2,1)S(1)}, bf16[64,16,128]{2,1,0:T(8,128)(2,1)S(1)}, u32[]{:S(2)}, u32[]{:S(2)}) collective-permute-start(bf16[64,16,128]{2,1,0:T(8,128)(2,1)S(1)} %get-tuple-element.77.refs_5_), channel_id=1, source_target_pairs={{0,2},{2,0},{4,6},{6,4},{1,3},{3,1},{5,7},{7,5},{8,10},{10,8},{12,... | collective-permute-start | bytes 786440 | tf_op jit(solution)/shard_map/ppermute | solution.py:372
  47.2 11.1 %collective-permute-start.9 = (bf16[2,32,16,128]{3,2,1,0:T(8,128)(2,1)S(1)}, bf16[2,32,16,128]{3,2,1,0:T(8,128)(2,1)S(1)}, u32[]{:S(2)}, u32[]{:S(2)}) collective-permute-start(bf16[2,32,16,128]{3,2,1,0:T(8,128)(2,1)S(1)} %get-tuple-element.86.refs_9_), channel_id=1, source_target_pairs={{0,8},{8,0},{16,24},{24,16},{1,9},{9,1},{17,25},{25,17},{2,10},{10... | collective-permute-start | bytes 786440 | tf_op jit(solution)/shard_map/ppermute | solution.py:372
  52.0 4.7 %collective-permute-start.11 = (bf16[2,32,768]{2,1,0:T(8,128)(2,1)S(1)}, bf16[2,32,768]{2,1,0:T(8,128)(2,1)S(1)}, u32[]{:S(2)}, u32[]{:S(2)}) collective-permute-start(bf16[2,32,768]{2,1,0:T(8,128)(2,1)S(1)} %get-tuple-element.98._), channel_id=1, source_target_pairs={{0,8},{8,0},{16,24},{24,16},{1,9},{9,1},{17,25},{25,17},{2,10},{10... | collective-permute-start | bytes 294920 | tf_op jit(solution)/shard_map/ppermute | solution.py:372
  56.7 4.6 %collective-permute-start.12 = (bf16[1,32,768]{2,1,0:T(8,128)(2,1)S(1)}, bf16[1,32,768]{2,1,0:T(8,128)(2,1)S(1)}, u32[]{:S(2)}, u32[]{:S(2)}) collective-permute-start(bf16[1,32,768]{2,1,0:T(8,128)(2,1)S(1)} %get-tuple-element.103), channel_id=1, source_target_pairs={{0,16},{8,24},{16,0},{24,8},{1,17},{9,25},{17,1},{25,9},{2,18},{10... | collective-permute-start | bytes 147464 | tf_op jit(solution)/shard_map/ppermute | solution.py:372
  58.4 14.2 %collective-permute-start.10 = (bf16[1,32,16,128]{3,2,1,0:T(8,128)(2,1)S(1)}, bf16[1,32,16,128]{3,2,1,0:T(8,128)(2,1)S(1)}, u32[]{:S(2)}, u32[]{:S(2)}) collective-permute-start(bf16[1,32,16,128]{3,2,1,0:T(8,128)(2,1)S(1)} %get-tuple-element.88.refs_0_), channel_id=1, source_target_pairs={{0,16},{8,24},{16,0},{24,8},{1,17},{9,25},{17,1},{25,9},{2,18},{10... | collective-permute-start | bytes 393224 | tf_op jit(solution)/shard_map/ppermute | solution.py:372
  61.4 6.6 %collective-permute-start.15 = (bf16[1,32,768]{2,1,0:T(8,128)(2,1)S(1)}, bf16[1,32,768]{2,1,0:T(8,128)(2,1)S(1)}, u32[]{:S(2)}, u32[]{:S(2)}) collective-permute-start(bf16[1,32,768]{2,1,0:T(8,128)(2,1)S(1)} %combine.2.refs_0_), channel_id=1, source_target_pairs={{0,6},{2,4},{4,2},{6,0},{1,7},{3,5},{5,3},{7,1},{8,14},{10,12},{12... | collective-permute-start | bytes 147464 | tf_op jit(solution)/shard_map/ppermute | solution.py:372
  62.2 6.4 %collective-permute-start.14 = (bf16[1,32,768]{2,1,0:T(8,128)(2,1)S(1)}, bf16[1,32,768]{2,1,0:T(8,128)(2,1)S(1)}, u32[]{:S(2)}, u32[]{:S(2)}) collective-permute-start(bf16[1,32,768]{2,1,0:T(8,128)(2,1)S(1)} %combine.2.refs_0_), channel_id=1, source_target_pairs={{0,4},{2,6},{4,0},{6,2},{1,5},{3,7},{5,1},{7,3},{8,12},{10,14},{12... | collective-permute-start | bytes 147464 | tf_op jit(solution)/shard_map/ppermute | solution.py:372
  64.9 4.2 %collective-permute-start.13 = (bf16[1,32,768]{2,1,0:T(8,128)(2,1)S(1)}, bf16[1,32,768]{2,1,0:T(8,128)(2,1)S(1)}, u32[]{:S(2)}, u32[]{:S(2)}) collective-permute-start(bf16[1,32,768]{2,1,0:T(8,128)(2,1)S(1)} %combine.2.refs_0_), channel_id=1, source_target_pairs={{0,2},{2,0},{4,6},{6,4},{1,3},{3,1},{5,7},{7,5},{8,10},{10,8},{12,... | collective-permute-start | bytes 147464 | tf_op jit(solution)/shard_map/ppermute | solution.py:372
  68.0 4.7 %copy-start.6 = (bf16[32,16,128]{2,1,0:T(8,128)(2,1)S(1)}, bf16[32,16,128]{2,1,0:T(8,128)(2,1)}, u32[]{:S(2)}) copy-start(bf16[32,16,128]{2,1,0:T(8,128)(2,1)} %raw.3) | copy-start | bytes 393220
  69.1 5.1 %collective-permute-start.18 = (bf16[1,32,768]{2,1,0:T(8,128)(2,1)S(1)}, bf16[1,32,768]{2,1,0:T(8,128)(2,1)S(1)}, u32[]{:S(2)}, u32[]{:S(2)}) collective-permute-start(bf16[1,32,768]{2,1,0:T(8,128)(2,1)S(1)} %combine.3.refs_0_), channel_id=1, source_target_pairs={{0,24},{8,16},{16,8},{24,0},{1,25},{9,17},{17,9},{25,1},{2,26},{10... | collective-permute-start | bytes 147464 | tf_op jit(solution)/shard_map/ppermute | solution.py:372
  71.0 4.1 %collective-permute-start.17 = (bf16[1,32,768]{2,1,0:T(8,128)(2,1)S(1)}, bf16[1,32,768]{2,1,0:T(8,128)(2,1)S(1)}, u32[]{:S(2)}, u32[]{:S(2)}) collective-permute-start(bf16[1,32,768]{2,1,0:T(8,128)(2,1)S(1)} %combine.3.refs_0_), channel_id=1, source_target_pairs={{0,16},{8,24},{16,0},{24,8},{1,17},{9,25},{17,1},{25,9},{2,18},{10... | collective-permute-start | bytes 147464 | tf_op jit(solution)/shard_map/ppermute | solution.py:372
  71.4 4.1 %collective-permute-start.16 = (bf16[1,32,768]{2,1,0:T(8,128)(2,1)S(1)}, bf16[1,32,768]{2,1,0:T(8,128)(2,1)S(1)}, u32[]{:S(2)}, u32[]{:S(2)}) collective-permute-start(bf16[1,32,768]{2,1,0:T(8,128)(2,1)S(1)} %combine.3.refs_0_), channel_id=1, source_target_pairs={{0,8},{8,0},{16,24},{24,16},{1,9},{9,1},{17,25},{25,17},{2,10},{10... | collective-permute-start | bytes 147464 | tf_op jit(solution)/shard_map/ppermute | solution.py:372

commit v13 on v12

--- a/solution.py
+++ b/solution.py
@@ -89,8 +89,7 @@
 
 
 def right_kernel(n_rows, n_blk, k_left, *refs):
-    raw = [stack.at[at] for stack in refs[:2] for at in range(stack.shape[0])]
-    weight, act_out, in_out, *flip_out = refs[2:]
+    raw, (weight, act_out, in_out, *flip_out) = refs[:n_rows], refs[n_rows:]
     n_j, k_right, width = raw[0].shape
     n_k = k_left * n_blk
     unit = math.gcd(k_left, k_right)
@@ -278,7 +277,7 @@
                     )
 
                 zeros = tuple(jnp.zeros((few, k_left, width), f32) for _ in blocks)
-                totals = lax.fori_loop(0, n_i, add, zeros, unroll=32)
+                totals = lax.fori_loop(0, n_i, add, zeros, unroll=True)
                 for s, total in zip(blocks, totals):
                     right_sum[pl.ds(at * 8 + half, few), s * k_left : (s + 1) * k_left, :] = total.astype(bf16)
             return 0
@@ -395,20 +394,21 @@
     return keep, came, send
 
 
-def forward_kernel(*refs):
-    for source, target in zip(refs[:2], refs[-2:]):
-        target[...] = source[...]
-
-
-def gather_left(block, n, after):
-    if n != 4:
-        return [(block,)] + [(exchange(block, "blk", n, s),) for s in range(1, n)]
-    across = exchange(block, "blk", n, 2)
-    beside = exchange(block, "blk", n, 1)
-    passed, own = call(forward_kernel, "forward", [shape(block.shape, block.dtype)] * 2, after=len(after))(across, block, *after)
-    outer = exchange(passed, "blk", n, 1)
-    inner = lax.ppermute(own, "blk", [(0, 0), (1, 2), (2, 1), (3, 3)])
-    return [(block,), (beside,), (across,), (outer, inner)]
+def forward_kernel(source, *refs):
+    refs[-1][...] = source[...]
+
+
+def forwarded(block, after):
+    (copy,) = call(forward_kernel, "forward", [shape(block.shape, block.dtype)], after=len(after))(block, *after)
+    return copy
+
+
+def outer_block(across, after):
+    return exchange(forwarded(across, after), "blk", 4, 1)
+
+
+def inner_block(block, after):
+    return lax.ppermute(forwarded(block, after), "blk", [(0, 0), (1, 2), (2, 1), (3, 3)])
 
 
 def order_kernel(*refs):
@@ -436,22 +436,6 @@
         after=len(after),
     )(*pieces, *after)
     return total
-
-
-def stack_kernel(own, came, both):
-    both[0 : own.shape[0]] = own[...]
-    both[own.shape[0] :] = came[...]
-
-
-def gather_doubling(part, axis, n):
-    came = exchange(part, axis, n, 1)
-    bit = 2
-    while bit < n:
-        both = shape((2 * part.shape[0],) + part.shape[1:], part.dtype)
-        (part,) = call(stack_kernel, "stack", [both])(part, came)
-        came = exchange(part, axis, n, bit)
-        bit *= 2
-    return part, came
 
 
 def deltas_kernel(n_rows, *refs):
@@ -503,7 +487,7 @@
     n_i, k_left, width = pair_left.shape
     n_j, k_right, _ = pair_right.shape
     n_k = k_left * n_blk
-    right_raw = gather_doubling(pair_right[None], "rows", n_rows)
+    right_raw = [pair_right] + [exchange(pair_right, "rows", n_rows, s) for s in range(1, n_rows)]
     middle_shape = (n_i, n_j, width)
     gate, middle_in, head_back, tri_up = call(
         middle_kernel,
@@ -517,7 +501,9 @@
         [shape((n_j * n_k, width), f32), shape((n_rows, n_j, k_right, width), bf16)]
         + [shape((k_left, n_j, width), f32)] * n_blk,
     )(*right_raw, right_weight)
-    left_raw = gather_left(pair_left, n_blk, (right_raw[0], middle_in))
+    left_raw = [[pair_left]] + [[exchange(pair_left, "blk", n_blk, s)] for s in range(1, 3 if n_blk == 4 else n_blk)]
+    if n_blk == 4:
+        left_raw.append([outer_block(left_raw[2][0], (right_in, middle_in))])
     left_act, left_in, total = [], [], []
     act_shape = shape(pair_left.shape, f32)
     in_shape = shape(pair_left.shape, bf16)
@@ -530,6 +516,8 @@
         left_act.append(act)
         left_in.append(inputs)
         total = [total]
+        if n_blk == 4 and s == 0:
+            left_raw[3].append(inner_block(pair_left, (act,)))
     act, inputs, tri_in, tri_back = call(
         functools.partial(triangle_kernel, len(left_raw[-1]), n_blk > 1),
         "triangle",

time: 76.4 us -> 75 us (0.982)
  local copies, waits for them, and re-layouts: 0.95 us -> 0.04 us
  starting transfers between devices: 30.7 us -> 29.8 us
    unnamed x18 -> x16, local copies, waits for them, and re-layouts: 0.95 us -> 0.04 us
    ppermute x18 -> x19, starting transfers between devices: 29.7 us -> 29 us  [exchange(): return lax.ppermute(x, axis, [(a, a ^ bit) for a in range(n)])]
    ppermute x18 -> x19, waiting for transfers between devices: 10.6 us -> 10.3 us  [exchange(): return lax.ppermute(x, axis, [(a, a ^ bit) for a in range(n)])]
  transfers between devices with their start and end apart: 19 -> 20, of which waited for: 8 -> 10; matrix products, arithmetic and copies ran while one was open for 0% -> 0% of each run, Pallas kernels for 36% -> 37%
where the time goes in v13:
time: 75 us; the launch traced here: 74.9 us
  Pallas kernels  33.8 us (45%)
  starting transfers between devices  29.8 us (40%)
  waiting for transfers between devices  10.3 us (14%)
  between operations  0.87 us (1%)
    pallas_call x24, Pallas kernels, run(): pl.pallas_call(kernel, in_specs=[pl.BlockSpec(memory_space=space) for spa...  33.8 us
    ppermute x19, starting transfers between devices, exchange(): return lax.ppermute(x, axis, [(a, a ^ bit) for a in range(n)])  29 us
    ppermute x19, waiting for transfers between devices, exchange(): return lax.ppermute(x, axis, [(a, a ^ bit) for a in range(n)])  10.3 us
  transfers between devices with their start and end apart: 20, of which 10 were waited for; matrix products, arithmetic and copies ran while one was open for 0% of the time, Pallas kernels for 37%

profile of v13, /device:TPU:0, one launch (start us, length us, event | category | flops | bytes accessed | tf_op | source)
XLA Modules:
  0.0 74.9 jit_solution(14176564710817819548)
XLA Ops:
  0.7 4.1 %collective-permute-start = (bf16[64,16,128]{2,1,0:T(8,128)(2,1)}, bf16[64,16,128]{2,1,0:T(8,128)(2,1)S(1)}, u32[]{:S(2)}, u32[]{:S(2)}) collective-permute-start(bf16[64,16,128]{2,1,0:T(8,128)(2,1)} %raw.2), channel_id=1, source_target_pairs={{0,4},{2,6},{4,0},{6,2},{1,5},{3,7},{5,1},{7,3},{8,12},{10,14},{12... | collective-permute-start | bytes 786440 | tf_op jit(solution)/shard_map/ppermute | solution.py:371
  4.8 2.4 %collective-permute-start.3 = (bf16[32,16,128]{2,1,0:T(8,128)(2,1)}, bf16[32,16,128]{2,1,0:T(8,128)(2,1)S(1)}, u32[]{:S(2)}, u32[]{:S(2)}) collective-permute-start(bf16[32,16,128]{2,1,0:T(8,128)(2,1)} %raw.3), channel_id=1, source_target_pairs={{0,24},{8,16},{16,8},{24,0},{1,25},{9,17},{17,9},{25,1},{2,26},{10... | collective-permute-start | bytes 393224 | tf_op jit(solution)/shard_map/ppermute | solution.py:371
  7.2 0.5 collective-permute-start.2
  7.7 0.5 collective-permute-start.1
  8.3 1.6 %collective-permute-start.6 = (bf16[64,16,128]{2,1,0:T(8,128)(2,1)}, bf16[64,16,128]{2,1,0:T(8,128)(2,1)S(1)}, u32[]{:S(2)}, u32[]{:S(2)}) collective-permute-start(bf16[64,16,128]{2,1,0:T(8,128)(2,1)} %raw.2), channel_id=1, source_target_pairs={{0,2},{2,0},{4,6},{6,4},{1,3},{3,1},{5,7},{7,5},{8,10},{10,8},{12,... | collective-permute-start | bytes 786440 | tf_op jit(solution)/shard_map/ppermute | solution.py:371
  9.9 0.0 copy-start.4
  9.9 2.3 %middle.3 = (f32[64,32,128]{2,1,0:T(8,128)S(1)}, bf16[64,32,128]{2,1,0:T(8,128)(2,1)S(1)}, bf16[64,32,128]{2,1,0:T(8,128)(2,1)S(1)}, f32[64,32,128]{2,1,0:T(8,128)S(1)}) custom-call(bf16[64,32,128]{2,1,0:T(8,128)(2,1)S(1)} %copy-done.2, bf16[64,32,128]{2,1,0:T(8,128)(2,1)S(1)} %copy-done.3, bf16[128,128]{1,0:T(8,128)(2,1)S(1)} %copy-done.7, ...), custom_call_target="tpu_custom_call" | custom-call | flops 1000 | bytes 1000 | tf_op jit(solution)/shard_map/middle/pallas_call | solution.py:461
  12.3 1.4 %collective-permute-done.2.refs_2_ = bf16[32,16,128]{2,1,0:T(8,128)(2,1)S(1)} collective-permute-done((bf16[32,16,128]{2,1,0:T(8,128)(2,1)}, bf16[32,16,128]{2,1,0:T(8,128)(2,1)S(1)}, u32[]{:S(2)}, u32[]{:S(2)}) %collective-permute-start.2) | collective-permute-done | bytes 131104 | tf_op jit(solution)/shard_map/ppermute | solution.py:371
  13.7 0.1 collective-permute-done.1.refs_1_
  13.7 1.9 %right.1 = (f32[2048,128]{1,0:T(8,128)S(1)}, bf16[4,32,16,128]{3,2,1,0:T(8,128)(2,1)S(1)}, f32[16,32,128]{2,1,0:T(8,128)S(1)}, f32[16,32,128]{2,1,0:T(8,128)S(1)...) custom-call(bf16[32,16,128]{2,1,0:T(8,128)(2,1)S(1)} %copy-done.5, ...), custom_call_target="tpu_custom_call" | custom-call | flops 1000 | bytes 1000 | tf_op jit(solution)/shard_map/right/pallas_call | solution.py:461
  15.7 1.9 %left.3 = (f32[64,16,128]{2,1,0:T(8,128)S(1)}, bf16[64,16,128]{2,1,0:T(8,128)(2,1)S(1)}, f32[64,32,128]{2,1,0:T(8,128)S(1)}) custom-call(bf16[64,16,128]{2,1,0:T(8,128)(2,1)S(1)} %copy-done, bf16[128,256]{1,0:T(8,128)(2,1)S(1)} %copy-done.1, f32[16,32,128]{2,1,0:T(8,128)S(1)} %get-tuple-element.59.refs_2_), custom_call_target="tpu_custom_call" | custom-call | flops 1000 | bytes 1000 | tf_op jit(solution)/shard_map/left/pallas_call | solution.py:461
  17.6 0.9 %collective-permute-start.5 = (bf16[64,16,128]{2,1,0:T(8,128)(2,1)S(1)}, bf16[64,16,128]{2,1,0:T(8,128)(2,1)S(1)}, u32[]{:S(2)}, u32[]{:S(2)}) collective-permute-start(bf16[64,16,128]{2,1,0:T(8,128)(2,1)S(1)} %forward.3), channel_id=1, source_target_pairs={{0,0},{2,4},{4,2},{6,6},{1,1},{3,5},{5,3},{7,7},{8,8},{10,12},{12,... | collective-permute-start | bytes 786440 | tf_op jit(solution)/shard_map/ppermute | solution.py:411
  18.5 2.9 %collective-permute-start.4 = (bf16[64,16,128]{2,1,0:T(8,128)(2,1)S(1)}, bf16[64,16,128]{2,1,0:T(8,128)(2,1)S(1)}, u32[]{:S(2)}, u32[]{:S(2)}) collective-permute-start(bf16[64,16,128]{2,1,0:T(8,128)(2,1)S(1)} %forward.2), channel_id=1, source_target_pairs={{0,2},{2,0},{4,6},{6,4},{1,3},{3,1},{5,7},{7,5},{8,10},{10,8},{12,... | collective-permute-start | bytes 786440 | tf_op jit(solution)/shard_map/ppermute | solution.py:371
  21.4 2.0 %left.4 = (f32[64,16,128]{2,1,0:T(8,128)S(1)}, bf16[64,16,128]{2,1,0:T(8,128)(2,1)S(1)}, f32[64,32,128]{2,1,0:T(8,128)S(1)}) custom-call(bf16[64,16,128]{2,1,0:T(8,128)(2,1)S(1)} %collective-permute-done.6.refs_0_, bf16[128,256]{1,0:T(8,128)(2,1)S(1)} %copy-done.1, f32[16,32,128]{2,1,0:T(8,128)S(1)} %get-tuple-element.64.refs_2_, ...), custom_call_target="tpu_custom_call" | custom-call | flops 1000 | bytes 1000 | tf_op jit(solution)/shard_map/left/pallas_call | solution.py:461
  23.4 2.0 %left.5 = (f32[64,16,128]{2,1,0:T(8,128)S(1)}, bf16[64,16,128]{2,1,0:T(8,128)(2,1)S(1)}, f32[64,32,128]{2,1,0:T(8,128)S(1)}) custom-call(bf16[64,16,128]{2,1,0:T(8,128)(2,1)S(1)} %collective-permute-done.source.refs_0_, bf16[128,256]{1,0:T(8,128)(2,1)S(1)} %copy-done.1, f32[16,32,128]{2,1,0:T(8,128)S(1)} %get-tuple-element.63.refs_2_, ...), custom_call_target="tpu_custom_call" | custom-call | flops 1000 | bytes 1000 | tf_op jit(solution)/shard_map/left/pallas_call | solution.py:461
  25.4 2.3 %collective-permute-done.4.refs_0_ = bf16[64,16,128]{2,1,0:T(8,128)(2,1)S(1)} collective-permute-done((bf16[64,16,128]{2,1,0:T(8,128)(2,1)S(1)}, bf16[64,16,128]{2,1,0:T(8,128)(2,1)S(1)}, u32[]{:S(2)}, u32[]{:S(2)}) %collective-permute-start.4) | collective-permute-done | bytes 262176 | tf_op jit(solution)/shard_map/ppermute | solution.py:371
  27.7 2.9 %triangle.1 = (f32[64,16,128]{2,1,0:T(8,128)S(1)}, bf16[64,16,128]{2,1,0:T(8,128)(2,1)S(1)}, bf16[64,32,128]{2,1,0:T(8,128)(2,1)S(1)}, f32[64,32,128]{2,1,0:T(8,128)S(1)}) custom-call(bf16[64,16,128]{2,1,0:T(8,128)(2,1)S(1)} %collective-permute-done.4.refs_0_, bf16[64,16,128]{2,1,0:T(8,128)(2,1)S(1)} %collective-permute-done.5.refs_1_, ...), custom_call_target="tpu_custom_call" | custom-call | flops 1000 | bytes 1000 | tf_op jit(solution)/shard_map/triangle/pallas_call | solution.py:461
  30.5 2.2 %left_back.3 = (bf16[64,16,128]{2,1,0:T(8,128)(2,1)S(1)}, bf16[64,16,128]{2,1,0:T(8,128)(2,1)S(1)}) custom-call(f32[64,32,128]{2,1,0:T(8,128)S(1)} %get-tuple-element.71.tri_back, f32[2048,128]{1,0:T(8,128)S(1)} %get-tuple-element.72.right_act), custom_call_target="tpu_custom_call" | custom-call | flops 1000 | bytes 1000 | tf_op jit(solution)/shard_map/left_back/pallas_call | solution.py:461
  32.8 3.0 %collective-permute-start.8 = (bf16[64,16,128]{2,1,0:T(8,128)(2,1)S(1)}, bf16[64,16,128]{2,1,0:T(8,128)(2,1)S(1)}, u32[]{:S(2)}, u32[]{:S(2)}) collective-permute-start(bf16[64,16,128]{2,1,0:T(8,128)(2,1)S(1)} %get-tuple-element.76.refs_6_), channel_id=1, source_target_pairs={{0,4},{2,6},{4,0},{6,2},{1,5},{3,7},{5,1},{7,3},{8,12},{10,14},{12... | collective-permute-start | bytes 786440 | tf_op jit(solution)/shard_map/ppermute | solution.py:371
  35.8 1.2 %collective-permute-start.9 = (bf16[64,16,128]{2,1,0:T(8,128)(2,1)S(1)}, bf16[64,16,128]{2,1,0:T(8,128)(2,1)S(1)}, u32[]{:S(2)}, u32[]{:S(2)}) collective-permute-start(bf16[64,16,128]{2,1,0:T(8,128)(2,1)S(1)} %get-tuple-element.77.refs_7_), channel_id=1, source_target_pairs={{0,6},{2,4},{4,2},{6,0},{1,7},{3,5},{5,3},{7,1},{8,14},{10,12},{12... | collective-permute-start | bytes 786440 | tf_op jit(solution)/shard_map/ppermute | solution.py:371
  37.0 2.2 %left_back.2 = (bf16[64,16,128]{2,1,0:T(8,128)(2,1)S(1)}, bf16[64,16,128]{2,1,0:T(8,128)(2,1)S(1)}) custom-call(f32[64,32,128]{2,1,0:T(8,128)S(1)} %get-tuple-element.71.tri_back, f32[2048,128]{1,0:T(8,128)S(1)} %get-tuple-element.72.right_act), custom_call_target="tpu_custom_call" | custom-call | flops 1000 | bytes 1000 | tf_op jit(solution)/shard_map/left_back/pallas_call | solution.py:461
  39.2 0.1 collective-permute-start.7
  39.3 6.2 %right_back.1 = (bf16[2,32,16,128]{3,2,1,0:T(8,128)(2,1)S(1)}, bf16[2,32,16,128]{3,2,1,0:T(8,128)(2,1)S(1)}) custom-call(f32[64,32,128]{2,1,0:T(8,128)S(1)} %get-tuple-element.71.tri_back, f32[64,16,128]{2,1,0:T(8,128)S(1)} %get-tuple-element.60.refs_0_, f32[64,16,128]{2,1,0:T(8,128)S(1)} %get-tuple-element.79.refs_1_, ...), custom_call_target="tpu_custom_call" | custom-call | flops 1000 | bytes 1000 | tf_op jit(solution)/shard_map/right_back/pallas_call | solution.py:461
  45.5 1.6 %collective-permute-start.10 = (bf16[2,32,16,128]{3,2,1,0:T(8,128)(2,1)S(1)}, bf16[2,32,16,128]{3,2,1,0:T(8,128)(2,1)S(1)}, u32[]{:S(2)}, u32[]{:S(2)}) collective-permute-start(bf16[2,32,16,128]{3,2,1,0:T(8,128)(2,1)S(1)} %get-tuple-element.83.refs_9_), channel_id=1, source_target_pairs={{0,8},{8,0},{16,24},{24,16},{1,9},{9,1},{17,25},{25,17},{2,10},{10... | collective-permute-start | bytes 786440 | tf_op jit(solution)/shard_map/ppermute | solution.py:371
  47.0 1.3 %heads.1 = (bf16[64,32,128]{2,1,0:T(8,128)(2,1)}, bf16[64,32,128]{2,1,0:T(8,128)(2,1)S(1)}, f32[128,128]{1,0:T(8,128)S(1)}, f32[128,128]{1,0:T(8,128)S(1)}) custom-call(bf16[64,32,128]{2,1,0:T(8,128)(2,1)S(1)} %get-tuple-element.68.tri_in, bf16[128,128]{1,0:T(8,128)(2,1)S(1)} %copy-done.6, f32[64,32,128]{2,1,0:T(8,128)S(1)} %get-tuple-element.69.gate, ...), custom_call_target="tpu_custom_call" | custom-call | flops 1000 | bytes 1000 | tf_op jit(solution)/shard_map/heads/pallas_call | solution.py:461
  48.4 2.0 %weights.1 = (f32[2,32,768]{2,1,0:T(8,128)S(1)}, bf16[2,32,768]{2,1,0:T(8,128)(2,1)S(1)}) custom-call(bf16[4,32,16,128]{3,2,1,0:T(8,128)(2,1)S(1)} %get-tuple-element.57.refs_0_.right_in, bf16[128,256]{1,0:T(8,128)(2,1)S(1)} %copy-done.1, bf16[128,256]{1,0:T(8,128)(2,1)S(1)} %copy-done.4, f32[128,128]{1,0:T(8,128)S(1)} %get-tuple-element.88.gate_part, ...), custom_call_target="tpu_custom_call" | custom-call | flops 1000 | bytes 1000 | tf_op jit(solution)/shard_map/weights/pallas_call | solution.py:461
  50.4 0.6 collective-permute-start.12
  51.0 2.3 %grad_middle.1 = (bf16[64,32,128]{2,1,0:T(8,128)(2,1)}, f32[8,128]{1,0:T(8,128)S(1)}) custom-call(bf16[64,32,128]{2,1,0:T(8,128)(2,1)S(1)} %copy-done.2, bf16[64,32,128]{2,1,0:T(8,128)(2,1)S(1)} %get-tuple-element.87.pre_back, bf16[128,128]{1,0:T(8,128)(2,1)S(1)} %copy-done.7, bf16[2,32,768]{2,1,0:T(8,128)(2,1)S(1)} %get-tuple-element.94._), custom_call_target="tpu_custom_call" | custom-call | flops 1000 | bytes 1000 | tf_op jit(solution)/shard_map/grad_middle/pallas_call | solution.py:461
  53.3 1.8 %collective-permute-done.12.came = bf16[2,32,768]{2,1,0:T(8,128)(2,1)S(1)} collective-permute-done((bf16[2,32,768]{2,1,0:T(8,128)(2,1)S(1)}, bf16[2,32,768]{2,1,0:T(8,128)(2,1)S(1)}, u32[]{:S(2)}, u32[]{:S(2)}) %collective-permute-start.12) | collective-permute-done | bytes 98336 | tf_op jit(solution)/shard_map/ppermute | solution.py:371
  55.1 0.8 %collective-permute-start.13 = (bf16[1,32,768]{2,1,0:T(8,128)(2,1)S(1)}, bf16[1,32,768]{2,1,0:T(8,128)(2,1)S(1)}, u32[]{:S(2)}, u32[]{:S(2)}) collective-permute-start(bf16[1,32,768]{2,1,0:T(8,128)(2,1)S(1)} %get-tuple-element.99), channel_id=1, source_target_pairs={{0,16},{8,24},{16,0},{24,8},{1,17},{9,25},{17,1},{25,9},{2,18},{10... | collective-permute-start | bytes 147464 | tf_op jit(solution)/shard_map/ppermute | solution.py:371
  55.9 0.1 collective-permute-done.7.refs_1_.refs_0_
  56.0 0.1 halve.2
  56.1 1.7 %collective-permute-start.11 = (bf16[1,32,16,128]{3,2,1,0:T(8,128)(2,1)S(1)}, bf16[1,32,16,128]{3,2,1,0:T(8,128)(2,1)S(1)}, u32[]{:S(2)}, u32[]{:S(2)}) collective-permute-start(bf16[1,32,16,128]{3,2,1,0:T(8,128)(2,1)S(1)} %get-tuple-element.85.refs_0_), channel_id=1, source_target_pairs={{0,16},{8,24},{16,0},{24,8},{1,17},{9,25},{17,1},{25,9},{2,18},{10... | collective-permute-start | bytes 393224 | tf_op jit(solution)/shard_map/ppermute | solution.py:371
  57.8 1.6 %collective-permute-done.13.refs_1_ = bf16[1,32,768]{2,1,0:T(8,128)(2,1)S(1)} collective-permute-done((bf16[1,32,768]{2,1,0:T(8,128)(2,1)S(1)}, bf16[1,32,768]{2,1,0:T(8,128)(2,1)S(1)}, u32[]{:S(2)}, u32[]{:S(2)}) %collective-permute-start.13) | collective-permute-done | bytes 49184 | tf_op jit(solution)/shard_map/ppermute | solution.py:371
  59.4 2.5 %collective-permute-start.16 = (bf16[1,32,768]{2,1,0:T(8,128)(2,1)S(1)}, bf16[1,32,768]{2,1,0:T(8,128)(2,1)S(1)}, u32[]{:S(2)}, u32[]{:S(2)}) collective-permute-start(bf16[1,32,768]{2,1,0:T(8,128)(2,1)S(1)} %combine.2.refs_0_), channel_id=1, source_target_pairs={{0,6},{2,4},{4,2},{6,0},{1,7},{3,5},{5,3},{7,1},{8,14},{10,12},{12... | collective-permute-start | bytes 147464 | tf_op jit(solution)/shard_map/ppermute | solution.py:371
  61.9 1.4 %collective-permute-start.15 = (bf16[1,32,768]{2,1,0:T(8,128)(2,1)S(1)}, bf16[1,32,768]{2,1,0:T(8,128)(2,1)S(1)}, u32[]{:S(2)}, u32[]{:S(2)}) collective-permute-start(bf16[1,32,768]{2,1,0:T(8,128)(2,1)S(1)} %combine.2.refs_0_), channel_id=1, source_target_pairs={{0,4},{2,6},{4,0},{6,2},{1,5},{3,7},{5,1},{7,3},{8,12},{10,14},{12... | collective-permute-start | bytes 147464 | tf_op jit(solution)/shard_map/ppermute | solution.py:371
  63.3 0.6 collective-permute-start.14
  63.9 2.1 %left_side.1 = (bf16[64,16,128]{2,1,0:T(8,128)(2,1)}, f32[8,128]{1,0:T(8,128)S(1)}) custom-call(bf16[64,16,128]{2,1,0:T(8,128)(2,1)S(1)} %copy-done, bf16[128,256]{1,0:T(8,128)(2,1)S(1)} %copy-done.1, bf16[64,16,128]{2,1,0:T(8,128)(2,1)S(1)} %get-tuple-element.73._.refs_0_.refs_4_, bf16[64,16,128]{2,1,0:T(8,128)(2,1)S(1)} %collective-permute-done.7.refs_1_.refs_0_, ...), custom_call_target="tpu_custom_call" | custom-call | flops 1000 | bytes 1000 | tf_op jit(solution)/shard_map/left_side/pallas_call | solution.py:461
  66.0 0.9 %collective-permute-done.15.refs_2_ = bf16[1,32,768]{2,1,0:T(8,128)(2,1)S(1)} collective-permute-done((bf16[1,32,768]{2,1,0:T(8,128)(2,1)S(1)}, bf16[1,32,768]{2,1,0:T(8,128)(2,1)S(1)}, u32[]{:S(2)}, u32[]{:S(2)}) %collective-permute-start.15) | collective-permute-done | bytes 49184 | tf_op jit(solution)/shard_map/ppermute | solution.py:371
  66.9 0.5 collective-permute-done.14.refs_1_
  67.5 1.6 %collective-permute-start.19 = (bf16[1,32,768]{2,1,0:T(8,128)(2,1)S(1)}, bf16[1,32,768]{2,1,0:T(8,128)(2,1)S(1)}, u32[]{:S(2)}, u32[]{:S(2)}) collective-permute-start(bf16[1,32,768]{2,1,0:T(8,128)(2,1)S(1)} %combine.3.refs_0_), channel_id=1, source_target_pairs={{0,24},{8,16},{16,8},{24,0},{1,25},{9,17},{17,9},{25,1},{2,26},{10... | collective-permute-start | bytes 147464 | tf_op jit(solution)/shard_map/ppermute | solution.py:371
  69.0 1.0 %collective-permute-start.18 = (bf16[1,32,768]{2,1,0:T(8,128)(2,1)S(1)}, bf16[1,32,768]{2,1,0:T(8,128)(2,1)S(1)}, u32[]{:S(2)}, u32[]{:S(2)}) collective-permute-start(bf16[1,32,768]{2,1,0:T(8,128)(2,1)S(1)} %combine.3.refs_0_), channel_id=1, source_target_pairs={{0,16},{8,24},{16,0},{24,8},{1,17},{9,25},{17,1},{25,9},{2,18},{10... | collective-permute-start | bytes 147464 | tf_op jit(solution)/shard_map/ppermute | solution.py:371
  70.0 1.0 %collective-permute-start.17 = (bf16[1,32,768]{2,1,0:T(8,128)(2,1)S(1)}, bf16[1,32,768]{2,1,0:T(8,128)(2,1)S(1)}, u32[]{:S(2)}, u32[]{:S(2)}) collective-permute-start(bf16[1,32,768]{2,1,0:T(8,128)(2,1)S(1)} %combine.3.refs_0_), channel_id=1, source_target_pairs={{0,8},{8,0},{16,24},{24,16},{1,9},{9,1},{17,25},{25,17},{2,10},{10... | collective-permute-start | bytes 147464 | tf_op jit(solution)/shard_map/ppermute | solution.py:371
  71.0 1.5 %right_side.1 = (bf16[32,16,128]{2,1,0:T(8,128)(2,1)}, f32[8,128]{1,0:T(8,128)S(1)}) custom-call(bf16[32,16,128]{2,1,0:T(8,128)(2,1)S(1)} %copy-done.5, bf16[128,256]{1,0:T(8,128)(2,1)S(1)} %copy-done.4, f32[32,16,128]{2,1,0:T(8,128)S(1)} %bitcast.2, bf16[32,16,128]{2,1,0:T(8,128)(2,1)S(1)} %bitcast.3), custom_call_target="tpu_custom_call" | custom-call | flops 1000 | bytes 1000 | tf_op jit(solution)/shard_map/right_side/pallas_call | solution.py:461
  72.5 0.0 collective-permute-done.19.refs_3_
  72.5 0.6 collective-permute-done.18.refs_2_
  73.1 1.0 %collective-permute-done.17.refs_1_ = bf16[1,32,768]{2,1,0:T(8,128)(2,1)S(1)} collective-permute-done((bf16[1,32,768]{2,1,0:T(8,128)(2,1)S(1)}, bf16[1,32,768]{2,1,0:T(8,128)(2,1)S(1)}, u32[]{:S(2)}, u32[]{:S(2)}) %collective-permute-start.17) | collective-permute-done | bytes 49184 | tf_op jit(solution)/shard_map/ppermute | solution.py:371
  74.1 0.8 %deltas.1 = (f32[128,256]{1,0:T(8,128)}, f32[128,256]{1,0:T(8,128)}, f32[128,128]{1,0:T(8,128)}, f32[128,128]{1,0:T(8,128)}) custom-call(bf16[1,32,768]{2,1,0:T(8,128)(2,1)S(1)} %combine.3.refs_0_, bf16[1,32,768]{2,1,0:T(8,128)(2,1)S(1)} %collective-permute-done.17.refs_1_, bf16[1,32,768]{2,1,0:T(8,128)(2,1)S(1)} %collective-permute-done.18.refs_2_, ...), custom_call_target="tpu_custom_call" | custom-call | flops 1000 | bytes 1000 | tf_op jit(solution)/shard_map/deltas/pallas_call | solution.py:461
  (32 shorter events, 0.2 us)
Async XLA Ops:
  0.6 9.2 %copy-start.6 = (bf16[128,128]{1,0:T(8,128)(2,1)S(1)}, bf16[128,128]{1,0:T(8,128)(2,1)}, u32[]{:S(2)}) copy-start(bf16[128,128]{1,0:T(8,128)(2,1)} %out_w.1) | copy-start | bytes 98308
  0.6 9.2 %copy-start.7 = (bf16[128,128]{1,0:T(8,128)(2,1)S(1)}, bf16[128,128]{1,0:T(8,128)(2,1)}, u32[]{:S(2)}) copy-start(bf16[128,128]{1,0:T(8,128)(2,1)} %gate_weight.3) | copy-start | bytes 98308
  0.7 9.2 %copy-start.3 = (bf16[64,32,128]{2,1,0:T(8,128)(2,1)S(1)}, bf16[64,32,128]{2,1,0:T(8,128)(2,1)}, u32[]{:S(2)}) copy-start(bf16[64,32,128]{2,1,0:T(8,128)(2,1)} %cotangent.3) | copy-start | bytes 1572868
  0.7 9.2 %copy-start.2 = (bf16[64,32,128]{2,1,0:T(8,128)(2,1)S(1)}, bf16[64,32,128]{2,1,0:T(8,128)(2,1)}, u32[]{:S(2)}) copy-start(bf16[64,32,128]{2,1,0:T(8,128)(2,1)} %middle.5) | copy-start | bytes 1572868
  0.7 17.8 %collective-permute-start = (bf16[64,16,128]{2,1,0:T(8,128)(2,1)}, bf16[64,16,128]{2,1,0:T(8,128)(2,1)S(1)}, u32[]{:S(2)}, u32[]{:S(2)}) collective-permute-start(bf16[64,16,128]{2,1,0:T(8,128)(2,1)} %raw.2), channel_id=1, source_target_pairs={{0,4},{2,6},{4,0},{6,2},{1,5},{3,7},{5,1},{7,3},{8,12},{10,14},{12... | collective-permute-start | bytes 786440 | tf_op jit(solution)/shard_map/ppermute | solution.py:371
  4.8 7.5 %collective-permute-start.3 = (bf16[32,16,128]{2,1,0:T(8,128)(2,1)}, bf16[32,16,128]{2,1,0:T(8,128)(2,1)S(1)}, u32[]{:S(2)}, u32[]{:S(2)}) collective-permute-start(bf16[32,16,128]{2,1,0:T(8,128)(2,1)} %raw.3), channel_id=1, source_target_pairs={{0,24},{8,16},{16,8},{24,0},{1,25},{9,17},{17,9},{25,1},{2,26},{10... | collective-permute-start | bytes 393224 | tf_op jit(solution)/shard_map/ppermute | solution.py:371
  7.2 6.4 %collective-permute-start.2 = (bf16[32,16,128]{2,1,0:T(8,128)(2,1)}, bf16[32,16,128]{2,1,0:T(8,128)(2,1)S(1)}, u32[]{:S(2)}, u32[]{:S(2)}) collective-permute-start(bf16[32,16,128]{2,1,0:T(8,128)(2,1)} %raw.3), channel_id=1, source_target_pairs={{0,16},{8,24},{16,0},{24,8},{1,17},{9,25},{17,1},{25,9},{2,18},{10... | collective-permute-start | bytes 393224 | tf_op jit(solution)/shard_map/ppermute | solution.py:371
  7.7 6.0 %collective-permute-start.1 = (bf16[32,16,128]{2,1,0:T(8,128)(2,1)}, bf16[32,16,128]{2,1,0:T(8,128)(2,1)S(1)}, u32[]{:S(2)}, u32[]{:S(2)}) collective-permute-start(bf16[32,16,128]{2,1,0:T(8,128)(2,1)} %raw.3), channel_id=1, source_target_pairs={{0,8},{8,0},{16,24},{24,16},{1,9},{9,1},{17,25},{25,17},{2,10},{10... | collective-permute-start | bytes 393224 | tf_op jit(solution)/shard_map/ppermute | solution.py:371
  8.3 13.2 %collective-permute-start.6 = (bf16[64,16,128]{2,1,0:T(8,128)(2,1)}, bf16[64,16,128]{2,1,0:T(8,128)(2,1)S(1)}, u32[]{:S(2)}, u32[]{:S(2)}) collective-permute-start(bf16[64,16,128]{2,1,0:T(8,128)(2,1)} %raw.2), channel_id=1, source_target_pairs={{0,2},{2,0},{4,6},{6,4},{1,3},{3,1},{5,7},{7,5},{8,10},{10,8},{12,... | collective-permute-start | bytes 786440 | tf_op jit(solution)/shard_map/ppermute | solution.py:371
  9.9 3.9 %copy-start.4 = (bf16[128,256]{1,0:T(8,128)(2,1)S(1)}, bf16[128,256]{1,0:T(8,128)(2,1)}, u32[]{:S(2)}) copy-start(bf16[128,256]{1,0:T(8,128)(2,1)} %right_w.1) | copy-start | bytes 196612
  9.9 3.8 %copy-start.5 = (bf16[32,16,128]{2,1,0:T(8,128)(2,1)S(1)}, bf16[32,16,128]{2,1,0:T(8,128)(2,1)}, u32[]{:S(2)}) copy-start(bf16[32,16,128]{2,1,0:T(8,128)(2,1)} %raw.3) | copy-start | bytes 393220
  12.2 3.4 %copy-start = (bf16[64,16,128]{2,1,0:T(8,128)(2,1)S(1)}, bf16[64,16,128]{2,1,0:T(8,128)(2,1)}, u32[]{:S(2)}) copy-start(bf16[64,16,128]{2,1,0:T(8,128)(2,1)} %raw.2) | copy-start | bytes 786436
  12.2 3.4 %copy-start.1 = (bf16[128,256]{1,0:T(8,128)(2,1)S(1)}, bf16[128,256]{1,0:T(8,128)(2,1)}, u32[]{:S(2)}) copy-start(bf16[128,256]{1,0:T(8,128)(2,1)} %left_w.1) | copy-start | bytes 196612
  17.6 7.7 %collective-permute-start.5 = (bf16[64,16,128]{2,1,0:T(8,128)(2,1)S(1)}, bf16[64,16,128]{2,1,0:T(8,128)(2,1)S(1)}, u32[]{:S(2)}, u32[]{:S(2)}) collective-permute-start(bf16[64,16,128]{2,1,0:T(8,128)(2,1)S(1)} %forward.3), channel_id=1, source_target_pairs={{0,0},{2,4},{4,2},{6,6},{1,1},{3,5},{5,3},{7,7},{8,8},{10,12},{12,... | collective-permute-start | bytes 786440 | tf_op jit(solution)/shard_map/ppermute | solution.py:411
  18.5 9.1 %collective-permute-start.4 = (bf16[64,16,128]{2,1,0:T(8,128)(2,1)S(1)}, bf16[64,16,128]{2,1,0:T(8,128)(2,1)S(1)}, u32[]{:S(2)}, u32[]{:S(2)}) collective-permute-start(bf16[64,16,128]{2,1,0:T(8,128)(2,1)S(1)} %forward.2), channel_id=1, source_target_pairs={{0,2},{2,0},{4,6},{6,4},{1,3},{3,1},{5,7},{7,5},{8,10},{10,8},{12,... | collective-permute-start | bytes 786440 | tf_op jit(solution)/shard_map/ppermute | solution.py:371
  32.8 23.1 %collective-permute-start.8 = (bf16[64,16,128]{2,1,0:T(8,128)(2,1)S(1)}, bf16[64,16,128]{2,1,0:T(8,128)(2,1)S(1)}, u32[]{:S(2)}, u32[]{:S(2)}) collective-permute-start(bf16[64,16,128]{2,1,0:T(8,128)(2,1)S(1)} %get-tuple-element.76.refs_6_), channel_id=1, source_target_pairs={{0,4},{2,6},{4,0},{6,2},{1,5},{3,7},{5,1},{7,3},{8,12},{10,14},{12... | collective-permute-start | bytes 786440 | tf_op jit(solution)/shard_map/ppermute | solution.py:371
  35.8 20.1 %collective-permute-start.9 = (bf16[64,16,128]{2,1,0:T(8,128)(2,1)S(1)}, bf16[64,16,128]{2,1,0:T(8,128)(2,1)S(1)}, u32[]{:S(2)}, u32[]{:S(2)}) collective-permute-start(bf16[64,16,128]{2,1,0:T(8,128)(2,1)S(1)} %get-tuple-element.77.refs_7_), channel_id=1, source_target_pairs={{0,6},{2,4},{4,2},{6,0},{1,7},{3,5},{5,3},{7,1},{8,14},{10,12},{12... | collective-permute-start | bytes 786440 | tf_op jit(solution)/shard_map/ppermute | solution.py:371
  39.2 16.8 %collective-permute-start.7 = (bf16[64,16,128]{2,1,0:T(8,128)(2,1)S(1)}, bf16[64,16,128]{2,1,0:T(8,128)(2,1)S(1)}, u32[]{:S(2)}, u32[]{:S(2)}) collective-permute-start(bf16[64,16,128]{2,1,0:T(8,128)(2,1)S(1)} %get-tuple-element.75.refs_5_), channel_id=1, source_target_pairs={{0,2},{2,0},{4,6},{6,4},{1,3},{3,1},{5,7},{7,5},{8,10},{10,8},{12,... | collective-permute-start | bytes 786440 | tf_op jit(solution)/shard_map/ppermute | solution.py:371
  45.5 10.6 %collective-permute-start.10 = (bf16[2,32,16,128]{3,2,1,0:T(8,128)(2,1)S(1)}, bf16[2,32,16,128]{3,2,1,0:T(8,128)(2,1)S(1)}, u32[]{:S(2)}, u32[]{:S(2)}) collective-permute-start(bf16[2,32,16,128]{3,2,1,0:T(8,128)(2,1)S(1)} %get-tuple-element.83.refs_9_), channel_id=1, source_target_pairs={{0,8},{8,0},{16,24},{24,16},{1,9},{9,1},{17,25},{25,17},{2,10},{10... | collective-permute-start | bytes 786440 | tf_op jit(solution)/shard_map/ppermute | solution.py:371
  50.4 4.7 %collective-permute-start.12 = (bf16[2,32,768]{2,1,0:T(8,128)(2,1)S(1)}, bf16[2,32,768]{2,1,0:T(8,128)(2,1)S(1)}, u32[]{:S(2)}, u32[]{:S(2)}) collective-permute-start(bf16[2,32,768]{2,1,0:T(8,128)(2,1)S(1)} %get-tuple-element.94._), channel_id=1, source_target_pairs={{0,8},{8,0},{16,24},{24,16},{1,9},{9,1},{17,25},{25,17},{2,10},{10... | collective-permute-start | bytes 294920 | tf_op jit(solution)/shard_map/ppermute | solution.py:371
  55.1 4.4 %collective-permute-start.13 = (bf16[1,32,768]{2,1,0:T(8,128)(2,1)S(1)}, bf16[1,32,768]{2,1,0:T(8,128)(2,1)S(1)}, u32[]{:S(2)}, u32[]{:S(2)}) collective-permute-start(bf16[1,32,768]{2,1,0:T(8,128)(2,1)S(1)} %get-tuple-element.99), channel_id=1, source_target_pairs={{0,16},{8,24},{16,0},{24,8},{1,17},{9,25},{17,1},{25,9},{2,18},{10... | collective-permute-start | bytes 147464 | tf_op jit(solution)/shard_map/ppermute | solution.py:371
  56.1 14.9 %collective-permute-start.11 = (bf16[1,32,16,128]{3,2,1,0:T(8,128)(2,1)S(1)}, bf16[1,32,16,128]{3,2,1,0:T(8,128)(2,1)S(1)}, u32[]{:S(2)}, u32[]{:S(2)}) collective-permute-start(bf16[1,32,16,128]{3,2,1,0:T(8,128)(2,1)S(1)} %get-tuple-element.85.refs_0_), channel_id=1, source_target_pairs={{0,16},{8,24},{16,0},{24,8},{1,17},{9,25},{17,1},{25,9},{2,18},{10... | collective-permute-start | bytes 393224 | tf_op jit(solution)/shard_map/ppermute | solution.py:371
  59.4 6.6 %collective-permute-start.16 = (bf16[1,32,768]{2,1,0:T(8,128)(2,1)S(1)}, bf16[1,32,768]{2,1,0:T(8,128)(2,1)S(1)}, u32[]{:S(2)}, u32[]{:S(2)}) collective-permute-start(bf16[1,32,768]{2,1,0:T(8,128)(2,1)S(1)} %combine.2.refs_0_), channel_id=1, source_target_pairs={{0,6},{2,4},{4,2},{6,0},{1,7},{3,5},{5,3},{7,1},{8,14},{10,12},{12... | collective-permute-start | bytes 147464 | tf_op jit(solution)/shard_map/ppermute | solution.py:371
  61.9 5.0 %collective-permute-start.15 = (bf16[1,32,768]{2,1,0:T(8,128)(2,1)S(1)}, bf16[1,32,768]{2,1,0:T(8,128)(2,1)S(1)}, u32[]{:S(2)}, u32[]{:S(2)}) collective-permute-start(bf16[1,32,768]{2,1,0:T(8,128)(2,1)S(1)} %combine.2.refs_0_), channel_id=1, source_target_pairs={{0,4},{2,6},{4,0},{6,2},{1,5},{3,7},{5,1},{7,3},{8,12},{10,14},{12... | collective-permute-start | bytes 147464 | tf_op jit(solution)/shard_map/ppermute | solution.py:371
  63.3 4.2 %collective-permute-start.14 = (bf16[1,32,768]{2,1,0:T(8,128)(2,1)S(1)}, bf16[1,32,768]{2,1,0:T(8,128)(2,1)S(1)}, u32[]{:S(2)}, u32[]{:S(2)}) collective-permute-start(bf16[1,32,768]{2,1,0:T(8,128)(2,1)S(1)} %combine.2.refs_0_), channel_id=1, source_target_pairs={{0,2},{2,0},{4,6},{6,4},{1,3},{3,1},{5,7},{7,5},{8,10},{10,8},{12,... | collective-permute-start | bytes 147464 | tf_op jit(solution)/shard_map/ppermute | solution.py:371
  67.5 5.1 %collective-permute-start.19 = (bf16[1,32,768]{2,1,0:T(8,128)(2,1)S(1)}, bf16[1,32,768]{2,1,0:T(8,128)(2,1)S(1)}, u32[]{:S(2)}, u32[]{:S(2)}) collective-permute-start(bf16[1,32,768]{2,1,0:T(8,128)(2,1)S(1)} %combine.3.refs_0_), channel_id=1, source_target_pairs={{0,24},{8,16},{16,8},{24,0},{1,25},{9,17},{17,9},{25,1},{2,26},{10... | collective-permute-start | bytes 147464 | tf_op jit(solution)/shard_map/ppermute | solution.py:371
  69.0 4.1 %collective-permute-start.18 = (bf16[1,32,768]{2,1,0:T(8,128)(2,1)S(1)}, bf16[1,32,768]{2,1,0:T(8,128)(2,1)S(1)}, u32[]{:S(2)}, u32[]{:S(2)}) collective-permute-start(bf16[1,32,768]{2,1,0:T(8,128)(2,1)S(1)} %combine.3.refs_0_), channel_id=1, source_target_pairs={{0,16},{8,24},{16,0},{24,8},{1,17},{9,25},{17,1},{25,9},{2,18},{10... | collective-permute-start | bytes 147464 | tf_op jit(solution)/shard_map/ppermute | solution.py:371
  70.0 4.1 %collective-permute-start.17 = (bf16[1,32,768]{2,1,0:T(8,128)(2,1)S(1)}, bf16[1,32,768]{2,1,0:T(8,128)(2,1)S(1)}, u32[]{:S(2)}, u32[]{:S(2)}) collective-permute-start(bf16[1,32,768]{2,1,0:T(8,128)(2,1)S(1)} %combine.3.refs_0_), channel_id=1, source_target_pairs={{0,8},{8,0},{16,24},{24,16},{1,9},{9,1},{17,25},{25,17},{2,10},{10... | collective-permute-start | bytes 147464 | tf_op jit(solution)/shard_map/ppermute | solution.py:371

commit v14 on v13

--- a/solution.py
+++ b/solution.py
@@ -89,7 +89,7 @@
 
 
 def right_kernel(n_rows, n_blk, k_left, *refs):
-    raw, (weight, act_out, in_out, *flip_out) = refs[:n_rows], refs[n_rows:]
+    raw, (weight, _, _, act_out, in_out, *flip_out) = refs[:n_rows], refs[n_rows:]
     n_j, k_right, width = raw[0].shape
     n_k = k_left * n_blk
     unit = math.gcd(k_left, k_right)
@@ -157,35 +157,44 @@
     return total
 
 
-def left_kernel(n_raw, first, *refs):
-    raw, (weight, flip, *refs) = refs[:n_raw], refs[n_raw:]
-    total_in, (act_out, in_out, total_out) = refs[: 0 if first else 1], refs[0 if first else 1 :]
+def own_kernel(raw, weight, act_out, in_out):
+    project_left([raw], weight, act_out, in_out)
+
+
+def own_sum_kernel(act, flip, total):
+    step = 8
+
+    def body(at, _):
+        rows = pl.ds(at * step, step)
+        total[rows] = add_vertices(rows, act, flip)
+        return 0
+
+    lax.fori_loop(0, total.shape[0] // step, body, 0, unroll=2)
+
+
+def left_kernel(raw, weight, flip, total_in, act_out, in_out, total_out):
     n_i, n_j, width = total_out.shape
     step = 8
-    project_left(raw, weight, act_out, in_out)
+    project_left([raw], weight, act_out, in_out)
 
     def body(at, _):
         rows = pl.ds(at * step, step)
-        total = add_vertices(rows, act_out, flip)
-        total_out[rows] = total if first else total_in[0][rows] + total
+        total_out[rows] = total_in[rows] + add_vertices(rows, act_out, flip)
         return 0
 
     lax.fori_loop(0, n_i // step, body, 0, unroll=2)
 
 
-def triangle_kernel(n_raw, has_total, *refs):
+def triangle_kernel(n_raw, *refs):
     raw, (left_w, flip, tri_up, *refs) = refs[:n_raw], refs[n_raw:]
-    total_in, refs = refs[: 1 if has_total else 0], refs[1 if has_total else 0 :]
-    act_out, in_out, tri_in, tri_back = refs
+    total_in, act_out, in_out, tri_in, tri_back = refs
     n_i, n_j, width = tri_in.shape
     step = 8
     project_left(raw, left_w, act_out, in_out)
 
     def triangle_rows(at, _):
         rows = pl.ds(at * step, step)
-        total = add_vertices(rows, act_out, flip)
-        if has_total:
-            total = total + total_in[0][rows]
+        total = total_in[rows] + add_vertices(rows, act_out, flip)
         flat = step * n_j
         total = total.reshape(flat, width)
         normed, inverse = normalize(total, row_mean(split(total), width))
@@ -265,24 +274,21 @@
     k_step = vertex_step(n_k, k_left)
     for k0 in range(0, n_k, k_step):
         blocks = range(k0 // k_left, (k0 + k_step) // k_left)
-
-        def rows_sum(at, _, k0=k0, blocks=blocks):
-            eight = pl.ds(pl.multiple_of(at * 8, 8), 8)
-            for half in range(0, 8, few):
-
-                def add(i, totals):
-                    some = tri_back[i, eight, :][half : half + few][:, None]
-                    return tuple(
-                        total + some * left_act[s][i][None] for s, total in zip(blocks, totals)
-                    )
-
-                zeros = tuple(jnp.zeros((few, k_left, width), f32) for _ in blocks)
-                totals = lax.fori_loop(0, n_i, add, zeros, unroll=True)
-                for s, total in zip(blocks, totals):
-                    right_sum[pl.ds(at * 8 + half, few), s * k_left : (s + 1) * k_left, :] = total.astype(bf16)
-            return 0
-
-        lax.fori_loop(0, n_j // 8, rows_sum, 0)
+        for first in range(0, n_j, few):
+
+            def add(i, totals, first=first, blocks=blocks):
+                acts = [left_act[s][i] for s in blocks]
+                added = []
+                for at in range(few):
+                    row = tri_back[i, first + at : first + at + 1, :]
+                    added += [total + row * act for total, act in zip(totals[at * len(acts) :], acts)]
+                return tuple(added)
+
+            zeros = (jnp.zeros((k_left, width), f32),) * (few * len(blocks))
+            totals = lax.fori_loop(0, n_i, add, zeros, unroll=16)
+            for at in range(few):
+                for s, total in zip(blocks, totals[at * len(blocks) :]):
+                    right_sum[first + at, s * k_left : (s + 1) * k_left, :] = total.astype(bf16)
     for s in range(n_rows):
         for part in range(k_right // unit):
             out = send if s % 2 else keep
@@ -495,31 +501,33 @@
         [shape(middle_shape, f32), shape(middle_shape, bf16), shape(middle_shape, bf16), shape(middle_shape, f32)],
         after=1,
     )(pair_middle, cotangent, gate_weight, output_weight, behind(cost=10**9))
+    act_shape = shape(pair_left.shape, f32)
+    in_shape = shape(pair_left.shape, bf16)
+    own_act, own_in = call(own_kernel, "own", [act_shape, in_shape], after=0)(pair_left, left_weight)
     right_act, right_in, *right_flip = call(
         functools.partial(right_kernel, n_rows, n_blk, k_left),
         "right",
         [shape((n_j * n_k, width), f32), shape((n_rows, n_j, k_right, width), bf16)]
         + [shape((k_left, n_j, width), f32)] * n_blk,
-    )(*right_raw, right_weight)
+        after=2,
+    )(*right_raw, right_weight, own_act, middle_in)
     left_raw = [[pair_left]] + [[exchange(pair_left, "blk", n_blk, s)] for s in range(1, 3 if n_blk == 4 else n_blk)]
     if n_blk == 4:
         left_raw.append([outer_block(left_raw[2][0], (right_in, middle_in))])
-    left_act, left_in, total = [], [], []
-    act_shape = shape(pair_left.shape, f32)
-    in_shape = shape(pair_left.shape, bf16)
-    for s in range(n_blk - 1):
-        act, inputs, total = call(
-            functools.partial(left_kernel, len(left_raw[s]), s == 0),
+    total = call(own_sum_kernel, "own_sum", [shape(middle_shape, f32)])(own_act, right_flip[0])
+    if n_blk == 4:
+        left_raw[3].append(inner_block(pair_left, tuple(total)))
+    left_act, left_in = [own_act], [own_in]
+    for s in range(1, n_blk - 1):
+        act, inputs, *total = call(
+            left_kernel,
             "left",
             [act_shape, in_shape, shape(middle_shape, f32)],
         )(*left_raw[s], left_weight, right_flip[s], *total)
         left_act.append(act)
         left_in.append(inputs)
-        total = [total]
-        if n_blk == 4 and s == 0:
-            left_raw[3].append(inner_block(pair_left, (act,)))
     act, inputs, tri_in, tri_back = call(
-        functools.partial(triangle_kernel, len(left_raw[-1]), n_blk > 1),
+        functools.partial(triangle_kernel, len(left_raw[-1])),
         "triangle",
         [act_shape, in_shape, shape(middle_shape, bf16), shape(middle_shape, f32)],
     )(*left_raw[-1], left_weight, right_flip[-1], tri_up, *total)

time: 75 us -> 72.6 us (0.968)
  waiting for transfers between devices: 10.3 us -> 7.09 us
  local copies, waits for them, and re-layouts: 0.04 us -> 3.01 us
  Pallas kernels: 33.8 us -> 32.6 us
  starting transfers between devices: 29.8 us -> 28.8 us
    ppermute x19, waiting for transfers between devices: 10.3 us -> 7.09 us  [exchange(): return lax.ppermute(x, axis, [(a, a ^ bit) for a in range(n)])]
    unnamed x16 -> x20, local copies, waits for them, and re-layouts: 0.04 us -> 3.01 us
    pallas_call x24 -> x25, Pallas kernels: 33.8 us -> 32.6 us  [run(): pl.pallas_call(kernel, in_specs=[pl.BlockSpec(memory_space=space) for spa...]
    ppermute x19, starting transfers between devices: 29 us -> 27.9 us  [exchange(): return lax.ppermute(x, axis, [(a, a ^ bit) for a in range(n)])]
  transfers between devices with their start and end apart: 20 -> 20, of which waited for: 10 -> 7; matrix products, arithmetic and copies ran while one was open for 0% -> 0% of each run, Pallas kernels for 37% -> 37%
where the time goes in v14:
time: 72.6 us; the launch traced here: 72.4 us
  Pallas kernels  32.6 us (45%)
  starting transfers between devices  28.8 us (40%)
  waiting for transfers between devices  7.09 us (10%)
  local copies, waits for them, and re-layouts  3.01 us (4%)
  between operations  0.9 us (1%)
    pallas_call x25, Pallas kernels, run(): pl.pallas_call(kernel, in_specs=[pl.BlockSpec(memory_space=space) for spa...  32.6 us
    ppermute x19, starting transfers between devices, exchange(): return lax.ppermute(x, axis, [(a, a ^ bit) for a in range(n)])  27.9 us
    ppermute x19, waiting for transfers between devices, exchange(): return lax.ppermute(x, axis, [(a, a ^ bit) for a in range(n)])  7.09 us
    unnamed x20, local copies, waits for them, and re-layouts  3.01 us
  transfers between devices with their start and end apart: 20, of which 7 were waited for; matrix products, arithmetic and copies ran while one was open for 0% of the time, Pallas kernels for 37%

profile of v14, /device:TPU:0, one launch (start us, length us, event | category | flops | bytes accessed | tf_op | source)
XLA Modules:
  0.0 72.4 jit_solution(18189889288788981052)
XLA Ops:
  0.6 4.1 %collective-permute-start = (bf16[64,16,128]{2,1,0:T(8,128)(2,1)}, bf16[64,16,128]{2,1,0:T(8,128)(2,1)S(1)}, u32[]{:S(2)}, u32[]{:S(2)}) collective-permute-start(bf16[64,16,128]{2,1,0:T(8,128)(2,1)} %raw.4), channel_id=1, source_target_pairs={{0,4},{2,6},{4,0},{6,2},{1,5},{3,7},{5,1},{7,3},{8,12},{10,14},{12... | collective-permute-start | bytes 786440 | tf_op jit(solution)/shard_map/ppermute | solution.py:377
  4.7 2.4 %collective-permute-start.3 = (bf16[32,16,128]{2,1,0:T(8,128)(2,1)}, bf16[32,16,128]{2,1,0:T(8,128)(2,1)S(1)}, u32[]{:S(2)}, u32[]{:S(2)}) collective-permute-start(bf16[32,16,128]{2,1,0:T(8,128)(2,1)} %raw.5), channel_id=1, source_target_pairs={{0,24},{8,16},{16,8},{24,0},{1,25},{9,17},{17,9},{25,1},{2,26},{10... | collective-permute-start | bytes 393224 | tf_op jit(solution)/shard_map/ppermute | solution.py:377
  7.2 0.5 collective-permute-start.2
  7.7 0.5 collective-permute-start.1
  8.2 1.6 %collective-permute-start.6 = (bf16[64,16,128]{2,1,0:T(8,128)(2,1)}, bf16[64,16,128]{2,1,0:T(8,128)(2,1)S(1)}, u32[]{:S(2)}, u32[]{:S(2)}) collective-permute-start(bf16[64,16,128]{2,1,0:T(8,128)(2,1)} %raw.4), channel_id=1, source_target_pairs={{0,2},{2,0},{4,6},{6,4},{1,3},{3,1},{5,7},{7,5},{8,10},{10,8},{12,... | collective-permute-start | bytes 786440 | tf_op jit(solution)/shard_map/ppermute | solution.py:377
  9.8 1.0 %copy-done = bf16[64,16,128]{2,1,0:T(8,128)(2,1)S(1)} copy-done((bf16[64,16,128]{2,1,0:T(8,128)(2,1)S(1)}, bf16[64,16,128]{2,1,0:T(8,128)(2,1)}, u32[]{:S(2)}) %copy-start) | copy-done | bytes 262168
  10.8 0.8 %copy-done.2 = bf16[128,256]{1,0:T(8,128)(2,1)S(1)} copy-done((bf16[128,256]{1,0:T(8,128)(2,1)S(1)}, bf16[128,256]{1,0:T(8,128)(2,1)}, u32[]{:S(2)}) %copy-start.2) | copy-done | bytes 65560
  11.6 0.8 %own.1 = (f32[64,16,128]{2,1,0:T(8,128)S(1)}, bf16[64,16,128]{2,1,0:T(8,128)(2,1)S(1)}) custom-call(bf16[64,16,128]{2,1,0:T(8,128)(2,1)S(1)} %copy-done, bf16[128,256]{1,0:T(8,128)(2,1)S(1)} %copy-done.2), custom_call_target="tpu_custom_call" | custom-call | flops 1000 | bytes 1000 | tf_op jit(solution)/shard_map/own/pallas_call | solution.py:467
  12.5 1.0 %copy-done.4 = bf16[64,32,128]{2,1,0:T(8,128)(2,1)S(1)} copy-done((bf16[64,32,128]{2,1,0:T(8,128)(2,1)S(1)}, bf16[64,32,128]{2,1,0:T(8,128)(2,1)}, u32[]{:S(2)}) %copy-start.4) | copy-done | bytes 524312
  13.5 0.2 copy-done.5
  13.6 2.3 %middle.3 = (f32[64,32,128]{2,1,0:T(8,128)S(1)}, bf16[64,32,128]{2,1,0:T(8,128)(2,1)S(1)}, bf16[64,32,128]{2,1,0:T(8,128)(2,1)S(1)}, f32[64,32,128]{2,1,0:T(8,128)S(1)}) custom-call(bf16[64,32,128]{2,1,0:T(8,128)(2,1)S(1)} %copy-done.4, bf16[64,32,128]{2,1,0:T(8,128)(2,1)S(1)} %copy-done.5, bf16[128,128]{1,0:T(8,128)(2,1)S(1)} %copy-done.9, ...), custom_call_target="tpu_custom_call" | custom-call | flops 1000 | bytes 1000 | tf_op jit(solution)/shard_map/middle/pallas_call | solution.py:467
  16.0 1.9 %right.1 = (f32[2048,128]{1,0:T(8,128)S(1)}, bf16[4,32,16,128]{3,2,1,0:T(8,128)(2,1)S(1)}, f32[16,32,128]{2,1,0:T(8,128)S(1)}, f32[16,32,128]{2,1,0:T(8,128)S(1)...) custom-call(bf16[32,16,128]{2,1,0:T(8,128)(2,1)S(1)} %copy-done.7, ...), custom_call_target="tpu_custom_call" | custom-call | flops 1000 | bytes 1000 | tf_op jit(solution)/shard_map/right/pallas_call | solution.py:467
  18.0 1.1 %own_sum.1.refs_0_.total_in = f32[64,32,128]{2,1,0:T(8,128)S(1)} custom-call(f32[64,16,128]{2,1,0:T(8,128)S(1)} %get-tuple-element.56.refs_5_.act.refs_0_, f32[16,32,128]{2,1,0:T(8,128)S(1)} %get-tuple-element.59.flip), custom_call_target="tpu_custom_call" | custom-call | flops 1000 | bytes 1000 | tf_op jit(solution)/shard_map/own_sum/pallas_call | solution.py:467
  19.2 0.9 %collective-permute-start.5 = (bf16[64,16,128]{2,1,0:T(8,128)(2,1)S(1)}, bf16[64,16,128]{2,1,0:T(8,128)(2,1)S(1)}, u32[]{:S(2)}, u32[]{:S(2)}) collective-permute-start(bf16[64,16,128]{2,1,0:T(8,128)(2,1)S(1)} %forward.3), channel_id=1, source_target_pairs={{0,0},{2,4},{4,2},{6,6},{1,1},{3,5},{5,3},{7,7},{8,8},{10,12},{12,... | collective-permute-start | bytes 786440 | tf_op jit(solution)/shard_map/ppermute | solution.py:417
  20.1 2.2 %collective-permute-start.4 = (bf16[64,16,128]{2,1,0:T(8,128)(2,1)S(1)}, bf16[64,16,128]{2,1,0:T(8,128)(2,1)S(1)}, u32[]{:S(2)}, u32[]{:S(2)}) collective-permute-start(bf16[64,16,128]{2,1,0:T(8,128)(2,1)S(1)} %forward.2), channel_id=1, source_target_pairs={{0,2},{2,0},{4,6},{6,4},{1,3},{3,1},{5,7},{7,5},{8,10},{10,8},{12,... | collective-permute-start | bytes 786440 | tf_op jit(solution)/shard_map/ppermute | solution.py:377
  22.3 2.0 %left.2 = (f32[64,16,128]{2,1,0:T(8,128)S(1)}, bf16[64,16,128]{2,1,0:T(8,128)(2,1)S(1)}, f32[64,32,128]{2,1,0:T(8,128)S(1)}) custom-call(bf16[64,16,128]{2,1,0:T(8,128)(2,1)S(1)} %collective-permute-done.6.raw, bf16[128,256]{1,0:T(8,128)(2,1)S(1)} %copy-done.3, f32[16,32,128]{2,1,0:T(8,128)S(1)} %get-tuple-element.63.flip, ...), custom_call_target="tpu_custom_call" | custom-call | flops 1000 | bytes 1000 | tf_op jit(solution)/shard_map/left/pallas_call | solution.py:467
  24.2 2.0 %left.3 = (f32[64,16,128]{2,1,0:T(8,128)S(1)}, bf16[64,16,128]{2,1,0:T(8,128)(2,1)S(1)}, f32[64,32,128]{2,1,0:T(8,128)S(1)}) custom-call(bf16[64,16,128]{2,1,0:T(8,128)(2,1)S(1)} %collective-permute-done.source.raw, bf16[128,256]{1,0:T(8,128)(2,1)S(1)} %copy-done.3, f32[16,32,128]{2,1,0:T(8,128)S(1)} %get-tuple-element.62.flip, ...), custom_call_target="tpu_custom_call" | custom-call | flops 1000 | bytes 1000 | tf_op jit(solution)/shard_map/left/pallas_call | solution.py:467
  26.2 0.7 collective-permute-done.4.refs_0_
  26.9 2.9 %triangle.1 = (f32[64,16,128]{2,1,0:T(8,128)S(1)}, bf16[64,16,128]{2,1,0:T(8,128)(2,1)S(1)}, bf16[64,32,128]{2,1,0:T(8,128)(2,1)S(1)}, f32[64,32,128]{2,1,0:T(8,128)S(1)}) custom-call(bf16[64,16,128]{2,1,0:T(8,128)(2,1)S(1)} %collective-permute-done.4.refs_0_, bf16[64,16,128]{2,1,0:T(8,128)(2,1)S(1)} %collective-permute-done.5.refs_1_, ...), custom_call_target="tpu_custom_call" | custom-call | flops 1000 | bytes 1000 | tf_op jit(solution)/shard_map/triangle/pallas_call | solution.py:467
  29.8 2.2 %left_back.3 = (bf16[64,16,128]{2,1,0:T(8,128)(2,1)S(1)}, bf16[64,16,128]{2,1,0:T(8,128)(2,1)S(1)}) custom-call(f32[64,32,128]{2,1,0:T(8,128)S(1)} %get-tuple-element.69.tri_back, f32[2048,128]{1,0:T(8,128)S(1)} %get-tuple-element.70.right_act), custom_call_target="tpu_custom_call" | custom-call | flops 1000 | bytes 1000 | tf_op jit(solution)/shard_map/left_back/pallas_call | solution.py:467
  32.0 2.9 %collective-permute-start.8 = (bf16[64,16,128]{2,1,0:T(8,128)(2,1)S(1)}, bf16[64,16,128]{2,1,0:T(8,128)(2,1)S(1)}, u32[]{:S(2)}, u32[]{:S(2)}) collective-permute-start(bf16[64,16,128]{2,1,0:T(8,128)(2,1)S(1)} %get-tuple-element.74.refs_6_), channel_id=1, source_target_pairs={{0,4},{2,6},{4,0},{6,2},{1,5},{3,7},{5,1},{7,3},{8,12},{10,14},{12... | collective-permute-start | bytes 786440 | tf_op jit(solution)/shard_map/ppermute | solution.py:377
  35.0 1.2 %collective-permute-start.9 = (bf16[64,16,128]{2,1,0:T(8,128)(2,1)S(1)}, bf16[64,16,128]{2,1,0:T(8,128)(2,1)S(1)}, u32[]{:S(2)}, u32[]{:S(2)}) collective-permute-start(bf16[64,16,128]{2,1,0:T(8,128)(2,1)S(1)} %get-tuple-element.75.refs_7_), channel_id=1, source_target_pairs={{0,6},{2,4},{4,2},{6,0},{1,7},{3,5},{5,3},{7,1},{8,14},{10,12},{12... | collective-permute-start | bytes 786440 | tf_op jit(solution)/shard_map/ppermute | solution.py:377
  36.2 2.2 %left_back.2 = (bf16[64,16,128]{2,1,0:T(8,128)(2,1)S(1)}, bf16[64,16,128]{2,1,0:T(8,128)(2,1)S(1)}) custom-call(f32[64,32,128]{2,1,0:T(8,128)S(1)} %get-tuple-element.69.tri_back, f32[2048,128]{1,0:T(8,128)S(1)} %get-tuple-element.70.right_act), custom_call_target="tpu_custom_call" | custom-call | flops 1000 | bytes 1000 | tf_op jit(solution)/shard_map/left_back/pallas_call | solution.py:467
  38.4 0.1 collective-permute-start.7
  38.5 5.0 %right_back.1 = (bf16[2,32,16,128]{3,2,1,0:T(8,128)(2,1)S(1)}, bf16[2,32,16,128]{3,2,1,0:T(8,128)(2,1)S(1)}) custom-call(f32[64,32,128]{2,1,0:T(8,128)S(1)} %get-tuple-element.69.tri_back, f32[64,16,128]{2,1,0:T(8,128)S(1)} %get-tuple-element.56.refs_5_.act.refs_0_, f32[64,16,128]{2,1,0:T(8,128)S(1)} %get-tuple-element.77.refs_1_, ...), custom_call_target="tpu_custom_call" | custom-call | flops 1000 | bytes 1000 | tf_op jit(solution)/shard_map/right_back/pallas_call | solution.py:467
  43.5 1.5 %collective-permute-start.10 = (bf16[2,32,16,128]{3,2,1,0:T(8,128)(2,1)S(1)}, bf16[2,32,16,128]{3,2,1,0:T(8,128)(2,1)S(1)}, u32[]{:S(2)}, u32[]{:S(2)}) collective-permute-start(bf16[2,32,16,128]{3,2,1,0:T(8,128)(2,1)S(1)} %get-tuple-element.81.refs_9_), channel_id=1, source_target_pairs={{0,8},{8,0},{16,24},{24,16},{1,9},{9,1},{17,25},{25,17},{2,10},{10... | collective-permute-start | bytes 786440 | tf_op jit(solution)/shard_map/ppermute | solution.py:377
  45.1 1.3 %heads.1 = (bf16[64,32,128]{2,1,0:T(8,128)(2,1)}, bf16[64,32,128]{2,1,0:T(8,128)(2,1)S(1)}, f32[128,128]{1,0:T(8,128)S(1)}, f32[128,128]{1,0:T(8,128)S(1)}) custom-call(bf16[64,32,128]{2,1,0:T(8,128)(2,1)S(1)} %get-tuple-element.66.tri_in, bf16[128,128]{1,0:T(8,128)(2,1)S(1)} %copy-done.8, f32[64,32,128]{2,1,0:T(8,128)S(1)} %get-tuple-element.67.gate, ...), custom_call_target="tpu_custom_call" | custom-call | flops 1000 | bytes 1000 | tf_op jit(solution)/shard_map/heads/pallas_call | solution.py:467
  46.4 2.0 %weights.1 = (f32[2,32,768]{2,1,0:T(8,128)S(1)}, bf16[2,32,768]{2,1,0:T(8,128)(2,1)S(1)}) custom-call(bf16[4,32,16,128]{3,2,1,0:T(8,128)(2,1)S(1)} %get-tuple-element.58.refs_0_.right_in, bf16[128,256]{1,0:T(8,128)(2,1)S(1)} %copy-done.3, bf16[128,256]{1,0:T(8,128)(2,1)S(1)} %copy-done.6, f32[128,128]{1,0:T(8,128)S(1)} %get-tuple-element.86.gate_part, ...), custom_call_target="tpu_custom_call" | custom-call | flops 1000 | bytes 1000 | tf_op jit(solution)/shard_map/weights/pallas_call | solution.py:467
  48.4 0.6 collective-permute-start.12
  49.0 2.3 %grad_middle.1 = (bf16[64,32,128]{2,1,0:T(8,128)(2,1)}, f32[8,128]{1,0:T(8,128)S(1)}) custom-call(bf16[64,32,128]{2,1,0:T(8,128)(2,1)S(1)} %copy-done.4, bf16[64,32,128]{2,1,0:T(8,128)(2,1)S(1)} %get-tuple-element.85.pre_back, bf16[128,128]{1,0:T(8,128)(2,1)S(1)} %copy-done.9, bf16[2,32,768]{2,1,0:T(8,128)(2,1)S(1)} %get-tuple-element.92._), custom_call_target="tpu_custom_call" | custom-call | flops 1000 | bytes 1000 | tf_op jit(solution)/shard_map/grad_middle/pallas_call | solution.py:467
  51.3 1.8 %collective-permute-done.12.came = bf16[2,32,768]{2,1,0:T(8,128)(2,1)S(1)} collective-permute-done((bf16[2,32,768]{2,1,0:T(8,128)(2,1)S(1)}, bf16[2,32,768]{2,1,0:T(8,128)(2,1)S(1)}, u32[]{:S(2)}, u32[]{:S(2)}) %collective-permute-start.12) | collective-permute-done | bytes 98336 | tf_op jit(solution)/shard_map/ppermute | solution.py:377
  53.1 1.6 %collective-permute-start.13 = (bf16[1,32,768]{2,1,0:T(8,128)(2,1)S(1)}, bf16[1,32,768]{2,1,0:T(8,128)(2,1)S(1)}, u32[]{:S(2)}, u32[]{:S(2)}) collective-permute-start(bf16[1,32,768]{2,1,0:T(8,128)(2,1)S(1)} %get-tuple-element.97), channel_id=1, source_target_pairs={{0,16},{8,24},{16,0},{24,8},{1,17},{9,25},{17,1},{25,9},{2,18},{10... | collective-permute-start | bytes 147464 | tf_op jit(solution)/shard_map/ppermute | solution.py:377
  54.8 0.1 halve.2
  54.8 0.5 collective-permute-start.11
  55.4 1.9 %collective-permute-done.13.refs_1_ = bf16[1,32,768]{2,1,0:T(8,128)(2,1)S(1)} collective-permute-done((bf16[1,32,768]{2,1,0:T(8,128)(2,1)S(1)}, bf16[1,32,768]{2,1,0:T(8,128)(2,1)S(1)}, u32[]{:S(2)}, u32[]{:S(2)}) %collective-permute-start.13) | collective-permute-done | bytes 49184 | tf_op jit(solution)/shard_map/ppermute | solution.py:377
  57.3 2.6 %collective-permute-start.16 = (bf16[1,32,768]{2,1,0:T(8,128)(2,1)S(1)}, bf16[1,32,768]{2,1,0:T(8,128)(2,1)S(1)}, u32[]{:S(2)}, u32[]{:S(2)}) collective-permute-start(bf16[1,32,768]{2,1,0:T(8,128)(2,1)S(1)} %combine.2.refs_0_), channel_id=1, source_target_pairs={{0,6},{2,4},{4,2},{6,0},{1,7},{3,5},{5,3},{7,1},{8,14},{10,12},{12... | collective-permute-start | bytes 147464 | tf_op jit(solution)/shard_map/ppermute | solution.py:377
  59.9 1.4 %collective-permute-start.15 = (bf16[1,32,768]{2,1,0:T(8,128)(2,1)S(1)}, bf16[1,32,768]{2,1,0:T(8,128)(2,1)S(1)}, u32[]{:S(2)}, u32[]{:S(2)}) collective-permute-start(bf16[1,32,768]{2,1,0:T(8,128)(2,1)S(1)} %combine.2.refs_0_), channel_id=1, source_target_pairs={{0,4},{2,6},{4,0},{6,2},{1,5},{3,7},{5,1},{7,3},{8,12},{10,14},{12... | collective-permute-start | bytes 147464 | tf_op jit(solution)/shard_map/ppermute | solution.py:377
  61.3 0.4 collective-permute-start.14
  61.7 2.1 %left_side.1 = (bf16[64,16,128]{2,1,0:T(8,128)(2,1)}, f32[8,128]{1,0:T(8,128)S(1)}) custom-call(bf16[64,16,128]{2,1,0:T(8,128)(2,1)S(1)} %copy-done.1, bf16[128,256]{1,0:T(8,128)(2,1)S(1)} %copy-done.3, bf16[64,16,128]{2,1,0:T(8,128)(2,1)S(1)} %get-tuple-element.71._.refs_0_.refs_4_, bf16[64,16,128]{2,1,0:T(8,128)(2,1)S(1)} %collective-permute-done.7.refs_1_.refs_0_, ...), custom_call_target="tpu_custom_call" | custom-call | flops 1000 | bytes 1000 | tf_op jit(solution)/shard_map/left_side/pallas_call | solution.py:467
  63.9 1.0 %collective-permute-done.15.refs_2_ = bf16[1,32,768]{2,1,0:T(8,128)(2,1)S(1)} collective-permute-done((bf16[1,32,768]{2,1,0:T(8,128)(2,1)S(1)}, bf16[1,32,768]{2,1,0:T(8,128)(2,1)S(1)}, u32[]{:S(2)}, u32[]{:S(2)}) %collective-permute-start.15) | collective-permute-done | bytes 49184 | tf_op jit(solution)/shard_map/ppermute | solution.py:377
  64.9 0.5 collective-permute-done.14.refs_1_
  65.5 1.6 %collective-permute-start.19 = (bf16[1,32,768]{2,1,0:T(8,128)(2,1)S(1)}, bf16[1,32,768]{2,1,0:T(8,128)(2,1)S(1)}, u32[]{:S(2)}, u32[]{:S(2)}) collective-permute-start(bf16[1,32,768]{2,1,0:T(8,128)(2,1)S(1)} %combine.3.refs_0_), channel_id=1, source_target_pairs={{0,24},{8,16},{16,8},{24,0},{1,25},{9,17},{17,9},{25,1},{2,26},{10... | collective-permute-start | bytes 147464 | tf_op jit(solution)/shard_map/ppermute | solution.py:377
  67.0 0.5 collective-permute-start.18
  67.5 1.5 %collective-permute-start.17 = (bf16[1,32,768]{2,1,0:T(8,128)(2,1)S(1)}, bf16[1,32,768]{2,1,0:T(8,128)(2,1)S(1)}, u32[]{:S(2)}, u32[]{:S(2)}) collective-permute-start(bf16[1,32,768]{2,1,0:T(8,128)(2,1)S(1)} %combine.3.refs_0_), channel_id=1, source_target_pairs={{0,8},{8,0},{16,24},{24,16},{1,9},{9,1},{17,25},{25,17},{2,10},{10... | collective-permute-start | bytes 147464 | tf_op jit(solution)/shard_map/ppermute | solution.py:377
  69.0 1.4 %right_side.1 = (bf16[32,16,128]{2,1,0:T(8,128)(2,1)}, f32[8,128]{1,0:T(8,128)S(1)}) custom-call(bf16[32,16,128]{2,1,0:T(8,128)(2,1)S(1)} %copy-done.7, bf16[128,256]{1,0:T(8,128)(2,1)S(1)} %copy-done.6, f32[32,16,128]{2,1,0:T(8,128)S(1)} %bitcast.2, bf16[32,16,128]{2,1,0:T(8,128)(2,1)S(1)} %bitcast.3), custom_call_target="tpu_custom_call" | custom-call | flops 1000 | bytes 1000 | tf_op jit(solution)/shard_map/right_side/pallas_call | solution.py:467
  70.5 0.6 collective-permute-done.18.refs_2_
  71.1 0.5 collective-permute-done.17.refs_1_
  71.6 0.8 %deltas.1 = (f32[128,256]{1,0:T(8,128)}, f32[128,256]{1,0:T(8,128)}, f32[128,128]{1,0:T(8,128)}, f32[128,128]{1,0:T(8,128)}) custom-call(bf16[1,32,768]{2,1,0:T(8,128)(2,1)S(1)} %combine.3.refs_0_, bf16[1,32,768]{2,1,0:T(8,128)(2,1)S(1)} %collective-permute-done.17.refs_1_, bf16[1,32,768]{2,1,0:T(8,128)(2,1)S(1)} %collective-permute-done.18.refs_2_, ...), custom_call_target="tpu_custom_call" | custom-call | flops 1000 | bytes 1000 | tf_op jit(solution)/shard_map/deltas/pallas_call | solution.py:467
  (37 shorter events, 0.2 us)
Async XLA Ops:
  0.6 19.4 %collective-permute-start = (bf16[64,16,128]{2,1,0:T(8,128)(2,1)}, bf16[64,16,128]{2,1,0:T(8,128)(2,1)S(1)}, u32[]{:S(2)}, u32[]{:S(2)}) collective-permute-start(bf16[64,16,128]{2,1,0:T(8,128)(2,1)} %raw.4), channel_id=1, source_target_pairs={{0,4},{2,6},{4,0},{6,2},{1,5},{3,7},{5,1},{7,3},{8,12},{10,14},{12... | collective-permute-start | bytes 786440 | tf_op jit(solution)/shard_map/ppermute | solution.py:377
  4.7 11.2 %collective-permute-start.3 = (bf16[32,16,128]{2,1,0:T(8,128)(2,1)}, bf16[32,16,128]{2,1,0:T(8,128)(2,1)S(1)}, u32[]{:S(2)}, u32[]{:S(2)}) collective-permute-start(bf16[32,16,128]{2,1,0:T(8,128)(2,1)} %raw.5), channel_id=1, source_target_pairs={{0,24},{8,16},{16,8},{24,0},{1,25},{9,17},{17,9},{25,1},{2,26},{10... | collective-permute-start | bytes 393224 | tf_op jit(solution)/shard_map/ppermute | solution.py:377
  7.2 8.8 %collective-permute-start.2 = (bf16[32,16,128]{2,1,0:T(8,128)(2,1)}, bf16[32,16,128]{2,1,0:T(8,128)(2,1)S(1)}, u32[]{:S(2)}, u32[]{:S(2)}) collective-permute-start(bf16[32,16,128]{2,1,0:T(8,128)(2,1)} %raw.5), channel_id=1, source_target_pairs={{0,16},{8,24},{16,0},{24,8},{1,17},{9,25},{17,1},{25,9},{2,18},{10... | collective-permute-start | bytes 393224 | tf_op jit(solution)/shard_map/ppermute | solution.py:377
  7.7 8.3 %collective-permute-start.1 = (bf16[32,16,128]{2,1,0:T(8,128)(2,1)}, bf16[32,16,128]{2,1,0:T(8,128)(2,1)S(1)}, u32[]{:S(2)}, u32[]{:S(2)}) collective-permute-start(bf16[32,16,128]{2,1,0:T(8,128)(2,1)} %raw.5), channel_id=1, source_target_pairs={{0,8},{8,0},{16,24},{24,16},{1,9},{9,1},{17,25},{25,17},{2,10},{10... | collective-permute-start | bytes 393224 | tf_op jit(solution)/shard_map/ppermute | solution.py:377
  8.2 14.0 %collective-permute-start.6 = (bf16[64,16,128]{2,1,0:T(8,128)(2,1)}, bf16[64,16,128]{2,1,0:T(8,128)(2,1)S(1)}, u32[]{:S(2)}, u32[]{:S(2)}) collective-permute-start(bf16[64,16,128]{2,1,0:T(8,128)(2,1)} %raw.4), channel_id=1, source_target_pairs={{0,2},{2,0},{4,6},{6,4},{1,3},{3,1},{5,7},{7,5},{8,10},{10,8},{12,... | collective-permute-start | bytes 786440 | tf_op jit(solution)/shard_map/ppermute | solution.py:377
  9.8 1.0 %copy-start = (bf16[64,16,128]{2,1,0:T(8,128)(2,1)S(1)}, bf16[64,16,128]{2,1,0:T(8,128)(2,1)}, u32[]{:S(2)}) copy-start(bf16[64,16,128]{2,1,0:T(8,128)(2,1)} %raw.4) | copy-start | bytes 786436
  10.8 0.8 %copy-start.2 = (bf16[128,256]{1,0:T(8,128)(2,1)S(1)}, bf16[128,256]{1,0:T(8,128)(2,1)}, u32[]{:S(2)}) copy-start(bf16[128,256]{1,0:T(8,128)(2,1)} %left_w.1) | copy-start | bytes 196612
  12.4 1.0 %copy-start.4 = (bf16[64,32,128]{2,1,0:T(8,128)(2,1)S(1)}, bf16[64,32,128]{2,1,0:T(8,128)(2,1)}, u32[]{:S(2)}) copy-start(bf16[64,32,128]{2,1,0:T(8,128)(2,1)} %middle.5) | copy-start | bytes 1572868
  12.4 1.2 %copy-start.5 = (bf16[64,32,128]{2,1,0:T(8,128)(2,1)S(1)}, bf16[64,32,128]{2,1,0:T(8,128)(2,1)}, u32[]{:S(2)}) copy-start(bf16[64,32,128]{2,1,0:T(8,128)(2,1)} %cotangent.3) | copy-start | bytes 1572868
  12.4 1.2 %copy-start.8 = (bf16[128,128]{1,0:T(8,128)(2,1)S(1)}, bf16[128,128]{1,0:T(8,128)(2,1)}, u32[]{:S(2)}) copy-start(bf16[128,128]{1,0:T(8,128)(2,1)} %out_w.1) | copy-start | bytes 98308
  12.4 1.2 %copy-start.9 = (bf16[128,128]{1,0:T(8,128)(2,1)S(1)}, bf16[128,128]{1,0:T(8,128)(2,1)}, u32[]{:S(2)}) copy-start(bf16[128,128]{1,0:T(8,128)(2,1)} %gate_weight.3) | copy-start | bytes 98308
  13.6 2.4 %copy-start.6 = (bf16[128,256]{1,0:T(8,128)(2,1)S(1)}, bf16[128,256]{1,0:T(8,128)(2,1)}, u32[]{:S(2)}) copy-start(bf16[128,256]{1,0:T(8,128)(2,1)} %right_w.1) | copy-start | bytes 196612
  13.6 2.4 %copy-start.7 = (bf16[32,16,128]{2,1,0:T(8,128)(2,1)S(1)}, bf16[32,16,128]{2,1,0:T(8,128)(2,1)}, u32[]{:S(2)}) copy-start(bf16[32,16,128]{2,1,0:T(8,128)(2,1)} %raw.5) | copy-start | bytes 393220
  18.0 1.2 %copy-start.1 = (bf16[64,16,128]{2,1,0:T(8,128)(2,1)S(1)}, bf16[64,16,128]{2,1,0:T(8,128)(2,1)}, u32[]{:S(2)}) copy-start(bf16[64,16,128]{2,1,0:T(8,128)(2,1)} %raw.4) | copy-start | bytes 786436
  19.2 7.1 %collective-permute-start.5 = (bf16[64,16,128]{2,1,0:T(8,128)(2,1)S(1)}, bf16[64,16,128]{2,1,0:T(8,128)(2,1)S(1)}, u32[]{:S(2)}, u32[]{:S(2)}) collective-permute-start(bf16[64,16,128]{2,1,0:T(8,128)(2,1)S(1)} %forward.3), channel_id=1, source_target_pairs={{0,0},{2,4},{4,2},{6,6},{1,1},{3,5},{5,3},{7,7},{8,8},{10,12},{12,... | collective-permute-start | bytes 786440 | tf_op jit(solution)/shard_map/ppermute | solution.py:417
  20.0 2.2 %copy-start.3 = (bf16[128,256]{1,0:T(8,128)(2,1)S(1)}, bf16[128,256]{1,0:T(8,128)(2,1)}, u32[]{:S(2)}) copy-start(bf16[128,256]{1,0:T(8,128)(2,1)} %left_w.1) | copy-start | bytes 196612
  20.1 6.9 %collective-permute-start.4 = (bf16[64,16,128]{2,1,0:T(8,128)(2,1)S(1)}, bf16[64,16,128]{2,1,0:T(8,128)(2,1)S(1)}, u32[]{:S(2)}, u32[]{:S(2)}) collective-permute-start(bf16[64,16,128]{2,1,0:T(8,128)(2,1)S(1)} %forward.2), channel_id=1, source_target_pairs={{0,2},{2,0},{4,6},{6,4},{1,3},{3,1},{5,7},{7,5},{8,10},{10,8},{12,... | collective-permute-start | bytes 786440 | tf_op jit(solution)/shard_map/ppermute | solution.py:377
  32.0 22.7 %collective-permute-start.8 = (bf16[64,16,128]{2,1,0:T(8,128)(2,1)S(1)}, bf16[64,16,128]{2,1,0:T(8,128)(2,1)S(1)}, u32[]{:S(2)}, u32[]{:S(2)}) collective-permute-start(bf16[64,16,128]{2,1,0:T(8,128)(2,1)S(1)} %get-tuple-element.74.refs_6_), channel_id=1, source_target_pairs={{0,4},{2,6},{4,0},{6,2},{1,5},{3,7},{5,1},{7,3},{8,12},{10,14},{12... | collective-permute-start | bytes 786440 | tf_op jit(solution)/shard_map/ppermute | solution.py:377
  35.0 19.8 %collective-permute-start.9 = (bf16[64,16,128]{2,1,0:T(8,128)(2,1)S(1)}, bf16[64,16,128]{2,1,0:T(8,128)(2,1)S(1)}, u32[]{:S(2)}, u32[]{:S(2)}) collective-permute-start(bf16[64,16,128]{2,1,0:T(8,128)(2,1)S(1)} %get-tuple-element.75.refs_7_), channel_id=1, source_target_pairs={{0,6},{2,4},{4,2},{6,0},{1,7},{3,5},{5,3},{7,1},{8,14},{10,12},{12... | collective-permute-start | bytes 786440 | tf_op jit(solution)/shard_map/ppermute | solution.py:377
  38.4 16.3 %collective-permute-start.7 = (bf16[64,16,128]{2,1,0:T(8,128)(2,1)S(1)}, bf16[64,16,128]{2,1,0:T(8,128)(2,1)S(1)}, u32[]{:S(2)}, u32[]{:S(2)}) collective-permute-start(bf16[64,16,128]{2,1,0:T(8,128)(2,1)S(1)} %get-tuple-element.73.refs_5_), channel_id=1, source_target_pairs={{0,2},{2,0},{4,6},{6,4},{1,3},{3,1},{5,7},{7,5},{8,10},{10,8},{12,... | collective-permute-start | bytes 786440 | tf_op jit(solution)/shard_map/ppermute | solution.py:377
  43.5 11.2 %collective-permute-start.10 = (bf16[2,32,16,128]{3,2,1,0:T(8,128)(2,1)S(1)}, bf16[2,32,16,128]{3,2,1,0:T(8,128)(2,1)S(1)}, u32[]{:S(2)}, u32[]{:S(2)}) collective-permute-start(bf16[2,32,16,128]{3,2,1,0:T(8,128)(2,1)S(1)} %get-tuple-element.81.refs_9_), channel_id=1, source_target_pairs={{0,8},{8,0},{16,24},{24,16},{1,9},{9,1},{17,25},{25,17},{2,10},{10... | collective-permute-start | bytes 786440 | tf_op jit(solution)/shard_map/ppermute | solution.py:377
  48.4 4.7 %collective-permute-start.12 = (bf16[2,32,768]{2,1,0:T(8,128)(2,1)S(1)}, bf16[2,32,768]{2,1,0:T(8,128)(2,1)S(1)}, u32[]{:S(2)}, u32[]{:S(2)}) collective-permute-start(bf16[2,32,768]{2,1,0:T(8,128)(2,1)S(1)} %get-tuple-element.92._), channel_id=1, source_target_pairs={{0,8},{8,0},{16,24},{24,16},{1,9},{9,1},{17,25},{25,17},{2,10},{10... | collective-permute-start | bytes 294920 | tf_op jit(solution)/shard_map/ppermute | solution.py:377
  53.1 4.2 %collective-permute-start.13 = (bf16[1,32,768]{2,1,0:T(8,128)(2,1)S(1)}, bf16[1,32,768]{2,1,0:T(8,128)(2,1)S(1)}, u32[]{:S(2)}, u32[]{:S(2)}) collective-permute-start(bf16[1,32,768]{2,1,0:T(8,128)(2,1)S(1)} %get-tuple-element.97), channel_id=1, source_target_pairs={{0,16},{8,24},{16,0},{24,8},{1,17},{9,25},{17,1},{25,9},{2,18},{10... | collective-permute-start | bytes 147464 | tf_op jit(solution)/shard_map/ppermute | solution.py:377
  54.8 14.2 %collective-permute-start.11 = (bf16[1,32,16,128]{3,2,1,0:T(8,128)(2,1)S(1)}, bf16[1,32,16,128]{3,2,1,0:T(8,128)(2,1)S(1)}, u32[]{:S(2)}, u32[]{:S(2)}) collective-permute-start(bf16[1,32,16,128]{3,2,1,0:T(8,128)(2,1)S(1)} %get-tuple-element.83.refs_0_), channel_id=1, source_target_pairs={{0,16},{8,24},{16,0},{24,8},{1,17},{9,25},{17,1},{25,9},{2,18},{10... | collective-permute-start | bytes 393224 | tf_op jit(solution)/shard_map/ppermute | solution.py:377
  57.3 6.6 %collective-permute-start.16 = (bf16[1,32,768]{2,1,0:T(8,128)(2,1)S(1)}, bf16[1,32,768]{2,1,0:T(8,128)(2,1)S(1)}, u32[]{:S(2)}, u32[]{:S(2)}) collective-permute-start(bf16[1,32,768]{2,1,0:T(8,128)(2,1)S(1)} %combine.2.refs_0_), channel_id=1, source_target_pairs={{0,6},{2,4},{4,2},{6,0},{1,7},{3,5},{5,3},{7,1},{8,14},{10,12},{12... | collective-permute-start | bytes 147464 | tf_op jit(solution)/shard_map/ppermute | solution.py:377
  59.9 5.0 %collective-permute-start.15 = (bf16[1,32,768]{2,1,0:T(8,128)(2,1)S(1)}, bf16[1,32,768]{2,1,0:T(8,128)(2,1)S(1)}, u32[]{:S(2)}, u32[]{:S(2)}) collective-permute-start(bf16[1,32,768]{2,1,0:T(8,128)(2,1)S(1)} %combine.2.refs_0_), channel_id=1, source_target_pairs={{0,4},{2,6},{4,0},{6,2},{1,5},{3,7},{5,1},{7,3},{8,12},{10,14},{12... | collective-permute-start | bytes 147464 | tf_op jit(solution)/shard_map/ppermute | solution.py:377
  61.3 4.1 %collective-permute-start.14 = (bf16[1,32,768]{2,1,0:T(8,128)(2,1)S(1)}, bf16[1,32,768]{2,1,0:T(8,128)(2,1)S(1)}, u32[]{:S(2)}, u32[]{:S(2)}) collective-permute-start(bf16[1,32,768]{2,1,0:T(8,128)(2,1)S(1)} %combine.2.refs_0_), channel_id=1, source_target_pairs={{0,2},{2,0},{4,6},{6,4},{1,3},{3,1},{5,7},{7,5},{8,10},{10,8},{12,... | collective-permute-start | bytes 147464 | tf_op jit(solution)/shard_map/ppermute | solution.py:377
  65.5 5.1 %collective-permute-start.19 = (bf16[1,32,768]{2,1,0:T(8,128)(2,1)S(1)}, bf16[1,32,768]{2,1,0:T(8,128)(2,1)S(1)}, u32[]{:S(2)}, u32[]{:S(2)}) collective-permute-start(bf16[1,32,768]{2,1,0:T(8,128)(2,1)S(1)} %combine.3.refs_0_), channel_id=1, source_target_pairs={{0,24},{8,16},{16,8},{24,0},{1,25},{9,17},{17,9},{25,1},{2,26},{10... | collective-permute-start | bytes 147464 | tf_op jit(solution)/shard_map/ppermute | solution.py:377
  67.0 4.1 %collective-permute-start.18 = (bf16[1,32,768]{2,1,0:T(8,128)(2,1)S(1)}, bf16[1,32,768]{2,1,0:T(8,128)(2,1)S(1)}, u32[]{:S(2)}, u32[]{:S(2)}) collective-permute-start(bf16[1,32,768]{2,1,0:T(8,128)(2,1)S(1)} %combine.3.refs_0_), channel_id=1, source_target_pairs={{0,16},{8,24},{16,0},{24,8},{1,17},{9,25},{17,1},{25,9},{2,18},{10... | collective-permute-start | bytes 147464 | tf_op jit(solution)/shard_map/ppermute | solution.py:377
  67.5 4.1 %collective-permute-start.17 = (bf16[1,32,768]{2,1,0:T(8,128)(2,1)S(1)}, bf16[1,32,768]{2,1,0:T(8,128)(2,1)S(1)}, u32[]{:S(2)}, u32[]{:S(2)}) collective-permute-start(bf16[1,32,768]{2,1,0:T(8,128)(2,1)S(1)} %combine.3.refs_0_), channel_id=1, source_target_pairs={{0,8},{8,0},{16,24},{24,16},{1,9},{9,1},{17,25},{25,17},{2,10},{10... | collective-permute-start | bytes 147464 | tf_op jit(solution)/shard_map/ppermute | solution.py:377

commit v15 on v14

--- a/solution.py
+++ b/solution.py
@@ -157,7 +157,7 @@
     return total
 
 
-def own_kernel(raw, weight, act_out, in_out):
+def own_kernel(raw, weight, _, act_out, in_out):
     project_left([raw], weight, act_out, in_out)
 
 
@@ -495,15 +495,16 @@
     n_k = k_left * n_blk
     right_raw = [pair_right] + [exchange(pair_right, "rows", n_rows, s) for s in range(1, n_rows)]
     middle_shape = (n_i, n_j, width)
+    begun = behind(cost=10**9)
     gate, middle_in, head_back, tri_up = call(
         middle_kernel,
         "middle",
         [shape(middle_shape, f32), shape(middle_shape, bf16), shape(middle_shape, bf16), shape(middle_shape, f32)],
         after=1,
-    )(pair_middle, cotangent, gate_weight, output_weight, behind(cost=10**9))
+    )(pair_middle, cotangent, gate_weight, output_weight, begun)
     act_shape = shape(pair_left.shape, f32)
     in_shape = shape(pair_left.shape, bf16)
-    own_act, own_in = call(own_kernel, "own", [act_shape, in_shape], after=0)(pair_left, left_weight)
+    own_act, own_in = call(own_kernel, "own", [act_shape, in_shape], after=1)(pair_left, left_weight, begun)
     right_act, right_in, *right_flip = call(
         functools.partial(right_kernel, n_rows, n_blk, k_left),
         "right",

time: 72.6 us -> 72.8 us (level)
  local copies, waits for them, and re-layouts: 3.01 us -> 0.39 us
  waiting for transfers between devices: 7.09 us -> 9.04 us
  starting transfers between devices: 28.8 us -> 29.8 us
    unnamed x20 -> x16, local copies, waits for them, and re-layouts: 3.01 us -> 0.39 us
    ppermute x19, waiting for transfers between devices: 7.09 us -> 9.04 us  [exchange(): return lax.ppermute(x, axis, [(a, a ^ bit) for a in range(n)])]
    ppermute x19, starting transfers between devices: 27.9 us -> 28.9 us  [exchange(): return lax.ppermute(x, axis, [(a, a ^ bit) for a in range(n)])]
  transfers between devices with their start and end apart: 20 -> 20, of which waited for: 7 -> 9; matrix products, arithmetic and copies ran while one was open for 0% -> 0% of each run, Pallas kernels for 37% -> 37%
where the time goes in v15:
time: 72.8 us; the launch traced here: 72.7 us
  Pallas kernels  32.6 us (45%)
  starting transfers between devices  29.8 us (41%)
  waiting for transfers between devices  9.04 us (12%)
  between operations  0.83 us (1%)
    pallas_call x25, Pallas kernels, run(): pl.pallas_call(kernel, in_specs=[pl.BlockSpec(memory_space=space) for spa...  32.6 us
    ppermute x19, starting transfers between devices, exchange(): return lax.ppermute(x, axis, [(a, a ^ bit) for a in range(n)])  28.9 us
    ppermute x19, waiting for transfers between devices, exchange(): return lax.ppermute(x, axis, [(a, a ^ bit) for a in range(n)])  9.04 us
  transfers between devices with their start and end apart: 20, of which 9 were waited for; matrix products, arithmetic and copies ran while one was open for 0% of the time, Pallas kernels for 37%

profile of v15, /device:TPU:0, one launch (start us, length us, event | category | flops | bytes accessed | tf_op | source)
XLA Modules:
  0.0 72.7 jit_solution(15274747152970046735)
XLA Ops:
  0.7 4.1 %collective-permute-start = (bf16[64,16,128]{2,1,0:T(8,128)(2,1)}, bf16[64,16,128]{2,1,0:T(8,128)(2,1)S(1)}, u32[]{:S(2)}, u32[]{:S(2)}) collective-permute-start(bf16[64,16,128]{2,1,0:T(8,128)(2,1)} %raw.4), channel_id=1, source_target_pairs={{0,4},{2,6},{4,0},{6,2},{1,5},{3,7},{5,1},{7,3},{8,12},{10,14},{12... | collective-permute-start | bytes 786440 | tf_op jit(solution)/shard_map/ppermute | solution.py:377
  4.8 2.4 %collective-permute-start.3 = (bf16[32,16,128]{2,1,0:T(8,128)(2,1)}, bf16[32,16,128]{2,1,0:T(8,128)(2,1)S(1)}, u32[]{:S(2)}, u32[]{:S(2)}) collective-permute-start(bf16[32,16,128]{2,1,0:T(8,128)(2,1)} %raw.5), channel_id=1, source_target_pairs={{0,24},{8,16},{16,8},{24,0},{1,25},{9,17},{17,9},{25,1},{2,26},{10... | collective-permute-start | bytes 393224 | tf_op jit(solution)/shard_map/ppermute | solution.py:377
  7.2 0.5 collective-permute-start.2
  7.7 0.5 collective-permute-start.1
  8.2 1.6 %collective-permute-start.6 = (bf16[64,16,128]{2,1,0:T(8,128)(2,1)}, bf16[64,16,128]{2,1,0:T(8,128)(2,1)S(1)}, u32[]{:S(2)}, u32[]{:S(2)}) collective-permute-start(bf16[64,16,128]{2,1,0:T(8,128)(2,1)} %raw.4), channel_id=1, source_target_pairs={{0,2},{2,0},{4,6},{6,4},{1,3},{3,1},{5,7},{7,5},{8,10},{10,8},{12,... | collective-permute-start | bytes 786440 | tf_op jit(solution)/shard_map/ppermute | solution.py:377
  9.9 0.8 %own.1 = (f32[64,16,128]{2,1,0:T(8,128)S(1)}, bf16[64,16,128]{2,1,0:T(8,128)(2,1)S(1)}) custom-call(bf16[64,16,128]{2,1,0:T(8,128)(2,1)S(1)} %copy-done, bf16[128,256]{1,0:T(8,128)(2,1)S(1)} %copy-done.1, f32[8,128]{1,0:T(8,128)S(1)} %order.3._), custom_call_target="tpu_custom_call" | custom-call | flops 1000 | bytes 1000 | tf_op jit(solution)/shard_map/own/pallas_call | solution.py:467
  10.7 0.2 copy-done.2
  10.9 0.2 copy-done.3
  11.0 2.3 %middle.3 = (f32[64,32,128]{2,1,0:T(8,128)S(1)}, bf16[64,32,128]{2,1,0:T(8,128)(2,1)S(1)}, bf16[64,32,128]{2,1,0:T(8,128)(2,1)S(1)}, f32[64,32,128]{2,1,0:T(8,128)S(1)}) custom-call(bf16[64,32,128]{2,1,0:T(8,128)(2,1)S(1)} %copy-done.2, bf16[64,32,128]{2,1,0:T(8,128)(2,1)S(1)} %copy-done.3, bf16[128,128]{1,0:T(8,128)(2,1)S(1)} %copy-done.7, ...), custom_call_target="tpu_custom_call" | custom-call | flops 1000 | bytes 1000 | tf_op jit(solution)/shard_map/middle/pallas_call | solution.py:467
  13.4 0.2 collective-permute-done.2.refs_2_
  13.6 0.1 collective-permute-done.1.refs_1_
  13.7 1.9 %right.1 = (f32[2048,128]{1,0:T(8,128)S(1)}, bf16[4,32,16,128]{3,2,1,0:T(8,128)(2,1)S(1)}, f32[16,32,128]{2,1,0:T(8,128)S(1)}, f32[16,32,128]{2,1,0:T(8,128)S(1)...) custom-call(bf16[32,16,128]{2,1,0:T(8,128)(2,1)S(1)} %copy-done.5, ...), custom_call_target="tpu_custom_call" | custom-call | flops 1000 | bytes 1000 | tf_op jit(solution)/shard_map/right/pallas_call | solution.py:467
  15.6 1.1 %own_sum.1.refs_0_.total_in = f32[64,32,128]{2,1,0:T(8,128)S(1)} custom-call(f32[64,16,128]{2,1,0:T(8,128)S(1)} %get-tuple-element.56.refs_5_.act.refs_0_, f32[16,32,128]{2,1,0:T(8,128)S(1)} %get-tuple-element.59.flip), custom_call_target="tpu_custom_call" | custom-call | flops 1000 | bytes 1000 | tf_op jit(solution)/shard_map/own_sum/pallas_call | solution.py:467
  16.8 0.9 %collective-permute-start.5 = (bf16[64,16,128]{2,1,0:T(8,128)(2,1)S(1)}, bf16[64,16,128]{2,1,0:T(8,128)(2,1)S(1)}, u32[]{:S(2)}, u32[]{:S(2)}) collective-permute-start(bf16[64,16,128]{2,1,0:T(8,128)(2,1)S(1)} %forward.3), channel_id=1, source_target_pairs={{0,0},{2,4},{4,2},{6,6},{1,1},{3,5},{5,3},{7,7},{8,8},{10,12},{12,... | collective-permute-start | bytes 786440 | tf_op jit(solution)/shard_map/ppermute | solution.py:417
  17.7 2.9 %collective-permute-start.4 = (bf16[64,16,128]{2,1,0:T(8,128)(2,1)S(1)}, bf16[64,16,128]{2,1,0:T(8,128)(2,1)S(1)}, u32[]{:S(2)}, u32[]{:S(2)}) collective-permute-start(bf16[64,16,128]{2,1,0:T(8,128)(2,1)S(1)} %forward.2), channel_id=1, source_target_pairs={{0,2},{2,0},{4,6},{6,4},{1,3},{3,1},{5,7},{7,5},{8,10},{10,8},{12,... | collective-permute-start | bytes 786440 | tf_op jit(solution)/shard_map/ppermute | solution.py:377
  20.6 2.0 %left.2 = (f32[64,16,128]{2,1,0:T(8,128)S(1)}, bf16[64,16,128]{2,1,0:T(8,128)(2,1)S(1)}, f32[64,32,128]{2,1,0:T(8,128)S(1)}) custom-call(bf16[64,16,128]{2,1,0:T(8,128)(2,1)S(1)} %collective-permute-done.6.raw, bf16[128,256]{1,0:T(8,128)(2,1)S(1)} %copy-done.1, f32[16,32,128]{2,1,0:T(8,128)S(1)} %get-tuple-element.63.flip, ...), custom_call_target="tpu_custom_call" | custom-call | flops 1000 | bytes 1000 | tf_op jit(solution)/shard_map/left/pallas_call | solution.py:467
  22.6 2.0 %left.3 = (f32[64,16,128]{2,1,0:T(8,128)S(1)}, bf16[64,16,128]{2,1,0:T(8,128)(2,1)S(1)}, f32[64,32,128]{2,1,0:T(8,128)S(1)}) custom-call(bf16[64,16,128]{2,1,0:T(8,128)(2,1)S(1)} %collective-permute-done.source.raw, bf16[128,256]{1,0:T(8,128)(2,1)S(1)} %copy-done.1, f32[16,32,128]{2,1,0:T(8,128)S(1)} %get-tuple-element.62.flip, ...), custom_call_target="tpu_custom_call" | custom-call | flops 1000 | bytes 1000 | tf_op jit(solution)/shard_map/left/pallas_call | solution.py:467
  24.6 2.3 %collective-permute-done.4.refs_0_ = bf16[64,16,128]{2,1,0:T(8,128)(2,1)S(1)} collective-permute-done((bf16[64,16,128]{2,1,0:T(8,128)(2,1)S(1)}, bf16[64,16,128]{2,1,0:T(8,128)(2,1)S(1)}, u32[]{:S(2)}, u32[]{:S(2)}) %collective-permute-start.4) | collective-permute-done | bytes 262176 | tf_op jit(solution)/shard_map/ppermute | solution.py:377
  26.9 2.9 %triangle.1 = (f32[64,16,128]{2,1,0:T(8,128)S(1)}, bf16[64,16,128]{2,1,0:T(8,128)(2,1)S(1)}, bf16[64,32,128]{2,1,0:T(8,128)(2,1)S(1)}, f32[64,32,128]{2,1,0:T(8,128)S(1)}) custom-call(bf16[64,16,128]{2,1,0:T(8,128)(2,1)S(1)} %collective-permute-done.4.refs_0_, bf16[64,16,128]{2,1,0:T(8,128)(2,1)S(1)} %collective-permute-done.5.refs_1_, ...), custom_call_target="tpu_custom_call" | custom-call | flops 1000 | bytes 1000 | tf_op jit(solution)/shard_map/triangle/pallas_call | solution.py:467
  29.7 2.2 %left_back.3 = (bf16[64,16,128]{2,1,0:T(8,128)(2,1)S(1)}, bf16[64,16,128]{2,1,0:T(8,128)(2,1)S(1)}) custom-call(f32[64,32,128]{2,1,0:T(8,128)S(1)} %get-tuple-element.69.tri_back, f32[2048,128]{1,0:T(8,128)S(1)} %get-tuple-element.70.right_act), custom_call_target="tpu_custom_call" | custom-call | flops 1000 | bytes 1000 | tf_op jit(solution)/shard_map/left_back/pallas_call | solution.py:467
  32.0 3.0 %collective-permute-start.8 = (bf16[64,16,128]{2,1,0:T(8,128)(2,1)S(1)}, bf16[64,16,128]{2,1,0:T(8,128)(2,1)S(1)}, u32[]{:S(2)}, u32[]{:S(2)}) collective-permute-start(bf16[64,16,128]{2,1,0:T(8,128)(2,1)S(1)} %get-tuple-element.74.refs_6_), channel_id=1, source_target_pairs={{0,4},{2,6},{4,0},{6,2},{1,5},{3,7},{5,1},{7,3},{8,12},{10,14},{12... | collective-permute-start | bytes 786440 | tf_op jit(solution)/shard_map/ppermute | solution.py:377
  34.9 1.2 %collective-permute-start.9 = (bf16[64,16,128]{2,1,0:T(8,128)(2,1)S(1)}, bf16[64,16,128]{2,1,0:T(8,128)(2,1)S(1)}, u32[]{:S(2)}, u32[]{:S(2)}) collective-permute-start(bf16[64,16,128]{2,1,0:T(8,128)(2,1)S(1)} %get-tuple-element.75.refs_7_), channel_id=1, source_target_pairs={{0,6},{2,4},{4,2},{6,0},{1,7},{3,5},{5,3},{7,1},{8,14},{10,12},{12... | collective-permute-start | bytes 786440 | tf_op jit(solution)/shard_map/ppermute | solution.py:377
  36.1 2.2 %left_back.2 = (bf16[64,16,128]{2,1,0:T(8,128)(2,1)S(1)}, bf16[64,16,128]{2,1,0:T(8,128)(2,1)S(1)}) custom-call(f32[64,32,128]{2,1,0:T(8,128)S(1)} %get-tuple-element.69.tri_back, f32[2048,128]{1,0:T(8,128)S(1)} %get-tuple-element.70.right_act), custom_call_target="tpu_custom_call" | custom-call | flops 1000 | bytes 1000 | tf_op jit(solution)/shard_map/left_back/pallas_call | solution.py:467
  38.4 0.1 collective-permute-start.7
  38.5 5.0 %right_back.1 = (bf16[2,32,16,128]{3,2,1,0:T(8,128)(2,1)S(1)}, bf16[2,32,16,128]{3,2,1,0:T(8,128)(2,1)S(1)}) custom-call(f32[64,32,128]{2,1,0:T(8,128)S(1)} %get-tuple-element.69.tri_back, f32[64,16,128]{2,1,0:T(8,128)S(1)} %get-tuple-element.56.refs_5_.act.refs_0_, f32[64,16,128]{2,1,0:T(8,128)S(1)} %get-tuple-element.77.refs_1_, ...), custom_call_target="tpu_custom_call" | custom-call | flops 1000 | bytes 1000 | tf_op jit(solution)/shard_map/right_back/pallas_call | solution.py:467
  43.5 1.6 %collective-permute-start.10 = (bf16[2,32,16,128]{3,2,1,0:T(8,128)(2,1)S(1)}, bf16[2,32,16,128]{3,2,1,0:T(8,128)(2,1)S(1)}, u32[]{:S(2)}, u32[]{:S(2)}) collective-permute-start(bf16[2,32,16,128]{3,2,1,0:T(8,128)(2,1)S(1)} %get-tuple-element.81.refs_9_), channel_id=1, source_target_pairs={{0,8},{8,0},{16,24},{24,16},{1,9},{9,1},{17,25},{25,17},{2,10},{10... | collective-permute-start | bytes 786440 | tf_op jit(solution)/shard_map/ppermute | solution.py:377
  45.0 1.3 %heads.1 = (bf16[64,32,128]{2,1,0:T(8,128)(2,1)}, bf16[64,32,128]{2,1,0:T(8,128)(2,1)S(1)}, f32[128,128]{1,0:T(8,128)S(1)}, f32[128,128]{1,0:T(8,128)S(1)}) custom-call(bf16[64,32,128]{2,1,0:T(8,128)(2,1)S(1)} %get-tuple-element.66.tri_in, bf16[128,128]{1,0:T(8,128)(2,1)S(1)} %copy-done.6, f32[64,32,128]{2,1,0:T(8,128)S(1)} %get-tuple-element.67.gate, ...), custom_call_target="tpu_custom_call" | custom-call | flops 1000 | bytes 1000 | tf_op jit(solution)/shard_map/heads/pallas_call | solution.py:467
  46.3 2.0 %weights.1 = (f32[2,32,768]{2,1,0:T(8,128)S(1)}, bf16[2,32,768]{2,1,0:T(8,128)(2,1)S(1)}) custom-call(bf16[4,32,16,128]{3,2,1,0:T(8,128)(2,1)S(1)} %get-tuple-element.58.refs_0_.right_in, bf16[128,256]{1,0:T(8,128)(2,1)S(1)} %copy-done.1, bf16[128,256]{1,0:T(8,128)(2,1)S(1)} %copy-done.4, f32[128,128]{1,0:T(8,128)S(1)} %get-tuple-element.86.gate_part, ...), custom_call_target="tpu_custom_call" | custom-call | flops 1000 | bytes 1000 | tf_op jit(solution)/shard_map/weights/pallas_call | solution.py:467
  48.3 0.6 collective-permute-start.12
  48.9 2.3 %grad_middle.1 = (bf16[64,32,128]{2,1,0:T(8,128)(2,1)}, f32[8,128]{1,0:T(8,128)S(1)}) custom-call(bf16[64,32,128]{2,1,0:T(8,128)(2,1)S(1)} %copy-done.2, bf16[64,32,128]{2,1,0:T(8,128)(2,1)S(1)} %get-tuple-element.85.pre_back, bf16[128,128]{1,0:T(8,128)(2,1)S(1)} %copy-done.7, bf16[2,32,768]{2,1,0:T(8,128)(2,1)S(1)} %get-tuple-element.92._), custom_call_target="tpu_custom_call" | custom-call | flops 1000 | bytes 1000 | tf_op jit(solution)/shard_map/grad_middle/pallas_call | solution.py:467
  51.2 1.8 %collective-permute-done.12.came = bf16[2,32,768]{2,1,0:T(8,128)(2,1)S(1)} collective-permute-done((bf16[2,32,768]{2,1,0:T(8,128)(2,1)S(1)}, bf16[2,32,768]{2,1,0:T(8,128)(2,1)S(1)}, u32[]{:S(2)}, u32[]{:S(2)}) %collective-permute-start.12) | collective-permute-done | bytes 98336 | tf_op jit(solution)/shard_map/ppermute | solution.py:377
  53.0 0.8 %collective-permute-start.13 = (bf16[1,32,768]{2,1,0:T(8,128)(2,1)S(1)}, bf16[1,32,768]{2,1,0:T(8,128)(2,1)S(1)}, u32[]{:S(2)}, u32[]{:S(2)}) collective-permute-start(bf16[1,32,768]{2,1,0:T(8,128)(2,1)S(1)} %get-tuple-element.97), channel_id=1, source_target_pairs={{0,16},{8,24},{16,0},{24,8},{1,17},{9,25},{17,1},{25,9},{2,18},{10... | collective-permute-start | bytes 147464 | tf_op jit(solution)/shard_map/ppermute | solution.py:377
  53.9 1.3 %collective-permute-done.7.refs_1_.refs_0_ = bf16[64,16,128]{2,1,0:T(8,128)(2,1)S(1)} collective-permute-done((bf16[64,16,128]{2,1,0:T(8,128)(2,1)S(1)}, bf16[64,16,128]{2,1,0:T(8,128)(2,1)S(1)}, u32[]{:S(2)}, u32[]{:S(2)}) %collective-permute-start.7) | collective-permute-done | bytes 262176 | tf_op jit(solution)/shard_map/ppermute | solution.py:377
  55.2 0.1 halve.2
  55.3 1.7 %collective-permute-start.11 = (bf16[1,32,16,128]{3,2,1,0:T(8,128)(2,1)S(1)}, bf16[1,32,16,128]{3,2,1,0:T(8,128)(2,1)S(1)}, u32[]{:S(2)}, u32[]{:S(2)}) collective-permute-start(bf16[1,32,16,128]{3,2,1,0:T(8,128)(2,1)S(1)} %get-tuple-element.83.refs_0_), channel_id=1, source_target_pairs={{0,16},{8,24},{16,0},{24,8},{1,17},{9,25},{17,1},{25,9},{2,18},{10... | collective-permute-start | bytes 393224 | tf_op jit(solution)/shard_map/ppermute | solution.py:377
  56.9 0.8 %collective-permute-done.13.refs_1_ = bf16[1,32,768]{2,1,0:T(8,128)(2,1)S(1)} collective-permute-done((bf16[1,32,768]{2,1,0:T(8,128)(2,1)S(1)}, bf16[1,32,768]{2,1,0:T(8,128)(2,1)S(1)}, u32[]{:S(2)}, u32[]{:S(2)}) %collective-permute-start.13) | collective-permute-done | bytes 49184 | tf_op jit(solution)/shard_map/ppermute | solution.py:377
  57.7 2.6 %collective-permute-start.16 = (bf16[1,32,768]{2,1,0:T(8,128)(2,1)S(1)}, bf16[1,32,768]{2,1,0:T(8,128)(2,1)S(1)}, u32[]{:S(2)}, u32[]{:S(2)}) collective-permute-start(bf16[1,32,768]{2,1,0:T(8,128)(2,1)S(1)} %combine.2.refs_0_), channel_id=1, source_target_pairs={{0,6},{2,4},{4,2},{6,0},{1,7},{3,5},{5,3},{7,1},{8,14},{10,12},{12... | collective-permute-start | bytes 147464 | tf_op jit(solution)/shard_map/ppermute | solution.py:377
  60.4 0.7 collective-permute-start.15
  61.1 1.1 %collective-permute-start.14 = (bf16[1,32,768]{2,1,0:T(8,128)(2,1)S(1)}, bf16[1,32,768]{2,1,0:T(8,128)(2,1)S(1)}, u32[]{:S(2)}, u32[]{:S(2)}) collective-permute-start(bf16[1,32,768]{2,1,0:T(8,128)(2,1)S(1)} %combine.2.refs_0_), channel_id=1, source_target_pairs={{0,2},{2,0},{4,6},{6,4},{1,3},{3,1},{5,7},{7,5},{8,10},{10,8},{12,... | collective-permute-start | bytes 147464 | tf_op jit(solution)/shard_map/ppermute | solution.py:377
  62.2 2.1 %left_side.1 = (bf16[64,16,128]{2,1,0:T(8,128)(2,1)}, f32[8,128]{1,0:T(8,128)S(1)}) custom-call(bf16[64,16,128]{2,1,0:T(8,128)(2,1)S(1)} %copy-done, bf16[128,256]{1,0:T(8,128)(2,1)S(1)} %copy-done.1, bf16[64,16,128]{2,1,0:T(8,128)(2,1)S(1)} %get-tuple-element.71._.refs_0_.refs_4_, bf16[64,16,128]{2,1,0:T(8,128)(2,1)S(1)} %collective-permute-done.7.refs_1_.refs_0_, ...), custom_call_target="tpu_custom_call" | custom-call | flops 1000 | bytes 1000 | tf_op jit(solution)/shard_map/left_side/pallas_call | solution.py:467
  64.3 1.6 %collective-permute-done.15.refs_2_ = bf16[1,32,768]{2,1,0:T(8,128)(2,1)S(1)} collective-permute-done((bf16[1,32,768]{2,1,0:T(8,128)(2,1)S(1)}, bf16[1,32,768]{2,1,0:T(8,128)(2,1)S(1)}, u32[]{:S(2)}, u32[]{:S(2)}) %collective-permute-start.15) | collective-permute-done | bytes 49184 | tf_op jit(solution)/shard_map/ppermute | solution.py:377
  65.9 1.5 %collective-permute-start.19 = (bf16[1,32,768]{2,1,0:T(8,128)(2,1)S(1)}, bf16[1,32,768]{2,1,0:T(8,128)(2,1)S(1)}, u32[]{:S(2)}, u32[]{:S(2)}) collective-permute-start(bf16[1,32,768]{2,1,0:T(8,128)(2,1)S(1)} %combine.3.refs_0_), channel_id=1, source_target_pairs={{0,24},{8,16},{16,8},{24,0},{1,25},{9,17},{17,9},{25,1},{2,26},{10... | collective-permute-start | bytes 147464 | tf_op jit(solution)/shard_map/ppermute | solution.py:377
  67.4 0.4 collective-permute-start.18
  67.8 1.7 %collective-permute-start.17 = (bf16[1,32,768]{2,1,0:T(8,128)(2,1)S(1)}, bf16[1,32,768]{2,1,0:T(8,128)(2,1)S(1)}, u32[]{:S(2)}, u32[]{:S(2)}) collective-permute-start(bf16[1,32,768]{2,1,0:T(8,128)(2,1)S(1)} %combine.3.refs_0_), channel_id=1, source_target_pairs={{0,8},{8,0},{16,24},{24,16},{1,9},{9,1},{17,25},{25,17},{2,10},{10... | collective-permute-start | bytes 147464 | tf_op jit(solution)/shard_map/ppermute | solution.py:377
  69.5 1.4 %right_side.1 = (bf16[32,16,128]{2,1,0:T(8,128)(2,1)}, f32[8,128]{1,0:T(8,128)S(1)}) custom-call(bf16[32,16,128]{2,1,0:T(8,128)(2,1)S(1)} %copy-done.5, bf16[128,256]{1,0:T(8,128)(2,1)S(1)} %copy-done.4, f32[32,16,128]{2,1,0:T(8,128)S(1)} %bitcast.2, bf16[32,16,128]{2,1,0:T(8,128)(2,1)S(1)} %bitcast.3), custom_call_target="tpu_custom_call" | custom-call | flops 1000 | bytes 1000 | tf_op jit(solution)/shard_map/right_side/pallas_call | solution.py:467
  71.0 0.5 collective-permute-done.18.refs_2_
  71.5 0.4 collective-permute-done.17.refs_1_
  71.9 0.8 %deltas.1 = (f32[128,256]{1,0:T(8,128)}, f32[128,256]{1,0:T(8,128)}, f32[128,128]{1,0:T(8,128)}, f32[128,128]{1,0:T(8,128)}) custom-call(bf16[1,32,768]{2,1,0:T(8,128)(2,1)S(1)} %combine.3.refs_0_, bf16[1,32,768]{2,1,0:T(8,128)(2,1)S(1)} %collective-permute-done.17.refs_1_, bf16[1,32,768]{2,1,0:T(8,128)(2,1)S(1)} %collective-permute-done.18.refs_2_, ...), custom_call_target="tpu_custom_call" | custom-call | flops 1000 | bytes 1000 | tf_op jit(solution)/shard_map/deltas/pallas_call | solution.py:467
  (33 shorter events, 0.2 us)
Async XLA Ops:
  0.6 9.2 %copy-start = (bf16[64,16,128]{2,1,0:T(8,128)(2,1)S(1)}, bf16[64,16,128]{2,1,0:T(8,128)(2,1)}, u32[]{:S(2)}) copy-start(bf16[64,16,128]{2,1,0:T(8,128)(2,1)} %raw.4) | copy-start | bytes 786436
  0.6 9.2 %copy-start.1 = (bf16[128,256]{1,0:T(8,128)(2,1)S(1)}, bf16[128,256]{1,0:T(8,128)(2,1)}, u32[]{:S(2)}) copy-start(bf16[128,256]{1,0:T(8,128)(2,1)} %left_w.1) | copy-start | bytes 196612
  0.7 17.0 %collective-permute-start = (bf16[64,16,128]{2,1,0:T(8,128)(2,1)}, bf16[64,16,128]{2,1,0:T(8,128)(2,1)S(1)}, u32[]{:S(2)}, u32[]{:S(2)}) collective-permute-start(bf16[64,16,128]{2,1,0:T(8,128)(2,1)} %raw.4), channel_id=1, source_target_pairs={{0,4},{2,6},{4,0},{6,2},{1,5},{3,7},{5,1},{7,3},{8,12},{10,14},{12... | collective-permute-start | bytes 786440 | tf_op jit(solution)/shard_map/ppermute | solution.py:377
  4.8 8.6 %collective-permute-start.3 = (bf16[32,16,128]{2,1,0:T(8,128)(2,1)}, bf16[32,16,128]{2,1,0:T(8,128)(2,1)S(1)}, u32[]{:S(2)}, u32[]{:S(2)}) collective-permute-start(bf16[32,16,128]{2,1,0:T(8,128)(2,1)} %raw.5), channel_id=1, source_target_pairs={{0,24},{8,16},{16,8},{24,0},{1,25},{9,17},{17,9},{25,1},{2,26},{10... | collective-permute-start | bytes 393224 | tf_op jit(solution)/shard_map/ppermute | solution.py:377
  7.2 6.4 %collective-permute-start.2 = (bf16[32,16,128]{2,1,0:T(8,128)(2,1)}, bf16[32,16,128]{2,1,0:T(8,128)(2,1)S(1)}, u32[]{:S(2)}, u32[]{:S(2)}) collective-permute-start(bf16[32,16,128]{2,1,0:T(8,128)(2,1)} %raw.5), channel_id=1, source_target_pairs={{0,16},{8,24},{16,0},{24,8},{1,17},{9,25},{17,1},{25,9},{2,18},{10... | collective-permute-start | bytes 393224 | tf_op jit(solution)/shard_map/ppermute | solution.py:377
  7.7 6.0 %collective-permute-start.1 = (bf16[32,16,128]{2,1,0:T(8,128)(2,1)}, bf16[32,16,128]{2,1,0:T(8,128)(2,1)S(1)}, u32[]{:S(2)}, u32[]{:S(2)}) collective-permute-start(bf16[32,16,128]{2,1,0:T(8,128)(2,1)} %raw.5), channel_id=1, source_target_pairs={{0,8},{8,0},{16,24},{24,16},{1,9},{9,1},{17,25},{25,17},{2,10},{10... | collective-permute-start | bytes 393224 | tf_op jit(solution)/shard_map/ppermute | solution.py:377
  8.2 12.4 %collective-permute-start.6 = (bf16[64,16,128]{2,1,0:T(8,128)(2,1)}, bf16[64,16,128]{2,1,0:T(8,128)(2,1)S(1)}, u32[]{:S(2)}, u32[]{:S(2)}) collective-permute-start(bf16[64,16,128]{2,1,0:T(8,128)(2,1)} %raw.4), channel_id=1, source_target_pairs={{0,2},{2,0},{4,6},{6,4},{1,3},{3,1},{5,7},{7,5},{8,10},{10,8},{12,... | collective-permute-start | bytes 786440 | tf_op jit(solution)/shard_map/ppermute | solution.py:377
  9.8 1.0 %copy-start.2 = (bf16[64,32,128]{2,1,0:T(8,128)(2,1)S(1)}, bf16[64,32,128]{2,1,0:T(8,128)(2,1)}, u32[]{:S(2)}) copy-start(bf16[64,32,128]{2,1,0:T(8,128)(2,1)} %middle.5) | copy-start | bytes 1572868
  9.8 1.2 %copy-start.3 = (bf16[64,32,128]{2,1,0:T(8,128)(2,1)S(1)}, bf16[64,32,128]{2,1,0:T(8,128)(2,1)}, u32[]{:S(2)}) copy-start(bf16[64,32,128]{2,1,0:T(8,128)(2,1)} %cotangent.3) | copy-start | bytes 1572868
  9.8 1.2 %copy-start.6 = (bf16[128,128]{1,0:T(8,128)(2,1)S(1)}, bf16[128,128]{1,0:T(8,128)(2,1)}, u32[]{:S(2)}) copy-start(bf16[128,128]{1,0:T(8,128)(2,1)} %out_w.1) | copy-start | bytes 98308
  9.9 1.2 %copy-start.7 = (bf16[128,128]{1,0:T(8,128)(2,1)S(1)}, bf16[128,128]{1,0:T(8,128)(2,1)}, u32[]{:S(2)}) copy-start(bf16[128,128]{1,0:T(8,128)(2,1)} %gate_weight.3) | copy-start | bytes 98308
  11.0 2.7 %copy-start.4 = (bf16[128,256]{1,0:T(8,128)(2,1)S(1)}, bf16[128,256]{1,0:T(8,128)(2,1)}, u32[]{:S(2)}) copy-start(bf16[128,256]{1,0:T(8,128)(2,1)} %right_w.1) | copy-start | bytes 196612
  11.0 2.7 %copy-start.5 = (bf16[32,16,128]{2,1,0:T(8,128)(2,1)S(1)}, bf16[32,16,128]{2,1,0:T(8,128)(2,1)}, u32[]{:S(2)}) copy-start(bf16[32,16,128]{2,1,0:T(8,128)(2,1)} %raw.5) | copy-start | bytes 393220
  16.8 7.7 %collective-permute-start.5 = (bf16[64,16,128]{2,1,0:T(8,128)(2,1)S(1)}, bf16[64,16,128]{2,1,0:T(8,128)(2,1)S(1)}, u32[]{:S(2)}, u32[]{:S(2)}) collective-permute-start(bf16[64,16,128]{2,1,0:T(8,128)(2,1)S(1)} %forward.3), channel_id=1, source_target_pairs={{0,0},{2,4},{4,2},{6,6},{1,1},{3,5},{5,3},{7,7},{8,8},{10,12},{12,... | collective-permute-start | bytes 786440 | tf_op jit(solution)/shard_map/ppermute | solution.py:417
  17.7 9.1 %collective-permute-start.4 = (bf16[64,16,128]{2,1,0:T(8,128)(2,1)S(1)}, bf16[64,16,128]{2,1,0:T(8,128)(2,1)S(1)}, u32[]{:S(2)}, u32[]{:S(2)}) collective-permute-start(bf16[64,16,128]{2,1,0:T(8,128)(2,1)S(1)} %forward.2), channel_id=1, source_target_pairs={{0,2},{2,0},{4,6},{6,4},{1,3},{3,1},{5,7},{7,5},{8,10},{10,8},{12,... | collective-permute-start | bytes 786440 | tf_op jit(solution)/shard_map/ppermute | solution.py:377
  32.0 21.9 %collective-permute-start.8 = (bf16[64,16,128]{2,1,0:T(8,128)(2,1)S(1)}, bf16[64,16,128]{2,1,0:T(8,128)(2,1)S(1)}, u32[]{:S(2)}, u32[]{:S(2)}) collective-permute-start(bf16[64,16,128]{2,1,0:T(8,128)(2,1)S(1)} %get-tuple-element.74.refs_6_), channel_id=1, source_target_pairs={{0,4},{2,6},{4,0},{6,2},{1,5},{3,7},{5,1},{7,3},{8,12},{10,14},{12... | collective-permute-start | bytes 786440 | tf_op jit(solution)/shard_map/ppermute | solution.py:377
  34.9 18.9 %collective-permute-start.9 = (bf16[64,16,128]{2,1,0:T(8,128)(2,1)S(1)}, bf16[64,16,128]{2,1,0:T(8,128)(2,1)S(1)}, u32[]{:S(2)}, u32[]{:S(2)}) collective-permute-start(bf16[64,16,128]{2,1,0:T(8,128)(2,1)S(1)} %get-tuple-element.75.refs_7_), channel_id=1, source_target_pairs={{0,6},{2,4},{4,2},{6,0},{1,7},{3,5},{5,3},{7,1},{8,14},{10,12},{12... | collective-permute-start | bytes 786440 | tf_op jit(solution)/shard_map/ppermute | solution.py:377
  38.4 16.8 %collective-permute-start.7 = (bf16[64,16,128]{2,1,0:T(8,128)(2,1)S(1)}, bf16[64,16,128]{2,1,0:T(8,128)(2,1)S(1)}, u32[]{:S(2)}, u32[]{:S(2)}) collective-permute-start(bf16[64,16,128]{2,1,0:T(8,128)(2,1)S(1)} %get-tuple-element.73.refs_5_), channel_id=1, source_target_pairs={{0,2},{2,0},{4,6},{6,4},{1,3},{3,1},{5,7},{7,5},{8,10},{10,8},{12,... | collective-permute-start | bytes 786440 | tf_op jit(solution)/shard_map/ppermute | solution.py:377
  43.5 11.8 %collective-permute-start.10 = (bf16[2,32,16,128]{3,2,1,0:T(8,128)(2,1)S(1)}, bf16[2,32,16,128]{3,2,1,0:T(8,128)(2,1)S(1)}, u32[]{:S(2)}, u32[]{:S(2)}) collective-permute-start(bf16[2,32,16,128]{3,2,1,0:T(8,128)(2,1)S(1)} %get-tuple-element.81.refs_9_), channel_id=1, source_target_pairs={{0,8},{8,0},{16,24},{24,16},{1,9},{9,1},{17,25},{25,17},{2,10},{10... | collective-permute-start | bytes 786440 | tf_op jit(solution)/shard_map/ppermute | solution.py:377
  48.3 4.7 %collective-permute-start.12 = (bf16[2,32,768]{2,1,0:T(8,128)(2,1)S(1)}, bf16[2,32,768]{2,1,0:T(8,128)(2,1)S(1)}, u32[]{:S(2)}, u32[]{:S(2)}) collective-permute-start(bf16[2,32,768]{2,1,0:T(8,128)(2,1)S(1)} %get-tuple-element.92._), channel_id=1, source_target_pairs={{0,8},{8,0},{16,24},{24,16},{1,9},{9,1},{17,25},{25,17},{2,10},{10... | collective-permute-start | bytes 294920 | tf_op jit(solution)/shard_map/ppermute | solution.py:377
  53.0 4.7 %collective-permute-start.13 = (bf16[1,32,768]{2,1,0:T(8,128)(2,1)S(1)}, bf16[1,32,768]{2,1,0:T(8,128)(2,1)S(1)}, u32[]{:S(2)}, u32[]{:S(2)}) collective-permute-start(bf16[1,32,768]{2,1,0:T(8,128)(2,1)S(1)} %get-tuple-element.97), channel_id=1, source_target_pairs={{0,16},{8,24},{16,0},{24,8},{1,17},{9,25},{17,1},{25,9},{2,18},{10... | collective-permute-start | bytes 147464 | tf_op jit(solution)/shard_map/ppermute | solution.py:377
  55.3 14.2 %collective-permute-start.11 = (bf16[1,32,16,128]{3,2,1,0:T(8,128)(2,1)S(1)}, bf16[1,32,16,128]{3,2,1,0:T(8,128)(2,1)S(1)}, u32[]{:S(2)}, u32[]{:S(2)}) collective-permute-start(bf16[1,32,16,128]{3,2,1,0:T(8,128)(2,1)S(1)} %get-tuple-element.83.refs_0_), channel_id=1, source_target_pairs={{0,16},{8,24},{16,0},{24,8},{1,17},{9,25},{17,1},{25,9},{2,18},{10... | collective-permute-start | bytes 393224 | tf_op jit(solution)/shard_map/ppermute | solution.py:377
  57.7 6.6 %collective-permute-start.16 = (bf16[1,32,768]{2,1,0:T(8,128)(2,1)S(1)}, bf16[1,32,768]{2,1,0:T(8,128)(2,1)S(1)}, u32[]{:S(2)}, u32[]{:S(2)}) collective-permute-start(bf16[1,32,768]{2,1,0:T(8,128)(2,1)S(1)} %combine.2.refs_0_), channel_id=1, source_target_pairs={{0,6},{2,4},{4,2},{6,0},{1,7},{3,5},{5,3},{7,1},{8,14},{10,12},{12... | collective-permute-start | bytes 147464 | tf_op jit(solution)/shard_map/ppermute | solution.py:377
  60.4 5.5 %collective-permute-start.15 = (bf16[1,32,768]{2,1,0:T(8,128)(2,1)S(1)}, bf16[1,32,768]{2,1,0:T(8,128)(2,1)S(1)}, u32[]{:S(2)}, u32[]{:S(2)}) collective-permute-start(bf16[1,32,768]{2,1,0:T(8,128)(2,1)S(1)} %combine.2.refs_0_), channel_id=1, source_target_pairs={{0,4},{2,6},{4,0},{6,2},{1,5},{3,7},{5,1},{7,3},{8,12},{10,14},{12... | collective-permute-start | bytes 147464 | tf_op jit(solution)/shard_map/ppermute | solution.py:377
  61.1 4.8 %collective-permute-start.14 = (bf16[1,32,768]{2,1,0:T(8,128)(2,1)S(1)}, bf16[1,32,768]{2,1,0:T(8,128)(2,1)S(1)}, u32[]{:S(2)}, u32[]{:S(2)}) collective-permute-start(bf16[1,32,768]{2,1,0:T(8,128)(2,1)S(1)} %combine.2.refs_0_), channel_id=1, source_target_pairs={{0,2},{2,0},{4,6},{6,4},{1,3},{3,1},{5,7},{7,5},{8,10},{10,8},{12,... | collective-permute-start | bytes 147464 | tf_op jit(solution)/shard_map/ppermute | solution.py:377
  65.9 5.1 %collective-permute-start.19 = (bf16[1,32,768]{2,1,0:T(8,128)(2,1)S(1)}, bf16[1,32,768]{2,1,0:T(8,128)(2,1)S(1)}, u32[]{:S(2)}, u32[]{:S(2)}) collective-permute-start(bf16[1,32,768]{2,1,0:T(8,128)(2,1)S(1)} %combine.3.refs_0_), channel_id=1, source_target_pairs={{0,24},{8,16},{16,8},{24,0},{1,25},{9,17},{17,9},{25,1},{2,26},{10... | collective-permute-start | bytes 147464 | tf_op jit(solution)/shard_map/ppermute | solution.py:377
  67.4 4.1 %collective-permute-start.18 = (bf16[1,32,768]{2,1,0:T(8,128)(2,1)S(1)}, bf16[1,32,768]{2,1,0:T(8,128)(2,1)S(1)}, u32[]{:S(2)}, u32[]{:S(2)}) collective-permute-start(bf16[1,32,768]{2,1,0:T(8,128)(2,1)S(1)} %combine.3.refs_0_), channel_id=1, source_target_pairs={{0,16},{8,24},{16,0},{24,8},{1,17},{9,25},{17,1},{25,9},{2,18},{10... | collective-permute-start | bytes 147464 | tf_op jit(solution)/shard_map/ppermute | solution.py:377
  67.8 4.1 %collective-permute-start.17 = (bf16[1,32,768]{2,1,0:T(8,128)(2,1)S(1)}, bf16[1,32,768]{2,1,0:T(8,128)(2,1)S(1)}, u32[]{:S(2)}, u32[]{:S(2)}) collective-permute-start(bf16[1,32,768]{2,1,0:T(8,128)(2,1)S(1)} %combine.3.refs_0_), channel_id=1, source_target_pairs={{0,8},{8,0},{16,24},{24,16},{1,9},{9,1},{17,25},{25,17},{2,10},{10... | collective-permute-start | bytes 147464 | tf_op jit(solution)/shard_map/ppermute | solution.py:377

commit v16 on v15

--- a/solution.py
+++ b/solution.py
@@ -139,7 +139,7 @@
         if len(raws) > 1:
             place = jnp.full(raw.shape, lax.axis_index("blk"), jnp.int32)
             inner = jnp.logical_or(place == 1, place == 2)
-            raw = jnp.where(inner, raws[1][rows].astype(f32), raw.astype(f32)).astype(bf16)
+            raw = jnp.where(inner, raw.astype(f32), raws[1][rows].astype(f32)).astype(bf16)
         normed, _ = normalize_raw(raw.reshape(step * k_left, width))
         inputs = normed.astype(bf16)
         in_out[rows] = inputs.reshape(step, k_left, width)
@@ -161,7 +161,7 @@
     project_left([raw], weight, act_out, in_out)
 
 
-def own_sum_kernel(act, flip, total):
+def own_sum_kernel(act, flip, _, total):
     step = 8
 
     def body(at, _):
@@ -407,10 +407,6 @@
 def forwarded(block, after):
     (copy,) = call(forward_kernel, "forward", [shape(block.shape, block.dtype)], after=len(after))(block, *after)
     return copy
-
-
-def outer_block(across, after):
-    return exchange(forwarded(across, after), "blk", 4, 1)
 
 
 def inner_block(block, after):
@@ -513,11 +509,13 @@
         after=2,
     )(*right_raw, right_weight, own_act, middle_in)
     left_raw = [[pair_left]] + [[exchange(pair_left, "blk", n_blk, s)] for s in range(1, 3 if n_blk == 4 else n_blk)]
+    passed = right_in
     if n_blk == 4:
-        left_raw.append([outer_block(left_raw[2][0], (right_in, middle_in))])
-    total = call(own_sum_kernel, "own_sum", [shape(middle_shape, f32)])(own_act, right_flip[0])
+        passed = forwarded(left_raw[2][0], (right_in, middle_in))
+        left_raw.append([exchange(passed, "blk", 4, 1)])
+    total = call(own_sum_kernel, "own_sum", [shape(middle_shape, f32)], after=1)(own_act, right_flip[0], passed)
     if n_blk == 4:
-        left_raw[3].append(inner_block(pair_left, tuple(total)))
+        left_raw[3].insert(0, inner_block(pair_left, tuple(total)))
     left_act, left_in = [own_act], [own_in]
     for s in range(1, n_blk - 1):
         act, inputs, *total = call(

time: 72.8 us -> 75.4 us (1.036)
  starting transfers between devices: 29.8 us -> 32 us
    ppermute x19, starting transfers between devices: 28.9 us -> 31.1 us  [exchange(): return lax.ppermute(x, axis, [(a, a ^ bit) for a in range(n)])]
  transfers between devices with their start and end apart: 20 -> 20, of which waited for: 9 -> 11; matrix products, arithmetic and copies ran while one was open for 0% -> 0% of each run, Pallas kernels for 37% -> 36%
where the time goes in v16:
time: 75.4 us; the launch traced here: 75.2 us
  Pallas kernels  32.6 us (43%)
  starting transfers between devices  32 us (42%)
  waiting for transfers between devices  9.43 us (13%)
  between operations  0.82 us (1%)
    pallas_call x25, Pallas kernels, run(): pl.pallas_call(kernel, in_specs=[pl.BlockSpec(memory_space=space) for spa...  32.6 us
    ppermute x19, starting transfers between devices, exchange(): return lax.ppermute(x, axis, [(a, a ^ bit) for a in range(n)])  31.1 us
    ppermute x19, waiting for transfers between devices, exchange(): return lax.ppermute(x, axis, [(a, a ^ bit) for a in range(n)])  9.42 us
  transfers between devices with their start and end apart: 20, of which 11 were waited for; matrix products, arithmetic and copies ran while one was open for 0% of the time, Pallas kernels for 36%

profile of v16, /device:TPU:0, one launch (start us, length us, event | category | flops | bytes accessed | tf_op | source)
XLA Modules:
  0.0 75.2 jit_solution(17865099246172078455)
XLA Ops:
  0.7 4.1 %collective-permute-start.3 = (bf16[64,16,128]{2,1,0:T(8,128)(2,1)}, bf16[64,16,128]{2,1,0:T(8,128)(2,1)S(1)}, u32[]{:S(2)}, u32[]{:S(2)}) collective-permute-start(bf16[64,16,128]{2,1,0:T(8,128)(2,1)} %raw.4), channel_id=1, source_target_pairs={{0,4},{2,6},{4,0},{6,2},{1,5},{3,7},{5,1},{7,3},{8,12},{10,14},{12... | collective-permute-start | bytes 786440 | tf_op jit(solution)/shard_map/ppermute | solution.py:377
  4.8 2.4 %collective-permute-start.2 = (bf16[32,16,128]{2,1,0:T(8,128)(2,1)}, bf16[32,16,128]{2,1,0:T(8,128)(2,1)S(1)}, u32[]{:S(2)}, u32[]{:S(2)}) collective-permute-start(bf16[32,16,128]{2,1,0:T(8,128)(2,1)} %raw.5), channel_id=1, source_target_pairs={{0,24},{8,16},{16,8},{24,0},{1,25},{9,17},{17,9},{25,1},{2,26},{10... | collective-permute-start | bytes 393224 | tf_op jit(solution)/shard_map/ppermute | solution.py:377
  7.2 0.5 collective-permute-start.1
  7.7 0.5 collective-permute-start
  8.2 1.6 %collective-permute-start.6 = (bf16[64,16,128]{2,1,0:T(8,128)(2,1)}, bf16[64,16,128]{2,1,0:T(8,128)(2,1)S(1)}, u32[]{:S(2)}, u32[]{:S(2)}) collective-permute-start(bf16[64,16,128]{2,1,0:T(8,128)(2,1)} %raw.4), channel_id=1, source_target_pairs={{0,2},{2,0},{4,6},{6,4},{1,3},{3,1},{5,7},{7,5},{8,10},{10,8},{12,... | collective-permute-start | bytes 786440 | tf_op jit(solution)/shard_map/ppermute | solution.py:377
  9.9 0.8 %own.1 = (f32[64,16,128]{2,1,0:T(8,128)S(1)}, bf16[64,16,128]{2,1,0:T(8,128)(2,1)S(1)}) custom-call(bf16[64,16,128]{2,1,0:T(8,128)(2,1)S(1)} %copy-done, bf16[128,256]{1,0:T(8,128)(2,1)S(1)} %copy-done.1, f32[8,128]{1,0:T(8,128)S(1)} %order.3._), custom_call_target="tpu_custom_call" | custom-call | flops 1000 | bytes 1000 | tf_op jit(solution)/shard_map/own/pallas_call | solution.py:463
  10.7 0.2 copy-done.2
  10.9 0.2 copy-done.3
  11.0 2.3 %middle.3 = (f32[64,32,128]{2,1,0:T(8,128)S(1)}, bf16[64,32,128]{2,1,0:T(8,128)(2,1)S(1)}, bf16[64,32,128]{2,1,0:T(8,128)(2,1)S(1)}, f32[64,32,128]{2,1,0:T(8,128)S(1)}) custom-call(bf16[64,32,128]{2,1,0:T(8,128)(2,1)S(1)} %copy-done.2, bf16[64,32,128]{2,1,0:T(8,128)(2,1)S(1)} %copy-done.3, bf16[128,128]{1,0:T(8,128)(2,1)S(1)} %copy-done.7, ...), custom_call_target="tpu_custom_call" | custom-call | flops 1000 | bytes 1000 | tf_op jit(solution)/shard_map/middle/pallas_call | solution.py:463
  13.4 0.2 collective-permute-done.1.refs_2_
  13.7 1.9 %right.1 = (f32[2048,128]{1,0:T(8,128)S(1)}, bf16[4,32,16,128]{3,2,1,0:T(8,128)(2,1)S(1)}, f32[16,32,128]{2,1,0:T(8,128)S(1)}, f32[16,32,128]{2,1,0:T(8,128)S(1)...) custom-call(bf16[32,16,128]{2,1,0:T(8,128)(2,1)S(1)} %copy-done.5, ...), custom_call_target="tpu_custom_call" | custom-call | flops 1000 | bytes 1000 | tf_op jit(solution)/shard_map/right/pallas_call | solution.py:463
  15.6 1.4 %collective-permute-done.3.source.raw = bf16[64,16,128]{2,1,0:T(8,128)(2,1)S(1)} collective-permute-done((bf16[64,16,128]{2,1,0:T(8,128)(2,1)}, bf16[64,16,128]{2,1,0:T(8,128)(2,1)S(1)}, u32[]{:S(2)}, u32[]{:S(2)}) %collective-permute-start.3) | collective-permute-done | bytes 262176 | tf_op jit(solution)/shard_map/ppermute | solution.py:377
  17.0 1.1 %own_sum.1.refs_0_.total_in = f32[64,32,128]{2,1,0:T(8,128)S(1)} custom-call(f32[64,16,128]{2,1,0:T(8,128)S(1)} %get-tuple-element.56.refs_5_.act.refs_0_, f32[16,32,128]{2,1,0:T(8,128)S(1)} %get-tuple-element.58.flip, bf16[64,16,128]{2,1,0:T(8,128)(2,1)S(1)} %forward.2._), custom_call_target="tpu_custom_call" | custom-call | flops 1000 | bytes 1000 | tf_op jit(solution)/shard_map/own_sum/pallas_call | solution.py:463
  18.2 0.8 %collective-permute-start.5 = (bf16[64,16,128]{2,1,0:T(8,128)(2,1)S(1)}, bf16[64,16,128]{2,1,0:T(8,128)(2,1)S(1)}, u32[]{:S(2)}, u32[]{:S(2)}) collective-permute-start(bf16[64,16,128]{2,1,0:T(8,128)(2,1)S(1)} %forward.2._), channel_id=1, source_target_pairs={{0,2},{2,0},{4,6},{6,4},{1,3},{3,1},{5,7},{7,5},{8,10},{10,8},{12,... | collective-permute-start | bytes 786440 | tf_op jit(solution)/shard_map/ppermute | solution.py:377
  19.0 0.9 %collective-permute-start.4 = (bf16[64,16,128]{2,1,0:T(8,128)(2,1)S(1)}, bf16[64,16,128]{2,1,0:T(8,128)(2,1)S(1)}, u32[]{:S(2)}, u32[]{:S(2)}) collective-permute-start(bf16[64,16,128]{2,1,0:T(8,128)(2,1)S(1)} %forward.3), channel_id=1, source_target_pairs={{0,0},{2,4},{4,2},{6,6},{1,1},{3,5},{5,3},{7,7},{8,8},{10,12},{12,... | collective-permute-start | bytes 786440 | tf_op jit(solution)/shard_map/ppermute | solution.py:413
  19.9 2.0 %left.2 = (f32[64,16,128]{2,1,0:T(8,128)S(1)}, bf16[64,16,128]{2,1,0:T(8,128)(2,1)S(1)}, f32[64,32,128]{2,1,0:T(8,128)S(1)}) custom-call(bf16[64,16,128]{2,1,0:T(8,128)(2,1)S(1)} %collective-permute-done.6.raw, bf16[128,256]{1,0:T(8,128)(2,1)S(1)} %copy-done.1, f32[16,32,128]{2,1,0:T(8,128)S(1)} %get-tuple-element.63.flip, ...), custom_call_target="tpu_custom_call" | custom-call | flops 1000 | bytes 1000 | tf_op jit(solution)/shard_map/left/pallas_call | solution.py:463
  21.9 2.0 %left.3 = (f32[64,16,128]{2,1,0:T(8,128)S(1)}, bf16[64,16,128]{2,1,0:T(8,128)(2,1)S(1)}, f32[64,32,128]{2,1,0:T(8,128)S(1)}) custom-call(bf16[64,16,128]{2,1,0:T(8,128)(2,1)S(1)} %collective-permute-done.3.source.raw, bf16[128,256]{1,0:T(8,128)(2,1)S(1)} %copy-done.1, f32[16,32,128]{2,1,0:T(8,128)S(1)} %get-tuple-element.62.flip, ...), custom_call_target="tpu_custom_call" | custom-call | flops 1000 | bytes 1000 | tf_op jit(solution)/shard_map/left/pallas_call | solution.py:463
  23.8 1.8 %collective-permute-done.5.refs_1_ = bf16[64,16,128]{2,1,0:T(8,128)(2,1)S(1)} collective-permute-done((bf16[64,16,128]{2,1,0:T(8,128)(2,1)S(1)}, bf16[64,16,128]{2,1,0:T(8,128)(2,1)S(1)}, u32[]{:S(2)}, u32[]{:S(2)}) %collective-permute-start.5) | collective-permute-done | bytes 262176 | tf_op jit(solution)/shard_map/ppermute | solution.py:377
  25.7 2.9 %triangle.1 = (f32[64,16,128]{2,1,0:T(8,128)S(1)}, bf16[64,16,128]{2,1,0:T(8,128)(2,1)S(1)}, bf16[64,32,128]{2,1,0:T(8,128)(2,1)S(1)}, f32[64,32,128]{2,1,0:T(8,128)S(1)}) custom-call(bf16[64,16,128]{2,1,0:T(8,128)(2,1)S(1)} %collective-permute-done.4.refs_0_, bf16[64,16,128]{2,1,0:T(8,128)(2,1)S(1)} %collective-permute-done.5.refs_1_, ...), custom_call_target="tpu_custom_call" | custom-call | flops 1000 | bytes 1000 | tf_op jit(solution)/shard_map/triangle/pallas_call | solution.py:463
  28.5 2.2 %left_back.3 = (bf16[64,16,128]{2,1,0:T(8,128)(2,1)S(1)}, bf16[64,16,128]{2,1,0:T(8,128)(2,1)S(1)}) custom-call(f32[64,32,128]{2,1,0:T(8,128)S(1)} %get-tuple-element.69.tri_back, f32[2048,128]{1,0:T(8,128)S(1)} %get-tuple-element.70.right_act), custom_call_target="tpu_custom_call" | custom-call | flops 1000 | bytes 1000 | tf_op jit(solution)/shard_map/left_back/pallas_call | solution.py:463
  30.8 6.5 %collective-permute-start.8 = (bf16[64,16,128]{2,1,0:T(8,128)(2,1)S(1)}, bf16[64,16,128]{2,1,0:T(8,128)(2,1)S(1)}, u32[]{:S(2)}, u32[]{:S(2)}) collective-permute-start(bf16[64,16,128]{2,1,0:T(8,128)(2,1)S(1)} %get-tuple-element.74.refs_6_), channel_id=1, source_target_pairs={{0,4},{2,6},{4,0},{6,2},{1,5},{3,7},{5,1},{7,3},{8,12},{10,14},{12... | collective-permute-start | bytes 786440 | tf_op jit(solution)/shard_map/ppermute | solution.py:377
  37.3 1.2 %collective-permute-start.9 = (bf16[64,16,128]{2,1,0:T(8,128)(2,1)S(1)}, bf16[64,16,128]{2,1,0:T(8,128)(2,1)S(1)}, u32[]{:S(2)}, u32[]{:S(2)}) collective-permute-start(bf16[64,16,128]{2,1,0:T(8,128)(2,1)S(1)} %get-tuple-element.75.refs_7_), channel_id=1, source_target_pairs={{0,6},{2,4},{4,2},{6,0},{1,7},{3,5},{5,3},{7,1},{8,14},{10,12},{12... | collective-permute-start | bytes 786440 | tf_op jit(solution)/shard_map/ppermute | solution.py:377
  38.5 2.2 %left_back.2 = (bf16[64,16,128]{2,1,0:T(8,128)(2,1)S(1)}, bf16[64,16,128]{2,1,0:T(8,128)(2,1)S(1)}) custom-call(f32[64,32,128]{2,1,0:T(8,128)S(1)} %get-tuple-element.69.tri_back, f32[2048,128]{1,0:T(8,128)S(1)} %get-tuple-element.70.right_act), custom_call_target="tpu_custom_call" | custom-call | flops 1000 | bytes 1000 | tf_op jit(solution)/shard_map/left_back/pallas_call | solution.py:463
  40.8 0.1 collective-permute-start.7
  40.8 5.0 %right_back.1 = (bf16[2,32,16,128]{3,2,1,0:T(8,128)(2,1)S(1)}, bf16[2,32,16,128]{3,2,1,0:T(8,128)(2,1)S(1)}) custom-call(f32[64,32,128]{2,1,0:T(8,128)S(1)} %get-tuple-element.69.tri_back, f32[64,16,128]{2,1,0:T(8,128)S(1)} %get-tuple-element.56.refs_5_.act.refs_0_, f32[64,16,128]{2,1,0:T(8,128)S(1)} %get-tuple-element.77.refs_1_, ...), custom_call_target="tpu_custom_call" | custom-call | flops 1000 | bytes 1000 | tf_op jit(solution)/shard_map/right_back/pallas_call | solution.py:463
  45.8 1.6 %collective-permute-start.10 = (bf16[2,32,16,128]{3,2,1,0:T(8,128)(2,1)S(1)}, bf16[2,32,16,128]{3,2,1,0:T(8,128)(2,1)S(1)}, u32[]{:S(2)}, u32[]{:S(2)}) collective-permute-start(bf16[2,32,16,128]{3,2,1,0:T(8,128)(2,1)S(1)} %get-tuple-element.81.refs_9_), channel_id=1, source_target_pairs={{0,8},{8,0},{16,24},{24,16},{1,9},{9,1},{17,25},{25,17},{2,10},{10... | collective-permute-start | bytes 786440 | tf_op jit(solution)/shard_map/ppermute | solution.py:377
  47.4 1.3 %heads.1 = (bf16[64,32,128]{2,1,0:T(8,128)(2,1)}, bf16[64,32,128]{2,1,0:T(8,128)(2,1)S(1)}, f32[128,128]{1,0:T(8,128)S(1)}, f32[128,128]{1,0:T(8,128)S(1)}) custom-call(bf16[64,32,128]{2,1,0:T(8,128)(2,1)S(1)} %get-tuple-element.66.tri_in, bf16[128,128]{1,0:T(8,128)(2,1)S(1)} %copy-done.6, f32[64,32,128]{2,1,0:T(8,128)S(1)} %get-tuple-element.67.gate, ...), custom_call_target="tpu_custom_call" | custom-call | flops 1000 | bytes 1000 | tf_op jit(solution)/shard_map/heads/pallas_call | solution.py:463
  48.7 2.0 %weights.1 = (f32[2,32,768]{2,1,0:T(8,128)S(1)}, bf16[2,32,768]{2,1,0:T(8,128)(2,1)S(1)}) custom-call(bf16[4,32,16,128]{3,2,1,0:T(8,128)(2,1)S(1)} %get-tuple-element.59.refs_0_.right_in, bf16[128,256]{1,0:T(8,128)(2,1)S(1)} %copy-done.1, bf16[128,256]{1,0:T(8,128)(2,1)S(1)} %copy-done.4, f32[128,128]{1,0:T(8,128)S(1)} %get-tuple-element.86.gate_part, ...), custom_call_target="tpu_custom_call" | custom-call | flops 1000 | bytes 1000 | tf_op jit(solution)/shard_map/weights/pallas_call | solution.py:463
  50.7 0.6 collective-permute-start.12
  51.3 2.3 %grad_middle.1 = (bf16[64,32,128]{2,1,0:T(8,128)(2,1)}, f32[8,128]{1,0:T(8,128)S(1)}) custom-call(bf16[64,32,128]{2,1,0:T(8,128)(2,1)S(1)} %copy-done.2, bf16[64,32,128]{2,1,0:T(8,128)(2,1)S(1)} %get-tuple-element.85.pre_back, bf16[128,128]{1,0:T(8,128)(2,1)S(1)} %copy-done.7, bf16[2,32,768]{2,1,0:T(8,128)(2,1)S(1)} %get-tuple-element.92._), custom_call_target="tpu_custom_call" | custom-call | flops 1000 | bytes 1000 | tf_op jit(solution)/shard_map/grad_middle/pallas_call | solution.py:463
  53.6 1.8 %collective-permute-done.12.came = bf16[2,32,768]{2,1,0:T(8,128)(2,1)S(1)} collective-permute-done((bf16[2,32,768]{2,1,0:T(8,128)(2,1)S(1)}, bf16[2,32,768]{2,1,0:T(8,128)(2,1)S(1)}, u32[]{:S(2)}, u32[]{:S(2)}) %collective-permute-start.12) | collective-permute-done | bytes 98336 | tf_op jit(solution)/shard_map/ppermute | solution.py:377
  55.4 1.6 %collective-permute-start.13 = (bf16[1,32,768]{2,1,0:T(8,128)(2,1)S(1)}, bf16[1,32,768]{2,1,0:T(8,128)(2,1)S(1)}, u32[]{:S(2)}, u32[]{:S(2)}) collective-permute-start(bf16[1,32,768]{2,1,0:T(8,128)(2,1)S(1)} %get-tuple-element.97), channel_id=1, source_target_pairs={{0,16},{8,24},{16,0},{24,8},{1,17},{9,25},{17,1},{25,9},{2,18},{10... | collective-permute-start | bytes 147464 | tf_op jit(solution)/shard_map/ppermute | solution.py:377
  57.0 0.5 collective-permute-done.7.refs_1_.refs_0_
  57.5 1.6 %collective-permute-start.11 = (bf16[1,32,16,128]{3,2,1,0:T(8,128)(2,1)S(1)}, bf16[1,32,16,128]{3,2,1,0:T(8,128)(2,1)S(1)}, u32[]{:S(2)}, u32[]{:S(2)}) collective-permute-start(bf16[1,32,16,128]{3,2,1,0:T(8,128)(2,1)S(1)} %get-tuple-element.83.refs_0_), channel_id=1, source_target_pairs={{0,16},{8,24},{16,0},{24,8},{1,17},{9,25},{17,1},{25,9},{2,18},{10... | collective-permute-start | bytes 393224 | tf_op jit(solution)/shard_map/ppermute | solution.py:377
  59.1 1.0 %collective-permute-done.13.refs_1_ = bf16[1,32,768]{2,1,0:T(8,128)(2,1)S(1)} collective-permute-done((bf16[1,32,768]{2,1,0:T(8,128)(2,1)S(1)}, bf16[1,32,768]{2,1,0:T(8,128)(2,1)S(1)}, u32[]{:S(2)}, u32[]{:S(2)}) %collective-permute-start.13) | collective-permute-done | bytes 49184 | tf_op jit(solution)/shard_map/ppermute | solution.py:377
  60.1 2.2 %collective-permute-start.16 = (bf16[1,32,768]{2,1,0:T(8,128)(2,1)S(1)}, bf16[1,32,768]{2,1,0:T(8,128)(2,1)S(1)}, u32[]{:S(2)}, u32[]{:S(2)}) collective-permute-start(bf16[1,32,768]{2,1,0:T(8,128)(2,1)S(1)} %combine.2.refs_0_), channel_id=1, source_target_pairs={{0,6},{2,4},{4,2},{6,0},{1,7},{3,5},{5,3},{7,1},{8,14},{10,12},{12... | collective-permute-start | bytes 147464 | tf_op jit(solution)/shard_map/ppermute | solution.py:377
  62.3 1.1 %collective-permute-start.15 = (bf16[1,32,768]{2,1,0:T(8,128)(2,1)S(1)}, bf16[1,32,768]{2,1,0:T(8,128)(2,1)S(1)}, u32[]{:S(2)}, u32[]{:S(2)}) collective-permute-start(bf16[1,32,768]{2,1,0:T(8,128)(2,1)S(1)} %combine.2.refs_0_), channel_id=1, source_target_pairs={{0,4},{2,6},{4,0},{6,2},{1,5},{3,7},{5,1},{7,3},{8,12},{10,14},{12... | collective-permute-start | bytes 147464 | tf_op jit(solution)/shard_map/ppermute | solution.py:377
  63.4 1.2 %collective-permute-start.14 = (bf16[1,32,768]{2,1,0:T(8,128)(2,1)S(1)}, bf16[1,32,768]{2,1,0:T(8,128)(2,1)S(1)}, u32[]{:S(2)}, u32[]{:S(2)}) collective-permute-start(bf16[1,32,768]{2,1,0:T(8,128)(2,1)S(1)} %combine.2.refs_0_), channel_id=1, source_target_pairs={{0,2},{2,0},{4,6},{6,4},{1,3},{3,1},{5,7},{7,5},{8,10},{10,8},{12,... | collective-permute-start | bytes 147464 | tf_op jit(solution)/shard_map/ppermute | solution.py:377
  64.6 2.1 %left_side.1 = (bf16[64,16,128]{2,1,0:T(8,128)(2,1)}, f32[8,128]{1,0:T(8,128)S(1)}) custom-call(bf16[64,16,128]{2,1,0:T(8,128)(2,1)S(1)} %copy-done, bf16[128,256]{1,0:T(8,128)(2,1)S(1)} %copy-done.1, bf16[64,16,128]{2,1,0:T(8,128)(2,1)S(1)} %get-tuple-element.71._.refs_0_.refs_4_, bf16[64,16,128]{2,1,0:T(8,128)(2,1)S(1)} %collective-permute-done.7.refs_1_.refs_0_, ...), custom_call_target="tpu_custom_call" | custom-call | flops 1000 | bytes 1000 | tf_op jit(solution)/shard_map/left_side/pallas_call | solution.py:463
  66.7 0.6 collective-permute-done.15.refs_2_
  67.3 0.5 collective-permute-done.14.refs_1_
  67.8 1.8 %collective-permute-start.19 = (bf16[1,32,768]{2,1,0:T(8,128)(2,1)S(1)}, bf16[1,32,768]{2,1,0:T(8,128)(2,1)S(1)}, u32[]{:S(2)}, u32[]{:S(2)}) collective-permute-start(bf16[1,32,768]{2,1,0:T(8,128)(2,1)S(1)} %combine.3.refs_0_), channel_id=1, source_target_pairs={{0,24},{8,16},{16,8},{24,0},{1,25},{9,17},{17,9},{25,1},{2,26},{10... | collective-permute-start | bytes 147464 | tf_op jit(solution)/shard_map/ppermute | solution.py:377
  69.6 0.7 collective-permute-start.18
  70.4 1.0 %collective-permute-start.17 = (bf16[1,32,768]{2,1,0:T(8,128)(2,1)S(1)}, bf16[1,32,768]{2,1,0:T(8,128)(2,1)S(1)}, u32[]{:S(2)}, u32[]{:S(2)}) collective-permute-start(bf16[1,32,768]{2,1,0:T(8,128)(2,1)S(1)} %combine.3.refs_0_), channel_id=1, source_target_pairs={{0,8},{8,0},{16,24},{24,16},{1,9},{9,1},{17,25},{25,17},{2,10},{10... | collective-permute-start | bytes 147464 | tf_op jit(solution)/shard_map/ppermute | solution.py:377
  71.4 1.5 %right_side.1 = (bf16[32,16,128]{2,1,0:T(8,128)(2,1)}, f32[8,128]{1,0:T(8,128)S(1)}) custom-call(bf16[32,16,128]{2,1,0:T(8,128)(2,1)S(1)} %copy-done.5, bf16[128,256]{1,0:T(8,128)(2,1)S(1)} %copy-done.4, f32[32,16,128]{2,1,0:T(8,128)S(1)} %bitcast.2, bf16[32,16,128]{2,1,0:T(8,128)(2,1)S(1)} %bitcast.3), custom_call_target="tpu_custom_call" | custom-call | flops 1000 | bytes 1000 | tf_op jit(solution)/shard_map/right_side/pallas_call | solution.py:463
  72.9 0.8 %collective-permute-done.18.refs_2_ = bf16[1,32,768]{2,1,0:T(8,128)(2,1)S(1)} collective-permute-done((bf16[1,32,768]{2,1,0:T(8,128)(2,1)S(1)}, bf16[1,32,768]{2,1,0:T(8,128)(2,1)S(1)}, u32[]{:S(2)}, u32[]{:S(2)}) %collective-permute-start.18) | collective-permute-done | bytes 49184 | tf_op jit(solution)/shard_map/ppermute | solution.py:377
  73.7 0.7 collective-permute-done.17.refs_1_
  74.5 0.8 %deltas.1 = (f32[128,256]{1,0:T(8,128)}, f32[128,256]{1,0:T(8,128)}, f32[128,128]{1,0:T(8,128)}, f32[128,128]{1,0:T(8,128)}) custom-call(bf16[1,32,768]{2,1,0:T(8,128)(2,1)S(1)} %combine.3.refs_0_, bf16[1,32,768]{2,1,0:T(8,128)(2,1)S(1)} %collective-permute-done.17.refs_1_, bf16[1,32,768]{2,1,0:T(8,128)(2,1)S(1)} %collective-permute-done.18.refs_2_, ...), custom_call_target="tpu_custom_call" | custom-call | flops 1000 | bytes 1000 | tf_op jit(solution)/shard_map/deltas/pallas_call | solution.py:463
  (33 shorter events, 0.3 us)
Async XLA Ops:
  0.6 9.2 %copy-start = (bf16[64,16,128]{2,1,0:T(8,128)(2,1)S(1)}, bf16[64,16,128]{2,1,0:T(8,128)(2,1)}, u32[]{:S(2)}) copy-start(bf16[64,16,128]{2,1,0:T(8,128)(2,1)} %raw.4) | copy-start | bytes 786436
  0.6 9.2 %copy-start.1 = (bf16[128,256]{1,0:T(8,128)(2,1)S(1)}, bf16[128,256]{1,0:T(8,128)(2,1)}, u32[]{:S(2)}) copy-start(bf16[128,256]{1,0:T(8,128)(2,1)} %left_w.1) | copy-start | bytes 196612
  0.7 16.3 %collective-permute-start.3 = (bf16[64,16,128]{2,1,0:T(8,128)(2,1)}, bf16[64,16,128]{2,1,0:T(8,128)(2,1)S(1)}, u32[]{:S(2)}, u32[]{:S(2)}) collective-permute-start(bf16[64,16,128]{2,1,0:T(8,128)(2,1)} %raw.4), channel_id=1, source_target_pairs={{0,4},{2,6},{4,0},{6,2},{1,5},{3,7},{5,1},{7,3},{8,12},{10,14},{12... | collective-permute-start | bytes 786440 | tf_op jit(solution)/shard_map/ppermute | solution.py:377
  4.8 8.6 %collective-permute-start.2 = (bf16[32,16,128]{2,1,0:T(8,128)(2,1)}, bf16[32,16,128]{2,1,0:T(8,128)(2,1)S(1)}, u32[]{:S(2)}, u32[]{:S(2)}) collective-permute-start(bf16[32,16,128]{2,1,0:T(8,128)(2,1)} %raw.5), channel_id=1, source_target_pairs={{0,24},{8,16},{16,8},{24,0},{1,25},{9,17},{17,9},{25,1},{2,26},{10... | collective-permute-start | bytes 393224 | tf_op jit(solution)/shard_map/ppermute | solution.py:377
  7.2 6.4 %collective-permute-start.1 = (bf16[32,16,128]{2,1,0:T(8,128)(2,1)}, bf16[32,16,128]{2,1,0:T(8,128)(2,1)S(1)}, u32[]{:S(2)}, u32[]{:S(2)}) collective-permute-start(bf16[32,16,128]{2,1,0:T(8,128)(2,1)} %raw.5), channel_id=1, source_target_pairs={{0,16},{8,24},{16,0},{24,8},{1,17},{9,25},{17,1},{25,9},{2,18},{10... | collective-permute-start | bytes 393224 | tf_op jit(solution)/shard_map/ppermute | solution.py:377
  7.7 6.0 %collective-permute-start = (bf16[32,16,128]{2,1,0:T(8,128)(2,1)}, bf16[32,16,128]{2,1,0:T(8,128)(2,1)S(1)}, u32[]{:S(2)}, u32[]{:S(2)}) collective-permute-start(bf16[32,16,128]{2,1,0:T(8,128)(2,1)} %raw.5), channel_id=1, source_target_pairs={{0,8},{8,0},{16,24},{24,16},{1,9},{9,1},{17,25},{25,17},{2,10},{10... | collective-permute-start | bytes 393224 | tf_op jit(solution)/shard_map/ppermute | solution.py:377
  8.2 11.6 %collective-permute-start.6 = (bf16[64,16,128]{2,1,0:T(8,128)(2,1)}, bf16[64,16,128]{2,1,0:T(8,128)(2,1)S(1)}, u32[]{:S(2)}, u32[]{:S(2)}) collective-permute-start(bf16[64,16,128]{2,1,0:T(8,128)(2,1)} %raw.4), channel_id=1, source_target_pairs={{0,2},{2,0},{4,6},{6,4},{1,3},{3,1},{5,7},{7,5},{8,10},{10,8},{12,... | collective-permute-start | bytes 786440 | tf_op jit(solution)/shard_map/ppermute | solution.py:377
  9.8 1.0 %copy-start.2 = (bf16[64,32,128]{2,1,0:T(8,128)(2,1)S(1)}, bf16[64,32,128]{2,1,0:T(8,128)(2,1)}, u32[]{:S(2)}) copy-start(bf16[64,32,128]{2,1,0:T(8,128)(2,1)} %middle.5) | copy-start | bytes 1572868
  9.8 1.2 %copy-start.3 = (bf16[64,32,128]{2,1,0:T(8,128)(2,1)S(1)}, bf16[64,32,128]{2,1,0:T(8,128)(2,1)}, u32[]{:S(2)}) copy-start(bf16[64,32,128]{2,1,0:T(8,128)(2,1)} %cotangent.3) | copy-start | bytes 1572868
  9.8 1.2 %copy-start.6 = (bf16[128,128]{1,0:T(8,128)(2,1)S(1)}, bf16[128,128]{1,0:T(8,128)(2,1)}, u32[]{:S(2)}) copy-start(bf16[128,128]{1,0:T(8,128)(2,1)} %out_w.1) | copy-start | bytes 98308
  9.9 1.2 %copy-start.7 = (bf16[128,128]{1,0:T(8,128)(2,1)S(1)}, bf16[128,128]{1,0:T(8,128)(2,1)}, u32[]{:S(2)}) copy-start(bf16[128,128]{1,0:T(8,128)(2,1)} %gate_weight.3) | copy-start | bytes 98308
  11.0 2.7 %copy-start.4 = (bf16[128,256]{1,0:T(8,128)(2,1)S(1)}, bf16[128,256]{1,0:T(8,128)(2,1)}, u32[]{:S(2)}) copy-start(bf16[128,256]{1,0:T(8,128)(2,1)} %right_w.1) | copy-start | bytes 196612
  11.0 2.7 %copy-start.5 = (bf16[32,16,128]{2,1,0:T(8,128)(2,1)S(1)}, bf16[32,16,128]{2,1,0:T(8,128)(2,1)}, u32[]{:S(2)}) copy-start(bf16[32,16,128]{2,1,0:T(8,128)(2,1)} %raw.5) | copy-start | bytes 393220
  18.2 7.5 %collective-permute-start.5 = (bf16[64,16,128]{2,1,0:T(8,128)(2,1)S(1)}, bf16[64,16,128]{2,1,0:T(8,128)(2,1)S(1)}, u32[]{:S(2)}, u32[]{:S(2)}) collective-permute-start(bf16[64,16,128]{2,1,0:T(8,128)(2,1)S(1)} %forward.2._), channel_id=1, source_target_pairs={{0,2},{2,0},{4,6},{6,4},{1,3},{3,1},{5,7},{7,5},{8,10},{10,8},{12,... | collective-permute-start | bytes 786440 | tf_op jit(solution)/shard_map/ppermute | solution.py:377
  19.0 6.6 %collective-permute-start.4 = (bf16[64,16,128]{2,1,0:T(8,128)(2,1)S(1)}, bf16[64,16,128]{2,1,0:T(8,128)(2,1)S(1)}, u32[]{:S(2)}, u32[]{:S(2)}) collective-permute-start(bf16[64,16,128]{2,1,0:T(8,128)(2,1)S(1)} %forward.3), channel_id=1, source_target_pairs={{0,0},{2,4},{4,2},{6,6},{1,1},{3,5},{5,3},{7,7},{8,8},{10,12},{12,... | collective-permute-start | bytes 786440 | tf_op jit(solution)/shard_map/ppermute | solution.py:413
  30.8 26.2 %collective-permute-start.8 = (bf16[64,16,128]{2,1,0:T(8,128)(2,1)S(1)}, bf16[64,16,128]{2,1,0:T(8,128)(2,1)S(1)}, u32[]{:S(2)}, u32[]{:S(2)}) collective-permute-start(bf16[64,16,128]{2,1,0:T(8,128)(2,1)S(1)} %get-tuple-element.74.refs_6_), channel_id=1, source_target_pairs={{0,4},{2,6},{4,0},{6,2},{1,5},{3,7},{5,1},{7,3},{8,12},{10,14},{12... | collective-permute-start | bytes 786440 | tf_op jit(solution)/shard_map/ppermute | solution.py:377
  37.3 19.7 %collective-permute-start.9 = (bf16[64,16,128]{2,1,0:T(8,128)(2,1)S(1)}, bf16[64,16,128]{2,1,0:T(8,128)(2,1)S(1)}, u32[]{:S(2)}, u32[]{:S(2)}) collective-permute-start(bf16[64,16,128]{2,1,0:T(8,128)(2,1)S(1)} %get-tuple-element.75.refs_7_), channel_id=1, source_target_pairs={{0,6},{2,4},{4,2},{6,0},{1,7},{3,5},{5,3},{7,1},{8,14},{10,12},{12... | collective-permute-start | bytes 786440 | tf_op jit(solution)/shard_map/ppermute | solution.py:377
  40.8 16.7 %collective-permute-start.7 = (bf16[64,16,128]{2,1,0:T(8,128)(2,1)S(1)}, bf16[64,16,128]{2,1,0:T(8,128)(2,1)S(1)}, u32[]{:S(2)}, u32[]{:S(2)}) collective-permute-start(bf16[64,16,128]{2,1,0:T(8,128)(2,1)S(1)} %get-tuple-element.73.refs_5_), channel_id=1, source_target_pairs={{0,2},{2,0},{4,6},{6,4},{1,3},{3,1},{5,7},{7,5},{8,10},{10,8},{12,... | collective-permute-start | bytes 786440 | tf_op jit(solution)/shard_map/ppermute | solution.py:377
  45.8 11.6 %collective-permute-start.10 = (bf16[2,32,16,128]{3,2,1,0:T(8,128)(2,1)S(1)}, bf16[2,32,16,128]{3,2,1,0:T(8,128)(2,1)S(1)}, u32[]{:S(2)}, u32[]{:S(2)}) collective-permute-start(bf16[2,32,16,128]{3,2,1,0:T(8,128)(2,1)S(1)} %get-tuple-element.81.refs_9_), channel_id=1, source_target_pairs={{0,8},{8,0},{16,24},{24,16},{1,9},{9,1},{17,25},{25,17},{2,10},{10... | collective-permute-start | bytes 786440 | tf_op jit(solution)/shard_map/ppermute | solution.py:377
  50.7 4.7 %collective-permute-start.12 = (bf16[2,32,768]{2,1,0:T(8,128)(2,1)S(1)}, bf16[2,32,768]{2,1,0:T(8,128)(2,1)S(1)}, u32[]{:S(2)}, u32[]{:S(2)}) collective-permute-start(bf16[2,32,768]{2,1,0:T(8,128)(2,1)S(1)} %get-tuple-element.92._), channel_id=1, source_target_pairs={{0,8},{8,0},{16,24},{24,16},{1,9},{9,1},{17,25},{25,17},{2,10},{10... | collective-permute-start | bytes 294920 | tf_op jit(solution)/shard_map/ppermute | solution.py:377
  55.4 4.7 %collective-permute-start.13 = (bf16[1,32,768]{2,1,0:T(8,128)(2,1)S(1)}, bf16[1,32,768]{2,1,0:T(8,128)(2,1)S(1)}, u32[]{:S(2)}, u32[]{:S(2)}) collective-permute-start(bf16[1,32,768]{2,1,0:T(8,128)(2,1)S(1)} %get-tuple-element.97), channel_id=1, source_target_pairs={{0,16},{8,24},{16,0},{24,8},{1,17},{9,25},{17,1},{25,9},{2,18},{10... | collective-permute-start | bytes 147464 | tf_op jit(solution)/shard_map/ppermute | solution.py:377
  57.5 13.9 %collective-permute-start.11 = (bf16[1,32,16,128]{3,2,1,0:T(8,128)(2,1)S(1)}, bf16[1,32,16,128]{3,2,1,0:T(8,128)(2,1)S(1)}, u32[]{:S(2)}, u32[]{:S(2)}) collective-permute-start(bf16[1,32,16,128]{3,2,1,0:T(8,128)(2,1)S(1)} %get-tuple-element.83.refs_0_), channel_id=1, source_target_pairs={{0,16},{8,24},{16,0},{24,8},{1,17},{9,25},{17,1},{25,9},{2,18},{10... | collective-permute-start | bytes 393224 | tf_op jit(solution)/shard_map/ppermute | solution.py:377
  60.1 6.6 %collective-permute-start.16 = (bf16[1,32,768]{2,1,0:T(8,128)(2,1)S(1)}, bf16[1,32,768]{2,1,0:T(8,128)(2,1)S(1)}, u32[]{:S(2)}, u32[]{:S(2)}) collective-permute-start(bf16[1,32,768]{2,1,0:T(8,128)(2,1)S(1)} %combine.2.refs_0_), channel_id=1, source_target_pairs={{0,6},{2,4},{4,2},{6,0},{1,7},{3,5},{5,3},{7,1},{8,14},{10,12},{12... | collective-permute-start | bytes 147464 | tf_op jit(solution)/shard_map/ppermute | solution.py:377
  62.3 5.0 %collective-permute-start.15 = (bf16[1,32,768]{2,1,0:T(8,128)(2,1)S(1)}, bf16[1,32,768]{2,1,0:T(8,128)(2,1)S(1)}, u32[]{:S(2)}, u32[]{:S(2)}) collective-permute-start(bf16[1,32,768]{2,1,0:T(8,128)(2,1)S(1)} %combine.2.refs_0_), channel_id=1, source_target_pairs={{0,4},{2,6},{4,0},{6,2},{1,5},{3,7},{5,1},{7,3},{8,12},{10,14},{12... | collective-permute-start | bytes 147464 | tf_op jit(solution)/shard_map/ppermute | solution.py:377
  63.4 4.4 %collective-permute-start.14 = (bf16[1,32,768]{2,1,0:T(8,128)(2,1)S(1)}, bf16[1,32,768]{2,1,0:T(8,128)(2,1)S(1)}, u32[]{:S(2)}, u32[]{:S(2)}) collective-permute-start(bf16[1,32,768]{2,1,0:T(8,128)(2,1)S(1)} %combine.2.refs_0_), channel_id=1, source_target_pairs={{0,2},{2,0},{4,6},{6,4},{1,3},{3,1},{5,7},{7,5},{8,10},{10,8},{12,... | collective-permute-start | bytes 147464 | tf_op jit(solution)/shard_map/ppermute | solution.py:377
  67.8 5.1 %collective-permute-start.19 = (bf16[1,32,768]{2,1,0:T(8,128)(2,1)S(1)}, bf16[1,32,768]{2,1,0:T(8,128)(2,1)S(1)}, u32[]{:S(2)}, u32[]{:S(2)}) collective-permute-start(bf16[1,32,768]{2,1,0:T(8,128)(2,1)S(1)} %combine.3.refs_0_), channel_id=1, source_target_pairs={{0,24},{8,16},{16,8},{24,0},{1,25},{9,17},{17,9},{25,1},{2,26},{10... | collective-permute-start | bytes 147464 | tf_op jit(solution)/shard_map/ppermute | solution.py:377
  69.6 4.1 %collective-permute-start.18 = (bf16[1,32,768]{2,1,0:T(8,128)(2,1)S(1)}, bf16[1,32,768]{2,1,0:T(8,128)(2,1)S(1)}, u32[]{:S(2)}, u32[]{:S(2)}) collective-permute-start(bf16[1,32,768]{2,1,0:T(8,128)(2,1)S(1)} %combine.3.refs_0_), channel_id=1, source_target_pairs={{0,16},{8,24},{16,0},{24,8},{1,17},{9,25},{17,1},{25,9},{2,18},{10... | collective-permute-start | bytes 147464 | tf_op jit(solution)/shard_map/ppermute | solution.py:377
  70.4 4.1 %collective-permute-start.17 = (bf16[1,32,768]{2,1,0:T(8,128)(2,1)S(1)}, bf16[1,32,768]{2,1,0:T(8,128)(2,1)S(1)}, u32[]{:S(2)}, u32[]{:S(2)}) collective-permute-start(bf16[1,32,768]{2,1,0:T(8,128)(2,1)S(1)} %combine.3.refs_0_), channel_id=1, source_target_pairs={{0,8},{8,0},{16,24},{24,16},{1,9},{9,1},{17,25},{25,17},{2,10},{10... | collective-permute-start | bytes 147464 | tf_op jit(solution)/shard_map/ppermute | solution.py:377
